TPU v7x, 256 devices: a whole 4x4x8 slice. The times are simulated.
256 devices in a mesh: dp: 32 (over x_lo, z, core), section: 8 (over y, x_hi).
Axes of the slice: x: 4 (x_hi: 2, x_lo: 2; x = x_hi * 2 + x_lo), y: 4, z: 8, core: 2. Of those that a mesh axis runs over, the one named last changes fastest.
Arguments:
- first_input: bfloat16 [4, 1024, 8192], P(None, 'dp'), may hold values from -6 to 6
- example_ids: int32 [32, 4, 8], P('dp'), may hold values from 0 to 7, each once within a row
- out_store: bfloat16 [8, 256, 8, 8192], P('section', 'dp'), may hold values from -6 to 6
- in_store: bfloat16 [8, 256, 8, 8192], P('section', 'dp'), may hold values from -6 to 6
- norm_gain: float32 [8, 8192], P('section'), may hold values from 0.25 to 1.75
- adapter_in: bfloat16 [8, 8192, 128], P('section'), may hold values from -0.0625 to 0.0625
- adapter_out: bfloat16 [8, 128, 8192], P('section'), may hold values from -0.5 to 0.5
Outputs:
- grad_in: float32 [8, 8192, 128], P('section', 'dp')
- grad_out: float32 [8, 128, 8192], P('section', None, 'dp')
Inputs may be any that keep to these rules, and one draw needn't show every extreme that they name: Each row of example_ids over its last dimension is a permutation of the 8 stored examples.
All inputs are finite; a program needn't handle non-finite values.
Results may differ from a plain program's by a relative error of at most 0.0045.
Values may be sent and summed in bfloat16 or wider, within the bound.
No kernel may reach another device: no remote copies, remote signals or barrier semaphores. Data moves between devices by JAX's collectives and lax.ppermute only.
A program may use at most 64 MiB of HBM per device.

v0:
```python
import jax
import jax.numpy as jnp
from jax import lax
from jax.sharding import PartitionSpec as P


def shifted(x, axis, by):
    devices = lax.axis_size(axis)
    pairs = [(i, i + by) for i in range(devices) if 0 <= i + by < devices]
    return lax.ppermute(x, axis, pairs)


def layer(entry, gain, w_in, w_out):
    inverse = lax.rsqrt(jnp.mean(entry * entry, -1, keepdims=True) + 1e-05)
    normed = (entry * inverse * gain).astype(jnp.bfloat16)
    inner = jnp.dot(normed, w_in, preferred_element_type=jnp.float32)
    active = jax.nn.silu(inner).astype(jnp.bfloat16)
    output = entry + jnp.dot(active, w_out, preferred_element_type=jnp.float32)
    return (output, inverse, normed, inner, active)


def backward(entry, parts, grad_b, gain, w_in, w_out):
    output, inverse, normed, inner, active = parts
    grad_f = grad_b.astype(jnp.float32)
    d_act = jnp.dot(grad_b, w_out.T, preferred_element_type=jnp.float32)
    sigm = jax.nn.sigmoid(inner)
    d_inner = (d_act * sigm * (1.0 + inner * (1.0 - sigm))).astype(jnp.bfloat16)
    g_out = jnp.dot(active.T, grad_b, preferred_element_type=jnp.float32)
    g_in = jnp.dot(normed.T, d_inner, preferred_element_type=jnp.float32)
    d_norm = jnp.dot(d_inner, w_in.T, preferred_element_type=jnp.float32)
    scaled = gain * d_norm
    d_entry = (
        grad_f + inverse * scaled - entry * inverse**3 * jnp.mean(entry * scaled, -1, keepdims=True)
    )
    return (d_entry, g_in, g_out)


def body(first_input, example_ids, out_store, in_store, norm_gain, adapter_in, adapter_out):
    section = lax.axis_index("section")
    sections = lax.axis_size("section")
    micro = first_input.shape[0]
    rows = first_input.shape[1]
    width = first_input.shape[2]
    picks = rows // out_store.shape[2]
    gain = norm_gain[0]
    w_in = adapter_in[0]
    w_out = adapter_out[0]
    ticks = micro + sections - 1

    def stored_rows(store, micro_idx):
        chosen = lax.dynamic_index_in_dim(example_ids[0], micro_idx, 0, keepdims=False)[:picks]
        return store[0][chosen].reshape(rows, width).astype(jnp.float32)

    def forward_tick(tick, carry):
        received, saved = carry
        micro_idx = tick - section
        valid = (micro_idx >= 0) & (micro_idx < micro)
        clipped = jnp.clip(micro_idx, 0, micro - 1)
        start_rows = lax.dynamic_index_in_dim(first_input, clipped, 0, keepdims=False).astype(
            jnp.float32
        )
        entry = jnp.where(
            section == 0, start_rows, stored_rows(in_store, clipped) + received.astype(jnp.float32)
        )
        output = layer(entry, gain, w_in, w_out)[0]
        delta = (output - stored_rows(out_store, clipped)).astype(jnp.bfloat16)
        received = shifted(delta, "section", 1)
        before = lax.dynamic_index_in_dim(saved, clipped, 0, keepdims=False)
        saved = lax.dynamic_update_index_in_dim(saved, jnp.where(valid, entry, before), clipped, 0)
        return (received, saved)

    received = jnp.zeros((rows, width), jnp.bfloat16)
    saved = jnp.zeros((micro, rows, width), jnp.float32)
    received, saved = lax.fori_loop(0, ticks, forward_tick, (received, saved))
    acc_in = jnp.zeros(w_in.shape, jnp.float32)
    acc_out = jnp.zeros(w_out.shape, jnp.float32)

    def backward_tick(tick, carry):
        incoming, total_in, total_out = carry
        micro_idx = tick - (sections - 1 - section)
        valid = ((micro_idx >= 0) & (micro_idx < micro)).astype(jnp.float32)
        clipped = jnp.clip(micro_idx, 0, micro - 1)
        entry = lax.dynamic_index_in_dim(saved, clipped, 0, keepdims=False)
        parts = layer(entry, gain, w_in, w_out)
        grad_b = jnp.where(section == sections - 1, parts[0].astype(jnp.bfloat16), incoming)
        d_entry, g_in, g_out = backward(entry, parts, grad_b, gain, w_in, w_out)
        g_in = g_in * valid
        g_out = g_out * valid
        total_in = total_in + g_in
        total_out = total_out + g_out
        incoming = shifted(d_entry.astype(jnp.bfloat16), "section", -1)
        return (incoming, total_in, total_out)

    incoming = jnp.zeros((rows, width), jnp.bfloat16)
    incoming, acc_in, acc_out = lax.fori_loop(0, ticks, backward_tick, (incoming, acc_in, acc_out))
    acc_in, acc_out = (
        lax.psum_scatter(acc_in, "dp", scatter_dimension=0, tiled=True),
        lax.psum_scatter(acc_out, "dp", scatter_dimension=1, tiled=True),
    )
    return (acc_in[None], acc_out[None])


def solution(mesh):
    placed = (
        P(None, "dp", None),
        P("dp", None, None),
        P("section", "dp", None, None),
        P("section", "dp", None, None),
        P("section", None),
        P("section", None, None),
        P("section", None, None),
    )
    return jax.shard_map(
        body,
        mesh=mesh,
        in_specs=placed,
        out_specs=(P("section", "dp", None), P("section", None, "dp")),
        check_vma=False,
    )
```

profile of v0, /device:TPU:32, one launch (start us, length us, event | category | flops | bytes accessed | tf_op | source)
XLA Modules:
  0.0 809.6 jit_solution(15985847356473817747)
XLA Ops:
  9.7 287.6 %while.36 = (s32[]{:T(128)}, bf16[32,8192]{1,0:T(8,128)(2,1)S(1)}, f32[4,32,8192]{2,1,0:T(8,128)}, pred[]{:T(512)}, s32[]{:T(128)}, /*index=5*/bf16[4,32,8192]{2...) while((s32[]{:T(128)}, bf16[32,8192]{1,0:T(8,128)(2,1)S(1)}, ...), condition=%wide.region_2.3_spmd, body=%wide.region_0.2_spmd.sunk | while | flops 142103600 | bytes 21012244 | solution.py:74
  20.3 5.7 collective-permute-start
  31.0 5.8 collective-permute-done
  48.4 6.8 collective-permute-start
  76.6 6.6 collective-permute-start
  103.7 6.8 collective-permute-start
  130.0 6.9 collective-permute-start
  155.6 7.6 collective-permute-start
  181.0 7.6 collective-permute-start
  206.4 7.6 collective-permute-start
  231.8 7.6 collective-permute-start
  257.1 7.6 collective-permute-start
  282.5 7.6 collective-permute-start
  297.4 263.6 %while.37 = (s32[]{:T(128)}, bf16[32,8192]{1,0:T(8,128)(2,1)S(1)}, f32[8192,128]{1,0:T(8,128)}, f32[128,8192]{1,0:T(8,128)}, pred[]{:T(512)}, /*index=5*/s32[]{:...) while((s32[]{:T(128)}, bf16[32,8192]{1,0:T(8,128)(2,1)S(1)}, ...), condition=%wide.region_6.7_spmd.clone, body=%wide.region_3.6_spmd.clone.sunk | while | flops 414527584 | bytes 64153416 | solution.py:95
  313.5 6.1 collective-permute-done.1
  329.0 5.3 fusion.81
  351.2 5.3 fusion.81
  372.9 5.3 fusion.81
  395.1 5.3 fusion.81
  418.6 5.3 fusion.81
  428.9 5.1 collective-permute-done.1
  443.3 5.3 fusion.81
  453.5 6.1 collective-permute-done.1
  469.0 5.3 fusion.81
  479.2 7.3 collective-permute-done.1
  495.9 5.3 fusion.81
  506.1 7.6 collective-permute-done.1
  523.1 5.3 fusion.81
  533.3 6.2 collective-permute-done.1
  548.9 5.3 fusion.81
  561.8 119.8 %reduce-scatter.3.cloned.1.call-done = f32[256,128]{1,0:T(8,128)} async-done(((f32[8192,128]{1,0:T(8,128)}), f32[256,128]{1,0:T(8,128)}) %reduce-scatter.3.cloned.1.call-update) | async-done | bytes 131088 | tf_op jit(solution)/shard_map/reduce_scatter | solution.py:97
  681.6 121.2 %reduce-scatter.5.cloned.1.call-done = f32[128,256]{1,0:T(8,128)} async-done(((f32[128,8192]{1,0:T(8,128)}), f32[128,256]{1,0:T(8,128)}) %reduce-scatter.5.cloned.1.call-update) | async-done | bytes 131088 | tf_op jit(solution)/shard_map/reduce_scatter | solution.py:98
  (304 shorter events, 378.0 us)
Async XLA Ops:
  7.2 674.4 %reduce-scatter.3.cloned.1.call-start = ((), (), s32[]{:S(2)}) async-start(), calls=%async_computation.2 | async-start | bytes 4325376 | tf_op jit(solution)/shard_map/reduce_scatter | solution.py:97
  20.3 16.4 %collective-permute-start = (bf16[32,8192]{1,0:T(8,128)(2,1)}, bf16[32,8192]{1,0:T(8,128)(2,1)}, u32[]{:S(2)}, u32[]{:S(2)}) collective-permute-start(bf16[32,8192]{1,0:T(8,128)(2,1)} %fusion.64), channel_id=1, source_target_pairs={{0,1},{1,2},{2,3},{3,4},{4,5},{5,6},{6,7},{8,9},{9,10},{10,11},{11... | collective-permute-start | bytes 1572872 | tf_op jit(solution)/shard_map/while/body/eval_jaxpr/ppermute | solution.py:10
  48.4 16.6 %collective-permute-start = (bf16[32,8192]{1,0:T(8,128)(2,1)}, bf16[32,8192]{1,0:T(8,128)(2,1)}, u32[]{:S(2)}, u32[]{:S(2)}) collective-permute-start(bf16[32,8192]{1,0:T(8,128)(2,1)} %fusion.64), channel_id=1, source_target_pairs={{0,1},{1,2},{2,3},{3,4},{4,5},{5,6},{6,7},{8,9},{9,10},{10,11},{11... | collective-permute-start | bytes 1572872 | tf_op jit(solution)/shard_map/while/body/eval_jaxpr/ppermute | solution.py:10
  76.6 15.5 %collective-permute-start = (bf16[32,8192]{1,0:T(8,128)(2,1)}, bf16[32,8192]{1,0:T(8,128)(2,1)}, u32[]{:S(2)}, u32[]{:S(2)}) collective-permute-start(bf16[32,8192]{1,0:T(8,128)(2,1)} %fusion.64), channel_id=1, source_target_pairs={{0,1},{1,2},{2,3},{3,4},{4,5},{5,6},{6,7},{8,9},{9,10},{10,11},{11... | collective-permute-start | bytes 1572872 | tf_op jit(solution)/shard_map/while/body/eval_jaxpr/ppermute | solution.py:10
  103.7 14.7 %collective-permute-start = (bf16[32,8192]{1,0:T(8,128)(2,1)}, bf16[32,8192]{1,0:T(8,128)(2,1)}, u32[]{:S(2)}, u32[]{:S(2)}) collective-permute-start(bf16[32,8192]{1,0:T(8,128)(2,1)} %fusion.64), channel_id=1, source_target_pairs={{0,1},{1,2},{2,3},{3,4},{4,5},{5,6},{6,7},{8,9},{9,10},{10,11},{11... | collective-permute-start | bytes 1572872 | tf_op jit(solution)/shard_map/while/body/eval_jaxpr/ppermute | solution.py:10
  130.0 14.0 %collective-permute-start = (bf16[32,8192]{1,0:T(8,128)(2,1)}, bf16[32,8192]{1,0:T(8,128)(2,1)}, u32[]{:S(2)}, u32[]{:S(2)}) collective-permute-start(bf16[32,8192]{1,0:T(8,128)(2,1)} %fusion.64), channel_id=1, source_target_pairs={{0,1},{1,2},{2,3},{3,4},{4,5},{5,6},{6,7},{8,9},{9,10},{10,11},{11... | collective-permute-start | bytes 1572872 | tf_op jit(solution)/shard_map/while/body/eval_jaxpr/ppermute | solution.py:10
  155.6 13.9 %collective-permute-start = (bf16[32,8192]{1,0:T(8,128)(2,1)}, bf16[32,8192]{1,0:T(8,128)(2,1)}, u32[]{:S(2)}, u32[]{:S(2)}) collective-permute-start(bf16[32,8192]{1,0:T(8,128)(2,1)} %fusion.64), channel_id=1, source_target_pairs={{0,1},{1,2},{2,3},{3,4},{4,5},{5,6},{6,7},{8,9},{9,10},{10,11},{11... | collective-permute-start | bytes 1572872 | tf_op jit(solution)/shard_map/while/body/eval_jaxpr/ppermute | solution.py:10
  181.0 13.8 %collective-permute-start = (bf16[32,8192]{1,0:T(8,128)(2,1)}, bf16[32,8192]{1,0:T(8,128)(2,1)}, u32[]{:S(2)}, u32[]{:S(2)}) collective-permute-start(bf16[32,8192]{1,0:T(8,128)(2,1)} %fusion.64), channel_id=1, source_target_pairs={{0,1},{1,2},{2,3},{3,4},{4,5},{5,6},{6,7},{8,9},{9,10},{10,11},{11... | collective-permute-start | bytes 1572872 | tf_op jit(solution)/shard_map/while/body/eval_jaxpr/ppermute | solution.py:10
  206.4 13.8 %collective-permute-start = (bf16[32,8192]{1,0:T(8,128)(2,1)}, bf16[32,8192]{1,0:T(8,128)(2,1)}, u32[]{:S(2)}, u32[]{:S(2)}) collective-permute-start(bf16[32,8192]{1,0:T(8,128)(2,1)} %fusion.64), channel_id=1, source_target_pairs={{0,1},{1,2},{2,3},{3,4},{4,5},{5,6},{6,7},{8,9},{9,10},{10,11},{11... | collective-permute-start | bytes 1572872 | tf_op jit(solution)/shard_map/while/body/eval_jaxpr/ppermute | solution.py:10
  231.8 13.8 %collective-permute-start = (bf16[32,8192]{1,0:T(8,128)(2,1)}, bf16[32,8192]{1,0:T(8,128)(2,1)}, u32[]{:S(2)}, u32[]{:S(2)}) collective-permute-start(bf16[32,8192]{1,0:T(8,128)(2,1)} %fusion.64), channel_id=1, source_target_pairs={{0,1},{1,2},{2,3},{3,4},{4,5},{5,6},{6,7},{8,9},{9,10},{10,11},{11... | collective-permute-start | bytes 1572872 | tf_op jit(solution)/shard_map/while/body/eval_jaxpr/ppermute | solution.py:10
  257.1 13.8 %collective-permute-start = (bf16[32,8192]{1,0:T(8,128)(2,1)}, bf16[32,8192]{1,0:T(8,128)(2,1)}, u32[]{:S(2)}, u32[]{:S(2)}) collective-permute-start(bf16[32,8192]{1,0:T(8,128)(2,1)} %fusion.64), channel_id=1, source_target_pairs={{0,1},{1,2},{2,3},{3,4},{4,5},{5,6},{6,7},{8,9},{9,10},{10,11},{11... | collective-permute-start | bytes 1572872 | tf_op jit(solution)/shard_map/while/body/eval_jaxpr/ppermute | solution.py:10
  282.5 13.8 %collective-permute-start = (bf16[32,8192]{1,0:T(8,128)(2,1)}, bf16[32,8192]{1,0:T(8,128)(2,1)}, u32[]{:S(2)}, u32[]{:S(2)}) collective-permute-start(bf16[32,8192]{1,0:T(8,128)(2,1)} %fusion.64), channel_id=1, source_target_pairs={{0,1},{1,2},{2,3},{3,4},{4,5},{5,6},{6,7},{8,9},{9,10},{10,11},{11... | collective-permute-start | bytes 1572872 | tf_op jit(solution)/shard_map/while/body/eval_jaxpr/ppermute | solution.py:10
  297.4 3.3 copy-start.1
  305.5 14.1 %collective-permute-start.1 = (bf16[32,8192]{1,0:T(8,128)(2,1)}, bf16[32,8192]{1,0:T(8,128)(2,1)S(1)}, u32[]{:S(2)}, u32[]{:S(2)}) collective-permute-start(bf16[32,8192]{1,0:T(8,128)(2,1)} %fusion.80), channel_id=1, source_target_pairs={{1,0},{2,1},{3,2},{4,3},{5,4},{6,5},{7,6},{9,8},{10,9},{11,10},{12... | collective-permute-start | bytes 1572872 | tf_op jit(solution)/shard_map/while/body/eval_jaxpr/ppermute | solution.py:10
  319.6 3.3 copy-start.1
  327.7 14.1 %collective-permute-start.1 = (bf16[32,8192]{1,0:T(8,128)(2,1)}, bf16[32,8192]{1,0:T(8,128)(2,1)S(1)}, u32[]{:S(2)}, u32[]{:S(2)}) collective-permute-start(bf16[32,8192]{1,0:T(8,128)(2,1)} %fusion.80), channel_id=1, source_target_pairs={{1,0},{2,1},{3,2},{4,3},{5,4},{6,5},{7,6},{9,8},{10,9},{11,10},{12... | collective-permute-start | bytes 1572872 | tf_op jit(solution)/shard_map/while/body/eval_jaxpr/ppermute | solution.py:10
  341.8 3.3 copy-start.1
  349.9 13.7 %collective-permute-start.1 = (bf16[32,8192]{1,0:T(8,128)(2,1)}, bf16[32,8192]{1,0:T(8,128)(2,1)S(1)}, u32[]{:S(2)}, u32[]{:S(2)}) collective-permute-start(bf16[32,8192]{1,0:T(8,128)(2,1)} %fusion.80), channel_id=1, source_target_pairs={{1,0},{2,1},{3,2},{4,3},{5,4},{6,5},{7,6},{9,8},{10,9},{11,10},{12... | collective-permute-start | bytes 1572872 | tf_op jit(solution)/shard_map/while/body/eval_jaxpr/ppermute | solution.py:10
  363.5 3.3 copy-start.1
  371.6 14.1 %collective-permute-start.1 = (bf16[32,8192]{1,0:T(8,128)(2,1)}, bf16[32,8192]{1,0:T(8,128)(2,1)S(1)}, u32[]{:S(2)}, u32[]{:S(2)}) collective-permute-start(bf16[32,8192]{1,0:T(8,128)(2,1)} %fusion.80), channel_id=1, source_target_pairs={{1,0},{2,1},{3,2},{4,3},{5,4},{6,5},{7,6},{9,8},{10,9},{11,10},{12... | collective-permute-start | bytes 1572872 | tf_op jit(solution)/shard_map/while/body/eval_jaxpr/ppermute | solution.py:10
  385.7 3.3 copy-start.1
  393.8 15.5 %collective-permute-start.1 = (bf16[32,8192]{1,0:T(8,128)(2,1)}, bf16[32,8192]{1,0:T(8,128)(2,1)S(1)}, u32[]{:S(2)}, u32[]{:S(2)}) collective-permute-start(bf16[32,8192]{1,0:T(8,128)(2,1)} %fusion.80), channel_id=1, source_target_pairs={{1,0},{2,1},{3,2},{4,3},{5,4},{6,5},{7,6},{9,8},{10,9},{11,10},{12... | collective-permute-start | bytes 1572872 | tf_op jit(solution)/shard_map/while/body/eval_jaxpr/ppermute | solution.py:10
  417.3 16.6 %collective-permute-start.1 = (bf16[32,8192]{1,0:T(8,128)(2,1)}, bf16[32,8192]{1,0:T(8,128)(2,1)S(1)}, u32[]{:S(2)}, u32[]{:S(2)}) collective-permute-start(bf16[32,8192]{1,0:T(8,128)(2,1)} %fusion.80), channel_id=1, source_target_pairs={{1,0},{2,1},{3,2},{4,3},{5,4},{6,5},{7,6},{9,8},{10,9},{11,10},{12... | collective-permute-start | bytes 1572872 | tf_op jit(solution)/shard_map/while/body/eval_jaxpr/ppermute | solution.py:10
  433.9 3.3 copy-start.1
  442.0 17.7 %collective-permute-start.1 = (bf16[32,8192]{1,0:T(8,128)(2,1)}, bf16[32,8192]{1,0:T(8,128)(2,1)S(1)}, u32[]{:S(2)}, u32[]{:S(2)}) collective-permute-start(bf16[32,8192]{1,0:T(8,128)(2,1)} %fusion.80), channel_id=1, source_target_pairs={{1,0},{2,1},{3,2},{4,3},{5,4},{6,5},{7,6},{9,8},{10,9},{11,10},{12... | collective-permute-start | bytes 1572872 | tf_op jit(solution)/shard_map/while/body/eval_jaxpr/ppermute | solution.py:10
  459.6 3.3 copy-start.1
  467.7 18.8 %collective-permute-start.1 = (bf16[32,8192]{1,0:T(8,128)(2,1)}, bf16[32,8192]{1,0:T(8,128)(2,1)S(1)}, u32[]{:S(2)}, u32[]{:S(2)}) collective-permute-start(bf16[32,8192]{1,0:T(8,128)(2,1)} %fusion.80), channel_id=1, source_target_pairs={{1,0},{2,1},{3,2},{4,3},{5,4},{6,5},{7,6},{9,8},{10,9},{11,10},{12... | collective-permute-start | bytes 1572872 | tf_op jit(solution)/shard_map/while/body/eval_jaxpr/ppermute | solution.py:10
  486.5 3.3 copy-start.1
  494.6 19.1 %collective-permute-start.1 = (bf16[32,8192]{1,0:T(8,128)(2,1)}, bf16[32,8192]{1,0:T(8,128)(2,1)S(1)}, u32[]{:S(2)}, u32[]{:S(2)}) collective-permute-start(bf16[32,8192]{1,0:T(8,128)(2,1)} %fusion.80), channel_id=1, source_target_pairs={{1,0},{2,1},{3,2},{4,3},{5,4},{6,5},{7,6},{9,8},{10,9},{11,10},{12... | collective-permute-start | bytes 1572872 | tf_op jit(solution)/shard_map/while/body/eval_jaxpr/ppermute | solution.py:10
  521.8 17.7 %collective-permute-start.1 = (bf16[32,8192]{1,0:T(8,128)(2,1)}, bf16[32,8192]{1,0:T(8,128)(2,1)S(1)}, u32[]{:S(2)}, u32[]{:S(2)}) collective-permute-start(bf16[32,8192]{1,0:T(8,128)(2,1)} %fusion.80), channel_id=1, source_target_pairs={{1,0},{2,1},{3,2},{4,3},{5,4},{6,5},{7,6},{9,8},{10,9},{11,10},{12... | collective-permute-start | bytes 1572872 | tf_op jit(solution)/shard_map/while/body/eval_jaxpr/ppermute | solution.py:10
  547.6 13.4 %collective-permute-start.1 = (bf16[32,8192]{1,0:T(8,128)(2,1)}, bf16[32,8192]{1,0:T(8,128)(2,1)S(1)}, u32[]{:S(2)}, u32[]{:S(2)}) collective-permute-start(bf16[32,8192]{1,0:T(8,128)(2,1)} %fusion.80), channel_id=1, source_target_pairs={{1,0},{2,1},{3,2},{4,3},{5,4},{6,5},{7,6},{9,8},{10,9},{11,10},{12... | collective-permute-start | bytes 1572872 | tf_op jit(solution)/shard_map/while/body/eval_jaxpr/ppermute | solution.py:10
  561.0 241.8 %reduce-scatter.5.cloned.1.call-start = ((), (), s32[]{:S(2)}) async-start(), calls=%async_computation.3 | async-start | bytes 4325376 | tf_op jit(solution)/shard_map/reduce_scatter | solution.py:98
  (16 other events, 44.4 us)
Sparse Core Ops, SparseCore 0:
  561.1 120.3 reduce-scatter.2
  684.7 118.0 reduce-scatter.4
where the time goes:
time: 818 us; the launch traced here: 810 us
  waiting for transfers between devices  322 us (39%)
  matrix products  211 us (26%)
  local copies, waits for them, and re-layouts  96 us (12%)
  starting transfers between devices  92.4 us (11%)
  other arithmetic  73.4 us (9%)
  between operations  14.1 us (2%)
    reduce_scatter x1, waiting for transfers between devices, body(): lax.psum_scatter(acc_out, 'dp', scatter_dimension=1, tiled=True)  121 us
    reduce_scatter x1, waiting for transfers between devices, body(): lax.psum_scatter(acc_in, 'dp', scatter_dimension=0, tiled=True)  120 us
    ppermute x22, starting transfers between devices, shifted(): return lax.ppermute(x, axis, pairs)  92.3 us
    ppermute x22, waiting for transfers between devices, shifted(): return lax.ppermute(x, axis, pairs)  80 us
    dot_general x22, matrix products, layer(): output = entry + jnp.dot(active, w_out, preferred_element_type=jnp.float32)  64.1 us
    dot_general x11, matrix products, backward(): g_in = jnp.dot(normed.T, d_inner, preferred_element_type=jnp.float32)  57.2 us
    dot_general x11, matrix products, backward(): g_out = jnp.dot(active.T, grad_b, preferred_element_type=jnp.float32)  51.7 us
    gather x22, local copies, waits for them, and re-layouts, stored_rows(): return store[0][chosen].reshape(rows, width).astype(jnp.float32)  48.9 us
  transfers between devices with their start and end apart: 24, of which 24 were waited for; matrix products, arithmetic and copies ran while one was open for 20% of the time, Pallas kernels for 0%

commit v1 on v0

v1 whole, which is shorter than its diff:
```python
import functools

import jax
import jax.numpy as jnp
from jax import lax
from jax.experimental import pallas as pl
from jax.experimental.pallas import tpu as pltpu
from jax.sharding import Mesh, PartitionSpec as P

F32 = jnp.float32
BF16 = jnp.bfloat16
EPS = 1e-05
PLANE = ("xl", "y", "xh")
SECTION = ("y", "xh")
SWAP = [(0, 1), (1, 0)]
NS = 8
R = 128
TOK = 8
MIC = 4
BLK = 128
PROJ = 29
NORM = 36
START = 37
GRAM = 45
LANES = 81 * BLK


def gram_at(t):
    return sum(NS - i for i in range(t))


def proj_at(s):
    return s * (s - 1) // 2


def dot_t(a, b):
    return lax.dot_general(a, b, (((1,), (1,)), ((), ())), preferred_element_type=F32)


def dot(a, b):
    return jnp.dot(a, b, preferred_element_type=F32)


def split(x):
    high = x.astype(BF16)
    return high, (x - high.astype(F32)).astype(BF16)


def project_kernel(core_ref, got_ref, out_w_ref, in_w_ref, start_ref, send_ref):
    cols = got_ref.shape[2]
    first = got_ref[:, 192:224, :].astype(F32).reshape(16, MIC, TOK, cols)
    running = None
    lane = lax.broadcasted_iota(jnp.int32, (R, BLK), 1)
    norms = jnp.zeros((R, BLK), F32)
    for s in range(1, NS):
        step = jnp.concatenate(
            [
                got_ref[x * NS + s, 0:64, :].astype(F32)
                - got_ref[x * NS + s - 1, 64:128, :].astype(F32)
                for x in range(2)
            ],
            0,
        )
        running = step if running is None else running + step
        rounded = running.astype(BF16)
        count = s if s < NS - 1 else NS
        at = proj_at(s) * BLK
        send_ref[:, at : at + count * BLK] = dot_t(
            rounded, out_w_ref[0:count].reshape(count * R, cols)
        ).astype(BF16)
        at = (PROJ + s - 1) * BLK
        send_ref[:, at : at + BLK] = dot(rounded, in_w_ref[s]).astype(BF16)
        for m in range(MIC):
            part = jnp.sum(
                running * (running + 2.0 * first[:, m].reshape(R, cols)), -1, keepdims=True
            )
            norms = jnp.where(lane == m * NS + s, part, norms)
    high, low = split(norms)
    merged = jnp.where(lane < 32, high.astype(F32), pltpu.roll(low.astype(F32), 32, 1))
    send_ref[:, NORM * BLK : (NORM + 1) * BLK] = merged.astype(BF16)
    send_ref[:, START * BLK : GRAM * BLK] = start_ref[...]

    @pl.when(core_ref[0] == 0)
    def _():
        for t in range(NS):
            at = (GRAM + gram_at(t)) * BLK
            send_ref[:, at : at + (NS - t) * BLK] = dot_t(
                out_w_ref[t], out_w_ref[t:NS].reshape((NS - t) * R, cols)
            ).astype(BF16)

    @pl.when(core_ref[0] != 0)
    def _():
        for t in range(NS):
            for s in range(t, NS):
                at = (GRAM + gram_at(t) + s - t) * BLK
                send_ref[:, at : at + BLK] = dot(out_w_ref[t], in_w_ref[s]).astype(BF16)


def chain_kernel(width, proj_ref, norm_ref, start_ref, mask_ref, oo_ref, oi_ref, send_ref):
    rows = MIC * TOK

    def spread(at, count=1):
        block = proj_ref[:, at * BLK : (at + count) * BLK]
        return jnp.concatenate([block] * MIC, 0)

    def pair(ref, t, s, count=1):
        at = (gram_at(t) + s - t) * BLK
        return ref[:, at : at + count * BLK]

    mask = mask_ref[:, 0:1]
    start_in = [start_ref[s, :, 0:R] for s in range(NS)]
    start_out = [start_ref[s, :, R : 2 * R] for s in range(NS)]
    run_out = [start_out[t] for t in range(NS)]
    run_in = [start_in[t] for t in range(NS)]
    inners, inverses, actives, crossed = [], [], [], []
    for s in range(NS):
        norm = norm_ref[:, s : s + 1]
        entry_out = []
        inner = run_in[s]
        if s > 0:
            inner = inner + spread(PROJ + s - 1)
            total = jnp.zeros((rows, R), F32)
            for t in range(s):
                base = spread(proj_at(s) + t)
                full = base + run_out[t]
                entry_out.append(full)
                total = total + actives[t].astype(F32) * (full + base + start_out[t])
            norm = norm + jnp.sum(total, -1, keepdims=True)
        inverse = lax.rsqrt(jnp.maximum(norm, 0.0) * (1.0 / width) + EPS)
        inner = inner * inverse
        active = (inner * jax.nn.sigmoid(inner) * mask).astype(BF16)
        inners.append(inner)
        inverses.append(inverse)
        actives.append(active)
        crossed.append(entry_out)
        send_ref[:, s * R : (s + 1) * R] = active
        grown = dot(active, pair(oo_ref, s, s, NS - s))
        for t in range(NS):
            if t >= s:
                run_out[t] = run_out[t] + grown[:, (t - s) * R : (t - s + 1) * R]
            else:
                run_out[t] = run_out[t] + dot_t(active, pair(oo_ref, t, s))
        if s < NS - 1:
            grown = dot(active, pair(oi_ref, s, s + 1, NS - 1 - s))
            for t in range(s + 1, NS):
                run_in[t] = run_in[t] + grown[:, (t - s - 1) * R : (t - s) * R]
    grads = [run_out[t] + spread(proj_at(NS - 1) + t) for t in range(NS)]
    lane = lax.broadcasted_iota(jnp.int32, (rows, BLK), 1)
    scalars = jnp.zeros((rows, BLK), F32)
    for s in range(NS - 1, -1, -1):
        inner = inners[s]
        sigm = jax.nn.sigmoid(inner)
        d_inner = (grads[s] * sigm * (1.0 + inner * (1.0 - sigm)) * mask).astype(BF16)
        send_ref[:, (NS + s) * R : (NS + s + 1) * R] = d_inner
        d_wide = d_inner.astype(F32)
        inverse = inverses[s]
        scale = (
            inverse * inverse * jnp.sum(d_wide * inner, -1, keepdims=True) * (1.0 / width)
        )
        for t in range(s):
            grads[t] = (
                grads[t] + inverse * dot_t(d_inner, pair(oi_ref, t, s)) - scale * crossed[s][t]
            )
        high, low = split(inverse)
        scalars = jnp.where(lane == s, high.astype(F32), scalars)
        scalars = jnp.where(lane == NS + s, low.astype(F32), scalars)
        high, low = split(scale)
        scalars = jnp.where(lane == 2 * NS + s, high.astype(F32), scalars)
        scalars = jnp.where(lane == 3 * NS + s, low.astype(F32), scalars)
    send_ref[:, 2 * NS * R : 2 * NS * R + BLK] = scalars.astype(BF16)


def grads_kernel(got_ref, out_w_ref, in_w_ref, chain_ref, g_in_ref, g_out_ref, kept_ref):
    cols = got_ref.shape[2]
    rows = 16 * MIC * TOK
    scalars = chain_ref[:, 2 * NS * R : 2 * NS * R + BLK].astype(F32)
    inverses = [scalars[:, s : s + 1] + scalars[:, NS + s : NS + s + 1] for s in range(NS)]
    scales = [
        scalars[:, 2 * NS + s : 2 * NS + s + 1] + scalars[:, 3 * NS + s : 3 * NS + s + 1]
        for s in range(NS)
    ]

    def active(s):
        return chain_ref[:, s * R : (s + 1) * R]

    def d_inner(s):
        return chain_ref[:, (NS + s) * R : (NS + s + 1) * R]

    def dot_rows(a, b):
        return lax.dot_general(a, b, (((0,), (0,)), ((), ())), preferred_element_type=F32)

    entry = got_ref[:, 192:224, :].astype(F32).reshape(rows, cols)
    for s in range(NS):
        if s > 0:
            step = jnp.concatenate(
                [
                    got_ref[x * NS + s, 0:64, :].astype(F32)
                    - got_ref[x * NS + s - 1, 64:128, :].astype(F32)
                    for x in range(2)
                ],
                0,
            )
            step = jnp.broadcast_to(step.reshape(16, 1, TOK, cols), (16, MIC, TOK, cols))
            entry = entry + step.reshape(rows, cols)
        kept_ref[s] = entry
        normed = (entry * inverses[s]).astype(BF16)
        g_in_ref[0, s] = dot_rows(normed, d_inner(s))
        entry = entry + dot(active(s), out_w_ref[s])
    grad = entry
    for s in range(NS - 1, -1, -1):
        g_out_ref[0, s] = dot_rows(active(s), grad.astype(BF16))
        if s > 0:
            grad = grad + inverses[s] * dot_t(d_inner(s), in_w_ref[s]) - scales[s] * kept_ref[s]


def vmem(n):
    return [pl.BlockSpec(memory_space=pltpu.VMEM)] * n


PARAMS = dict(vmem_limit_bytes=56 * 1024 * 1024)


def body(first_input, example_ids, out_store, in_store, norm_gain, adapter_in, adapter_out):
    width = first_input.shape[2]
    cols = width // 16
    half = cols // 2
    core = lax.axis_index("c")
    xl = lax.axis_index("xl")
    z = lax.axis_index("z")
    section = lax.axis_index(SECTION)
    quarter = xl * 2 + core
    ids = example_ids[0]
    start = first_input.reshape(MIC, 4, TOK, width)
    w_in = adapter_in[0]
    w_out = adapter_out[0]
    gained = (norm_gain[0][:, None] * w_in.astype(F32)).astype(BF16)

    picked = ids[:, :4]
    mine = picked == section
    own = jnp.zeros((MIC, TOK, width), BF16)
    for j in range(4):
        own = jnp.where(mine[:, j, None, None], start[:, j], own)
    own_norm = jnp.sum(jnp.square(own.astype(F32)), -1)
    mask = jnp.any(mine, 1).astype(F32)

    in_part = lax.dynamic_index_in_dim(gained.reshape(16, 4, R, R), quarter, 1, keepdims=False)
    in_part = in_part.reshape(16, 4, 32, R).transpose(2, 0, 1, 3).reshape(32, width)
    out_part = lax.dynamic_slice_in_dim(w_out, quarter * 32, 32, 0)
    send = jnp.concatenate(
        [
            in_store.reshape(64, width),
            out_store.reshape(64, width),
            out_part,
            in_part,
            own.reshape(32, width),
        ],
        0,
    )
    send = send.reshape(224, 16, cols).transpose(1, 0, 2)
    got = lax.all_to_all(send, PLANE, 0, 0, tiled=True)

    weights = got[:, 128:192]
    other = lax.ppermute(weights, "c", SWAP)
    both = jnp.stack(
        [jnp.where(core == 0, weights, other), jnp.where(core == 0, other, weights)]
    ).reshape(2, 2, NS, 64, cols)
    out_w = both[:, :, :, :32].transpose(2, 1, 0, 3, 4).reshape(NS, R, cols)
    in_w = (
        both[:, :, :, 32:]
        .reshape(2, 2, NS, 32, 4, R)
        .transpose(2, 1, 0, 4, 3, 5)
        .reshape(NS, cols, R)
    )

    flat = first_input.reshape(MIC * 32, width)
    start_proj = jnp.concatenate([dot(flat, gained), dot_t(flat, w_out)], 1)
    start_proj = start_proj.reshape(MIC, 4, TOK, 2 * R)
    placed = jnp.zeros((MIC, NS, TOK, 2 * R), F32)
    for j in range(4):
        here = picked[:, j, None] == jnp.arange(NS)[None, :]
        placed = jnp.where(here[:, :, None, None], start_proj[:, j, None], placed)
    placed = placed.transpose(1, 2, 0, 3).reshape(NS * TOK, MIC * 2 * R).astype(BF16)
    placed = jnp.concatenate([placed, placed], 0)

    parts = pl.pallas_call(
        project_kernel,
        out_shape=jax.ShapeDtypeStruct((R, LANES), BF16),
        in_specs=[pl.BlockSpec(memory_space=pltpu.SMEM)] + vmem(4),
        out_specs=pl.BlockSpec(memory_space=pltpu.VMEM),
        compiler_params=pltpu.CompilerParams(**PARAMS),
        name="project",
    )(core.reshape(1), got, out_w, in_w, placed)
    parts = lax.all_to_all(parts.reshape(16, TOK, LANES), PLANE, 0, 0, tiled=True)

    gram = jnp.sum(parts[:, :, GRAM * BLK :].astype(F32), 0).astype(BF16)
    gram = lax.all_to_all(
        jnp.broadcast_to(gram, (16,) + gram.shape), PLANE, 0, 0, tiled=True
    ).reshape(R, 36 * BLK)
    other = lax.ppermute(gram, "c", SWAP)
    oo = jnp.where(core == 0, gram, other)
    oi = jnp.where(core == 0, other, gram)

    proj = jnp.sum(parts[:, :, : START * BLK].astype(F32), 0)
    norm = proj[:, NORM * BLK : NORM * BLK + 64].reshape(TOK, 2, MIC, NS).sum(1)
    norm = norm.transpose(1, 0, 2) + own_norm[:, :, None]
    norm = jnp.pad(norm.reshape(MIC * TOK, NS), ((0, 0), (0, BLK - NS)))
    starts = lax.dynamic_slice_in_dim(parts[:, :, START * BLK : GRAM * BLK], xl * NS, NS, 0)
    starts = starts.reshape(NS, TOK, MIC, 2 * R).transpose(0, 2, 1, 3)
    starts = starts.reshape(NS, MIC * TOK, 2 * R).astype(F32)
    mask = jnp.broadcast_to(mask[:, None, None], (MIC, TOK, BLK)).reshape(MIC * TOK, BLK)
    latent = pl.pallas_call(
        functools.partial(chain_kernel, width),
        out_shape=jax.ShapeDtypeStruct((MIC * TOK, 17 * BLK), BF16),
        in_specs=vmem(6),
        out_specs=pl.BlockSpec(memory_space=pltpu.VMEM),
        compiler_params=pltpu.CompilerParams(**PARAMS),
        name="chain",
    )(proj, norm, starts, mask, oo, oi)

    latent = lax.all_to_all(
        jnp.broadcast_to(latent, (16,) + latent.shape), PLANE, 0, 0, tiled=True
    ).reshape(16 * MIC * TOK, 17 * BLK)

    g_in, g_out = pl.pallas_call(
        grads_kernel,
        grid=(2,),
        out_shape=(
            jax.ShapeDtypeStruct((2, NS, half, R), F32),
            jax.ShapeDtypeStruct((2, NS, R, half), F32),
        ),
        in_specs=[
            pl.BlockSpec((16, 224, half), lambda i: (0, 0, i)),
            pl.BlockSpec((NS, R, half), lambda i: (0, 0, i)),
            pl.BlockSpec((NS, half, R), lambda i: (0, i, 0)),
            pl.BlockSpec((16 * MIC * TOK, 17 * BLK), lambda i: (0, 0)),
        ],
        out_specs=(
            pl.BlockSpec((1, NS, half, R), lambda i: (i, 0, 0, 0)),
            pl.BlockSpec((1, NS, R, half), lambda i: (i, 0, 0, 0)),
        ),
        scratch_shapes=[pltpu.VMEM((NS, 16 * MIC * TOK, half), F32)],
        compiler_params=pltpu.CompilerParams(**PARAMS),
        name="grads",
    )(got, out_w, in_w, latent)

    def keep(x):
        return lax.dynamic_index_in_dim(x, core, 0, keepdims=False)

    def give(x):
        return lax.dynamic_index_in_dim(x, 1 - core, 0, keepdims=False).astype(BF16)

    sent = jnp.concatenate(
        [give(g_in), give(g_out).reshape(NS, R, 2, BLK).transpose(0, 2, 1, 3).reshape(NS, half, R)],
        1,
    )
    kept = jnp.concatenate(
        [keep(g_in), keep(g_out).reshape(NS, R, 2, BLK).transpose(0, 2, 1, 3).reshape(NS, half, R)],
        1,
    )
    total = (kept + lax.ppermute(sent, "c", SWAP).astype(F32)).astype(BF16)
    total = lax.all_to_all(total, "z", 0, 0, tiled=True)
    total = jnp.sum(total.astype(F32), 0)
    turned = [(a * NS + b, b * NS + a) for a in range(NS) for b in range(NS)]
    total = lax.ppermute(total, ("z",) + SECTION, turned)
    block = (xl * NS + z) * 2 + core
    gain = lax.dynamic_slice_in_dim(norm_gain[0], block * half, half, 0)
    grad_in = total[:half] * gain[:, None]
    grad_out = total[half:].reshape(2, R, BLK).transpose(1, 0, 2).reshape(R, half)
    return (grad_in[None], grad_out[None])


def solution(mesh):
    fine = Mesh(mesh.devices.reshape(2, 8, 2, 4, 2), ("xl", "z", "c", "y", "xh"))
    dp = ("xl", "z", "c")
    placed = (
        P(None, dp, None),
        P(dp, None, None),
        P(SECTION, dp, None, None),
        P(SECTION, dp, None, None),
        P(SECTION, None),
        P(SECTION, None, None),
        P(SECTION, None, None),
    )
    return jax.shard_map(
        body,
        mesh=fine,
        in_specs=placed,
        out_specs=(P(SECTION, dp, None), P(SECTION, None, dp)),
        check_vma=False,
    )
```

time: 818 us -> 321 us (0.39)
  the two profiles are of different devices: /device:TPU:32 before, /device:TPU:31 now
where the time goes in v1:
time: 321 us; the launch traced here: 320 us
  waiting for transfers between devices  122 us (38%)
  blocking collectives  94.4 us (29%)
  local copies, waits for them, and re-layouts  31.9 us (10%)
  Pallas kernels  26.1 us (8%)
  starting transfers between devices  21.4 us (7%)
  other arithmetic  19.2 us (6%)
  matrix products  4.41 us (1%)
    all_to_all x1, waiting for transfers between devices, body(): got = lax.all_to_all(send, PLANE, 0, 0, tiled=True)  53.9 us
    all_to_all x1, waiting for transfers between devices, body(): lax.all_to_all(jnp.broadcast_to(latent, (16,) + latent.shape), PLANE, 0,...  37.6 us
    all_to_all x1, blocking collectives, body(): total = lax.all_to_all(total, 'z', 0, 0, tiled=True)  37.2 us
    all_to_all x1, blocking collectives, body(): lax.all_to_all(parts.reshape(16, TOK, LANES), PLANE, 0, 0, tiled=True)  36.4 us
    ppermute x1, waiting for transfers between devices, body(): total = lax.ppermute(total, ('z',) + SECTION, turned)  29.2 us
    all_to_all x1, blocking collectives, body(): lax.all_to_all(jnp.broadcast_to(gram, (16,) + gram.shape), PLANE, 0, 0, t...  20.8 us
    unnamed x47, local copies, waits for them, and re-layouts  13.4 us
    pallas_call x1, Pallas kernels, body(): pl.pallas_call(grads_kernel, grid=(2,), out_shape=(jax.ShapeDtypeStruct((...  11.6 us
  transfers between devices with their start and end apart: 6, of which 4 were waited for; matrix products, arithmetic and copies ran while one was open for 4% of the time, Pallas kernels for 0%

profile of v1, /device:TPU:31, one launch (start us, length us, event | category | flops | bytes accessed | tf_op | source)
XLA Modules:
  0.0 320.2 jit_solution(18421025869330304575)
XLA Ops:
  0.7 1.7 copy.105
  2.4 1.6 copy_dynamic-update-slice_fusion.1
  6.2 2.5 convert.12
  8.6 1.7 fusion.21
  15.8 1.6 copy_dynamic-update-slice_fusion
  18.5 1.7 fusion.12
  21.0 2.0 fusion.18
  23.0 6.5 %all-to-all-start = ((bf16[16,224,512]{2,1,0:T(8,128)(2,1)}), bf16[16,224,512]{2,1,0:T(8,128)(2,1)}, u32[]{:S(2)}, u32[]{:S(2)}) async-start(bf16[16,224,512]{2,1,0:T(8,128)(2,1)} %bitcast.153), calls=%async_computation | async-start | bytes 7340032 | tf_op jit(solution)/shard_map/all_to_all | solution.py:260
  29.5 2.5 fusion.4
  32.3 2.0 fusion.7
  34.3 53.9 %all-to-all-done.got_ref = bf16[16,224,512]{2,1,0:T(8,128)(2,1)} async-done(((bf16[16,224,512]{2,1,0:T(8,128)(2,1)}), bf16[16,224,512]{2,1,0:T(8,128)(2,1)}, u32[]{:S(2)}, u32[]{:S(2)}) %all-to-all-start) | async-done | bytes 3670048 | tf_op jit(solution)/shard_map/all_to_all | solution.py:260
  88.2 1.3 slice.124
  89.6 2.0 collective-permute-start
  93.8 1.4 broadcast_select_fusion.2
  97.9 7.8 %project.1 = bf16[128,10368]{1,0:T(8,128)(2,1)} custom-call(s32[1]{0:T(128)} %bitcast.13.core_ref, bf16[16,224,512]{2,1,0:T(8,128)(2,1)} %all-to-all-done.got_ref, bf16[8,128,512]{2,1,0:T(8,128)(2,1)} %bitcast.149, bf16[8,512,128]{2,1,0:T(8,128)(2,1)} %bitcast.151, bf16[128,1024]{1,0:T(8,128)(2,1)} %pad_maximum_fusion.2.start_ref), custom_call_target="tpu_custom_call" | custom-call | tf_op jit(solution)/shard_map/project/pallas_call | solution.py:285
  105.7 36.4 %all_to_all.25 = bf16[16,8,10368]{2,1,0:T(8,128)(2,1)S(1)} all-to-all(bf16[16,8,10368]{2,1,0:T(8,128)(2,1)} %bitcast.148), channel_id=1, replica_groups=mesh['xl'=2,'z'=8,'c'=2,'y'=4,'xh'=2] {'xl','y','xh'}, dimensions={0} | all-to-all | bytes 5308416 | tf_op jit(solution)/shard_map/all_to_all | solution.py:293
  142.4 20.8 %all_to_all.26 = bf16[16,8,4608]{2,1,0:T(8,128)(2,1)S(1)} all-to-all(bf16[16,8,4608]{2,1,0:T(8,128)(2,1)S(1)} %broadcast_in_dim.196), channel_id=1, replica_groups=mesh['xl'=2,'z'=8,'c'=2,'y'=4,'xh'=2] {'xl','y','xh'}, dimensions={0} | all-to-all | bytes 2359296 | tf_op jit(solution)/shard_map/all_to_all | solution.py:296
  163.2 2.8 collective-permute-start.1
  167.4 1.5 convert_reduce_fusion.proj_ref
  170.4 2.8 broadcast_select_fusion
  173.9 6.7 %chain.1 = bf16[32,2176]{1,0:T(8,128)(2,1)} custom-call(f32[8,4736]{1,0:T(8,128)} %copy-done.13, f32[32,128]{1,0:T(8,128)} %pad.4.norm_ref, f32[8,32,256]{2,1,0:T(8,128)} %convert_bitcast_fusion.start_ref, f32[32,128]{1,0:T(8,128)} %broadcast_in_dim.195.mask_ref, bf16[128,4608]{1,0:T(8,128)(2,1)} %get-tuple-element.19.oo_ref, ...), custom_call_target="tpu_custom_call" | custom-call | tf_op jit(solution)/shard_map/chain/pallas_call | solution.py:311
  180.7 2.4 broadcast_in_dim.197
  183.1 7.5 %all-to-all-start.3 = ((bf16[16,32,2176]{2,1,0:T(8,128)(2,1)}), bf16[16,32,2176]{2,1,0:T(8,128)(2,1)}, u32[]{:S(2)}, u32[]{:S(2)}) async-start(bf16[16,32,2176]{2,1,0:T(8,128)(2,1)} %broadcast_in_dim.197), calls=%async_computation.3 | async-start | bytes 4456448 | tf_op jit(solution)/shard_map/all_to_all | solution.py:320
  190.5 37.6 %all-to-all-done.3 = bf16[16,32,2176]{2,1,0:T(8,128)(2,1)} async-done(((bf16[16,32,2176]{2,1,0:T(8,128)(2,1)}), bf16[16,32,2176]{2,1,0:T(8,128)(2,1)}, u32[]{:S(2)}, u32[]{:S(2)}) %all-to-all-start.3) | async-done | bytes 2228256 | tf_op jit(solution)/shard_map/all_to_all | solution.py:320
  228.1 11.6 %grads.1 = (f32[2,8,256,128]{3,2,1,0:T(8,128)}, f32[2,8,128,256]{3,2,1,0:T(8,128)}) custom-call(bf16[16,224,512]{2,1,0:T(8,128)(2,1)} %all-to-all-done.got_ref, bf16[8,128,512]{2,1,0:T(8,128)(2,1)} %bitcast.150, bf16[8,512,128]{2,1,0:T(8,128)(2,1)} %bitcast.152, bf16[512,2176]{1,0:T(8,128)(2,1)} %bitcast.40.chain_ref), custom_call_target="tpu_custom_call" | custom-call | tf_op jit(solution)/shard_map/grads/pallas_call | solution.py:324
  241.2 1.3 fusion.14
  244.4 1.3 constant_dynamic-slice_fusion.2
  246.4 1.3 dynamic-slice_bitcast_fusion
  247.7 1.6 fusion.3
  249.3 37.2 %all_to_all.27 = bf16[8,512,128]{2,1,0:T(8,128)(2,1)S(1)} all-to-all(bf16[8,512,128]{2,1,0:T(8,128)(2,1)S(1)} %fusion.3), channel_id=1, replica_groups=mesh['xl'=2,'z'=8,'c'=2,'y'=4,'xh'=2] {'z'}, dimensions={0} | all-to-all | bytes 2097152 | tf_op jit(solution)/shard_map/all_to_all | solution.py:361
  286.7 1.9 collective-permute-start.3
  289.3 29.2 %collective-permute-done.3 = f32[512,128]{1,0:T(8,128)S(1)} collective-permute-done((f32[512,128]{1,0:T(8,128)S(1)}, f32[512,128]{1,0:T(8,128)S(1)}, u32[]{:S(2)}, u32[]{:S(2)}) %collective-permute-start.3) | collective-permute-done | bytes 262176 | tf_op jit(solution)/shard_map/ppermute | solution.py:364
  (101 shorter events, 25.3 us)
Async XLA Ops:
  0.6 3.8 %copy-start = (bf16[1,128,8192]{2,1,0:T(8,128)(2,1)S(1)}, bf16[1,128,8192]{2,1,0:T(8,128)(2,1)}, u32[]{:S(2)}) copy-start(bf16[1,128,8192]{2,1,0:T(8,128)(2,1)} %param.13) | copy-start | bytes 6291460
  0.7 3.4 %copy-start.12 = (bf16[1,8,8,8192]{3,2,1,0:T(8,128)(2,1)S(1)}, bf16[1,8,8,8192]{3,2,1,0:T(8,128)(2,1)}, u32[]{:S(2)}) copy-start(bf16[1,8,8,8192]{3,2,1,0:T(8,128)(2,1)} %param.9) | copy-start | bytes 3145732
  4.4 1.8 copy-start.5
  10.3 4.0 %copy-start.14 = (s32[1,4,8]{2,1,0:T(4,128)S(1)}, s32[1,4,8]{2,1,0:T(4,128)}, u32[]{:S(2)}) copy-start(s32[1,4,8]{2,1,0:T(4,128)} %param.8) | copy-start | bytes 388
  13.3 5.1 %copy-start.15 = (f32[1,8192]{1,0:T(1,128)S(1)}, f32[1,8192]{1,0:T(1,128)}, u32[]{:S(2)}) copy-start(f32[1,8192]{1,0:T(1,128)} %param.11) | copy-start | bytes 98308
  15.1 5.0 %copy-start.16 = (pred[4]{0:T(512)(128)(4,1)}, pred[4]{0:T(512)(128)(4,1)S(1)}, u32[]{:S(2)}) copy-start(pred[4]{0:T(512)(128)(4,1)S(1)} %get-tuple-element.13) | copy-start | bytes 16
  15.8 1.6 copy-start.7
  17.3 3.7 %copy-start.8 = (bf16[4,8,16,512]{3,2,1,0:T(8,128)(2,1)S(1)}, bf16[4,8,16,512]{3,2,1,0:T(8,128)(2,1)}, u32[]{:S(2)}) copy-start(bf16[4,8,16,512]{3,2,1,0:T(8,128)(2,1)} %copy.108) | copy-start | bytes 1572868
  17.3 3.7 %copy-start.9 = (bf16[4,8,16,512]{3,2,1,0:T(8,128)(2,1)S(1)}, bf16[4,8,16,512]{3,2,1,0:T(8,128)(2,1)}, u32[]{:S(2)}) copy-start(bf16[4,8,16,512]{3,2,1,0:T(8,128)(2,1)} %copy.109) | copy-start | bytes 1572868
  18.5 2.5 copy-start.10
  18.5 2.5 copy-start.11
  23.0 65.3 %all-to-all-start = ((bf16[16,224,512]{2,1,0:T(8,128)(2,1)}), bf16[16,224,512]{2,1,0:T(8,128)(2,1)}, u32[]{:S(2)}, u32[]{:S(2)}) async-start(bf16[16,224,512]{2,1,0:T(8,128)(2,1)} %bitcast.153), calls=%async_computation | async-start | bytes 7340032 | tf_op jit(solution)/shard_map/all_to_all | solution.py:260
  29.5 2.5 copy-start.2
  29.5 2.8 copy-start.6
  89.6 4.2 %collective-permute-start = (bf16[16,64,512]{2,1,0:T(8,128)(2,1)S(1)}, bf16[16,64,512]{2,1,0:T(8,128)(2,1)S(1)}, u32[]{:S(2)}, u32[]{:S(2)}) collective-permute-start(bf16[16,64,512]{2,1,0:T(8,128)(2,1)S(1)} %slice.124), channel_id=1, source_target_pairs={{0,8},{8,0},{1,9},{9,1},{2,10},{10,2},{3,11},{11,3},{4,12},{12,4},... | collective-permute-start | bytes 3145736 | tf_op jit(solution)/shard_map/ppermute | solution.py:263
  142.1 21.1 %copy-start.4 = (bf16[16,8,10368]{2,1,0:T(8,128)(2,1)}, bf16[16,8,10368]{2,1,0:T(8,128)(2,1)S(1)}, u32[]{:S(2)}) copy-start(bf16[16,8,10368]{2,1,0:T(8,128)(2,1)S(1)} %all_to_all.25) | copy-start | bytes 7962628
  142.2 23.7 %copy-start.3 = (bf16[4,32,8192]{2,1,0:T(8,128)(2,1)S(1)}, bf16[4,32,8192]{2,1,0:T(8,128)(2,1)}, u32[]{:S(2)}) copy-start(bf16[4,32,8192]{2,1,0:T(8,128)(2,1)} %param.7) | copy-start | bytes 6291460
  142.3 23.7 %copy-start.17 = (pred[4]{0:T(512)(128)(4,1)S(1)}, pred[4]{0:T(512)(128)(4,1)}, u32[]{:S(2)}) copy-start(pred[4]{0:T(512)(128)(4,1)} %copy-done.16) | copy-start | bytes 16
  163.2 6.5 %slice-start = ((bf16[16,8,10368]{2,1,0:T(8,128)(2,1)}), bf16[16,8,1024]{2,1,0:T(8,128)(2,1)S(1)}, s32[]{:S(2)}) async-start(bf16[16,8,10368]{2,1,0:T(8,128)(2,1)} %copy-done.4), calls=%async_computation.5 | async-start | bytes 524288 | tf_op jit(solution)/shard_map/slice | solution.py:307
  163.2 7.2 %collective-permute-start.1 = (bf16[128,4608]{1,0:T(8,128)(2,1)S(1)}, bf16[128,4608]{1,0:T(8,128)(2,1)}, u32[]{:S(2)}, u32[]{:S(2)}) collective-permute-start(bf16[128,4608]{1,0:T(8,128)(2,1)S(1)} %bitcast.154), channel_id=1, source_target_pairs={{0,8},{8,0},{1,9},{9,1},{2,10},{10,2},{3,11},{11,3},{4,12},{12,4},... | collective-permute-start | bytes 3538952 | tf_op jit(solution)/shard_map/ppermute | solution.py:299
  168.8 4.4 %copy-start.13 = (f32[8,4736]{1,0:T(8,128)}, f32[8,4736]{1,0:T(8,128)S(1)}, u32[]{:S(2)}) copy-start(f32[8,4736]{1,0:T(8,128)S(1)} %convert_reduce_fusion.proj_ref) | copy-start | bytes 454660
  183.1 45.0 %all-to-all-start.3 = ((bf16[16,32,2176]{2,1,0:T(8,128)(2,1)}), bf16[16,32,2176]{2,1,0:T(8,128)(2,1)}, u32[]{:S(2)}, u32[]{:S(2)}) async-start(bf16[16,32,2176]{2,1,0:T(8,128)(2,1)} %broadcast_in_dim.197), calls=%async_computation.3 | async-start | bytes 4456448 | tf_op jit(solution)/shard_map/all_to_all | solution.py:320
  243.6 4.1 %collective-permute-start.2 = (bf16[8,512,128]{2,1,0:T(8,128)(2,1)}, bf16[8,512,128]{2,1,0:T(8,128)(2,1)}, u32[]{:S(2)}, u32[]{:S(2)}) collective-permute-start(bf16[8,512,128]{2,1,0:T(8,128)(2,1)} %pad_maximum_fusion.1), channel_id=1, source_target_pairs={{0,8},{8,0},{1,9},{9,1},{2,10},{10,2},{3,11},{11,3},{4,12},{12,4},... | collective-permute-start | bytes 3145736 | tf_op jit(solution)/shard_map/ppermute | solution.py:360
  247.7 72.5 %copy-start.1 = (bf16[1,128,8192]{2,1,0:T(8,128)(2,1)S(1)}, bf16[1,128,8192]{2,1,0:T(8,128)(2,1)}, u32[]{:S(2)}) copy-start(bf16[1,128,8192]{2,1,0:T(8,128)(2,1)} %param.13) | copy-start | bytes 6291460
  286.7 31.9 %collective-permute-start.3 = (f32[512,128]{1,0:T(8,128)S(1)}, f32[512,128]{1,0:T(8,128)S(1)}, u32[]{:S(2)}, u32[]{:S(2)}) collective-permute-start(f32[512,128]{1,0:T(8,128)S(1)} %convert_reduce_fusion.1), channel_id=1, source_target_pairs={{0,0},{1,16},{2,32},{3,48},{4,64},{5,80},{6,96},{7,112},{16,1},{17... | collective-permute-start | bytes 786440 | tf_op jit(solution)/shard_map/ppermute | solution.py:364

commit v2 on v1

v2 whole, which is shorter than its diff:
```python
import functools

import jax
import jax.numpy as jnp
from jax import lax
from jax.experimental import pallas as pl
from jax.experimental.pallas import tpu as pltpu
from jax.sharding import Mesh, PartitionSpec as P

F32 = jnp.float32
BF16 = jnp.bfloat16
EPS = 1e-05
PLANE = ("xl", "y", "xh")
SECTION = ("y", "xh")
SWAP = [(0, 1), (1, 0)]
NS = 8
R = 128
TOK = 8
MIC = 4
BLK = 128
OUT_ROW = 64
W_ROW = 128
X_ROW = 192
SENT = 224
PROJ = 29
NORM = 36
START = 37
GRAM = 45
SPLIT = 41
GRAMS = 36
PARAMS = pltpu.CompilerParams(vmem_limit_bytes=56 * 1024 * 1024)
VMEM = pl.BlockSpec(memory_space=pltpu.VMEM)
SMEM = pl.BlockSpec(memory_space=pltpu.SMEM)


def gram_at(t):
    return sum(NS - i for i in range(t))


def proj_at(s):
    return s * (s - 1) // 2


def dot_t(a, b):
    return lax.dot_general(a, b, (((1,), (1,)), ((), ())), preferred_element_type=F32)


def dot_rows(a, b):
    return lax.dot_general(a, b, (((0,), (0,)), ((), ())), preferred_element_type=F32)


def dot(a, b):
    return jnp.dot(a, b, preferred_element_type=F32)


def split(x):
    high = x.astype(BF16)
    return high, (x - high.astype(F32)).astype(BF16)


def interleave(tiles):
    lane = lax.broadcasted_iota(jnp.int32, tiles[0].shape, 1)
    low = lane < 64
    even = lane % 64 < 32
    a, b, c, d = tiles
    halves = []
    for p, q in ((a, c), (b, d)):
        halves.append(
            (
                jnp.where(low, p, pltpu.roll(q, 64, 1)),
                jnp.where(low, pltpu.roll(p, 64, 1), q),
            )
        )
    result = []
    for p, q in zip(halves[0], halves[1]):
        result.append(jnp.where(even, p, pltpu.roll(q, 32, 1)))
        result.append(jnp.where(even, pltpu.roll(p, 96, 1), q))
    return result


def pack_kernel(
    at_ref, ids_ref, in_ref, out_ref, w_out_ref, w_in_ref, gain_ref, first_ref, send_ref, row_ref
):
    section = at_ref[1]
    gain = gain_ref[...].reshape(8, BLK).T
    for s in range(NS):
        for j in range(4):
            column = 2 * j + s // 4
            scale = gain[(s % 4) * 32 : (s % 4) * 32 + 32, column : column + 1]
            send_ref[s, W_ROW + 32 : X_ROW, j * BLK : (j + 1) * BLK] = (
                w_in_ref[0, j, 0, s].astype(F32) * scale
            ).astype(BF16)
    picks = [[ids_ref[m, j] == section for j in range(4)] for m in range(MIC)]

    def own(at):
        rows = []
        for m in range(MIC):
            block = first_ref[m, :, at : at + BLK].astype(F32).reshape(4, TOK, BLK)
            total = jnp.zeros((TOK, BLK), F32)
            for j in range(4):
                total = jnp.where(picks[m][j], block[j], total)
            rows.append(total)
        return jnp.concatenate(rows, 0)

    squares = jnp.zeros((MIC * TOK, BLK), F32)
    for c in range(2):
        for zq in range(2):
            for h in range(2):
                lanes = [((4 * zq + j) * 4 + c * 2 + h) * BLK for j in range(4)]
                to = (c * 2 + zq) * BLK
                for ref, row, count in (
                    (in_ref, 0, 64),
                    (out_ref, OUT_ROW, 64),
                    (w_out_ref, W_ROW, 32),
                ):
                    tiles = interleave([ref[:, at : at + BLK].astype(F32) for at in lanes])
                    for i in range(4):
                        send_ref[4 * h + i, row : row + count, to : to + BLK] = tiles[i].astype(
                            BF16
                        )
                tiles = [own(at) for at in lanes]
                for tile in tiles:
                    squares = squares + tile * tile
                tiles = interleave(tiles)
                for i in range(4):
                    send_ref[4 * h + i, X_ROW:SENT, to : to + BLK] = tiles[i].astype(BF16)
    norm = jnp.sum(squares, -1, keepdims=True)
    lane = lax.broadcasted_iota(jnp.int32, (TOK, BLK), 1)
    for m in range(MIC):
        valid = picks[m][0] | picks[m][1] | picks[m][2] | picks[m][3]
        rows = slice(m * TOK, (m + 1) * TOK)
        mask = jnp.where(valid, 1.0, 0.0)
        fresh = jnp.where(lane == 1, mask, jnp.where(lane == 0, norm[rows], 0.0))

        @pl.when(pl.program_id(0) == 0)
        def _():
            row_ref[rows, :] = fresh

        @pl.when(pl.program_id(0) != 0)
        def _():
            row_ref[rows, :] = row_ref[rows, :] + jnp.where(lane == 0, fresh, 0.0)


def project_kernel(
    at_ref, got_ref, other_ref, start_ref, send_ref, out_w_ref, in_w_ref, wide_ref
):
    cols = got_ref.shape[2]
    first_core = at_ref[0] == 0
    for s in range(NS):
        for x in range(2):
            mine = got_ref[x * NS + s, W_ROW:X_ROW, :]
            theirs = other_ref[x * NS + s]
            for c in range(2):
                part = jnp.where(first_core == (c == 0), mine, theirs)
                k = 2 * x + c
                out_w_ref[s, 32 * k : 32 * k + 32, :] = part[:32]
                for g in range(4):
                    row = k * BLK + g * 32
                    in_w_ref[s, row : row + 32, :] = part[32:, g * BLK : (g + 1) * BLK]
    first = got_ref[:, X_ROW:SENT, :].astype(F32).reshape(16, MIC, TOK, cols)
    running = None
    lane = lax.broadcasted_iota(jnp.int32, (R, BLK), 1)
    norms = jnp.zeros((R, BLK), F32)
    for s in range(1, NS):
        step = jnp.concatenate(
            [
                got_ref[x * NS + s, 0:OUT_ROW, :].astype(F32)
                - got_ref[x * NS + s - 1, OUT_ROW:W_ROW, :].astype(F32)
                for x in range(2)
            ],
            0,
        )
        running = step if running is None else running + step
        rounded = running.astype(BF16)
        count = s if s < NS - 1 else NS
        at = proj_at(s) * BLK
        wide_ref[:, at : at + count * BLK] = dot_t(
            rounded, out_w_ref[0:count].reshape(count * R, cols)
        )
        at = (PROJ + s - 1) * BLK
        wide_ref[:, at : at + BLK] = dot(rounded, in_w_ref[s])
        for m in range(MIC):
            part = jnp.sum(
                running * (running + 2.0 * first[:, m].reshape(R, cols)), -1, keepdims=True
            )
            norms = jnp.where(lane == m * NS + s, part, norms)
    high = norms.astype(BF16).astype(F32)
    wide_ref[:, NORM * BLK : (NORM + 1) * BLK] = jnp.where(
        lane < 32, high, pltpu.roll(norms - high, 32, 1)
    )
    wide_ref[:, START * BLK : GRAM * BLK] = start_ref[...].astype(F32)
    wide_ref[:, (GRAM + GRAMS) * BLK :] = jnp.zeros((R, BLK), F32)

    @pl.when(first_core)
    def _():
        for t in range(NS):
            at = (GRAM + gram_at(t)) * BLK
            wide_ref[:, at : at + (NS - t) * BLK] = dot_t(
                out_w_ref[t], out_w_ref[t:NS].reshape((NS - t) * R, cols)
            )

    @pl.when(jnp.logical_not(first_core))
    def _():
        for t in range(NS):
            for s in range(t, NS):
                at = (GRAM + gram_at(t) + s - t) * BLK
                wide_ref[:, at : at + BLK] = dot(out_w_ref[t], in_w_ref[s])

    for b in range(SPLIT):
        pair = [
            wide_ref[:, at * BLK : (at + 1) * BLK].reshape(16, TOK, BLK) for at in (b, SPLIT + b)
        ]
        send_ref[:, :, b * BLK : (b + 1) * BLK] = jnp.concatenate(pair, 1).astype(BF16)


def chain_kernel(
    width, at_ref, parts_ref, row_ref, gram_ref, other_ref, send_ref, sum_ref, oo_ref, oi_ref
):
    rows = MIC * TOK
    first_core = at_ref[0] == 0
    for b in range(0, GRAMS, 4):
        at = slice(b * BLK, (b + 4) * BLK)
        mine, theirs = gram_ref[:, at], other_ref[:, at]
        oo_ref[:, at] = jnp.where(first_core, mine, theirs)
        oi_ref[:, at] = jnp.where(first_core, theirs, mine)
    for b in range(START):
        at = slice(b * BLK, (b + 1) * BLK)
        total = parts_ref[0, :, at].astype(F32)
        for q in range(1, 16):
            total = total + parts_ref[q, :, at].astype(F32)
        sum_ref[:, at] = total[:TOK]
    starts = []
    for s in range(NS):
        block = parts_ref[at_ref[2] * NS + s].astype(F32)
        pieces = []
        for m in range(MIC):
            b = START + 2 * m
            if b < SPLIT:
                pieces.append(block[:TOK, b * BLK : (b + 2) * BLK])
            else:
                pieces.append(block[TOK:, (b - SPLIT) * BLK : (b + 2 - SPLIT) * BLK])
        starts.append(jnp.concatenate(pieces, 0))

    def spread(at):
        block = sum_ref[:, at * BLK : (at + 1) * BLK]
        return jnp.concatenate([block] * MIC, 0)

    def pair(ref, t, s, count=1):
        at = (gram_at(t) + s - t) * BLK
        return ref[:, at : at + count * BLK]

    mask = row_ref[:, 1:2]
    own_norm = row_ref[:, 0:1]
    norm_block = sum_ref[:, NORM * BLK : (NORM + 1) * BLK]
    run_in = [start[:, :R] for start in starts]
    start_out = [start[:, R:] for start in starts]
    run_out = list(start_out)
    inners, inverses, actives, crossed = [], [], [], []
    for s in range(NS):
        norm = own_norm
        entry_out = []
        inner = run_in[s]
        if s > 0:
            inner = inner + spread(PROJ + s - 1)
            norm = norm + jnp.concatenate(
                [
                    norm_block[:, m * NS + s : m * NS + s + 1]
                    + norm_block[:, 32 + m * NS + s : 33 + m * NS + s]
                    for m in range(MIC)
                ],
                0,
            )
            total = jnp.zeros((rows, R), F32)
            for t in range(s):
                base = spread(proj_at(s) + t)
                full = base + run_out[t]
                entry_out.append(full)
                total = total + actives[t].astype(F32) * (full + base + start_out[t])
            norm = norm + jnp.sum(total, -1, keepdims=True)
        inverse = lax.rsqrt(jnp.maximum(norm, 0.0) * (1.0 / width) + EPS)
        inner = inner * inverse
        active = (inner * jax.nn.sigmoid(inner) * mask).astype(BF16)
        inners.append(inner)
        inverses.append(inverse)
        actives.append(active)
        crossed.append(entry_out)
        grown = dot(active, pair(oo_ref, s, s, NS - s))
        for t in range(NS):
            if t >= s:
                run_out[t] = run_out[t] + grown[:, (t - s) * R : (t - s + 1) * R]
            else:
                run_out[t] = run_out[t] + dot_t(active, pair(oo_ref, t, s))
        if s < NS - 1:
            grown = dot(active, pair(oi_ref, s, s + 1, NS - 1 - s))
            for t in range(s + 1, NS):
                run_in[t] = run_in[t] + grown[:, (t - s - 1) * R : (t - s) * R]
    grads = [run_out[t] + spread(proj_at(NS - 1) + t) for t in range(NS)]
    lane = lax.broadcasted_iota(jnp.int32, (rows, BLK), 1)
    scalars = jnp.zeros((rows, BLK), F32)
    d_inners = [None] * NS
    for s in range(NS - 1, -1, -1):
        inner = inners[s]
        sigm = jax.nn.sigmoid(inner)
        d_inner = (grads[s] * sigm * (1.0 + inner * (1.0 - sigm)) * mask).astype(BF16)
        d_inners[s] = d_inner
        d_wide = d_inner.astype(F32)
        inverse = inverses[s]
        scale = inverse * inverse * jnp.sum(d_wide * inner, -1, keepdims=True) * (1.0 / width)
        for t in range(s):
            grads[t] = (
                grads[t] + inverse * dot_t(d_inner, pair(oi_ref, t, s)) - scale * crossed[s][t]
            )
        for at, value in ((s, inverse), (2 * NS + s, scale)):
            high, low = split(value)
            scalars = jnp.where(lane == at, high.astype(F32), scalars)
            scalars = jnp.where(lane == at + NS, low.astype(F32), scalars)
    for q in range(16):
        for s in range(NS):
            send_ref[q, :, s * R : (s + 1) * R] = actives[s]
            send_ref[q, :, (NS + s) * R : (NS + s + 1) * R] = d_inners[s]
        send_ref[q, :, 2 * NS * R :] = scalars.astype(BF16)


def grads_kernel(at_ref, got_ref, out_w_ref, in_w_ref, chain_ref, *rest):
    *add, result_ref, kept_ref = rest
    cols = got_ref.shape[2]
    rows = 16 * MIC * TOK
    scalars = chain_ref[:, 2 * NS * R :].astype(F32)
    inverses = [scalars[:, s : s + 1] + scalars[:, NS + s : NS + s + 1] for s in range(NS)]
    scales = [
        scalars[:, 2 * NS + s : 2 * NS + s + 1] + scalars[:, 3 * NS + s : 3 * NS + s + 1]
        for s in range(NS)
    ]

    def active(s):
        return chain_ref[:, s * R : (s + 1) * R]

    def d_inner(s):
        return chain_ref[:, (NS + s) * R : (NS + s + 1) * R]

    def put(s, kind, value):
        value = value.reshape(8, 32, R)
        at = slice(32 * kind, 32 * kind + 32)
        if add:
            value = value + add[0][:, s, at, :].astype(F32)
        result_ref[:, s, at, :] = value.astype(BF16)

    entry = got_ref[:, X_ROW:SENT, :].astype(F32).reshape(rows, cols)
    for s in range(NS):
        if s > 0:
            step = jnp.concatenate(
                [
                    got_ref[x * NS + s, 0:OUT_ROW, :].astype(F32)
                    - got_ref[x * NS + s - 1, OUT_ROW:W_ROW, :].astype(F32)
                    for x in range(2)
                ],
                0,
            )
            step = jnp.broadcast_to(step.reshape(16, 1, TOK, cols), (16, MIC, TOK, cols))
            entry = entry + step.reshape(rows, cols)
        kept_ref[s] = entry
        put(s, 0, dot_rows((entry * inverses[s]).astype(BF16), d_inner(s)))
        entry = entry + dot(active(s), out_w_ref[s])
    grad = entry
    for s in range(NS - 1, -1, -1):
        put(s, 1, dot_rows(grad.astype(BF16), active(s)))
        if s > 0:
            grad = grad + inverses[s] * dot_t(d_inner(s), in_w_ref[s]) - scales[s] * kept_ref[s]


def final_kernel(parts_ref, gain_ref, in_ref, out_ref):
    total = parts_ref[0].astype(F32)
    for i in range(1, 8):
        total = total + parts_ref[i].astype(F32)
    gain = gain_ref[...].T
    for j in range(8):
        scale = gain[(j % 4) * 32 : (j % 4) * 32 + 32, j // 4 : j // 4 + 1]
        in_ref[j * 32 : j * 32 + 32, :] = total[j, :32] * scale
    out = total[:, 32:].reshape(2 * BLK, R)
    for i in range(2):
        out_ref[:, i * BLK : (i + 1) * BLK] = out[i * BLK : (i + 1) * BLK].T


def body(first_input, example_ids, out_store, in_store, norm_gain, adapter_in, adapter_out):
    width = first_input.shape[2]
    cols = width // 16
    half = cols // 2
    core = lax.axis_index("c")
    xl = lax.axis_index("xl")
    z = lax.axis_index("z")
    section = lax.axis_index(SECTION)
    quarter = xl * 2 + core
    at = jnp.stack([core, section, xl, quarter]).astype(jnp.int32)
    ids = example_ids[0]
    w_in = adapter_in[0]
    w_out = adapter_out[0]

    send, row = pl.pallas_call(
        pack_kernel,
        grid_spec=pltpu.PrefetchScalarGridSpec(
            num_scalar_prefetch=2,
            grid=(2,),
            in_specs=[
                pl.BlockSpec((64, width // 2), lambda i, at, ids: (0, i)),
                pl.BlockSpec((64, width // 2), lambda i, at, ids: (0, i)),
                pl.BlockSpec((32, width // 2), lambda i, at, ids: (at[3], i)),
                pl.BlockSpec(
                    (1, 4, 1, 8, 32, R),
                    lambda i, at, ids: (i, at[3] % 2, at[3] // 2, 0, 0, 0),
                ),
                pl.BlockSpec(
                    (1, 4, 1, 2, BLK), lambda i, at, ids: (i, at[3] % 2, at[3] // 2, 0, 0)
                ),
                pl.BlockSpec((MIC, 32, width // 2), lambda i, at, ids: (0, 0, i)),
            ],
            out_specs=[
                pl.BlockSpec((8, SENT, cols), lambda i, at, ids: (i, 0, 0)),
                pl.BlockSpec((MIC * TOK, BLK), lambda i, at, ids: (0, 0)),
            ],
        ),
        out_shape=(
            jax.ShapeDtypeStruct((16, SENT, cols), BF16),
            jax.ShapeDtypeStruct((MIC * TOK, BLK), F32),
        ),
        compiler_params=PARAMS,
        name="pack",
    )(
        at,
        ids,
        in_store.reshape(64, width),
        out_store.reshape(64, width),
        w_out,
        w_in.reshape(2, 8, 2, 8, 32, R),
        norm_gain.reshape(2, 8, 2, 2, BLK),
        first_input,
    )
    got = lax.all_to_all(send, PLANE, 0, 0, tiled=True)

    flat = first_input.reshape(MIC * 32, width)
    gained = (flat.astype(F32) * norm_gain).astype(BF16)
    start_proj = jnp.concatenate([dot(gained, w_in), dot_t(flat, w_out)], 1)
    start_proj = start_proj.reshape(MIC, 4, TOK, 2 * R)
    placed = jnp.zeros((MIC, NS, TOK, 2 * R), F32)
    for j in range(4):
        here = ids[:, j, None] == jnp.arange(NS)[None, :]
        placed = jnp.where(here[:, :, None, None], start_proj[:, j, None], placed)
    placed = placed.transpose(1, 2, 0, 3).reshape(NS * TOK, MIC * 2 * R).astype(BF16)
    placed = jnp.concatenate([placed, placed], 0)

    other = lax.ppermute(got[:, W_ROW:X_ROW], "c", SWAP)
    parts, out_w, in_w = pl.pallas_call(
        project_kernel,
        out_shape=(
            jax.ShapeDtypeStruct((16, 2 * TOK, SPLIT * BLK), BF16),
            jax.ShapeDtypeStruct((NS, R, cols), BF16),
            jax.ShapeDtypeStruct((NS, cols, R), BF16),
        ),
        in_specs=[SMEM, VMEM, VMEM, VMEM],
        out_specs=(VMEM, VMEM, VMEM),
        scratch_shapes=[pltpu.VMEM((R, 2 * SPLIT * BLK), F32)],
        compiler_params=PARAMS,
        name="project",
    )(at, got, other, placed)
    parts = lax.all_to_all(parts, PLANE, 0, 0, tiled=True)

    first_gram = (GRAM - SPLIT) * BLK
    gram = parts[:, TOK:, first_gram : first_gram + GRAMS * BLK].astype(F32)
    gram = jnp.sum(gram, 0).astype(BF16)
    gram = lax.all_to_all(
        jnp.broadcast_to(gram, (16,) + gram.shape), PLANE, 0, 0, tiled=True
    ).reshape(R, GRAMS * BLK)
    other = lax.ppermute(gram, "c", SWAP)

    latent = pl.pallas_call(
        functools.partial(chain_kernel, width),
        out_shape=jax.ShapeDtypeStruct((16, MIC * TOK, 17 * BLK), BF16),
        in_specs=[SMEM, VMEM, VMEM, VMEM, VMEM],
        out_specs=VMEM,
        scratch_shapes=[
            pltpu.VMEM((TOK, START * BLK), F32),
            pltpu.VMEM((R, GRAMS * BLK), BF16),
            pltpu.VMEM((R, GRAMS * BLK), BF16),
        ],
        compiler_params=PARAMS,
        name="chain",
    )(at, parts, row, gram, other)
    latent = lax.all_to_all(latent, PLANE, 0, 0, tiled=True).reshape(16 * MIC * TOK, 17 * BLK)

    def grads(own, *add):
        def side(at):
            return at[0] if own else 1 - at[0]

        return pl.pallas_call(
            grads_kernel,
            grid_spec=pltpu.PrefetchScalarGridSpec(
                num_scalar_prefetch=1,
                grid=(1,),
                in_specs=[
                    pl.BlockSpec((16, SENT, half), lambda i, at: (0, 0, side(at))),
                    pl.BlockSpec((NS, R, half), lambda i, at: (0, 0, side(at))),
                    pl.BlockSpec((NS, half, R), lambda i, at: (0, side(at), 0)),
                    pl.BlockSpec((16 * MIC * TOK, 17 * BLK), lambda i, at: (0, 0)),
                ]
                + [pl.BlockSpec((8, NS, 64, R), lambda i, at: (0, 0, 0, 0))] * len(add),
                out_specs=pl.BlockSpec((8, NS, 64, R), lambda i, at: (0, 0, 0, 0)),
                scratch_shapes=[pltpu.VMEM((NS, 16 * MIC * TOK, half), F32)],
            ),
            out_shape=jax.ShapeDtypeStruct((8, NS, 64, R), BF16),
            compiler_params=PARAMS,
            name="grads_own" if own else "grads_other",
        )(at, got, out_w, in_w, latent, *add)

    swapped = lax.ppermute(grads(False), "c", SWAP)
    total = grads(True, swapped).reshape(64, 64, R)
    total = lax.all_to_all(total, ("z",) + SECTION, 0, 0, tiled=True)
    block = (xl * NS + z) * 2 + core
    gain = lax.dynamic_slice_in_dim(norm_gain[0], block * half, half, 0)
    grad_in, grad_out = pl.pallas_call(
        final_kernel,
        out_shape=(
            jax.ShapeDtypeStruct((half, R), F32),
            jax.ShapeDtypeStruct((R, half), F32),
        ),
        in_specs=[VMEM, VMEM],
        out_specs=(VMEM, VMEM),
        compiler_params=PARAMS,
        name="final",
    )(total.reshape(8, 8, 64, R), gain.reshape(2, BLK))
    return (grad_in[None], grad_out[None])


def solution(mesh):
    fine = Mesh(mesh.devices.reshape(2, 8, 2, 4, 2), ("xl", "z", "c", "y", "xh"))
    dp = ("xl", "z", "c")
    placed = (
        P(None, dp, None),
        P(dp, None, None),
        P(SECTION, dp, None, None),
        P(SECTION, dp, None, None),
        P(SECTION, None),
        P(SECTION, None, None),
        P(SECTION, None, None),
    )
    return jax.shard_map(
        body,
        mesh=fine,
        in_specs=placed,
        out_specs=(P(SECTION, dp, None), P(SECTION, None, dp)),
        check_vma=False,
    )
```

time: 321 us -> 265 us (0.83)
  the two profiles are of different devices: /device:TPU:31 before, /device:TPU:32 now
where the time goes in v2:
time: 265 us
  blocking collectives  99.9 us (38%)
  waiting for transfers between devices  89.7 us (34%)
  Pallas kernels  43.9 us (17%)
  starting transfers between devices  17.5 us (7%)
  local copies, waits for them, and re-layouts  7.42 us (3%)
  matrix products  3.26 us (1%)
    all_to_all x1, waiting for transfers between devices, body(): got = lax.all_to_all(send, PLANE, 0, 0, tiled=True)  52.6 us
    all_to_all x1, blocking collectives, body(): parts = lax.all_to_all(parts, PLANE, 0, 0, tiled=True)  43.4 us
    all_to_all x1, blocking collectives, body(): lax.all_to_all(latent, PLANE, 0, 0, tiled=True)  35 us
    all_to_all x1, waiting for transfers between devices, body(): total = lax.all_to_all(total, ('z',) + SECTION, 0, 0, tiled=True)  30 us
    all_to_all x1, blocking collectives, body(): lax.all_to_all(jnp.broadcast_to(gram, (16,) + gram.shape), PLANE, 0, 0, t...  21.5 us
    pallas_call x2, Pallas kernels, grads(): pl.pallas_call(grads_kernel, grid_spec=pltpu.PrefetchScalarGridSpec(num_s...  15.3 us
    pallas_call x1, Pallas kernels, body(): pl.pallas_call(pack_kernel, grid_spec=pltpu.PrefetchScalarGridSpec(num_sc...  10.2 us
    all_to_all x1, starting transfers between devices, body(): total = lax.all_to_all(total, ('z',) + SECTION, 0, 0, tiled=True)  10.2 us
  transfers between devices with their start and end apart: 5, of which 5 were waited for; matrix products, arithmetic and copies ran while one was open for 2% of the time, Pallas kernels for 0%

profile of v2, /device:TPU:32, one launch (start us, length us, event | category | flops | bytes accessed | tf_op | source)
XLA Modules:
  0.0 264.7 jit_solution(15676889143361797445)
XLA Ops:
  0.6 0.7 pad_add_fusion.at_ref
  1.3 10.2 %pack.1 = (bf16[16,224,512]{2,1,0:T(8,128)(2,1)}, f32[32,128]{1,0:T(8,128)}) custom-call(s32[4]{0:T(128)} %pad_add_fusion.at_ref, s32[4,8]{1,0:T(4,128)} %bitcast.61, bf16[64,8192]{1,0:T(8,128)(2,1)} %bitcast.55, bf16[64,8192]{1,0:T(8,128)(2,1)} %bitcast.56, bf16[128,8192]{1,0:T(8,128)(2,1)} %bitcast.48, bf16[2,8,2,8,32,128]{5,4,3,2,1,0:T(8,128)(2,1)} %bitcast.49, ...), custom_call_target="tpu_custom_call" | custom-call | tf_op jit(solution)/shard_map/pack/pallas_call | solution.py:398
  11.5 7.2 %all-to-all-start = ((bf16[16,224,512]{2,1,0:T(8,128)(2,1)}), bf16[16,224,512]{2,1,0:T(8,128)(2,1)}, u32[]{:S(2)}, u32[]{:S(2)}) async-start(bf16[16,224,512]{2,1,0:T(8,128)(2,1)} %get-tuple-element.9), calls=%async_computation | async-start | bytes 7340032 | tf_op jit(solution)/shard_map/all_to_all | solution.py:437
  18.7 2.3 fusion.2
  21.1 0.4 multiply_convert_fusion
  21.5 1.2 copy-done.2
  22.7 1.0 fusion
  23.6 52.6 %all-to-all-done.got_ref = bf16[16,224,512]{2,1,0:T(8,128)(2,1)} async-done(((bf16[16,224,512]{2,1,0:T(8,128)(2,1)}), bf16[16,224,512]{2,1,0:T(8,128)(2,1)}, u32[]{:S(2)}, u32[]{:S(2)}) %all-to-all-start) | async-done | bytes 3670048 | tf_op jit(solution)/shard_map/all_to_all | solution.py:437
  76.3 1.3 slice.52
  77.7 0.2 slice_reduce_fusion.4
  77.9 0.1 copy.13
  78.1 0.2 select_convert_fusion
  78.3 0.7 pad_maximum_fusion.start_ref
  79.0 1.3 collective-permute-done.other_ref
  80.4 1.0 copy-done.6
  81.4 8.2 %project.1 = (bf16[16,16,5248]{2,1,0:T(8,128)(2,1)}, bf16[8,128,512]{2,1,0:T(8,128)(2,1)}, bf16[8,512,128]{2,1,0:T(8,128)(2,1)}) custom-call(s32[4]{0:T(128)} %pad_add_fusion.at_ref, bf16[16,224,512]{2,1,0:T(8,128)(2,1)} %all-to-all-done.got_ref, bf16[16,64,512]{2,1,0:T(8,128)(2,1)} %copy-done.6, bf16[128,1024]{1,0:T(8,128)(2,1)} %pad_maximum_fusion.start_ref), custom_call_target="tpu_custom_call" | custom-call | tf_op jit(solution)/shard_map/project/pallas_call | solution.py:451
  89.6 43.4 %all_to_all.25.parts_ref = bf16[16,16,5248]{2,1,0:T(8,128)(2,1)S(1)} all-to-all(bf16[16,16,5248]{2,1,0:T(8,128)(2,1)} %get-tuple-element.12), channel_id=1, replica_groups=mesh['xl'=2,'z'=8,'c'=2,'y'=4,'xh'=2] {'xl','y','xh'}, dimensions={0} | all-to-all | bytes 5373952 | tf_op jit(solution)/shard_map/all_to_all | solution.py:464
  132.9 0.2 slice_reduce_fusion
  133.2 21.5 %all_to_all.26 = bf16[16,8,4608]{2,1,0:T(8,128)(2,1)S(1)} all-to-all(bf16[16,8,4608]{2,1,0:T(8,128)(2,1)S(1)} %broadcast_in_dim.99), channel_id=1, replica_groups=mesh['xl'=2,'z'=8,'c'=2,'y'=4,'xh'=2] {'xl','y','xh'}, dimensions={0} | all-to-all | bytes 2359296 | tf_op jit(solution)/shard_map/all_to_all | solution.py:469
  154.7 2.8 %collective-permute-done.1.other_ref = bf16[128,4608]{1,0:T(8,128)(2,1)S(1)} collective-permute-done((bf16[128,4608]{1,0:T(8,128)(2,1)S(1)}, bf16[128,4608]{1,0:T(8,128)(2,1)S(1)}, u32[]{:S(2)}, u32[]{:S(2)}) %collective-permute-start.1) | collective-permute-done | bytes 1179680 | tf_op jit(solution)/shard_map/ppermute | solution.py:472
  157.6 1.0 copy-done.5
  158.6 8.1 %chain.1 = bf16[16,32,2176]{2,1,0:T(8,128)(2,1)} custom-call(s32[4]{0:T(128)} %pad_add_fusion.at_ref, bf16[16,16,5248]{2,1,0:T(8,128)(2,1)} %copy-done.1, f32[32,128]{1,0:T(8,128)} %get-tuple-element.13.row_ref, bf16[128,4608]{1,0:T(8,128)(2,1)} %bitcast.52, bf16[128,4608]{1,0:T(8,128)(2,1)} %copy-done.5), custom_call_target="tpu_custom_call" | custom-call | tf_op jit(solution)/shard_map/chain/pallas_call | solution.py:474
  166.7 35.0 %all_to_all.27 = bf16[16,32,2176]{2,1,0:T(8,128)(2,1)} all-to-all(bf16[16,32,2176]{2,1,0:T(8,128)(2,1)} %chain.1), channel_id=1, replica_groups=mesh['xl'=2,'z'=8,'c'=2,'y'=4,'xh'=2] {'xl','y','xh'}, dimensions={0} | all-to-all | bytes 4456448 | tf_op jit(solution)/shard_map/all_to_all | solution.py:487
  201.7 7.5 %grads_other.1 = bf16[8,8,64,128]{3,2,1,0:T(8,128)(2,1)} custom-call(s32[4]{0:T(128)} %pad_add_fusion.at_ref, bf16[16,224,512]{2,1,0:T(8,128)(2,1)} %all-to-all-done.got_ref, bf16[8,128,512]{2,1,0:T(8,128)(2,1)} %get-tuple-element.10.out_w_ref, bf16[8,512,128]{2,1,0:T(8,128)(2,1)} %get-tuple-element.11.in_w_ref, bf16[512,2176]{1,0:T(8,128)(2,1)} %bitcast.45), custom_call_target="tpu_custom_call" | custom-call | tf_op jit(solution)/shard_map/grads_other/pallas_call | solution.py:493
  209.2 2.9 %collective-permute-done.2.rest_0_ = bf16[8,8,64,128]{3,2,1,0:T(8,128)(2,1)S(1)} collective-permute-done((bf16[8,8,64,128]{3,2,1,0:T(8,128)(2,1)}, bf16[8,8,64,128]{3,2,1,0:T(8,128)(2,1)S(1)}, u32[]{:S(2)}, u32[]{:S(2)}) %collective-permute-start.2) | collective-permute-done | bytes 1048608 | tf_op jit(solution)/shard_map/ppermute | solution.py:513
  212.1 1.0 copy-done.7
  213.0 7.8 %grads_own.1 = bf16[8,8,64,128]{3,2,1,0:T(8,128)(2,1)} custom-call(s32[4]{0:T(128)} %pad_add_fusion.at_ref, bf16[16,224,512]{2,1,0:T(8,128)(2,1)} %all-to-all-done.got_ref, bf16[8,128,512]{2,1,0:T(8,128)(2,1)} %get-tuple-element.10.out_w_ref, bf16[8,512,128]{2,1,0:T(8,128)(2,1)} %get-tuple-element.11.in_w_ref, bf16[512,2176]{1,0:T(8,128)(2,1)} %bitcast.46, ...), custom_call_target="tpu_custom_call" | custom-call | tf_op jit(solution)/shard_map/grads_own/pallas_call | solution.py:493
  220.9 10.2 %all-to-all-start.4 = ((bf16[64,64,128]{2,1,0:T(8,128)(2,1)}), bf16[64,64,128]{2,1,0:T(8,128)(2,1)S(1)}, u32[]{:S(2)}, u32[]{:S(2)}) async-start(bf16[64,64,128]{2,1,0:T(8,128)(2,1)} %bitcast.53), calls=%async_computation.4 | async-start | bytes 2097152 | tf_op jit(solution)/shard_map/all_to_all | solution.py:515
  231.0 0.5 constant_dynamic-slice_fusion
  231.6 30.0 %all-to-all-done.4 = bf16[64,64,128]{2,1,0:T(8,128)(2,1)S(1)} async-done(((bf16[64,64,128]{2,1,0:T(8,128)(2,1)}), bf16[64,64,128]{2,1,0:T(8,128)(2,1)S(1)}, u32[]{:S(2)}, u32[]{:S(2)}) %all-to-all-start.4) | async-done | bytes 1048608 | tf_op jit(solution)/shard_map/all_to_all | solution.py:515
  261.6 1.0 copy-done.4
  262.5 2.1 final.1
  (23 shorter events, 0.2 us)
Async XLA Ops:
  11.5 7.2 %copy-start = (bf16[4,32,8192]{2,1,0:T(8,128)(2,1)S(1)}, bf16[4,32,8192]{2,1,0:T(8,128)(2,1)}, u32[]{:S(2)}) copy-start(bf16[4,32,8192]{2,1,0:T(8,128)(2,1)} %first_ref.1) | copy-start | bytes 6291460
  11.5 64.8 %all-to-all-start = ((bf16[16,224,512]{2,1,0:T(8,128)(2,1)}), bf16[16,224,512]{2,1,0:T(8,128)(2,1)}, u32[]{:S(2)}, u32[]{:S(2)}) async-start(bf16[16,224,512]{2,1,0:T(8,128)(2,1)} %get-tuple-element.9), calls=%async_computation | async-start | bytes 7340032 | tf_op jit(solution)/shard_map/all_to_all | solution.py:437
  18.7 2.3 copy-start.8
  21.1 1.6 copy-start.2
  23.6 54.1 %copy-start.9 = (s32[1,4,8]{2,1,0:T(4,128)S(1)}, s32[1,4,8]{2,1,0:T(4,128)}, u32[]{:S(2)}) copy-start(s32[1,4,8]{2,1,0:T(4,128)} %param.8) | copy-start | bytes 388
  77.6 2.7 %collective-permute-start = (bf16[16,64,512]{2,1,0:T(8,128)(2,1)S(1)}, bf16[16,64,512]{2,1,0:T(8,128)(2,1)S(1)}, u32[]{:S(2)}, u32[]{:S(2)}) collective-permute-start(bf16[16,64,512]{2,1,0:T(8,128)(2,1)S(1)} %slice.52), channel_id=1, source_target_pairs={{0,8},{8,0},{1,9},{9,1},{2,10},{10,2},{3,11},{11,3},{4,12},{12,4},... | collective-permute-start | bytes 3145736 | tf_op jit(solution)/shard_map/ppermute | solution.py:450
  80.4 1.0 copy-start.6
  132.9 21.8 %copy-start.1 = (bf16[16,16,5248]{2,1,0:T(8,128)(2,1)}, bf16[16,16,5248]{2,1,0:T(8,128)(2,1)S(1)}, u32[]{:S(2)}) copy-start(bf16[16,16,5248]{2,1,0:T(8,128)(2,1)S(1)} %all_to_all.25.parts_ref) | copy-start | bytes 8060932
  154.7 2.9 %copy-start.3 = (bf16[16,8,4608]{2,1,0:T(8,128)(2,1)}, bf16[16,8,4608]{2,1,0:T(8,128)(2,1)S(1)}, u32[]{:S(2)}) copy-start(bf16[16,8,4608]{2,1,0:T(8,128)(2,1)S(1)} %all_to_all.26) | copy-start | bytes 3538948
  154.7 2.8 %collective-permute-start.1 = (bf16[128,4608]{1,0:T(8,128)(2,1)S(1)}, bf16[128,4608]{1,0:T(8,128)(2,1)S(1)}, u32[]{:S(2)}, u32[]{:S(2)}) collective-permute-start(bf16[128,4608]{1,0:T(8,128)(2,1)S(1)} %bitcast.51), channel_id=1, source_target_pairs={{0,8},{8,0},{1,9},{9,1},{2,10},{10,2},{3,11},{11,3},{4,12},{12,4},... | collective-permute-start | bytes 3538952 | tf_op jit(solution)/shard_map/ppermute | solution.py:472
  157.6 1.0 copy-start.5
  209.2 2.9 %collective-permute-start.2 = (bf16[8,8,64,128]{3,2,1,0:T(8,128)(2,1)}, bf16[8,8,64,128]{3,2,1,0:T(8,128)(2,1)S(1)}, u32[]{:S(2)}, u32[]{:S(2)}) collective-permute-start(bf16[8,8,64,128]{3,2,1,0:T(8,128)(2,1)} %grads_other.1), channel_id=1, source_target_pairs={{0,8},{8,0},{1,9},{9,1},{2,10},{10,2},{3,11},{11,3},{4,12},{12,4},... | collective-permute-start | bytes 3145736 | tf_op jit(solution)/shard_map/ppermute | solution.py:513
  212.1 1.0 copy-start.7
  220.9 40.7 %all-to-all-start.4 = ((bf16[64,64,128]{2,1,0:T(8,128)(2,1)}), bf16[64,64,128]{2,1,0:T(8,128)(2,1)S(1)}, u32[]{:S(2)}, u32[]{:S(2)}) async-start(bf16[64,64,128]{2,1,0:T(8,128)(2,1)} %bitcast.53), calls=%async_computation.4 | async-start | bytes 2097152 | tf_op jit(solution)/shard_map/all_to_all | solution.py:515
  261.6 1.0 copy-start.4

commit v3 on v2

v3 whole, which is shorter than its diff:
```python
import functools

import jax
import jax.numpy as jnp
from jax import lax
from jax.experimental import pallas as pl
from jax.experimental.pallas import tpu as pltpu
from jax.sharding import Mesh, PartitionSpec as P

F32 = jnp.float32
BF16 = jnp.bfloat16
EPS = 1e-05
PLANE = ("xl", "y", "xh")
SECTION = ("y", "xh")
SWAP = [(0, 1), (1, 0)]
NS = 8
R = 128
TOK = 8
MIC = 4
BLK = 128
HALF = 1024
W_LANE = 2 * HALF
SENT = 3072
PROJ = 29
NORM = 36
START = 37
GRAM = 45
GRAMS = 32
SPLIT = 39
OO = 36
OI = 28
LARGE = pltpu.CompilerParams(vmem_limit_bytes=56 * 1024 * 1024)
PARAMS = pltpu.CompilerParams(vmem_limit_bytes=32 * 1024 * 1024)
VMEM = pl.BlockSpec(memory_space=pltpu.VMEM)
SMEM = pl.BlockSpec(memory_space=pltpu.SMEM)


def gram_at(t):
    return sum(NS - i for i in range(t))


def cross_at(t):
    return sum(NS - 1 - i for i in range(t))


def proj_at(s):
    return s * (s - 1) // 2


def dot_t(a, b):
    return lax.dot_general(a, b, (((1,), (1,)), ((), ())), preferred_element_type=F32)


def dot_rows(a, b):
    return lax.dot_general(a, b, (((0,), (0,)), ((), ())), preferred_element_type=F32)


def dot(a, b):
    return jnp.dot(a, b, preferred_element_type=F32)


def split(x):
    high = x.astype(BF16)
    return high, (x - high.astype(F32)).astype(BF16)


def interleave(tiles):
    lane = lax.broadcasted_iota(jnp.int32, tiles[0].shape, 1)
    low = lane < 64
    even = lane % 64 < 32
    a, b, c, d = tiles
    halves = []
    for p, q in ((a, c), (b, d)):
        halves.append(
            (
                jnp.where(low, p, pltpu.roll(q, 64, 1)),
                jnp.where(low, pltpu.roll(p, 64, 1), q),
            )
        )
    result = []
    for p, q in zip(halves[0], halves[1]):
        result.append(jnp.where(even, p, pltpu.roll(q, 32, 1)))
        result.append(jnp.where(even, pltpu.roll(p, 96, 1), q))
    return result


def pack_kernel(
    at_ref,
    ids_ref,
    in_ref,
    out_ref,
    w_out_ref,
    w_in_ref,
    gain_ref,
    first_ref,
    all_out_ref,
    all_in_ref,
    all_gain_ref,
    send_ref,
    row_ref,
    cols_ref,
    start_ref,
    sum_ref,
):
    section = at_ref[1]
    last = pl.program_id(0) != 0
    gain = gain_ref[...].reshape(8, BLK).T
    for s in range(NS):
        for j in range(4):
            column = 2 * j + s // 4
            scale = gain[(s % 4) * 32 : (s % 4) * 32 + 32, column : column + 1]
            to = W_LANE + 512 + j * BLK
            send_ref[s, :, to : to + BLK] = (w_in_ref[0, j, 0, s].astype(F32) * scale).astype(BF16)

    for c in range(2):
        for zq in range(2):
            for h in range(2):
                lanes = [((4 * zq + j) * 4 + c * 2 + h) * BLK for j in range(4)]
                to = c * 256 + zq * BLK
                for ref, row, at in (
                    (in_ref, 0, c * HALF + zq * BLK),
                    (in_ref, 32, c * HALF + 256 + zq * BLK),
                    (out_ref, 0, c * HALF + 512 + zq * BLK),
                    (out_ref, 32, c * HALF + 768 + zq * BLK),
                    (w_out_ref, 0, W_LANE + c * 256 + zq * BLK),
                ):
                    tiles = interleave(
                        [ref[row : row + 32, lane : lane + BLK].astype(F32) for lane in lanes]
                    )
                    for i in range(4):
                        send_ref[4 * h + i, :, at : at + BLK] = tiles[i].astype(BF16)
            tiles = []
            for j in range(4):
                lane = pl.multiple_of(((4 * zq + j) * 4 + c * 2 + section // 4) * BLK, BLK)
                tiles.append(
                    jnp.concatenate(
                        [first_ref[m, :, pl.ds(lane, BLK)].astype(F32) for m in range(MIC)], 0
                    )
                )
            tiles = interleave(tiles)
            tile = tiles[0]
            for i in range(1, 4):
                tile = jnp.where(section % 4 == i, tiles[i], tile)
            cols_ref[0, :, to : to + BLK] = tile.astype(BF16)

    lane = lax.broadcasted_iota(jnp.int32, (TOK, BLK), 1)
    for m in range(MIC):
        picks = [ids_ref[m, j] == section for j in range(4)]
        block = first_ref[m].astype(F32)
        total = jnp.zeros((TOK, block.shape[1]), F32)
        for j in range(4):
            total = jnp.where(picks[j], block[j * TOK : (j + 1) * TOK], total)
        norm = jnp.sum(total * total, -1, keepdims=True)
        valid = picks[0] | picks[1] | picks[2] | picks[3]
        rows = slice(m * TOK, (m + 1) * TOK)
        before = jnp.where(last, row_ref[rows, :], 0.0)
        fresh = jnp.where(lane == 0, before + norm, jnp.where(valid, 1.0, 0.0))
        row_ref[rows, :] = fresh

    flat = first_ref[...].reshape(R, first_ref.shape[2])
    scaled = (flat.astype(F32) * all_gain_ref[...]).astype(BF16)
    both = jnp.concatenate([dot(scaled, all_in_ref[...]), dot_t(flat, all_out_ref[...])], 1)
    sum_ref[...] = jnp.where(last, sum_ref[...], 0.0) + both

    @pl.when(last)
    def _():
        for m in range(MIC):
            blocks = [sum_ref[(4 * m + j) * TOK : (4 * m + j + 1) * TOK, :] for j in range(4)]
            for e in range(NS):
                total = jnp.zeros((TOK, 2 * R), F32)
                for j in range(4):
                    total = jnp.where(ids_ref[m, j] == e, blocks[j], total)
                start_ref[e * TOK : (e + 1) * TOK, m * 2 * R : (m + 1) * 2 * R] = total


def stores(got_ref, s, at, cols):
    pieces = []
    for x in range(2):
        for i in range(2):
            a, b = at + i * 256, at + 512 + i * 256
            pieces.append(
                got_ref[x * NS + s, :, a : a + cols].astype(F32)
                - got_ref[x * NS + s - 1, :, b : b + cols].astype(F32)
            )
    return jnp.concatenate(pieces, 0)


def project_kernel(
    at_ref,
    ids_ref,
    other_ids_ref,
    got_ref,
    other_ref,
    cols_ref,
    other_cols_ref,
    start_ref,
    send_ref,
    out_w_ref,
    in_w_ref,
    first_ref,
    wide_ref,
):
    cols = cols_ref.shape[1]
    first_core = at_ref[0] == 0
    for s in range(NS):
        for x in range(2):
            mine = got_ref[x * NS + s, :, W_LANE:SENT]
            theirs = other_ref[x * NS + s]
            for c in range(2):
                part = jnp.where(first_core == (c == 0), mine, theirs)
                k = 2 * x + c
                out_w_ref[s, 32 * k : 32 * k + 32, :] = part[:, :cols]
                for g in range(4):
                    row = k * BLK + g * 32
                    lane = cols + g * BLK
                    in_w_ref[s, row : row + 32, :] = part[:, lane : lane + BLK]
    first = [[] for _ in range(MIC)]
    for x in range(2):
        here = at_ref[2] == x
        rows = jnp.where(here, cols_ref[...], other_cols_ref[...]).astype(F32)
        picked = [
            [jnp.where(here, ids_ref[m, j], other_ids_ref[m, j]) for j in range(4)]
            for m in range(MIC)
        ]
        for e in range(NS):
            blocks = []
            for m in range(MIC):
                total = jnp.zeros((TOK, cols), F32)
                for j in range(4):
                    at = (4 * m + j) * TOK
                    total = jnp.where(picked[m][j] == e, rows[at : at + TOK], total)
                blocks.append(total)
                first[m].append(total)
            first_ref[x * NS + e] = jnp.concatenate(blocks, 0).astype(BF16)
    first = [2.0 * jnp.concatenate(blocks, 0) for blocks in first]
    running = None
    lane = lax.broadcasted_iota(jnp.int32, (R, BLK), 1)
    norms = jnp.zeros((R, BLK), F32)
    for s in range(1, NS):
        step = jnp.concatenate(
            [stores(got_ref, s, 0, cols // 2), stores(got_ref, s, HALF, cols // 2)], 1
        )
        running = step if running is None else running + step
        rounded = running.astype(BF16)
        count = s if s < NS - 1 else NS
        at = proj_at(s) * BLK
        wide_ref[:, at : at + count * BLK] = dot_t(
            rounded, out_w_ref[0:count].reshape(count * R, cols)
        )
        at = (PROJ + s - 1) * BLK
        wide_ref[:, at : at + BLK] = dot(rounded, in_w_ref[s])
        for m in range(MIC):
            part = jnp.sum(running * (running + first[m]), -1, keepdims=True)
            norms = jnp.where(lane == m * NS + s, part, norms)
    high = norms.astype(BF16).astype(F32)
    wide_ref[:, NORM * BLK : (NORM + 1) * BLK] = jnp.where(
        lane < 32, high, pltpu.roll(norms - high, 32, 1)
    )
    wide_ref[0:64, START * BLK : GRAM * BLK] = start_ref[...]
    wide_ref[64:128, START * BLK : GRAM * BLK] = start_ref[...]
    wide_ref[:, (GRAM + GRAMS) * BLK :] = jnp.zeros((R, BLK), F32)

    square = [(t, s) for t in range(NS) for s in range(t, NS)]

    @pl.when(first_core)
    def _():
        for t in range(5):
            at = (GRAM + gram_at(t)) * BLK
            wide_ref[:, at : at + (NS - t) * BLK] = dot_t(
                out_w_ref[t], out_w_ref[t:NS].reshape((NS - t) * R, cols)
            )
        for i in range(gram_at(5), GRAMS):
            t, s = square[i]
            at = (GRAM + i) * BLK
            wide_ref[:, at : at + BLK] = dot_t(out_w_ref[t], out_w_ref[s])

    @pl.when(jnp.logical_not(first_core))
    def _():
        for t in range(NS - 1):
            for s in range(t + 1, NS):
                at = (GRAM + cross_at(t) + s - t - 1) * BLK
                wide_ref[:, at : at + BLK] = dot(out_w_ref[t], in_w_ref[s])
        for i in range(GRAMS, OO):
            t, s = square[i]
            at = (GRAM + OI + i - GRAMS) * BLK
            wide_ref[:, at : at + BLK] = dot_t(out_w_ref[t], out_w_ref[s])

    for b in range(SPLIT):
        pair = [
            wide_ref[:, at * BLK : (at + 1) * BLK].reshape(16, TOK, BLK) for at in (b, SPLIT + b)
        ]
        send_ref[:, :, b * BLK : (b + 1) * BLK] = jnp.concatenate(pair, 1).astype(BF16)


def chain_kernel(
    width, at_ref, parts_ref, row_ref, gram_ref, other_ref, send_ref, sum_ref, oo_ref, oi_ref
):
    rows = MIC * TOK
    first_core = at_ref[0] == 0
    for b in range(0, GRAMS, 4):
        at = slice(b * BLK, (b + 4) * BLK)
        mine, theirs = gram_ref[:, at], other_ref[:, at]
        oo_ref[:, at] = jnp.where(first_core, mine, theirs)
        second = jnp.where(first_core, theirs, mine)
        if b < OI:
            oi_ref[:, at] = second
        else:
            oo_ref[:, (b + 4) * BLK : (b + 8) * BLK] = second
    for b in range(START):
        at = slice(b * BLK, (b + 1) * BLK)
        total = parts_ref[0, :, at].astype(F32)
        for q in range(1, 16):
            total = total + parts_ref[q, :, at].astype(F32)
        sum_ref[:, at] = total[:TOK]
    starts = []
    for s in range(NS):
        block = parts_ref[at_ref[2] * NS + s].astype(F32)
        pieces = []
        for m in range(MIC):
            b = START + 2 * m
            if b < SPLIT:
                pieces.append(block[:TOK, b * BLK : (b + 2) * BLK])
            else:
                pieces.append(block[TOK:, (b - SPLIT) * BLK : (b + 2 - SPLIT) * BLK])
        starts.append(jnp.concatenate(pieces, 0))

    def spread(at):
        block = sum_ref[:, at * BLK : (at + 1) * BLK]
        return jnp.concatenate([block] * MIC, 0)

    def square(t, s, count=1):
        at = (gram_at(t) + s - t) * BLK
        return oo_ref[:, at : at + count * BLK]

    def cross(t, s, count=1):
        at = (cross_at(t) + s - t - 1) * BLK
        return oi_ref[:, at : at + count * BLK]

    mask = row_ref[:, 1:2]
    own_norm = row_ref[:, 0:1]
    norm_block = sum_ref[:, NORM * BLK : (NORM + 1) * BLK]
    run_in = [start[:, :R] for start in starts]
    start_out = [start[:, R:] for start in starts]
    run_out = list(start_out)
    inners, inverses, actives, crossed = [], [], [], []
    for s in range(NS):
        norm = own_norm
        entry_out = []
        inner = run_in[s]
        if s > 0:
            inner = inner + spread(PROJ + s - 1)
            norm = norm + jnp.concatenate(
                [
                    norm_block[:, m * NS + s : m * NS + s + 1]
                    + norm_block[:, 32 + m * NS + s : 33 + m * NS + s]
                    for m in range(MIC)
                ],
                0,
            )
            total = jnp.zeros((rows, R), F32)
            for t in range(s):
                base = spread(proj_at(s) + t)
                full = base + run_out[t]
                entry_out.append(full)
                total = total + actives[t].astype(F32) * (full + base + start_out[t])
            norm = norm + jnp.sum(total, -1, keepdims=True)
        inverse = lax.rsqrt(jnp.maximum(norm, 0.0) * (1.0 / width) + EPS)
        inner = inner * inverse
        active = (inner * jax.nn.sigmoid(inner) * mask).astype(BF16)
        inners.append(inner)
        inverses.append(inverse)
        actives.append(active)
        crossed.append(entry_out)
        grown = dot(active, square(s, s, NS - s))
        for t in range(NS):
            if t >= s:
                run_out[t] = run_out[t] + grown[:, (t - s) * R : (t - s + 1) * R]
            else:
                run_out[t] = run_out[t] + dot_t(active, square(t, s))
        if s < NS - 1:
            grown = dot(active, cross(s, s + 1, NS - 1 - s))
            for t in range(s + 1, NS):
                run_in[t] = run_in[t] + grown[:, (t - s - 1) * R : (t - s) * R]
    grads = [run_out[t] + spread(proj_at(NS - 1) + t) for t in range(NS)]
    lane = lax.broadcasted_iota(jnp.int32, (rows, BLK), 1)
    scalars = jnp.zeros((rows, BLK), F32)
    d_inners = [None] * NS
    for s in range(NS - 1, -1, -1):
        inner = inners[s]
        sigm = jax.nn.sigmoid(inner)
        d_inner = (grads[s] * sigm * (1.0 + inner * (1.0 - sigm)) * mask).astype(BF16)
        d_inners[s] = d_inner
        d_wide = d_inner.astype(F32)
        inverse = inverses[s]
        scale = inverse * inverse * jnp.sum(d_wide * inner, -1, keepdims=True) * (1.0 / width)
        for t in range(s):
            grads[t] = (
                grads[t] + inverse * dot_t(d_inner, cross(t, s)) - scale * crossed[s][t]
            )
        for at, value in ((s, inverse), (2 * NS + s, scale)):
            high, low = split(value)
            scalars = jnp.where(lane == at, high.astype(F32), scalars)
            scalars = jnp.where(lane == at + NS, low.astype(F32), scalars)
    for q in range(16):
        for s in range(NS):
            send_ref[q, :, s * R : (s + 1) * R] = actives[s]
            send_ref[q, :, (NS + s) * R : (NS + s + 1) * R] = d_inners[s]
        send_ref[q, :, 2 * NS * R :] = scalars.astype(BF16)


def grads_kernel(at_ref, got_ref, first_ref, out_w_ref, in_w_ref, chain_ref, result_ref, kept_ref):
    cols = first_ref.shape[2]
    rows = 16 * MIC * TOK
    scalars = chain_ref[:, 2 * NS * R :].astype(F32)
    inverses = [scalars[:, s : s + 1] + scalars[:, NS + s : NS + s + 1] for s in range(NS)]
    scales = [
        scalars[:, 2 * NS + s : 2 * NS + s + 1] + scalars[:, 3 * NS + s : 3 * NS + s + 1]
        for s in range(NS)
    ]

    def active(s):
        return chain_ref[:, s * R : (s + 1) * R]

    def d_inner(s):
        return chain_ref[:, (NS + s) * R : (NS + s + 1) * R]

    def put(s, kind, value):
        result_ref[:, s, :, kind * R : (kind + 1) * R] = value.reshape(8, 32, R).astype(
            result_ref.dtype
        )

    entry = first_ref[...].astype(F32).reshape(rows, cols)
    for s in range(NS):
        if s > 0:
            step = stores(got_ref, s, 0, cols)
            step = jnp.broadcast_to(step.reshape(16, 1, TOK, cols), (16, MIC, TOK, cols))
            entry = entry + step.reshape(rows, cols)
        kept_ref[s] = entry
        put(s, 0, dot_rows((entry * inverses[s]).astype(BF16), d_inner(s)))
        entry = entry + dot(active(s), out_w_ref[s])
    grad = entry
    for s in range(NS - 1, -1, -1):
        put(s, 1, dot_rows(grad.astype(BF16), active(s)))
        if s > 0:
            grad = grad + inverses[s] * dot_t(d_inner(s), in_w_ref[s]) - scales[s] * kept_ref[s]


def final_kernel(parts_ref, gain_ref, in_ref, out_ref):
    total = parts_ref[0].astype(F32)
    for i in range(1, 8):
        total = total + parts_ref[i].astype(F32)
    gain = gain_ref[...].T
    for j in range(8):
        scale = gain[(j % 4) * 32 : (j % 4) * 32 + 32, j // 4 : j // 4 + 1]
        in_ref[j * 32 : j * 32 + 32, :] = total[j, :, :R] * scale
    out = total[:, :, R:].reshape(2 * BLK, R)
    for i in range(2):
        out_ref[:, i * BLK : (i + 1) * BLK] = out[i * BLK : (i + 1) * BLK].T


def body(first_input, example_ids, out_store, in_store, norm_gain, adapter_in, adapter_out):
    width = first_input.shape[2]
    cols = width // 16
    half = cols // 2
    wide = width // 2
    core = lax.axis_index("c")
    xl = lax.axis_index("xl")
    z = lax.axis_index("z")
    section = lax.axis_index(SECTION)
    quarter = xl * 2 + core
    at = jnp.stack([core, section, xl, quarter]).astype(jnp.int32)
    ids = example_ids[0]
    w_in = adapter_in[0]
    w_out = adapter_out[0]

    send, row, own_cols, start = pl.pallas_call(
        pack_kernel,
        grid_spec=pltpu.PrefetchScalarGridSpec(
            num_scalar_prefetch=2,
            grid=(2,),
            in_specs=[
                pl.BlockSpec((64, wide), lambda i, at, ids: (0, i)),
                pl.BlockSpec((64, wide), lambda i, at, ids: (0, i)),
                pl.BlockSpec((32, wide), lambda i, at, ids: (at[3], i)),
                pl.BlockSpec(
                    (1, 4, 1, 8, 32, R),
                    lambda i, at, ids: (i, at[3] % 2, at[3] // 2, 0, 0, 0),
                ),
                pl.BlockSpec(
                    (1, 4, 1, 2, BLK), lambda i, at, ids: (i, at[3] % 2, at[3] // 2, 0, 0)
                ),
                pl.BlockSpec((MIC, 32, wide), lambda i, at, ids: (0, 0, i)),
                pl.BlockSpec((R, wide), lambda i, at, ids: (0, i)),
                pl.BlockSpec((wide, R), lambda i, at, ids: (i, 0)),
                pl.BlockSpec((1, wide), lambda i, at, ids: (0, i)),
            ],
            out_specs=[
                pl.BlockSpec((8, 32, SENT), lambda i, at, ids: (i, 0, 0)),
                pl.BlockSpec((MIC * TOK, BLK), lambda i, at, ids: (0, 0)),
                pl.BlockSpec((1, R, cols), lambda i, at, ids: ((i + at[2]) % 2, 0, 0)),
                pl.BlockSpec((NS * TOK, 8 * BLK), lambda i, at, ids: (0, 0)),
            ],
            scratch_shapes=[pltpu.VMEM((R, 2 * R), F32)],
        ),
        out_shape=(
            jax.ShapeDtypeStruct((16, 32, SENT), BF16),
            jax.ShapeDtypeStruct((MIC * TOK, BLK), F32),
            jax.ShapeDtypeStruct((2, R, cols), BF16),
            jax.ShapeDtypeStruct((NS * TOK, 8 * BLK), F32),
        ),
        compiler_params=LARGE,
        name="pack",
    )(
        at,
        ids,
        in_store.reshape(64, width),
        out_store.reshape(64, width),
        w_out,
        w_in.reshape(2, 8, 2, 8, 32, R),
        norm_gain.reshape(2, 8, 2, 2, BLK),
        first_input,
        w_out,
        w_in,
        norm_gain,
    )
    other_ids = lax.ppermute(ids, "xl", SWAP)
    other_cols = lax.ppermute(own_cols[1], "xl", SWAP)
    got = lax.all_to_all(send, PLANE, 0, 0, tiled=True)
    other = lax.ppermute(got[:, :, W_LANE:], "c", SWAP)
    parts, out_w, in_w, first = pl.pallas_call(
        project_kernel,
        out_shape=(
            jax.ShapeDtypeStruct((16, 2 * TOK, SPLIT * BLK), BF16),
            jax.ShapeDtypeStruct((NS, R, cols), BF16),
            jax.ShapeDtypeStruct((NS, cols, R), BF16),
            jax.ShapeDtypeStruct((16, MIC * TOK, cols), BF16),
        ),
        in_specs=[SMEM, SMEM, SMEM, VMEM, VMEM, VMEM, VMEM, VMEM],
        out_specs=(VMEM, VMEM, VMEM, VMEM),
        scratch_shapes=[pltpu.VMEM((R, 2 * SPLIT * BLK), F32)],
        compiler_params=PARAMS,
        name="project",
    )(at, ids, other_ids, got, other, own_cols[0], other_cols, start)
    parts = lax.all_to_all(parts, PLANE, 0, 0, tiled=True)

    first_gram = (GRAM - SPLIT) * BLK
    gram = parts[:, TOK:, first_gram : first_gram + GRAMS * BLK].astype(F32)
    gram = jnp.sum(gram, 0).astype(BF16)
    gram = lax.all_to_all(
        jnp.broadcast_to(gram, (16,) + gram.shape), PLANE, 0, 0, tiled=True
    ).reshape(R, GRAMS * BLK)
    other = lax.ppermute(gram, "c", SWAP)

    latent = pl.pallas_call(
        functools.partial(chain_kernel, width),
        out_shape=jax.ShapeDtypeStruct((16, MIC * TOK, 17 * BLK), BF16),
        in_specs=[SMEM, VMEM, VMEM, VMEM, VMEM],
        out_specs=VMEM,
        scratch_shapes=[
            pltpu.VMEM((TOK, START * BLK), F32),
            pltpu.VMEM((R, OO * BLK), BF16),
            pltpu.VMEM((R, OI * BLK), BF16),
        ],
        compiler_params=PARAMS,
        name="chain",
    )(at, parts, row, gram, other)
    latent = lax.all_to_all(latent, PLANE, 0, 0, tiled=True).reshape(16 * MIC * TOK, 17 * BLK)

    def grads(own):
        def side(at):
            return at[0] if own else 1 - at[0]

        return pl.pallas_call(
            grads_kernel,
            grid_spec=pltpu.PrefetchScalarGridSpec(
                num_scalar_prefetch=1,
                grid=(1,),
                in_specs=[
                    pl.BlockSpec((16, 32, HALF), lambda i, at: (0, 0, side(at))),
                    pl.BlockSpec((16, MIC * TOK, half), lambda i, at: (0, 0, side(at))),
                    pl.BlockSpec((NS, R, half), lambda i, at: (0, 0, side(at))),
                    pl.BlockSpec((NS, half, R), lambda i, at: (0, side(at), 0)),
                    pl.BlockSpec((16 * MIC * TOK, 17 * BLK), lambda i, at: (0, 0)),
                ],
                out_specs=pl.BlockSpec((8, NS, 32, 2 * R), lambda i, at: (0, 0, 0, 0)),
                scratch_shapes=[pltpu.VMEM((NS, 16 * MIC * TOK, half), F32)],
            ),
            out_shape=jax.ShapeDtypeStruct((8, NS, 32, 2 * R), F32 if own else BF16),
            compiler_params=PARAMS,
            name="grads_own" if own else "grads_other",
        )(at, got, first, out_w, in_w, latent)

    swapped = lax.ppermute(grads(False), "c", SWAP)
    total = (grads(True) + swapped.astype(F32)).astype(BF16).reshape(64, 32, 2 * R)
    block = (xl * NS + z) * 2 + core
    gain = lax.dynamic_slice_in_dim(norm_gain[0], block * half, half, 0)
    total, gain = lax.optimization_barrier((total, gain))
    total = lax.all_to_all(total, ("z",) + SECTION, 0, 0, tiled=True)
    grad_in, grad_out = pl.pallas_call(
        final_kernel,
        out_shape=(
            jax.ShapeDtypeStruct((half, R), F32),
            jax.ShapeDtypeStruct((R, half), F32),
        ),
        in_specs=[VMEM, VMEM],
        out_specs=(VMEM, VMEM),
        compiler_params=PARAMS,
        name="final",
    )(total.reshape(8, 8, 32, 2 * R), gain.reshape(2, BLK))
    return (grad_in[None], grad_out[None])


def solution(mesh):
    fine = Mesh(mesh.devices.reshape(2, 8, 2, 4, 2), ("xl", "z", "c", "y", "xh"))
    dp = ("xl", "z", "c")
    placed = (
        P(None, dp, None),
        P(dp, None, None),
        P(SECTION, dp, None, None),
        P(SECTION, dp, None, None),
        P(SECTION, None),
        P(SECTION, None, None),
        P(SECTION, None, None),
    )
    return jax.shard_map(
        body,
        mesh=fine,
        in_specs=placed,
        out_specs=(P(SECTION, dp, None), P(SECTION, None, dp)),
        check_vma=False,
    )
```

time: 265 us -> 228 us (0.86)
  waiting for transfers between devices: 89.7 us -> 5.84 us
  blocking collectives: 99.9 us -> 177 us
  starting transfers between devices: 17.5 us -> 2.21 us
  Pallas kernels: 43.9 us -> 33.2 us
  matrix products: 3.26 us -> 0 us
    all_to_all x0 -> x2, blocking collectives: none -> 86.9 us  [the longest x1 46.2 us: body(): got = lax.all_to_all(send, PLANE, 0, 0, tiled=True)]
    all_to_all x2 -> x0, waiting for transfers between devices: 82.6 us -> none  [the longest x1 52.6 us: body(): got = lax.all_to_all(send, PLANE, 0, 0, tiled=True)]
    all_to_all x2 -> x0, starting transfers between devices: 17.4 us -> none  [the longest x1 10.2 us: body(): total = lax.all_to_all(total, ('z',) + SECTION, 0, 0, tiled=True)]
    all_to_all x1, blocking collectives: 43.4 us -> 35.7 us  [body(): parts = lax.all_to_all(parts, PLANE, 0, 0, tiled=True)]
    pallas_call x2, Pallas kernels: 15.3 us -> 9.41 us  [grads(): pl.pallas_call(grads_kernel, grid_spec=pltpu.PrefetchScalarGridSpec(num_s...]
    pallas_call x1, Pallas kernels: 8.06 us -> 4.71 us  [body(): pl.pallas_call(functools.partial(chain_kernel, width), out_shape=jax.Shap...]
    dot_general x2 -> x0, matrix products: 3.26 us -> none  [the longest x1 2.3 us: dot_t(): lax.dot_general(a, b, (((1,), (1,)), ((), ())), preferred_element_type=F32)]
    pallas_call x1, Pallas kernels: 8.2 us -> 4.97 us  [body(): pl.pallas_call(project_kernel, out_shape=(jax.ShapeDtypeStruct((16, 2 * T...]
  transfers between devices with their start and end apart: 5 -> 5, of which waited for: 5 -> 2; matrix products, arithmetic and copies ran while one was open for 2% -> 0% of each run, Pallas kernels for 0% -> 2%
where the time goes in v3:
time: 228 us
  blocking collectives  177 us (78%)
  Pallas kernels  33.2 us (15%)
  local copies, waits for them, and re-layouts  6.77 us (3%)
  waiting for transfers between devices  5.84 us (3%)
  other arithmetic  2.36 us (1%)
    all_to_all x1, blocking collectives, body(): got = lax.all_to_all(send, PLANE, 0, 0, tiled=True)  46.2 us
    all_to_all x1, blocking collectives, body(): total = lax.all_to_all(total, ('z',) + SECTION, 0, 0, tiled=True)  40.6 us
    all_to_all x1, blocking collectives, body(): parts = lax.all_to_all(parts, PLANE, 0, 0, tiled=True)  35.7 us
    all_to_all x1, blocking collectives, body(): lax.all_to_all(latent, PLANE, 0, 0, tiled=True)  33.5 us
    all_to_all x1, blocking collectives, body(): lax.all_to_all(jnp.broadcast_to(gram, (16,) + gram.shape), PLANE, 0, 0, t...  20.4 us
    pallas_call x1, Pallas kernels, body(): pl.pallas_call(pack_kernel, grid_spec=pltpu.PrefetchScalarGridSpec(num_sc...  13.1 us
    pallas_call x2, Pallas kernels, grads(): pl.pallas_call(grads_kernel, grid_spec=pltpu.PrefetchScalarGridSpec(num_s...  9.41 us
    unnamed x26, local copies, waits for them, and re-layouts  5.89 us
  transfers between devices with their start and end apart: 5, of which 2 were waited for; matrix products, arithmetic and copies ran while one was open for 0% of the time, Pallas kernels for 2%

profile of v3, /device:TPU:32, one launch (start us, length us, event | category | flops | bytes accessed | tf_op | source)
XLA Modules:
  0.0 227.6 jit_solution(11282347246493376720)
XLA Ops:
  0.6 0.6 pad_add_fusion.at_ref
  1.2 13.1 %pack.1 = (bf16[16,32,3072]{2,1,0:T(8,128)(2,1)}, f32[32,128]{1,0:T(8,128)}, bf16[2,128,512]{2,1,0:T(8,128)(2,1)}, f32[64,1024]{1,0:T(8,128)}) custom-call(s32[4]{0:T(128)} %pad_add_fusion.at_ref, s32[4,8]{1,0:T(4,128)} %bitcast.28, bf16[64,8192]{1,0:T(8,128)(2,1)} %bitcast.37, bf16[64,8192]{1,0:T(8,128)(2,1)} %bitcast.38, bf16[128,8192]{1,0:T(8,128)(2,1)} %bitcast.32, ...), custom_call_target="tpu_custom_call" | custom-call | tf_op jit(solution)/shard_map/pack/pallas_call | solution.py:476
  14.4 46.2 %all_to_all.25.got_ref = bf16[16,32,3072]{2,1,0:T(8,128)(2,1)S(1)} all-to-all(bf16[16,32,3072]{2,1,0:T(8,128)(2,1)} %get-tuple-element.14), channel_id=1, replica_groups=mesh['xl'=2,'z'=8,'c'=2,'y'=4,'xh'=2] {'xl','y','xh'}, dimensions={0} | all-to-all | bytes 6291456 | tf_op jit(solution)/shard_map/all_to_all | solution.py:528
  60.6 0.1 slice.16
  60.7 0.1 collective-permute-start.1
  60.8 0.7 copy-done.12
  61.6 0.7 collective-permute-start.2
  62.2 1.5 collective-permute-start
  63.7 3.2 %collective-permute-done.other_ids_ref = s32[4,8]{1,0:T(4,128)S(1)} collective-permute-done((s32[4,8]{1,0:T(4,128)S(1)}, s32[4,8]{1,0:T(4,128)S(1)}, u32[]{:S(2)}, u32[]{:S(2)}) %collective-permute-start) | collective-permute-done | bytes 160 | tf_op jit(solution)/shard_map/ppermute | solution.py:526
  66.8 0.0 collective-permute-done.2.other_cols_ref
  66.9 0.0 collective-permute-done.1.other_ref
  66.9 5.0 %project.1 = (bf16[16,16,4992]{2,1,0:T(8,128)(2,1)S(1)}, bf16[8,128,512]{2,1,0:T(8,128)(2,1)S(1)}, bf16[8,512,128]{2,1,0:T(8,128)(2,1)S(1)}, bf16[16,32,512]{2,1,0:T(8,128)(2,1)S(1)}) custom-call(s32[4]{0:T(128)S(1)} %copy-done.9, s32[4,8]{1,0:T(4,128)S(1)} %bitcast.30, s32[4,8]{1,0:T(4,128)S(1)} %collective-permute-done.other_ids_ref, ...), custom_call_target="tpu_custom_call" | custom-call | tf_op jit(solution)/shard_map/project/pallas_call | solution.py:530
  71.9 35.7 %all_to_all.26.parts_ref = bf16[16,16,4992]{2,1,0:T(8,128)(2,1)S(1)} all-to-all(bf16[16,16,4992]{2,1,0:T(8,128)(2,1)S(1)} %get-tuple-element.20), channel_id=1, replica_groups=mesh['xl'=2,'z'=8,'c'=2,'y'=4,'xh'=2] {'xl','y','xh'}, dimensions={0} | all-to-all | bytes 5111808 | tf_op jit(solution)/shard_map/all_to_all | solution.py:544
  107.6 0.1 slice_reduce_fusion
  107.7 0.1 broadcast_in_dim.9
  107.8 20.4 %all_to_all.27 = bf16[16,8,4096]{2,1,0:T(8,128)(2,1)S(1)} all-to-all(bf16[16,8,4096]{2,1,0:T(8,128)(2,1)S(1)} %broadcast_in_dim.9), channel_id=1, replica_groups=mesh['xl'=2,'z'=8,'c'=2,'y'=4,'xh'=2] {'xl','y','xh'}, dimensions={0} | all-to-all | bytes 2097152 | tf_op jit(solution)/shard_map/all_to_all | solution.py:549
  128.2 0.0 collective-permute-start.3
  128.2 2.7 %collective-permute-done.3.other_ref = bf16[128,4096]{1,0:T(8,128)(2,1)S(1)} collective-permute-done((bf16[128,4096]{1,0:T(8,128)(2,1)S(1)}, bf16[128,4096]{1,0:T(8,128)(2,1)S(1)}, u32[]{:S(2)}, u32[]{:S(2)}) %collective-permute-start.3) | collective-permute-done | bytes 1048608 | tf_op jit(solution)/shard_map/ppermute | solution.py:552
  130.9 4.7 %chain.1 = bf16[16,32,2176]{2,1,0:T(8,128)(2,1)S(1)} custom-call(s32[4]{0:T(128)S(1)} %copy-done.9, bf16[16,16,4992]{2,1,0:T(8,128)(2,1)S(1)} %all_to_all.26.parts_ref, f32[32,128]{1,0:T(8,128)S(1)} %copy-done.10, bf16[128,4096]{1,0:T(8,128)(2,1)S(1)} %bitcast.27, bf16[128,4096]{1,0:T(8,128)(2,1)S(1)} %collective-permute-done.3.other_ref), custom_call_target="tpu_custom_call" | custom-call | tf_op jit(solution)/shard_map/chain/pallas_call | solution.py:554
  135.6 33.5 %all_to_all.28 = bf16[16,32,2176]{2,1,0:T(8,128)(2,1)S(1)} all-to-all(bf16[16,32,2176]{2,1,0:T(8,128)(2,1)S(1)} %chain.1), channel_id=1, replica_groups=mesh['xl'=2,'z'=8,'c'=2,'y'=4,'xh'=2] {'xl','y','xh'}, dimensions={0} | all-to-all | bytes 4456448 | tf_op jit(solution)/shard_map/all_to_all | solution.py:567
  169.2 5.2 %grads_other.1 = bf16[8,8,32,256]{3,2,1,0:T(8,128)(2,1)} custom-call(s32[4]{0:T(128)S(1)} %copy-done.9, bf16[16,32,3072]{2,1,0:T(8,128)(2,1)S(1)} %all_to_all.25.got_ref, bf16[16,32,512]{2,1,0:T(8,128)(2,1)S(1)} %get-tuple-element.17.first_ref, bf16[8,128,512]{2,1,0:T(8,128)(2,1)S(1)} %get-tuple-element.18.out_w_ref, ...), custom_call_target="tpu_custom_call" | custom-call | tf_op jit(solution)/shard_map/grads_other/pallas_call | solution.py:573
  174.4 0.0 collective-permute-start.4
  174.4 0.7 constant_dynamic-slice_fusion
  175.1 1.6 copy-done.1
  176.7 1.2 copy-done.3
  177.9 1.2 copy-done.5
  179.1 1.0 copy-done.7
  180.2 4.2 %grads_own.1 = f32[8,8,32,256]{3,2,1,0:T(8,128)S(1)} custom-call(s32[4]{0:T(128)S(1)} %copy-done.9, bf16[16,32,3072]{2,1,0:T(8,128)(2,1)S(1)} %all_to_all.25.got_ref, bf16[16,32,512]{2,1,0:T(8,128)(2,1)S(1)} %copy-done.7, bf16[8,128,512]{2,1,0:T(8,128)(2,1)S(1)} %copy-done.3, bf16[8,512,128]{2,1,0:T(8,128)(2,1)S(1)} %copy-done.5, bf16[512,2176]{1,0:T(8,128)(2,1)S(1)} %bitcast.24), custom_call_target="tpu_custom_call" | custom-call | tf_op jit(solution)/shard_map/grads_own/pallas_call | solution.py:573
  184.4 0.0 collective-permute-done.4
  184.4 1.6 add_convert_fusion
  186.0 40.6 %all_to_all.29 = bf16[64,32,256]{2,1,0:T(8,128)(2,1)S(1)} all-to-all(bf16[64,32,256]{2,1,0:T(8,128)(2,1)S(1)} %bitcast.36), channel_id=1, replica_groups=mesh['xl'=2,'z'=8,'c'=2,'y'=4,'xh'=2] {'z','y','xh'}, dimensions={0} | all-to-all | bytes 2097152 | tf_op jit(solution)/shard_map/all_to_all | solution.py:598
  226.7 0.9 final.1
  (22 shorter events, 0.1 us)
Async XLA Ops:
  60.6 1.0 copy-start.12
  60.6 1.6 copy-start.11
  60.6 6.3 %copy-start.8 = (f32[64,1024]{1,0:T(8,128)S(1)}, f32[64,1024]{1,0:T(8,128)}, u32[]{:S(2)}) copy-start(f32[64,1024]{1,0:T(8,128)} %get-tuple-element.16.start_ref) | copy-start | bytes 786436
  60.6 6.3 %copy-start.9 = (s32[4]{0:T(128)S(1)}, s32[4]{0:T(128)}, u32[]{:S(2)}) copy-start(s32[4]{0:T(128)} %pad_add_fusion.at_ref) | copy-start | bytes 52
  60.7 6.2 %collective-permute-start.1 = (bf16[16,32,1024]{2,1,0:T(8,128)(2,1)S(1)}, bf16[16,32,1024]{2,1,0:T(8,128)(2,1)S(1)}, u32[]{:S(2)}, u32[]{:S(2)}) collective-permute-start(bf16[16,32,1024]{2,1,0:T(8,128)(2,1)S(1)} %slice.16), channel_id=1, source_target_pairs={{0,8},{8,0},{1,9},{9,1},{2,10},{10,2},{3,11},{11,3},{4,12},{12,4},... | collective-permute-start | bytes 3145736 | tf_op jit(solution)/shard_map/ppermute | solution.py:529
  61.6 5.3 %collective-permute-start.2 = (bf16[128,512]{1,0:T(8,128)(2,1)S(1)}, bf16[128,512]{1,0:T(8,128)(2,1)S(1)}, u32[]{:S(2)}, u32[]{:S(2)}) collective-permute-start(bf16[128,512]{1,0:T(8,128)(2,1)S(1)} %get-tuple-element.26), channel_id=1, source_target_pairs={{0,128},{128,0},{1,129},{129,1},{2,130},{130,2},{3,131},{131,3},{4... | collective-permute-start | bytes 393224 | tf_op jit(solution)/shard_map/ppermute | solution.py:527
  62.2 4.6 %collective-permute-start = (s32[4,8]{1,0:T(4,128)S(1)}, s32[4,8]{1,0:T(4,128)S(1)}, u32[]{:S(2)}, u32[]{:S(2)}) collective-permute-start(s32[4,8]{1,0:T(4,128)S(1)} %bitcast.29), channel_id=1, source_target_pairs={{0,128},{128,0},{1,129},{129,1},{2,130},{130,2},{3,131},{131,3},{4... | collective-permute-start | bytes 392 | tf_op jit(solution)/shard_map/ppermute | solution.py:526
  71.9 97.3 %copy-start.2 = (bf16[8,128,512]{2,1,0:T(8,128)(2,1)}, bf16[8,128,512]{2,1,0:T(8,128)(2,1)S(1)}, u32[]{:S(2)}) copy-start(bf16[8,128,512]{2,1,0:T(8,128)(2,1)S(1)} %get-tuple-element.18.out_w_ref) | copy-start | bytes 3145732
  71.9 97.3 %copy-start.4 = (bf16[8,512,128]{2,1,0:T(8,128)(2,1)}, bf16[8,512,128]{2,1,0:T(8,128)(2,1)S(1)}, u32[]{:S(2)}) copy-start(bf16[8,512,128]{2,1,0:T(8,128)(2,1)S(1)} %get-tuple-element.19.in_w_ref) | copy-start | bytes 3145732
  71.9 97.3 %copy-start.6 = (bf16[16,32,512]{2,1,0:T(8,128)(2,1)}, bf16[16,32,512]{2,1,0:T(8,128)(2,1)S(1)}, u32[]{:S(2)}) copy-start(bf16[16,32,512]{2,1,0:T(8,128)(2,1)S(1)} %get-tuple-element.17.first_ref) | copy-start | bytes 1572868
  107.6 23.3 %copy-start.10 = (f32[32,128]{1,0:T(8,128)S(1)}, f32[32,128]{1,0:T(8,128)}, u32[]{:S(2)}) copy-start(f32[32,128]{1,0:T(8,128)} %get-tuple-element.21.row_ref) | copy-start | bytes 49156
  128.2 2.7 %collective-permute-start.3 = (bf16[128,4096]{1,0:T(8,128)(2,1)S(1)}, bf16[128,4096]{1,0:T(8,128)(2,1)S(1)}, u32[]{:S(2)}, u32[]{:S(2)}) collective-permute-start(bf16[128,4096]{1,0:T(8,128)(2,1)S(1)} %bitcast.26), channel_id=1, source_target_pairs={{0,8},{8,0},{1,9},{9,1},{2,10},{10,2},{3,11},{11,3},{4,12},{12,4},... | collective-permute-start | bytes 3145736 | tf_op jit(solution)/shard_map/ppermute | solution.py:552
  169.2 5.2 %copy-start = (bf16[16,32,2176]{2,1,0:T(8,128)(2,1)}, bf16[16,32,2176]{2,1,0:T(8,128)(2,1)S(1)}, u32[]{:S(2)}) copy-start(bf16[16,32,2176]{2,1,0:T(8,128)(2,1)S(1)} %all_to_all.28) | copy-start | bytes 6684676
  174.4 10.0 %collective-permute-start.4 = (bf16[8,8,32,256]{3,2,1,0:T(8,128)(2,1)}, bf16[8,8,32,256]{3,2,1,0:T(8,128)(2,1)}, u32[]{:S(2)}, u32[]{:S(2)}) collective-permute-start(bf16[8,8,32,256]{3,2,1,0:T(8,128)(2,1)} %grads_other.1), channel_id=1, source_target_pairs={{0,8},{8,0},{1,9},{9,1},{2,10},{10,2},{3,11},{11,3},{4,12},{12,4},... | collective-permute-start | bytes 3145736 | tf_op jit(solution)/shard_map/ppermute | solution.py:593
  175.1 1.6 copy-start.1
  176.7 1.2 copy-start.3
  177.9 1.2 copy-start.5
  179.1 1.0 copy-start.7

commit v4 on v3

--- a/solution.py
+++ b/solution.py
@@ -30,7 +30,7 @@
 OO = 36
 OI = 28
 LARGE = pltpu.CompilerParams(vmem_limit_bytes=56 * 1024 * 1024)
-PARAMS = pltpu.CompilerParams(vmem_limit_bytes=32 * 1024 * 1024)
+PARAMS = pltpu.CompilerParams(vmem_limit_bytes=16 * 1024 * 1024)
 VMEM = pl.BlockSpec(memory_space=pltpu.VMEM)
 SMEM = pl.BlockSpec(memory_space=pltpu.SMEM)
 
@@ -64,46 +64,21 @@
     return high, (x - high.astype(F32)).astype(BF16)
 
 
-def interleave(tiles):
-    lane = lax.broadcasted_iota(jnp.int32, tiles[0].shape, 1)
-    low = lane < 64
-    even = lane % 64 < 32
-    a, b, c, d = tiles
-    halves = []
-    for p, q in ((a, c), (b, d)):
-        halves.append(
-            (
-                jnp.where(low, p, pltpu.roll(q, 64, 1)),
-                jnp.where(low, pltpu.roll(p, 64, 1), q),
-            )
-        )
-    result = []
-    for p, q in zip(halves[0], halves[1]):
-        result.append(jnp.where(even, p, pltpu.roll(q, 32, 1)))
-        result.append(jnp.where(even, pltpu.roll(p, 96, 1), q))
-    return result
-
-
 def pack_kernel(
-    at_ref,
-    ids_ref,
-    in_ref,
-    out_ref,
-    w_out_ref,
-    w_in_ref,
-    gain_ref,
-    first_ref,
-    all_out_ref,
-    all_in_ref,
-    all_gain_ref,
-    send_ref,
-    row_ref,
-    cols_ref,
-    start_ref,
-    sum_ref,
+    at_ref, in_ref, out_ref, w_out_ref, w_in_ref, gain_ref, first_ref,
+    send_ref, cols_ref, give_ref, turn_ref,
 ):
     section = at_ref[1]
-    last = pl.program_id(0) != 0
+
+    @pl.when(pl.program_id(0) == 0)
+    def _():
+        shape = (4 * BLK, 4 * BLK)
+        row = lax.broadcasted_iota(jnp.int32, shape, 0)
+        col = lax.broadcasted_iota(jnp.int32, shape, 1)
+        same = (row // BLK == col % BLK // 32) & (row % BLK // 32 == col // BLK)
+        same = same & (row % 32 == col % 32)
+        turn_ref[...] = jnp.where(same, 1.0, 0.0).astype(BF16)
+
     gain = gain_ref[...].reshape(8, BLK).T
     for s in range(NS):
         for j in range(4):
@@ -112,37 +87,65 @@
             to = W_LANE + 512 + j * BLK
             send_ref[s, :, to : to + BLK] = (w_in_ref[0, j, 0, s].astype(F32) * scale).astype(BF16)
 
+    pieces, places = [], []
     for c in range(2):
         for zq in range(2):
+            to = c * 256 + zq * BLK
             for h in range(2):
                 lanes = [((4 * zq + j) * 4 + c * 2 + h) * BLK for j in range(4)]
-                to = c * 256 + zq * BLK
                 for ref, row, at in (
                     (in_ref, 0, c * HALF + zq * BLK),
                     (in_ref, 32, c * HALF + 256 + zq * BLK),
                     (out_ref, 0, c * HALF + 512 + zq * BLK),
                     (out_ref, 32, c * HALF + 768 + zq * BLK),
-                    (w_out_ref, 0, W_LANE + c * 256 + zq * BLK),
+                    (w_out_ref, 0, W_LANE + to),
                 ):
-                    tiles = interleave(
-                        [ref[row : row + 32, lane : lane + BLK].astype(F32) for lane in lanes]
+                    pieces.append(
+                        jnp.concatenate(
+                            [ref[row : row + 32, lane : lane + BLK] for lane in lanes], 1
+                        )
                     )
-                    for i in range(4):
-                        send_ref[4 * h + i, :, at : at + BLK] = tiles[i].astype(BF16)
-            tiles = []
-            for j in range(4):
-                lane = pl.multiple_of(((4 * zq + j) * 4 + c * 2 + section // 4) * BLK, BLK)
-                tiles.append(
-                    jnp.concatenate(
-                        [first_ref[m, :, pl.ds(lane, BLK)].astype(F32) for m in range(MIC)], 0
-                    )
+                    places.append((4 * h, at))
+    turned = dot(jnp.concatenate(pieces, 0), turn_ref[...]).astype(BF16)
+    for n, (first, at) in enumerate(places):
+        for i in range(4):
+            send_ref[first + i, :, at : at + BLK] = turned[
+                32 * n : 32 * n + 32, i * BLK : (i + 1) * BLK
+            ]
+
+    pieces = []
+    for c in range(2):
+        for zq in range(2):
+            lanes = [
+                pl.multiple_of(((4 * zq + j) * 4 + c * 2 + section // 4) * BLK, BLK)
+                for j in range(4)
+            ]
+            for m in range(MIC):
+                pieces.append(
+                    jnp.concatenate([first_ref[m, :, pl.ds(lane, BLK)] for lane in lanes], 1)
                 )
-            tiles = interleave(tiles)
-            tile = tiles[0]
-            for i in range(1, 4):
-                tile = jnp.where(section % 4 == i, tiles[i], tile)
-            cols_ref[0, :, to : to + BLK] = tile.astype(BF16)
-
+    group = pl.multiple_of(section % 4 * BLK, BLK)
+    turned = dot(jnp.concatenate(pieces, 0), turn_ref[:, pl.ds(group, BLK)]).astype(BF16)
+    mine = pl.program_id(0) == at_ref[2]
+
+    def put(ref):
+        for n in range(4):
+            ref[:, n * BLK : (n + 1) * BLK] = turned[n * R : (n + 1) * R]
+
+    @pl.when(mine)
+    def _():
+        put(cols_ref)
+
+    @pl.when(jnp.logical_not(mine))
+    def _():
+        put(give_ref)
+
+
+def start_kernel(
+    at_ref, ids_ref, first_ref, w_out_ref, w_in_ref, gain_ref, after_ref, row_ref, start_ref
+):
+    del after_ref
+    section = at_ref[1]
     lane = lax.broadcasted_iota(jnp.int32, (TOK, BLK), 1)
     for m in range(MIC):
         picks = [ids_ref[m, j] == section for j in range(4)]
@@ -152,25 +155,19 @@
             total = jnp.where(picks[j], block[j * TOK : (j + 1) * TOK], total)
         norm = jnp.sum(total * total, -1, keepdims=True)
         valid = picks[0] | picks[1] | picks[2] | picks[3]
-        rows = slice(m * TOK, (m + 1) * TOK)
-        before = jnp.where(last, row_ref[rows, :], 0.0)
-        fresh = jnp.where(lane == 0, before + norm, jnp.where(valid, 1.0, 0.0))
-        row_ref[rows, :] = fresh
-
+        row_ref[m * TOK : (m + 1) * TOK, :] = jnp.where(
+            lane == 0, norm, jnp.where(valid, 1.0, 0.0)
+        )
     flat = first_ref[...].reshape(R, first_ref.shape[2])
-    scaled = (flat.astype(F32) * all_gain_ref[...]).astype(BF16)
-    both = jnp.concatenate([dot(scaled, all_in_ref[...]), dot_t(flat, all_out_ref[...])], 1)
-    sum_ref[...] = jnp.where(last, sum_ref[...], 0.0) + both
-
-    @pl.when(last)
-    def _():
-        for m in range(MIC):
-            blocks = [sum_ref[(4 * m + j) * TOK : (4 * m + j + 1) * TOK, :] for j in range(4)]
-            for e in range(NS):
-                total = jnp.zeros((TOK, 2 * R), F32)
-                for j in range(4):
-                    total = jnp.where(ids_ref[m, j] == e, blocks[j], total)
-                start_ref[e * TOK : (e + 1) * TOK, m * 2 * R : (m + 1) * 2 * R] = total
+    scaled = (flat.astype(F32) * gain_ref[...]).astype(BF16)
+    both = jnp.concatenate([dot(scaled, w_in_ref[...]), dot_t(flat, w_out_ref[...])], 1)
+    for m in range(MIC):
+        blocks = [both[(4 * m + j) * TOK : (4 * m + j + 1) * TOK] for j in range(4)]
+        for e in range(NS):
+            total = jnp.zeros((TOK, 2 * R), F32)
+            for j in range(4):
+                total = jnp.where(ids_ref[m, j] == e, blocks[j], total)
+            start_ref[e * TOK : (e + 1) * TOK, m * 2 * R : (m + 1) * 2 * R] = total
 
 
 def stores(got_ref, s, at, cols):
@@ -473,60 +470,60 @@
     w_in = adapter_in[0]
     w_out = adapter_out[0]
 
-    send, row, own_cols, start = pl.pallas_call(
+    send, own_cols, give_cols = pl.pallas_call(
         pack_kernel,
         grid_spec=pltpu.PrefetchScalarGridSpec(
-            num_scalar_prefetch=2,
+            num_scalar_prefetch=1,
             grid=(2,),
             in_specs=[
-                pl.BlockSpec((64, wide), lambda i, at, ids: (0, i)),
-                pl.BlockSpec((64, wide), lambda i, at, ids: (0, i)),
-                pl.BlockSpec((32, wide), lambda i, at, ids: (at[3], i)),
+                pl.BlockSpec((64, wide), lambda i, at: (0, i)),
+                pl.BlockSpec((64, wide), lambda i, at: (0, i)),
+                pl.BlockSpec((32, wide), lambda i, at: (at[3], i)),
                 pl.BlockSpec(
-                    (1, 4, 1, 8, 32, R),
-                    lambda i, at, ids: (i, at[3] % 2, at[3] // 2, 0, 0, 0),
+                    (1, 4, 1, 8, 32, R), lambda i, at: (i, at[3] % 2, at[3] // 2, 0, 0, 0)
                 ),
-                pl.BlockSpec(
-                    (1, 4, 1, 2, BLK), lambda i, at, ids: (i, at[3] % 2, at[3] // 2, 0, 0)
-                ),
-                pl.BlockSpec((MIC, 32, wide), lambda i, at, ids: (0, 0, i)),
-                pl.BlockSpec((R, wide), lambda i, at, ids: (0, i)),
-                pl.BlockSpec((wide, R), lambda i, at, ids: (i, 0)),
-                pl.BlockSpec((1, wide), lambda i, at, ids: (0, i)),
+                pl.BlockSpec((1, 4, 1, 2, BLK), lambda i, at: (i, at[3] % 2, at[3] // 2, 0, 0)),
+                pl.BlockSpec((MIC, 32, wide), lambda i, at: (0, 0, i)),
             ],
             out_specs=[
-                pl.BlockSpec((8, 32, SENT), lambda i, at, ids: (i, 0, 0)),
-                pl.BlockSpec((MIC * TOK, BLK), lambda i, at, ids: (0, 0)),
-                pl.BlockSpec((1, R, cols), lambda i, at, ids: ((i + at[2]) % 2, 0, 0)),
-                pl.BlockSpec((NS * TOK, 8 * BLK), lambda i, at, ids: (0, 0)),
+                pl.BlockSpec((8, 32, SENT), lambda i, at: (i, 0, 0)),
+                pl.BlockSpec((R, cols), lambda i, at: (0, 0)),
+                pl.BlockSpec((R, cols), lambda i, at: (0, 0)),
             ],
-            scratch_shapes=[pltpu.VMEM((R, 2 * R), F32)],
+            scratch_shapes=[pltpu.VMEM((4 * BLK, 4 * BLK), BF16)],
         ),
         out_shape=(
             jax.ShapeDtypeStruct((16, 32, SENT), BF16),
-            jax.ShapeDtypeStruct((MIC * TOK, BLK), F32),
-            jax.ShapeDtypeStruct((2, R, cols), BF16),
-            jax.ShapeDtypeStruct((NS * TOK, 8 * BLK), F32),
+            jax.ShapeDtypeStruct((R, cols), BF16),
+            jax.ShapeDtypeStruct((R, cols), BF16),
         ),
         compiler_params=LARGE,
         name="pack",
     )(
         at,
-        ids,
         in_store.reshape(64, width),
         out_store.reshape(64, width),
         w_out,
         w_in.reshape(2, 8, 2, 8, 32, R),
         norm_gain.reshape(2, 8, 2, 2, BLK),
         first_input,
-        w_out,
-        w_in,
-        norm_gain,
     )
     other_ids = lax.ppermute(ids, "xl", SWAP)
-    other_cols = lax.ppermute(own_cols[1], "xl", SWAP)
+    other_cols = lax.ppermute(give_cols, "xl", SWAP)
     got = lax.all_to_all(send, PLANE, 0, 0, tiled=True)
     other = lax.ppermute(got[:, :, W_LANE:], "c", SWAP)
+    row, start = pl.pallas_call(
+        start_kernel,
+        out_shape=(
+            jax.ShapeDtypeStruct((MIC * TOK, BLK), F32),
+            jax.ShapeDtypeStruct((NS * TOK, 8 * BLK), F32),
+        ),
+        in_specs=[SMEM, SMEM, VMEM, VMEM, VMEM, VMEM, pl.BlockSpec(memory_space=pl.ANY)],
+        out_specs=(VMEM, VMEM),
+        compiler_params=PARAMS,
+        cost_estimate=pl.CostEstimate(flops=600000000, bytes_accessed=7000000, transcendentals=0),
+        name="start",
+    )(at, ids, first_input, w_out, w_in, norm_gain, got)
     parts, out_w, in_w, first = pl.pallas_call(
         project_kernel,
         out_shape=(
@@ -540,7 +537,7 @@
         scratch_shapes=[pltpu.VMEM((R, 2 * SPLIT * BLK), F32)],
         compiler_params=PARAMS,
         name="project",
-    )(at, ids, other_ids, got, other, own_cols[0], other_cols, start)
+    )(at, ids, other_ids, got, other, own_cols, other_cols, start)
     parts = lax.all_to_all(parts, PLANE, 0, 0, tiled=True)
 
     first_gram = (GRAM - SPLIT) * BLK

time: 228 us -> 220 us (0.965)
  Pallas kernels: 33.2 us -> 28.4 us
    pallas_call x1, Pallas kernels: 13.1 us -> 6.04 us  [body(): pl.pallas_call(pack_kernel, grid_spec=pltpu.PrefetchScalarGridSpec(num_sc...]
    pallas_call x0 -> x1, Pallas kernels: none -> 2.33 us  [body(): pl.pallas_call(start_kernel, out_shape=(jax.ShapeDtypeStruct((MIC * TOK,...]
    unnamed x26 -> x32, local copies, waits for them, and re-layouts: 5.89 us -> 5.17 us
  transfers between devices with their start and end apart: 5 -> 5, of which waited for: 2 -> 2; matrix products, arithmetic and copies ran while one was open for 0% -> 0% of each run, Pallas kernels for 2% -> 3%
where the time goes in v4:
time: 220 us
  blocking collectives  177 us (80%)
  Pallas kernels  28.4 us (13%)
  local copies, waits for them, and re-layouts  5.34 us (2%)
  waiting for transfers between devices  4.15 us (2%)
  other arithmetic  2.37 us (1%)
  starting transfers between devices  2.21 us (1%)
    all_to_all x1, blocking collectives, body(): got = lax.all_to_all(send, PLANE, 0, 0, tiled=True)  46.5 us
    all_to_all x1, blocking collectives, body(): total = lax.all_to_all(total, ('z',) + SECTION, 0, 0, tiled=True)  40.6 us
    all_to_all x1, blocking collectives, body(): parts = lax.all_to_all(parts, PLANE, 0, 0, tiled=True)  36.3 us
    all_to_all x1, blocking collectives, body(): lax.all_to_all(latent, PLANE, 0, 0, tiled=True)  33.5 us
    all_to_all x1, blocking collectives, body(): lax.all_to_all(jnp.broadcast_to(gram, (16,) + gram.shape), PLANE, 0, 0, t...  19.7 us
    pallas_call x2, Pallas kernels, grads(): pl.pallas_call(grads_kernel, grid_spec=pltpu.PrefetchScalarGridSpec(num_s...  9.41 us
    pallas_call x1, Pallas kernels, body(): pl.pallas_call(pack_kernel, grid_spec=pltpu.PrefetchScalarGridSpec(num_sc...  6.04 us
    unnamed x32, local copies, waits for them, and re-layouts  5.17 us
  transfers between devices with their start and end apart: 5, of which 2 were waited for; matrix products, arithmetic and copies ran while one was open for 0% of the time, Pallas kernels for 3%

profile of v4, /device:TPU:32, one launch (start us, length us, event | category | flops | bytes accessed | tf_op | source)
XLA Modules:
  0.0 219.9 jit_solution(12619087859328074503)
XLA Ops:
  0.6 0.6 pad_add_fusion.at_ref
  1.2 6.0 %pack.1 = (bf16[16,32,3072]{2,1,0:T(8,128)(2,1)}, bf16[128,512]{1,0:T(8,128)(2,1)}, bf16[128,512]{1,0:T(8,128)(2,1)}) custom-call(s32[4]{0:T(128)} %pad_add_fusion.at_ref, bf16[64,8192]{1,0:T(8,128)(2,1)} %bitcast.34, bf16[64,8192]{1,0:T(8,128)(2,1)} %bitcast.35, bf16[128,8192]{1,0:T(8,128)(2,1)} %bitcast.21, bf16[2,8,2,8,32,128]{5,4,3,2,1,0:T(8,128)(2,1)} %bitcast.23, ...), custom_call_target="tpu_custom_call" | custom-call | tf_op jit(solution)/shard_map/pack/pallas_call | solution.py:473
  7.3 0.0 copy-start.14
  7.3 0.0 copy-start.3
  7.3 0.0 copy-start.4
  7.3 0.0 copy-start.11
  7.3 46.5 %all_to_all.25.after_ref.got_ref = bf16[16,32,3072]{2,1,0:T(8,128)(2,1)S(1)} all-to-all(bf16[16,32,3072]{2,1,0:T(8,128)(2,1)} %get-tuple-element.15), channel_id=1, replica_groups=mesh['xl'=2,'z'=8,'c'=2,'y'=4,'xh'=2] {'xl','y','xh'}, dimensions={0} | all-to-all | bytes 6291456 | tf_op jit(solution)/shard_map/all_to_all | solution.py:513
  53.8 0.1 slice.8
  53.9 0.1 collective-permute-start.1
  54.0 0.7 collective-permute-start.2
  54.7 1.5 collective-permute-start
  56.2 0.0 copy-start.12
  56.2 2.3 %start.1 = (f32[32,128]{1,0:T(8,128)S(1)}, f32[64,1024]{1,0:T(8,128)S(1)}) custom-call(s32[4]{0:T(128)S(1)} %copy-done.13, s32[4,8]{1,0:T(4,128)S(1)} %bitcast.30, bf16[4,32,8192]{2,1,0:T(8,128)(2,1)S(1)} %copy-done.4, bf16[128,8192]{1,0:T(8,128)(2,1)S(1)} %bitcast.22, bf16[8192,128]{1,0:T(8,128)(2,1)S(1)} %bitcast.24, f32[1,8192]{1,0:T(1,128)S(1)} %copy-done.11, ...), custom_call_target="tpu_custom_call" | custom-call | flops 600000000 | bytes 7000000 | tf_op jit(solution)/shard_map/start/pallas_call | solution.py:515
  58.5 1.5 collective-permute-done.other_ids_ref
  60.0 5.0 %project.1 = (bf16[16,16,4992]{2,1,0:T(8,128)(2,1)S(1)}, bf16[8,128,512]{2,1,0:T(8,128)(2,1)S(1)}, bf16[8,512,128]{2,1,0:T(8,128)(2,1)S(1)}, bf16[16,32,512]{2,1,0:T(8,128)(2,1)S(1)}) custom-call(s32[4]{0:T(128)S(1)} %copy-done.13, s32[4,8]{1,0:T(4,128)S(1)} %bitcast.31, s32[4,8]{1,0:T(4,128)S(1)} %collective-permute-done.other_ids_ref, ...), custom_call_target="tpu_custom_call" | custom-call | tf_op jit(solution)/shard_map/project/pallas_call | solution.py:527
  65.0 36.3 %all_to_all.26.parts_ref = bf16[16,16,4992]{2,1,0:T(8,128)(2,1)S(1)} all-to-all(bf16[16,16,4992]{2,1,0:T(8,128)(2,1)S(1)} %get-tuple-element.22), channel_id=1, replica_groups=mesh['xl'=2,'z'=8,'c'=2,'y'=4,'xh'=2] {'xl','y','xh'}, dimensions={0} | all-to-all | bytes 5111808 | tf_op jit(solution)/shard_map/all_to_all | solution.py:541
  101.3 0.1 slice_reduce_fusion
  101.4 0.1 broadcast_in_dim.9
  101.5 19.7 %all_to_all.27 = bf16[16,8,4096]{2,1,0:T(8,128)(2,1)S(1)} all-to-all(bf16[16,8,4096]{2,1,0:T(8,128)(2,1)S(1)} %broadcast_in_dim.9), channel_id=1, replica_groups=mesh['xl'=2,'z'=8,'c'=2,'y'=4,'xh'=2] {'xl','y','xh'}, dimensions={0} | all-to-all | bytes 2097152 | tf_op jit(solution)/shard_map/all_to_all | solution.py:546
  121.2 0.0 collective-permute-start.3
  121.3 2.7 %collective-permute-done.3.other_ref = bf16[128,4096]{1,0:T(8,128)(2,1)S(1)} collective-permute-done((bf16[128,4096]{1,0:T(8,128)(2,1)S(1)}, bf16[128,4096]{1,0:T(8,128)(2,1)S(1)}, u32[]{:S(2)}, u32[]{:S(2)}) %collective-permute-start.3) | collective-permute-done | bytes 1048608 | tf_op jit(solution)/shard_map/ppermute | solution.py:549
  123.9 4.7 %chain.1 = bf16[16,32,2176]{2,1,0:T(8,128)(2,1)S(1)} custom-call(s32[4]{0:T(128)S(1)} %copy-done.13, bf16[16,16,4992]{2,1,0:T(8,128)(2,1)S(1)} %all_to_all.26.parts_ref, f32[32,128]{1,0:T(8,128)S(1)} %get-tuple-element.23.row_ref, bf16[128,4096]{1,0:T(8,128)(2,1)S(1)} %bitcast.27, bf16[128,4096]{1,0:T(8,128)(2,1)S(1)} %collective-permute-done.3.other_ref), custom_call_target="tpu_custom_call" | custom-call | tf_op jit(solution)/shard_map/chain/pallas_call | solution.py:551
  128.6 33.5 %all_to_all.28 = bf16[16,32,2176]{2,1,0:T(8,128)(2,1)S(1)} all-to-all(bf16[16,32,2176]{2,1,0:T(8,128)(2,1)S(1)} %chain.1), channel_id=1, replica_groups=mesh['xl'=2,'z'=8,'c'=2,'y'=4,'xh'=2] {'xl','y','xh'}, dimensions={0} | all-to-all | bytes 4456448 | tf_op jit(solution)/shard_map/all_to_all | solution.py:564
  162.1 5.2 %grads_other.1 = bf16[8,8,32,256]{3,2,1,0:T(8,128)(2,1)} custom-call(s32[4]{0:T(128)S(1)} %copy-done.13, bf16[16,32,3072]{2,1,0:T(8,128)(2,1)S(1)} %all_to_all.25.after_ref.got_ref, bf16[16,32,512]{2,1,0:T(8,128)(2,1)S(1)} %get-tuple-element.19.first_ref, bf16[8,128,512]{2,1,0:T(8,128)(2,1)S(1)} %get-tuple-element.20.out_w_ref, ...), custom_call_target="tpu_custom_call" | custom-call | tf_op jit(solution)/shard_map/grads_other/pallas_call | solution.py:570
  167.3 1.6 copy-done.1
  169.0 1.2 copy-done.6
  170.2 1.2 copy-done.8
  171.4 1.0 copy-done.10
  172.5 4.2 %grads_own.1 = f32[8,8,32,256]{3,2,1,0:T(8,128)S(1)} custom-call(s32[4]{0:T(128)S(1)} %copy-done.13, bf16[16,32,3072]{2,1,0:T(8,128)(2,1)S(1)} %all_to_all.25.after_ref.got_ref, bf16[16,32,512]{2,1,0:T(8,128)(2,1)S(1)} %copy-done.10, bf16[8,128,512]{2,1,0:T(8,128)(2,1)S(1)} %copy-done.6, bf16[8,512,128]{2,1,0:T(8,128)(2,1)S(1)} %copy-done.8, ...), custom_call_target="tpu_custom_call" | custom-call | tf_op jit(solution)/shard_map/grads_own/pallas_call | solution.py:570
  176.7 1.6 add_convert_fusion
  178.3 40.6 %all_to_all.29 = bf16[64,32,256]{2,1,0:T(8,128)(2,1)S(1)} all-to-all(bf16[64,32,256]{2,1,0:T(8,128)(2,1)S(1)} %bitcast.33), channel_id=1, replica_groups=mesh['xl'=2,'z'=8,'c'=2,'y'=4,'xh'=2] {'z','y','xh'}, dimensions={0} | all-to-all | bytes 2097152 | tf_op jit(solution)/shard_map/all_to_all | solution.py:595
  219.0 0.9 final.1
  (28 shorter events, 0.1 us)
Async XLA Ops:
  7.3 46.7 %copy-start.15 = (bf16[128,512]{1,0:T(8,128)(2,1)S(1)}, bf16[128,512]{1,0:T(8,128)(2,1)}, u32[]{:S(2)}) copy-start(bf16[128,512]{1,0:T(8,128)(2,1)} %get-tuple-element.17) | copy-start | bytes 393220
  7.3 47.4 %copy-start.14 = (s32[1,4,8]{2,1,0:T(4,128)S(1)}, s32[1,4,8]{2,1,0:T(4,128)}, u32[]{:S(2)}) copy-start(s32[1,4,8]{2,1,0:T(4,128)} %param.8) | copy-start | bytes 388
  7.3 48.8 %copy-start.3 = (bf16[1,8192,128]{2,1,0:T(8,128)(2,1)S(1)}, bf16[1,8192,128]{2,1,0:T(8,128)(2,1)}, u32[]{:S(2)}) copy-start(bf16[1,8192,128]{2,1,0:T(8,128)(2,1)} %param.12) | copy-start | bytes 6291460
  7.3 48.8 %copy-start.4 = (bf16[4,32,8192]{2,1,0:T(8,128)(2,1)S(1)}, bf16[4,32,8192]{2,1,0:T(8,128)(2,1)}, u32[]{:S(2)}) copy-start(bf16[4,32,8192]{2,1,0:T(8,128)(2,1)} %first_ref.3) | copy-start | bytes 6291460
  7.3 48.8 %copy-start.11 = (f32[1,8192]{1,0:T(1,128)S(1)}, f32[1,8192]{1,0:T(1,128)}, u32[]{:S(2)}) copy-start(f32[1,8192]{1,0:T(1,128)} %gain_ref.1) | copy-start | bytes 98308
  7.3 48.8 %copy-start.13 = (s32[4]{0:T(128)S(1)}, s32[4]{0:T(128)}, u32[]{:S(2)}) copy-start(s32[4]{0:T(128)} %pad_add_fusion.at_ref) | copy-start | bytes 52
  53.8 2.3 %copy-start.2 = (bf16[1,128,8192]{2,1,0:T(8,128)(2,1)S(1)}, bf16[1,128,8192]{2,1,0:T(8,128)(2,1)}, u32[]{:S(2)}) copy-start(bf16[1,128,8192]{2,1,0:T(8,128)(2,1)} %param.13) | copy-start | bytes 6291460
  53.9 6.1 %collective-permute-start.1 = (bf16[16,32,1024]{2,1,0:T(8,128)(2,1)S(1)}, bf16[16,32,1024]{2,1,0:T(8,128)(2,1)S(1)}, u32[]{:S(2)}, u32[]{:S(2)}) collective-permute-start(bf16[16,32,1024]{2,1,0:T(8,128)(2,1)S(1)} %slice.8), channel_id=1, source_target_pairs={{0,8},{8,0},{1,9},{9,1},{2,10},{10,2},{3,11},{11,3},{4,12},{12,4},... | collective-permute-start | bytes 3145736 | tf_op jit(solution)/shard_map/ppermute | solution.py:514
  54.0 6.0 %collective-permute-start.2 = (bf16[128,512]{1,0:T(8,128)(2,1)S(1)}, bf16[128,512]{1,0:T(8,128)(2,1)S(1)}, u32[]{:S(2)}, u32[]{:S(2)}) collective-permute-start(bf16[128,512]{1,0:T(8,128)(2,1)S(1)} %copy-done.15), channel_id=1, source_target_pairs={{0,128},{128,0},{1,129},{129,1},{2,130},{130,2},{3,131},{131,3},{4... | collective-permute-start | bytes 393224 | tf_op jit(solution)/shard_map/ppermute | solution.py:512
  54.7 5.3 %collective-permute-start = (s32[4,8]{1,0:T(4,128)S(1)}, s32[4,8]{1,0:T(4,128)S(1)}, u32[]{:S(2)}, u32[]{:S(2)}) collective-permute-start(s32[4,8]{1,0:T(4,128)S(1)} %bitcast.29), channel_id=1, source_target_pairs={{0,128},{128,0},{1,129},{129,1},{2,130},{130,2},{3,131},{131,3},{4... | collective-permute-start | bytes 392 | tf_op jit(solution)/shard_map/ppermute | solution.py:511
  56.2 3.8 %copy-start.12 = (bf16[128,512]{1,0:T(8,128)(2,1)S(1)}, bf16[128,512]{1,0:T(8,128)(2,1)}, u32[]{:S(2)}) copy-start(bf16[128,512]{1,0:T(8,128)(2,1)} %get-tuple-element.16.cols_ref) | copy-start | bytes 393220
  65.0 97.1 %copy-start.5 = (bf16[8,128,512]{2,1,0:T(8,128)(2,1)}, bf16[8,128,512]{2,1,0:T(8,128)(2,1)S(1)}, u32[]{:S(2)}) copy-start(bf16[8,128,512]{2,1,0:T(8,128)(2,1)S(1)} %get-tuple-element.20.out_w_ref) | copy-start | bytes 3145732
  65.0 97.1 %copy-start.7 = (bf16[8,512,128]{2,1,0:T(8,128)(2,1)}, bf16[8,512,128]{2,1,0:T(8,128)(2,1)S(1)}, u32[]{:S(2)}) copy-start(bf16[8,512,128]{2,1,0:T(8,128)(2,1)S(1)} %get-tuple-element.21.in_w_ref) | copy-start | bytes 3145732
  65.0 97.1 %copy-start.9 = (bf16[16,32,512]{2,1,0:T(8,128)(2,1)}, bf16[16,32,512]{2,1,0:T(8,128)(2,1)S(1)}, u32[]{:S(2)}) copy-start(bf16[16,32,512]{2,1,0:T(8,128)(2,1)S(1)} %get-tuple-element.19.first_ref) | copy-start | bytes 1572868
  121.2 2.7 %collective-permute-start.3 = (bf16[128,4096]{1,0:T(8,128)(2,1)S(1)}, bf16[128,4096]{1,0:T(8,128)(2,1)S(1)}, u32[]{:S(2)}, u32[]{:S(2)}) collective-permute-start(bf16[128,4096]{1,0:T(8,128)(2,1)S(1)} %bitcast.26), channel_id=1, source_target_pairs={{0,8},{8,0},{1,9},{9,1},{2,10},{10,2},{3,11},{11,3},{4,12},{12,4},... | collective-permute-start | bytes 3145736 | tf_op jit(solution)/shard_map/ppermute | solution.py:549
  162.1 5.2 %copy-start = (bf16[16,32,2176]{2,1,0:T(8,128)(2,1)}, bf16[16,32,2176]{2,1,0:T(8,128)(2,1)S(1)}, u32[]{:S(2)}) copy-start(bf16[16,32,2176]{2,1,0:T(8,128)(2,1)S(1)} %all_to_all.28) | copy-start | bytes 6684676
  167.3 9.3 %collective-permute-start.4 = (bf16[8,8,32,256]{3,2,1,0:T(8,128)(2,1)}, bf16[8,8,32,256]{3,2,1,0:T(8,128)(2,1)}, u32[]{:S(2)}, u32[]{:S(2)}) collective-permute-start(bf16[8,8,32,256]{3,2,1,0:T(8,128)(2,1)} %grads_other.1), channel_id=1, source_target_pairs={{0,8},{8,0},{1,9},{9,1},{2,10},{10,2},{3,11},{11,3},{4,12},{12,4},... | collective-permute-start | bytes 3145736 | tf_op jit(solution)/shard_map/ppermute | solution.py:590
  167.3 1.6 copy-start.1
  169.0 1.2 copy-start.6
  170.2 1.2 copy-start.8
  171.4 1.0 copy-start.10

commit v5 on v4

--- a/solution.py
+++ b/solution.py
@@ -23,10 +23,11 @@
 SENT = 3072
 PROJ = 29
 NORM = 36
-START = 37
-GRAM = 45
+GRAM = 37
 GRAMS = 32
-SPLIT = 39
+SPLIT = 35
+START = SPLIT * BLK
+WIDE = START + 16 * BLK
 OO = 36
 OI = 28
 LARGE = pltpu.CompilerParams(vmem_limit_bytes=56 * 1024 * 1024)
@@ -141,33 +142,12 @@
         put(give_ref)
 
 
-def start_kernel(
-    at_ref, ids_ref, first_ref, w_out_ref, w_in_ref, gain_ref, after_ref, row_ref, start_ref
-):
+def start_kernel(first_ref, w_out_ref, w_in_ref, gain_ref, after_ref, start_ref):
     del after_ref
-    section = at_ref[1]
-    lane = lax.broadcasted_iota(jnp.int32, (TOK, BLK), 1)
-    for m in range(MIC):
-        picks = [ids_ref[m, j] == section for j in range(4)]
-        block = first_ref[m].astype(F32)
-        total = jnp.zeros((TOK, block.shape[1]), F32)
-        for j in range(4):
-            total = jnp.where(picks[j], block[j * TOK : (j + 1) * TOK], total)
-        norm = jnp.sum(total * total, -1, keepdims=True)
-        valid = picks[0] | picks[1] | picks[2] | picks[3]
-        row_ref[m * TOK : (m + 1) * TOK, :] = jnp.where(
-            lane == 0, norm, jnp.where(valid, 1.0, 0.0)
-        )
     flat = first_ref[...].reshape(R, first_ref.shape[2])
     scaled = (flat.astype(F32) * gain_ref[...]).astype(BF16)
-    both = jnp.concatenate([dot(scaled, w_in_ref[...]), dot_t(flat, w_out_ref[...])], 1)
-    for m in range(MIC):
-        blocks = [both[(4 * m + j) * TOK : (4 * m + j + 1) * TOK] for j in range(4)]
-        for e in range(NS):
-            total = jnp.zeros((TOK, 2 * R), F32)
-            for j in range(4):
-                total = jnp.where(ids_ref[m, j] == e, blocks[j], total)
-            start_ref[e * TOK : (e + 1) * TOK, m * 2 * R : (m + 1) * 2 * R] = total
+    start_ref[:, :R] = dot(scaled, w_in_ref[...]).astype(BF16)
+    start_ref[:, R:] = dot_t(flat, w_out_ref[...]).astype(BF16)
 
 
 def stores(got_ref, s, at, cols):
@@ -176,26 +156,25 @@
         for i in range(2):
             a, b = at + i * 256, at + 512 + i * 256
             pieces.append(
-                got_ref[x * NS + s, :, a : a + cols].astype(F32)
-                - got_ref[x * NS + s - 1, :, b : b + cols].astype(F32)
+                got_ref[x * NS + s, :, pl.ds(a, cols)].astype(F32)
+                - got_ref[x * NS + s - 1, :, pl.ds(b, cols)].astype(F32)
             )
     return jnp.concatenate(pieces, 0)
 
 
+def picks_of(at_ref, ids_ref, other_ids_ref):
+    picks = []
+    for x in range(2):
+        here = at_ref[2] == x
+        for m in range(MIC):
+            for j in range(4):
+                picks.append(x * NS + jnp.where(here, ids_ref[m, j], other_ids_ref[m, j]))
+    return picks
+
+
 def project_kernel(
-    at_ref,
-    ids_ref,
-    other_ids_ref,
-    got_ref,
-    other_ref,
-    cols_ref,
-    other_cols_ref,
-    start_ref,
-    send_ref,
-    out_w_ref,
-    in_w_ref,
-    first_ref,
-    wide_ref,
+    at_ref, ids_ref, other_ids_ref, got_ref, other_ref, cols_ref, other_cols_ref, start_ref,
+    send_ref, out_w_ref, in_w_ref, first_ref, wide_ref,
 ):
     cols = cols_ref.shape[1]
     first_core = at_ref[0] == 0
@@ -211,28 +190,28 @@
                     row = k * BLK + g * 32
                     lane = cols + g * BLK
                     in_w_ref[s, row : row + 32, :] = part[:, lane : lane + BLK]
-    first = [[] for _ in range(MIC)]
+    picks = picks_of(at_ref, ids_ref, other_ids_ref)
+    placed = [[] for _ in range(MIC)]
     for x in range(2):
-        here = at_ref[2] == x
-        rows = jnp.where(here, cols_ref[...], other_cols_ref[...]).astype(F32)
-        picked = [
-            [jnp.where(here, ids_ref[m, j], other_ids_ref[m, j]) for j in range(4)]
-            for m in range(MIC)
-        ]
+        rows = jnp.where(at_ref[2] == x, cols_ref[...], other_cols_ref[...])
+        first_ref[x * R : (x + 1) * R, :] = rows
+        rows = rows.astype(F32)
         for e in range(NS):
-            blocks = []
             for m in range(MIC):
                 total = jnp.zeros((TOK, cols), F32)
                 for j in range(4):
-                    at = (4 * m + j) * TOK
-                    total = jnp.where(picked[m][j] == e, rows[at : at + TOK], total)
-                blocks.append(total)
-                first[m].append(total)
-            first_ref[x * NS + e] = jnp.concatenate(blocks, 0).astype(BF16)
-    first = [2.0 * jnp.concatenate(blocks, 0) for blocks in first]
+                    n = 4 * m + j
+                    total = jnp.where(
+                        picks[16 * x + n] == x * NS + e, rows[n * TOK : (n + 1) * TOK], total
+                    )
+                placed[m].append(total)
+    placed = [jnp.concatenate(blocks, 0) for blocks in placed]
     running = None
     lane = lax.broadcasted_iota(jnp.int32, (R, BLK), 1)
     norms = jnp.zeros((R, BLK), F32)
+    for m in range(MIC):
+        part = jnp.sum(placed[m] * placed[m], -1, keepdims=True)
+        norms = jnp.where(lane == m * NS, part, norms)
     for s in range(1, NS):
         step = jnp.concatenate(
             [stores(got_ref, s, 0, cols // 2), stores(got_ref, s, HALF, cols // 2)], 1
@@ -247,14 +226,13 @@
         at = (PROJ + s - 1) * BLK
         wide_ref[:, at : at + BLK] = dot(rounded, in_w_ref[s])
         for m in range(MIC):
-            part = jnp.sum(running * (running + first[m]), -1, keepdims=True)
+            entry = running + placed[m]
+            part = jnp.sum(entry * entry, -1, keepdims=True)
             norms = jnp.where(lane == m * NS + s, part, norms)
     high = norms.astype(BF16).astype(F32)
     wide_ref[:, NORM * BLK : (NORM + 1) * BLK] = jnp.where(
         lane < 32, high, pltpu.roll(norms - high, 32, 1)
     )
-    wide_ref[0:64, START * BLK : GRAM * BLK] = start_ref[...]
-    wide_ref[64:128, START * BLK : GRAM * BLK] = start_ref[...]
     wide_ref[:, (GRAM + GRAMS) * BLK :] = jnp.zeros((R, BLK), F32)
 
     square = [(t, s) for t in range(NS) for s in range(t, NS)]
@@ -287,43 +265,63 @@
             wide_ref[:, at * BLK : (at + 1) * BLK].reshape(16, TOK, BLK) for at in (b, SPLIT + b)
         ]
         send_ref[:, :, b * BLK : (b + 1) * BLK] = jnp.concatenate(pair, 1).astype(BF16)
+    for g in range(8):
+        at = START + g * 2 * R
+        for q in range(16):
+            send_ref[q, :, at : at + 2 * R] = start_ref[g * 16 : (g + 1) * 16, :]
+
+
+def sum_kernel(parts_ref, send_ref):
+    lane = lax.broadcasted_iota(jnp.int32, (2 * TOK, BLK), 1)
+    row = lax.broadcasted_iota(jnp.int32, (2 * TOK, BLK), 0)
+    for b in range(SPLIT):
+        at = slice(b * BLK, (b + 1) * BLK)
+        total = parts_ref[0, :, at].astype(F32)
+        for q in range(1, 16):
+            total = total + parts_ref[q, :, at].astype(F32)
+        if b == NORM - SPLIT:
+            norm = total + pltpu.roll(total, 96, 1)
+            high = norm.astype(BF16).astype(F32)
+            norm = jnp.where(lane < 32, high, pltpu.roll(norm - high, 32, 1))
+            total = jnp.where(row < TOK, total, norm)
+        total = total.astype(BF16)
+        for q in range(16):
+            send_ref[q, :, at] = total
 
 
 def chain_kernel(
-    width, at_ref, parts_ref, row_ref, gram_ref, other_ref, send_ref, sum_ref, oo_ref, oi_ref
+    width, at_ref, ids_ref, other_ids_ref, parts_ref, sums_ref, other_ref,
+    latent_ref, scalar_ref, proj_ref, oo_ref, oi_ref,
 ):
-    rows = MIC * TOK
+    rows = 2 * R
     first_core = at_ref[0] == 0
+    for b in range(GRAM):
+        upper = b >= SPLIT
+        at = (b - SPLIT * upper) * BLK
+        block = sums_ref[:, :, at : at + BLK].astype(F32)
+        proj_ref[:, b * BLK : (b + 1) * BLK] = block[:, TOK * upper : TOK * upper + TOK].reshape(
+            R, BLK
+        )
     for b in range(0, GRAMS, 4):
+        at = (GRAM - SPLIT + b) * BLK
+        mine = sums_ref[:, :, at : at + 4 * BLK].astype(F32)[:, TOK:]
+        mine = mine.reshape(R, 4 * BLK).astype(BF16)
         at = slice(b * BLK, (b + 4) * BLK)
-        mine, theirs = gram_ref[:, at], other_ref[:, at]
+        theirs = other_ref[:, at]
         oo_ref[:, at] = jnp.where(first_core, mine, theirs)
         second = jnp.where(first_core, theirs, mine)
         if b < OI:
             oi_ref[:, at] = second
         else:
             oo_ref[:, (b + 4) * BLK : (b + 8) * BLK] = second
-    for b in range(START):
-        at = slice(b * BLK, (b + 1) * BLK)
-        total = parts_ref[0, :, at].astype(F32)
-        for q in range(1, 16):
-            total = total + parts_ref[q, :, at].astype(F32)
-        sum_ref[:, at] = total[:TOK]
-    starts = []
-    for s in range(NS):
-        block = parts_ref[at_ref[2] * NS + s].astype(F32)
-        pieces = []
-        for m in range(MIC):
-            b = START + 2 * m
-            if b < SPLIT:
-                pieces.append(block[:TOK, b * BLK : (b + 2) * BLK])
-            else:
-                pieces.append(block[TOK:, (b - SPLIT) * BLK : (b + 2 - SPLIT) * BLK])
-        starts.append(jnp.concatenate(pieces, 0))
+    places = [
+        pl.multiple_of(pick * TOK, TOK) for pick in picks_of(at_ref, ids_ref, other_ids_ref)
+    ]
 
     def spread(at):
-        block = sum_ref[:, at * BLK : (at + 1) * BLK]
-        return jnp.concatenate([block] * MIC, 0)
+        return jnp.concatenate(
+            [proj_ref[pl.ds(place, TOK), at * BLK : (at + 1) * BLK] for place in places], 0
+        )
 
     def square(t, s, count=1):
         at = (gram_at(t) + s - t) * BLK
@@ -333,27 +331,33 @@
         at = (cross_at(t) + s - t - 1) * BLK
         return oi_ref[:, at : at + count * BLK]
 
-    mask = row_ref[:, 1:2]
-    own_norm = row_ref[:, 0:1]
-    norm_block = sum_ref[:, NORM * BLK : (NORM + 1) * BLK]
-    run_in = [start[:, :R] for start in starts]
-    start_out = [start[:, R:] for start in starts]
+    norms = spread(NORM)
+    norms = norms + pltpu.roll(norms, 96, 1)
+    pieces = []
+    for n in range(32):
+        m = n % 16 // 4
+        piece = norms[n * TOK : (n + 1) * TOK]
+        pieces.append(pltpu.roll(piece, BLK - m * NS, 1) if m else piece)
+    norms = jnp.concatenate(pieces, 0)
+
+    starts = []
+    for s in range(NS):
+        pieces = []
+        for x in range(2):
+            for g in range(8):
+                at = START + g * 2 * R
+                pieces.append(parts_ref[x * NS + s, :, at : at + 2 * R])
+        starts.append(jnp.concatenate(pieces, 0))
+    start_out = [start[:, R:].astype(F32) for start in starts]
+    run_in = [start[:, :R].astype(F32) for start in starts]
     run_out = list(start_out)
     inners, inverses, actives, crossed = [], [], [], []
     for s in range(NS):
-        norm = own_norm
+        norm = norms[:, s : s + 1]
         entry_out = []
         inner = run_in[s]
         if s > 0:
             inner = inner + spread(PROJ + s - 1)
-            norm = norm + jnp.concatenate(
-                [
-                    norm_block[:, m * NS + s : m * NS + s + 1]
-                    + norm_block[:, 32 + m * NS + s : 33 + m * NS + s]
-                    for m in range(MIC)
-                ],
-                0,
-            )
             total = jnp.zeros((rows, R), F32)
             for t in range(s):
                 base = spread(proj_at(s) + t)
@@ -363,7 +367,8 @@
             norm = norm + jnp.sum(total, -1, keepdims=True)
         inverse = lax.rsqrt(jnp.maximum(norm, 0.0) * (1.0 / width) + EPS)
         inner = inner * inverse
-        active = (inner * jax.nn.sigmoid(inner) * mask).astype(BF16)
+        active = (inner * jax.nn.sigmoid(inner)).astype(BF16)
+        latent_ref[:, s * R : (s + 1) * R] = active
         inners.append(inner)
         inverses.append(inverse)
         actives.append(active)
@@ -381,65 +386,69 @@
     grads = [run_out[t] + spread(proj_at(NS - 1) + t) for t in range(NS)]
     lane = lax.broadcasted_iota(jnp.int32, (rows, BLK), 1)
     scalars = jnp.zeros((rows, BLK), F32)
-    d_inners = [None] * NS
     for s in range(NS - 1, -1, -1):
         inner = inners[s]
         sigm = jax.nn.sigmoid(inner)
-        d_inner = (grads[s] * sigm * (1.0 + inner * (1.0 - sigm)) * mask).astype(BF16)
-        d_inners[s] = d_inner
-        d_wide = d_inner.astype(F32)
+        d_inner = (grads[s] * sigm * (1.0 + inner * (1.0 - sigm))).astype(BF16)
+        latent_ref[:, (NS + s) * R : (NS + s + 1) * R] = d_inner
         inverse = inverses[s]
-        scale = inverse * inverse * jnp.sum(d_wide * inner, -1, keepdims=True) * (1.0 / width)
+        total = jnp.sum(d_inner.astype(F32) * inner, -1, keepdims=True)
+        scale = inverse * inverse * total * (1.0 / width)
         for t in range(s):
             grads[t] = (
                 grads[t] + inverse * dot_t(d_inner, cross(t, s)) - scale * crossed[s][t]
             )
-        for at, value in ((s, inverse), (2 * NS + s, scale)):
-            high, low = split(value)
-            scalars = jnp.where(lane == at, high.astype(F32), scalars)
-            scalars = jnp.where(lane == at + NS, low.astype(F32), scalars)
-    for q in range(16):
+        scalars = jnp.where(lane == s, inverse, scalars)
+        scalars = jnp.where(lane == NS + s, scale, scalars)
+    scalar_ref[...] = scalars
+
+
+def grads_kernel(
+    at_ref, ids_ref, other_ids_ref, got_ref, first_ref, out_w_ref, in_w_ref, latent_ref, scalar_ref,
+    give_ref, keep_ref, entry_ref, step_ref,
+):
+    cols = step_ref.shape[1]
+    scalars = scalar_ref[...]
+    inverses = [scalars[:, s : s + 1] for s in range(NS)]
+    scales = [scalars[:, NS + s : NS + s + 1] for s in range(NS)]
+    places = [
+        pl.multiple_of(pick * TOK, TOK) for pick in picks_of(at_ref, ids_ref, other_ids_ref)
+    ]
+
+    def active(s):
+        return latent_ref[:, s * R : (s + 1) * R]
+
+    def d_inner(s):
+        return latent_ref[:, (NS + s) * R : (NS + s + 1) * R]
+
+    for side, result_ref in ((1 - at_ref[0], give_ref), (at_ref[0], keep_ref)):
+        here = pl.ds(pl.multiple_of(side * cols, cols), cols)
+        at = pl.multiple_of(side * HALF, HALF)
+
+        def put(s, kind, value, result_ref=result_ref):
+            result_ref[:, s, :, kind * R : (kind + 1) * R] = value.reshape(8, 32, R).astype(
+                result_ref.dtype
+            )
+
+        entry = first_ref[:, here].astype(F32)
         for s in range(NS):
-            send_ref[q, :, s * R : (s + 1) * R] = actives[s]
-            send_ref[q, :, (NS + s) * R : (NS + s + 1) * R] = d_inners[s]
-        send_ref[q, :, 2 * NS * R :] = scalars.astype(BF16)
-
-
-def grads_kernel(at_ref, got_ref, first_ref, out_w_ref, in_w_ref, chain_ref, result_ref, kept_ref):
-    cols = first_ref.shape[2]
-    rows = 16 * MIC * TOK
-    scalars = chain_ref[:, 2 * NS * R :].astype(F32)
-    inverses = [scalars[:, s : s + 1] + scalars[:, NS + s : NS + s + 1] for s in range(NS)]
-    scales = [
-        scalars[:, 2 * NS + s : 2 * NS + s + 1] + scalars[:, 3 * NS + s : 3 * NS + s + 1]
-        for s in range(NS)
-    ]
-
-    def active(s):
-        return chain_ref[:, s * R : (s + 1) * R]
-
-    def d_inner(s):
-        return chain_ref[:, (NS + s) * R : (NS + s + 1) * R]
-
-    def put(s, kind, value):
-        result_ref[:, s, :, kind * R : (kind + 1) * R] = value.reshape(8, 32, R).astype(
-            result_ref.dtype
-        )
-
-    entry = first_ref[...].astype(F32).reshape(rows, cols)
-    for s in range(NS):
-        if s > 0:
-            step = stores(got_ref, s, 0, cols)
-            step = jnp.broadcast_to(step.reshape(16, 1, TOK, cols), (16, MIC, TOK, cols))
-            entry = entry + step.reshape(rows, cols)
-        kept_ref[s] = entry
-        put(s, 0, dot_rows((entry * inverses[s]).astype(BF16), d_inner(s)))
-        entry = entry + dot(active(s), out_w_ref[s])
-    grad = entry
-    for s in range(NS - 1, -1, -1):
-        put(s, 1, dot_rows(grad.astype(BF16), active(s)))
-        if s > 0:
-            grad = grad + inverses[s] * dot_t(d_inner(s), in_w_ref[s]) - scales[s] * kept_ref[s]
+            if s > 0:
+                step_ref[...] = stores(got_ref, s, at, cols)
+                entry = entry + jnp.concatenate(
+                    [step_ref[pl.ds(place, TOK), :] for place in places], 0
+                )
+            entry_ref[s] = entry
+            put(s, 0, dot_rows((entry * inverses[s]).astype(BF16), d_inner(s)))
+            entry = entry + dot(active(s), out_w_ref[s, :, here])
+        grad = entry
+        for s in range(NS - 1, -1, -1):
+            put(s, 1, dot_rows(grad.astype(BF16), active(s)))
+            if s > 0:
+                grad = (
+                    grad
+                    + inverses[s] * dot_t(d_inner(s), in_w_ref[s, here, :])
+                    - scales[s] * entry_ref[s]
+                )
 
 
 def final_kernel(parts_ref, gain_ref, in_ref, out_ref):
@@ -512,25 +521,22 @@
     other_cols = lax.ppermute(give_cols, "xl", SWAP)
     got = lax.all_to_all(send, PLANE, 0, 0, tiled=True)
     other = lax.ppermute(got[:, :, W_LANE:], "c", SWAP)
-    row, start = pl.pallas_call(
+    start = pl.pallas_call(
         start_kernel,
-        out_shape=(
-            jax.ShapeDtypeStruct((MIC * TOK, BLK), F32),
-            jax.ShapeDtypeStruct((NS * TOK, 8 * BLK), F32),
-        ),
-        in_specs=[SMEM, SMEM, VMEM, VMEM, VMEM, VMEM, pl.BlockSpec(memory_space=pl.ANY)],
-        out_specs=(VMEM, VMEM),
+        out_shape=jax.ShapeDtypeStruct((R, 2 * R), BF16),
+        in_specs=[VMEM, VMEM, VMEM, VMEM, pl.BlockSpec(memory_space=pl.ANY)],
+        out_specs=VMEM,
         compiler_params=PARAMS,
         cost_estimate=pl.CostEstimate(flops=600000000, bytes_accessed=7000000, transcendentals=0),
         name="start",
-    )(at, ids, first_input, w_out, w_in, norm_gain, got)
+    )(first_input, w_out, w_in, norm_gain, got)
     parts, out_w, in_w, first = pl.pallas_call(
         project_kernel,
         out_shape=(
-            jax.ShapeDtypeStruct((16, 2 * TOK, SPLIT * BLK), BF16),
+            jax.ShapeDtypeStruct((16, 2 * TOK, WIDE), BF16),
             jax.ShapeDtypeStruct((NS, R, cols), BF16),
             jax.ShapeDtypeStruct((NS, cols, R), BF16),
-            jax.ShapeDtypeStruct((16, MIC * TOK, cols), BF16),
+            jax.ShapeDtypeStruct((2 * R, cols), BF16),
         ),
         in_specs=[SMEM, SMEM, SMEM, VMEM, VMEM, VMEM, VMEM, VMEM],
         out_specs=(VMEM, VMEM, VMEM, VMEM),
@@ -539,56 +545,48 @@
         name="project",
     )(at, ids, other_ids, got, other, own_cols, other_cols, start)
     parts = lax.all_to_all(parts, PLANE, 0, 0, tiled=True)
-
-    first_gram = (GRAM - SPLIT) * BLK
-    gram = parts[:, TOK:, first_gram : first_gram + GRAMS * BLK].astype(F32)
-    gram = jnp.sum(gram, 0).astype(BF16)
-    gram = lax.all_to_all(
-        jnp.broadcast_to(gram, (16,) + gram.shape), PLANE, 0, 0, tiled=True
-    ).reshape(R, GRAMS * BLK)
-    other = lax.ppermute(gram, "c", SWAP)
-
-    latent = pl.pallas_call(
+    sums = pl.pallas_call(
+        sum_kernel,
+        out_shape=jax.ShapeDtypeStruct((16, 2 * TOK, SPLIT * BLK), BF16),
+        in_specs=[VMEM],
+        out_specs=VMEM,
+        compiler_params=PARAMS,
+        name="sums",
+    )(parts)
+    sums = lax.all_to_all(sums, PLANE, 0, 0, tiled=True)
+    gram = sums[:, TOK:, (GRAM - SPLIT) * BLK : (GRAM - SPLIT + GRAMS) * BLK]
+    other = lax.ppermute(gram.reshape(R, GRAMS * BLK), "c", SWAP)
+    latent, scalars = pl.pallas_call(
         functools.partial(chain_kernel, width),
-        out_shape=jax.ShapeDtypeStruct((16, MIC * TOK, 17 * BLK), BF16),
-        in_specs=[SMEM, VMEM, VMEM, VMEM, VMEM],
-        out_specs=VMEM,
+        out_shape=(
+            jax.ShapeDtypeStruct((2 * R, 16 * BLK), BF16),
+            jax.ShapeDtypeStruct((2 * R, BLK), F32),
+        ),
+        in_specs=[SMEM, SMEM, SMEM, VMEM, VMEM, VMEM],
+        out_specs=(VMEM, VMEM),
         scratch_shapes=[
-            pltpu.VMEM((TOK, START * BLK), F32),
+            pltpu.VMEM((R, GRAM * BLK), F32),
             pltpu.VMEM((R, OO * BLK), BF16),
             pltpu.VMEM((R, OI * BLK), BF16),
         ],
         compiler_params=PARAMS,
         name="chain",
-    )(at, parts, row, gram, other)
-    latent = lax.all_to_all(latent, PLANE, 0, 0, tiled=True).reshape(16 * MIC * TOK, 17 * BLK)
-
-    def grads(own):
-        def side(at):
-            return at[0] if own else 1 - at[0]
-
-        return pl.pallas_call(
-            grads_kernel,
-            grid_spec=pltpu.PrefetchScalarGridSpec(
-                num_scalar_prefetch=1,
-                grid=(1,),
-                in_specs=[
-                    pl.BlockSpec((16, 32, HALF), lambda i, at: (0, 0, side(at))),
-                    pl.BlockSpec((16, MIC * TOK, half), lambda i, at: (0, 0, side(at))),
-                    pl.BlockSpec((NS, R, half), lambda i, at: (0, 0, side(at))),
-                    pl.BlockSpec((NS, half, R), lambda i, at: (0, side(at), 0)),
-                    pl.BlockSpec((16 * MIC * TOK, 17 * BLK), lambda i, at: (0, 0)),
-                ],
-                out_specs=pl.BlockSpec((8, NS, 32, 2 * R), lambda i, at: (0, 0, 0, 0)),
-                scratch_shapes=[pltpu.VMEM((NS, 16 * MIC * TOK, half), F32)],
-            ),
-            out_shape=jax.ShapeDtypeStruct((8, NS, 32, 2 * R), F32 if own else BF16),
-            compiler_params=PARAMS,
-            name="grads_own" if own else "grads_other",
-        )(at, got, first, out_w, in_w, latent)
-
-    swapped = lax.ppermute(grads(False), "c", SWAP)
-    total = (grads(True) + swapped.astype(F32)).astype(BF16).reshape(64, 32, 2 * R)
+    )(at, ids, other_ids, parts, sums, other)
+    give, keep = pl.pallas_call(
+        grads_kernel,
+        out_shape=(
+            jax.ShapeDtypeStruct((8, NS, 32, 2 * R), BF16),
+            jax.ShapeDtypeStruct((8, NS, 32, 2 * R), F32),
+        ),
+        in_specs=[SMEM, SMEM, SMEM] + [VMEM] * 6,
+        out_specs=(VMEM, VMEM),
+        scratch_shapes=[pltpu.VMEM((NS, 2 * R, half), F32), pltpu.VMEM((R, half), F32)],
+        compiler_params=PARAMS,
+        name="grads",
+    )(at, ids, other_ids, got, first, out_w, in_w, latent, scalars)
+
+    swapped = lax.ppermute(give, "c", SWAP)
+    total = (keep + swapped.astype(F32)).astype(BF16).reshape(64, 32, 2 * R)
     block = (xl * NS + z) * 2 + core
     gain = lax.dynamic_slice_in_dim(norm_gain[0], block * half, half, 0)
     total, gain = lax.optimization_barrier((total, gain))

time: 220 us -> 205 us (0.932)
  blocking collectives: 177 us -> 166 us
  local copies, waits for them, and re-layouts: 5.34 us -> 0.23 us
  waiting for transfers between devices: 4.15 us -> 7.86 us
  Pallas kernels: 28.4 us -> 25.1 us
    all_to_all x2 -> x1, blocking collectives: 53.2 us -> 32.6 us  [body(): sums = lax.all_to_all(sums, PLANE, 0, 0, tiled=True)]
    all_to_all x1, blocking collectives: 36.3 us -> 45 us  [body(): parts = lax.all_to_all(parts, PLANE, 0, 0, tiled=True)]
    unnamed x32 -> x16, local copies, waits for them, and re-layouts: 5.17 us -> 0.04 us
    pallas_call x4, Pallas kernels: 16.4 us -> 13.3 us  [the longest x1 6.92 us: body(): pl.pallas_call(functools.partial(chain_kernel, width), out_shape=(jax.Sha...]
    ppermute x2, waiting for transfers between devices: 2.66 us -> 5.29 us  [the longest x1 2.65 us: body(): swapped = lax.ppermute(give, 'c', SWAP)]
  transfers between devices with their start and end apart: 5 -> 5, of which waited for: 2 -> 3; matrix products, arithmetic and copies ran while one was open for 0% -> 0% of each run, Pallas kernels for 3% -> 1%
where the time goes in v5:
time: 205 us
  blocking collectives  166 us (81%)
  Pallas kernels  25.1 us (12%)
  waiting for transfers between devices  7.86 us (4%)
  starting transfers between devices  2.71 us (1%)
  other arithmetic  2.18 us (1%)
    all_to_all x1, blocking collectives, body(): got = lax.all_to_all(send, PLANE, 0, 0, tiled=True)  46.5 us
    all_to_all x1, blocking collectives, body(): parts = lax.all_to_all(parts, PLANE, 0, 0, tiled=True)  45 us
    all_to_all x1, blocking collectives, body(): total = lax.all_to_all(total, ('z',) + SECTION, 0, 0, tiled=True)  41.5 us
    all_to_all x1, blocking collectives, body(): sums = lax.all_to_all(sums, PLANE, 0, 0, tiled=True)  32.6 us
    pallas_call x1, Pallas kernels, body(): pl.pallas_call(functools.partial(chain_kernel, width), out_shape=(jax.Sha...  6.92 us
    pallas_call x1, Pallas kernels, body(): pl.pallas_call(pack_kernel, grid_spec=pltpu.PrefetchScalarGridSpec(num_sc...  6.04 us
    pallas_call x1, Pallas kernels, body(): pl.pallas_call(project_kernel, out_shape=(jax.ShapeDtypeStruct((16, 2 * T...  4.93 us
    pallas_call x1, Pallas kernels, body(): pl.pallas_call(grads_kernel, out_shape=(jax.ShapeDtypeStruct((8, NS, 32,...  4.67 us
  transfers between devices with their start and end apart: 5, of which 3 were waited for; matrix products, arithmetic and copies ran while one was open for 0% of the time, Pallas kernels for 1%

profile of v5, /device:TPU:32, one launch (start us, length us, event | category | flops | bytes accessed | tf_op | source)
XLA Modules:
  0.0 204.6 jit_solution(17672090469821739508)
XLA Ops:
  0.6 0.6 pad_add_fusion.at_ref
  1.2 6.0 %pack.1 = (bf16[16,32,3072]{2,1,0:T(8,128)(2,1)}, bf16[128,512]{1,0:T(8,128)(2,1)}, bf16[128,512]{1,0:T(8,128)(2,1)}) custom-call(s32[4]{0:T(128)} %pad_add_fusion.at_ref, bf16[64,8192]{1,0:T(8,128)(2,1)} %bitcast.31, bf16[64,8192]{1,0:T(8,128)(2,1)} %bitcast.32, bf16[128,8192]{1,0:T(8,128)(2,1)} %bitcast.19, bf16[2,8,2,8,32,128]{5,4,3,2,1,0:T(8,128)(2,1)} %bitcast.21, ...), custom_call_target="tpu_custom_call" | custom-call | tf_op jit(solution)/shard_map/pack/pallas_call | solution.py:482
  7.3 0.0 copy-start.5
  7.3 0.0 copy-start.1
  7.3 0.0 copy-start.2
  7.3 0.0 copy-start.3
  7.3 46.5 %all_to_all.20.after_ref.got_ref = bf16[16,32,3072]{2,1,0:T(8,128)(2,1)S(1)} all-to-all(bf16[16,32,3072]{2,1,0:T(8,128)(2,1)} %get-tuple-element.17), channel_id=1, replica_groups=mesh['xl'=2,'z'=8,'c'=2,'y'=4,'xh'=2] {'xl','y','xh'}, dimensions={0} | all-to-all | bytes 6291456 | tf_op jit(solution)/shard_map/all_to_all | solution.py:522
  53.8 0.1 slice.8
  53.9 0.1 collective-permute-start.1
  54.0 0.0 copy-done.7
  54.0 0.7 collective-permute-start.2
  54.7 1.5 collective-permute-start
  56.1 0.0 copy-done.1
  56.1 0.0 copy-start.4
  56.2 1.2 start.1.start_ref
  57.4 2.6 %collective-permute-done.other_ids_ref = s32[4,8]{1,0:T(4,128)S(1)} collective-permute-done((s32[4,8]{1,0:T(4,128)S(1)}, s32[4,8]{1,0:T(4,128)S(1)}, u32[]{:S(2)}, u32[]{:S(2)}) %collective-permute-start) | collective-permute-done | bytes 160 | tf_op jit(solution)/shard_map/ppermute | solution.py:520
  60.0 0.0 collective-permute-done.2.other_cols_ref
  60.0 0.0 collective-permute-done.1.other_ref
  60.0 4.9 %project.1 = (bf16[16,16,6528]{2,1,0:T(8,128)(2,1)S(1)}, bf16[8,128,512]{2,1,0:T(8,128)(2,1)S(1)}, bf16[8,512,128]{2,1,0:T(8,128)(2,1)S(1)}, bf16[256,512]{1,0:T(8,128)(2,1)S(1)}) custom-call(s32[4]{0:T(128)S(1)} %copy-done.6, s32[4,8]{1,0:T(4,128)S(1)} %bitcast.26, s32[4,8]{1,0:T(4,128)S(1)} %collective-permute-done.other_ids_ref, ...), custom_call_target="tpu_custom_call" | custom-call | tf_op jit(solution)/shard_map/project/pallas_call | solution.py:533
  64.9 45.0 %all_to_all.21.parts_ref = bf16[16,16,6528]{2,1,0:T(8,128)(2,1)S(1)} all-to-all(bf16[16,16,6528]{2,1,0:T(8,128)(2,1)S(1)} %get-tuple-element.23), channel_id=1, replica_groups=mesh['xl'=2,'z'=8,'c'=2,'y'=4,'xh'=2] {'xl','y','xh'}, dimensions={0} | all-to-all | bytes 6684672 | tf_op jit(solution)/shard_map/all_to_all | solution.py:547
  110.0 0.4 sums.1
  110.4 32.6 %all_to_all.22.sums_ref = bf16[16,16,4480]{2,1,0:T(8,128)(2,1)S(1)} all-to-all(bf16[16,16,4480]{2,1,0:T(8,128)(2,1)S(1)} %sums.1), channel_id=1, replica_groups=mesh['xl'=2,'z'=8,'c'=2,'y'=4,'xh'=2] {'xl','y','xh'}, dimensions={0} | all-to-all | bytes 4587520 | tf_op jit(solution)/shard_map/all_to_all | solution.py:556
  143.0 0.1 slice_bitcast_fusion
  143.1 0.3 collective-permute-start.3
  143.4 2.6 %collective-permute-done.3.other_ref = bf16[128,4096]{1,0:T(8,128)(2,1)S(1)} collective-permute-done((bf16[128,4096]{1,0:T(8,128)(2,1)S(1)}, bf16[128,4096]{1,0:T(8,128)(2,1)S(1)}, u32[]{:S(2)}, u32[]{:S(2)}) %collective-permute-start.3) | collective-permute-done | bytes 1048608 | tf_op jit(solution)/shard_map/ppermute | solution.py:558
  146.1 6.9 %chain.1 = (bf16[256,2048]{1,0:T(8,128)(2,1)S(1)}, f32[256,128]{1,0:T(8,128)S(1)}) custom-call(s32[4]{0:T(128)S(1)} %copy-done.6, s32[4,8]{1,0:T(4,128)S(1)} %bitcast.27, s32[4,8]{1,0:T(4,128)S(1)} %collective-permute-done.other_ids_ref, bf16[16,16,6528]{2,1,0:T(8,128)(2,1)S(1)} %all_to_all.21.parts_ref, bf16[16,16,4480]{2,1,0:T(8,128)(2,1)S(1)} %all_to_all.22.sums_ref, ...), custom_call_target="tpu_custom_call" | custom-call | tf_op jit(solution)/shard_map/chain/pallas_call | solution.py:559
  153.0 4.7 %grads.1 = (bf16[8,8,32,256]{3,2,1,0:T(8,128)(2,1)S(1)}, f32[8,8,32,256]{3,2,1,0:T(8,128)S(1)}) custom-call(s32[4]{0:T(128)S(1)} %copy-done.6, s32[4,8]{1,0:T(4,128)S(1)} %bitcast.28, s32[4,8]{1,0:T(4,128)S(1)} %collective-permute-done.other_ids_ref, bf16[16,32,3072]{2,1,0:T(8,128)(2,1)S(1)} %all_to_all.20.after_ref.got_ref, ...), custom_call_target="tpu_custom_call" | custom-call | tf_op jit(solution)/shard_map/grads/pallas_call | solution.py:575
  157.7 0.2 collective-permute-start.4
  157.9 2.6 %collective-permute-done.4 = bf16[8,8,32,256]{3,2,1,0:T(8,128)(2,1)} collective-permute-done((bf16[8,8,32,256]{3,2,1,0:T(8,128)(2,1)S(1)}, bf16[8,8,32,256]{3,2,1,0:T(8,128)(2,1)}, u32[]{:S(2)}, u32[]{:S(2)}) %collective-permute-start.4) | collective-permute-done | bytes 1048608 | tf_op jit(solution)/shard_map/ppermute | solution.py:588
  160.6 1.6 add_convert_fusion
  162.2 41.5 %all_to_all.23 = bf16[64,32,256]{2,1,0:T(8,128)(2,1)S(1)} all-to-all(bf16[64,32,256]{2,1,0:T(8,128)(2,1)S(1)} %bitcast.30), channel_id=1, replica_groups=mesh['xl'=2,'z'=8,'c'=2,'y'=4,'xh'=2] {'z','y','xh'}, dimensions={0} | all-to-all | bytes 2097152 | tf_op jit(solution)/shard_map/all_to_all | solution.py:593
  203.6 0.9 final.1
  (10 shorter events, 0.0 us)
Async XLA Ops:
  7.3 46.7 %copy-start.7 = (bf16[128,512]{1,0:T(8,128)(2,1)S(1)}, bf16[128,512]{1,0:T(8,128)(2,1)}, u32[]{:S(2)}) copy-start(bf16[128,512]{1,0:T(8,128)(2,1)} %get-tuple-element.19) | copy-start | bytes 393220
  7.3 47.4 %copy-start.5 = (s32[1,4,8]{2,1,0:T(4,128)S(1)}, s32[1,4,8]{2,1,0:T(4,128)}, u32[]{:S(2)}) copy-start(s32[1,4,8]{2,1,0:T(4,128)} %param.8) | copy-start | bytes 388
  7.3 48.9 %copy-start.1 = (bf16[1,8192,128]{2,1,0:T(8,128)(2,1)S(1)}, bf16[1,8192,128]{2,1,0:T(8,128)(2,1)}, u32[]{:S(2)}) copy-start(bf16[1,8192,128]{2,1,0:T(8,128)(2,1)} %param.12) | copy-start | bytes 6291460
  7.3 48.8 %copy-start.2 = (bf16[4,32,8192]{2,1,0:T(8,128)(2,1)S(1)}, bf16[4,32,8192]{2,1,0:T(8,128)(2,1)}, u32[]{:S(2)}) copy-start(bf16[4,32,8192]{2,1,0:T(8,128)(2,1)} %first_ref.3) | copy-start | bytes 6291460
  7.3 48.8 %copy-start.3 = (f32[1,8192]{1,0:T(1,128)S(1)}, f32[1,8192]{1,0:T(1,128)}, u32[]{:S(2)}) copy-start(f32[1,8192]{1,0:T(1,128)} %gain_ref.1) | copy-start | bytes 98308
  53.8 2.3 %copy-start = (bf16[1,128,8192]{2,1,0:T(8,128)(2,1)S(1)}, bf16[1,128,8192]{2,1,0:T(8,128)(2,1)}, u32[]{:S(2)}) copy-start(bf16[1,128,8192]{2,1,0:T(8,128)(2,1)} %param.13) | copy-start | bytes 6291460
  53.9 6.1 %collective-permute-start.1 = (bf16[16,32,1024]{2,1,0:T(8,128)(2,1)S(1)}, bf16[16,32,1024]{2,1,0:T(8,128)(2,1)S(1)}, u32[]{:S(2)}, u32[]{:S(2)}) collective-permute-start(bf16[16,32,1024]{2,1,0:T(8,128)(2,1)S(1)} %slice.8), channel_id=1, source_target_pairs={{0,8},{8,0},{1,9},{9,1},{2,10},{10,2},{3,11},{11,3},{4,12},{12,4},... | collective-permute-start | bytes 3145736 | tf_op jit(solution)/shard_map/ppermute | solution.py:523
  54.0 6.0 %collective-permute-start.2 = (bf16[128,512]{1,0:T(8,128)(2,1)S(1)}, bf16[128,512]{1,0:T(8,128)(2,1)S(1)}, u32[]{:S(2)}, u32[]{:S(2)}) collective-permute-start(bf16[128,512]{1,0:T(8,128)(2,1)S(1)} %copy-done.7), channel_id=1, source_target_pairs={{0,128},{128,0},{1,129},{129,1},{2,130},{130,2},{3,131},{131,3},{4... | collective-permute-start | bytes 393224 | tf_op jit(solution)/shard_map/ppermute | solution.py:521
  54.7 5.3 %collective-permute-start = (s32[4,8]{1,0:T(4,128)S(1)}, s32[4,8]{1,0:T(4,128)S(1)}, u32[]{:S(2)}, u32[]{:S(2)}) collective-permute-start(s32[4,8]{1,0:T(4,128)S(1)} %bitcast.25), channel_id=1, source_target_pairs={{0,128},{128,0},{1,129},{129,1},{2,130},{130,2},{3,131},{131,3},{4... | collective-permute-start | bytes 392 | tf_op jit(solution)/shard_map/ppermute | solution.py:520
  56.1 3.8 %copy-start.4 = (bf16[128,512]{1,0:T(8,128)(2,1)S(1)}, bf16[128,512]{1,0:T(8,128)(2,1)}, u32[]{:S(2)}) copy-start(bf16[128,512]{1,0:T(8,128)(2,1)} %get-tuple-element.18.cols_ref) | copy-start | bytes 393220
  56.2 3.8 %copy-start.6 = (s32[4]{0:T(128)S(1)}, s32[4]{0:T(128)}, u32[]{:S(2)}) copy-start(s32[4]{0:T(128)} %pad_add_fusion.at_ref) | copy-start | bytes 52
  143.1 2.9 %collective-permute-start.3 = (bf16[128,4096]{1,0:T(8,128)(2,1)S(1)}, bf16[128,4096]{1,0:T(8,128)(2,1)S(1)}, u32[]{:S(2)}, u32[]{:S(2)}) collective-permute-start(bf16[128,4096]{1,0:T(8,128)(2,1)S(1)} %slice_bitcast_fusion), channel_id=1, source_target_pairs={{0,8},{8,0},{1,9},{9,1},{2,10},{10,2},{3,11},{11,3},{4,12},{12,4},... | collective-permute-start | bytes 3145736 | tf_op jit(solution)/shard_map/ppermute | solution.py:558
  157.7 2.9 %collective-permute-start.4 = (bf16[8,8,32,256]{3,2,1,0:T(8,128)(2,1)S(1)}, bf16[8,8,32,256]{3,2,1,0:T(8,128)(2,1)}, u32[]{:S(2)}, u32[]{:S(2)}) collective-permute-start(bf16[8,8,32,256]{3,2,1,0:T(8,128)(2,1)S(1)} %get-tuple-element.27), channel_id=1, source_target_pairs={{0,8},{8,0},{1,9},{9,1},{2,10},{10,2},{3,11},{11,3},{4,12},{12,4},... | collective-permute-start | bytes 3145736 | tf_op jit(solution)/shard_map/ppermute | solution.py:588

commit v6 on v5

--- a/solution.py
+++ b/solution.py
@@ -22,7 +22,7 @@
 W_LANE = 2 * HALF
 SENT = 3072
 PROJ = 29
-NORM = 36
+NORM = 34
 GRAM = 37
 GRAMS = 32
 SPLIT = 35
@@ -46,6 +46,10 @@
 
 def proj_at(s):
     return s * (s - 1) // 2
+
+
+def inner_at(s):
+    return PROJ + s - 1 + (PROJ + s - 1 >= NORM)
 
 
 def dot_t(a, b):
@@ -172,11 +176,20 @@
     return picks
 
 
+def running_sums(got_ref, cols):
+    running = None
+    for s in range(1, NS):
+        step = jnp.concatenate(
+            [stores(got_ref, s, 0, cols // 2), stores(got_ref, s, HALF, cols // 2)], 1
+        )
+        running = step if running is None else running + step
+        yield s, running
+
+
 def project_kernel(
-    at_ref, ids_ref, other_ids_ref, got_ref, other_ref, cols_ref, other_cols_ref, start_ref,
-    send_ref, out_w_ref, in_w_ref, first_ref, wide_ref,
+    at_ref, got_ref, other_ref, start_ref, send_ref, out_w_ref, in_w_ref, wide_ref
 ):
-    cols = cols_ref.shape[1]
+    cols = in_w_ref.shape[1]
     first_core = at_ref[0] == 0
     for s in range(NS):
         for x in range(2):
@@ -190,6 +203,60 @@
                     row = k * BLK + g * 32
                     lane = cols + g * BLK
                     in_w_ref[s, row : row + 32, :] = part[:, lane : lane + BLK]
+    for s, running in running_sums(got_ref, cols):
+        rounded = running.astype(BF16)
+        count = s if s < NS - 1 else NS
+        at = proj_at(s) * BLK
+        wide_ref[:, at : at + count * BLK] = dot_t(
+            rounded, out_w_ref[0:count].reshape(count * R, cols)
+        )
+        at = inner_at(s) * BLK
+        wide_ref[:, at : at + BLK] = dot(rounded, in_w_ref[s])
+    for b in (NORM, GRAM + GRAMS):
+        wide_ref[:, b * BLK : (b + 1) * BLK] = jnp.zeros((R, BLK), F32)
+
+    square = [(t, s) for t in range(NS) for s in range(t, NS)]
+
+    @pl.when(first_core)
+    def _():
+        for t in range(5):
+            at = (GRAM + gram_at(t)) * BLK
+            wide_ref[:, at : at + (NS - t) * BLK] = dot_t(
+                out_w_ref[t], out_w_ref[t:NS].reshape((NS - t) * R, cols)
+            )
+        for i in range(gram_at(5), GRAMS):
+            t, s = square[i]
+            at = (GRAM + i) * BLK
+            wide_ref[:, at : at + BLK] = dot_t(out_w_ref[t], out_w_ref[s])
+
+    @pl.when(jnp.logical_not(first_core))
+    def _():
+        for t in range(NS - 1):
+            for s in range(t + 1, NS):
+                at = (GRAM + cross_at(t) + s - t - 1) * BLK
+                wide_ref[:, at : at + BLK] = dot(out_w_ref[t], in_w_ref[s])
+        for i in range(GRAMS, OO):
+            t, s = square[i]
+            at = (GRAM + OI + i - GRAMS) * BLK
+            wide_ref[:, at : at + BLK] = dot_t(out_w_ref[t], out_w_ref[s])
+
+    for b in range(SPLIT):
+        pair = [
+            wide_ref[:, at * BLK : (at + 1) * BLK].reshape(16, TOK, BLK) for at in (b, SPLIT + b)
+        ]
+        send_ref[:, :, b * BLK : (b + 1) * BLK] = jnp.concatenate(pair, 1).astype(BF16)
+    for g in range(8):
+        at = START + g * 2 * R
+        for q in range(16):
+            send_ref[q, :, at : at + 2 * R] = start_ref[g * 16 : (g + 1) * 16, :]
+
+
+def norm_kernel(
+    at_ref, ids_ref, other_ids_ref, got_ref, cols_ref, other_cols_ref, before_ref,
+    send_ref, first_ref, block_ref, sem,
+):
+    del before_ref
+    cols = cols_ref.shape[1]
     picks = picks_of(at_ref, ids_ref, other_ids_ref)
     placed = [[] for _ in range(MIC)]
     for x in range(2):
@@ -206,69 +273,24 @@
                     )
                 placed[m].append(total)
     placed = [jnp.concatenate(blocks, 0) for blocks in placed]
-    running = None
     lane = lax.broadcasted_iota(jnp.int32, (R, BLK), 1)
     norms = jnp.zeros((R, BLK), F32)
     for m in range(MIC):
         part = jnp.sum(placed[m] * placed[m], -1, keepdims=True)
         norms = jnp.where(lane == m * NS, part, norms)
-    for s in range(1, NS):
-        step = jnp.concatenate(
-            [stores(got_ref, s, 0, cols // 2), stores(got_ref, s, HALF, cols // 2)], 1
-        )
-        running = step if running is None else running + step
-        rounded = running.astype(BF16)
-        count = s if s < NS - 1 else NS
-        at = proj_at(s) * BLK
-        wide_ref[:, at : at + count * BLK] = dot_t(
-            rounded, out_w_ref[0:count].reshape(count * R, cols)
-        )
-        at = (PROJ + s - 1) * BLK
-        wide_ref[:, at : at + BLK] = dot(rounded, in_w_ref[s])
+    for s, running in running_sums(got_ref, cols):
         for m in range(MIC):
             entry = running + placed[m]
             part = jnp.sum(entry * entry, -1, keepdims=True)
             norms = jnp.where(lane == m * NS + s, part, norms)
     high = norms.astype(BF16).astype(F32)
-    wide_ref[:, NORM * BLK : (NORM + 1) * BLK] = jnp.where(
-        lane < 32, high, pltpu.roll(norms - high, 32, 1)
+    norms = jnp.where(lane < 32, high, pltpu.roll(norms - high, 32, 1)).reshape(16, TOK, BLK)
+    block_ref[...] = jnp.concatenate([norms, jnp.zeros_like(norms)], 1).astype(BF16)
+    copy = pltpu.make_async_copy(
+        block_ref, send_ref.at[:, :, NORM * BLK : (NORM + 1) * BLK], sem
     )
-    wide_ref[:, (GRAM + GRAMS) * BLK :] = jnp.zeros((R, BLK), F32)
-
-    square = [(t, s) for t in range(NS) for s in range(t, NS)]
-
-    @pl.when(first_core)
-    def _():
-        for t in range(5):
-            at = (GRAM + gram_at(t)) * BLK
-            wide_ref[:, at : at + (NS - t) * BLK] = dot_t(
-                out_w_ref[t], out_w_ref[t:NS].reshape((NS - t) * R, cols)
-            )
-        for i in range(gram_at(5), GRAMS):
-            t, s = square[i]
-            at = (GRAM + i) * BLK
-            wide_ref[:, at : at + BLK] = dot_t(out_w_ref[t], out_w_ref[s])
-
-    @pl.when(jnp.logical_not(first_core))
-    def _():
-        for t in range(NS - 1):
-            for s in range(t + 1, NS):
-                at = (GRAM + cross_at(t) + s - t - 1) * BLK
-                wide_ref[:, at : at + BLK] = dot(out_w_ref[t], in_w_ref[s])
-        for i in range(GRAMS, OO):
-            t, s = square[i]
-            at = (GRAM + OI + i - GRAMS) * BLK
-            wide_ref[:, at : at + BLK] = dot_t(out_w_ref[t], out_w_ref[s])
-
-    for b in range(SPLIT):
-        pair = [
-            wide_ref[:, at * BLK : (at + 1) * BLK].reshape(16, TOK, BLK) for at in (b, SPLIT + b)
-        ]
-        send_ref[:, :, b * BLK : (b + 1) * BLK] = jnp.concatenate(pair, 1).astype(BF16)
-    for g in range(8):
-        at = START + g * 2 * R
-        for q in range(16):
-            send_ref[q, :, at : at + 2 * R] = start_ref[g * 16 : (g + 1) * 16, :]
+    copy.start()
+    copy.wait()
 
 
 def sum_kernel(parts_ref, send_ref):
@@ -279,11 +301,11 @@
         total = parts_ref[0, :, at].astype(F32)
         for q in range(1, 16):
             total = total + parts_ref[q, :, at].astype(F32)
-        if b == NORM - SPLIT:
+        if b == NORM:
             norm = total + pltpu.roll(total, 96, 1)
             high = norm.astype(BF16).astype(F32)
             norm = jnp.where(lane < 32, high, pltpu.roll(norm - high, 32, 1))
-            total = jnp.where(row < TOK, total, norm)
+            total = jnp.where(row < TOK, norm, 0.0)
         total = total.astype(BF16)
         for q in range(16):
             send_ref[q, :, at] = total
@@ -291,7 +313,7 @@
 
 def chain_kernel(
     width, at_ref, ids_ref, other_ids_ref, parts_ref, sums_ref, other_ref,
-    latent_ref, scalar_ref, proj_ref, oo_ref, oi_ref,
+    latent_ref, scalar_ref, proj_ref, oo_ref, oi_ref, oo_rows_ref, oi_rows_ref,
 ):
     rows = 2 * R
     first_core = at_ref[0] == 0
@@ -331,6 +353,15 @@
         at = (cross_at(t) + s - t - 1) * BLK
         return oi_ref[:, at : at + count * BLK]
 
+    for s in range(1, NS):
+        for t in range(s):
+            at = slice((proj_at(s) + t) * R, (proj_at(s) + t + 1) * R)
+            oo_rows_ref[at, :] = square(t, s)
+            oi_rows_ref[at, :] = cross(t, s)
+
+    def above(ref, s):
+        return ref[proj_at(s) * R : (proj_at(s) + s) * R, :]
+
     norms = spread(NORM)
     norms = norms + pltpu.roll(norms, 96, 1)
     pieces = []
@@ -357,7 +388,7 @@
         entry_out = []
         inner = run_in[s]
         if s > 0:
-            inner = inner + spread(PROJ + s - 1)
+            inner = inner + spread(inner_at(s))
             total = jnp.zeros((rows, R), F32)
             for t in range(s):
                 base = spread(proj_at(s) + t)
@@ -374,11 +405,10 @@
         actives.append(active)
         crossed.append(entry_out)
         grown = dot(active, square(s, s, NS - s))
+        if s > 0:
+            grown = jnp.concatenate([dot_t(active, above(oo_rows_ref, s)), grown], 1)
         for t in range(NS):
-            if t >= s:
-                run_out[t] = run_out[t] + grown[:, (t - s) * R : (t - s + 1) * R]
-            else:
-                run_out[t] = run_out[t] + dot_t(active, square(t, s))
+            run_out[t] = run_out[t] + grown[:, t * R : (t + 1) * R]
         if s < NS - 1:
             grown = dot(active, cross(s, s + 1, NS - 1 - s))
             for t in range(s + 1, NS):
@@ -394,9 +424,11 @@
         inverse = inverses[s]
         total = jnp.sum(d_inner.astype(F32) * inner, -1, keepdims=True)
         scale = inverse * inverse * total * (1.0 / width)
+        if s > 0:
+            back = dot_t(d_inner, above(oi_rows_ref, s))
         for t in range(s):
             grads[t] = (
-                grads[t] + inverse * dot_t(d_inner, cross(t, s)) - scale * crossed[s][t]
+                grads[t] + inverse * back[:, t * R : (t + 1) * R] - scale * crossed[s][t]
             )
         scalars = jnp.where(lane == s, inverse, scalars)
         scalars = jnp.where(lane == NS + s, scale, scalars)
@@ -449,6 +481,11 @@
                     + inverses[s] * dot_t(d_inner(s), in_w_ref[s, here, :])
                     - scales[s] * entry_ref[s]
                 )
+
+
+def add_kernel(keep_ref, swapped_ref, total_ref):
+    for i in range(8):
+        total_ref[i] = (keep_ref[i] + swapped_ref[i].astype(F32)).astype(BF16)
 
 
 def final_kernel(parts_ref, gain_ref, in_ref, out_ref):
@@ -530,20 +567,33 @@
         cost_estimate=pl.CostEstimate(flops=600000000, bytes_accessed=7000000, transcendentals=0),
         name="start",
     )(first_input, w_out, w_in, norm_gain, got)
-    parts, out_w, in_w, first = pl.pallas_call(
+    parts, out_w, in_w = pl.pallas_call(
         project_kernel,
         out_shape=(
             jax.ShapeDtypeStruct((16, 2 * TOK, WIDE), BF16),
             jax.ShapeDtypeStruct((NS, R, cols), BF16),
             jax.ShapeDtypeStruct((NS, cols, R), BF16),
+        ),
+        in_specs=[SMEM, VMEM, VMEM, VMEM],
+        out_specs=(VMEM, VMEM, VMEM),
+        scratch_shapes=[pltpu.VMEM((R, 2 * SPLIT * BLK), F32)],
+        compiler_params=PARAMS,
+        cost_estimate=pl.CostEstimate(flops=2000000000, bytes_accessed=9000000, transcendentals=0),
+        name="project",
+    )(at, got, other, start)
+    parts, first = pl.pallas_call(
+        norm_kernel,
+        out_shape=(
+            jax.ShapeDtypeStruct((16, 2 * TOK, WIDE), BF16),
             jax.ShapeDtypeStruct((2 * R, cols), BF16),
         ),
-        in_specs=[SMEM, SMEM, SMEM, VMEM, VMEM, VMEM, VMEM, VMEM],
-        out_specs=(VMEM, VMEM, VMEM, VMEM),
-        scratch_shapes=[pltpu.VMEM((R, 2 * SPLIT * BLK), F32)],
-        compiler_params=PARAMS,
-        name="project",
-    )(at, ids, other_ids, got, other, own_cols, other_cols, start)
+        in_specs=[SMEM, SMEM, SMEM, VMEM, VMEM, VMEM, pl.BlockSpec(memory_space=pl.ANY)],
+        out_specs=(pl.BlockSpec(memory_space=pl.ANY), VMEM),
+        scratch_shapes=[pltpu.VMEM((16, 2 * TOK, BLK), BF16), pltpu.SemaphoreType.DMA],
+        input_output_aliases={6: 0},
+        compiler_params=PARAMS,
+        name="norms",
+    )(at, ids, other_ids, got, own_cols, other_cols, parts)
     parts = lax.all_to_all(parts, PLANE, 0, 0, tiled=True)
     sums = pl.pallas_call(
         sum_kernel,
@@ -568,6 +618,8 @@
             pltpu.VMEM((R, GRAM * BLK), F32),
             pltpu.VMEM((R, OO * BLK), BF16),
             pltpu.VMEM((R, OI * BLK), BF16),
+            pltpu.VMEM((OI * R, R), BF16),
+            pltpu.VMEM((OI * R, R), BF16),
         ],
         compiler_params=PARAMS,
         name="chain",
@@ -586,7 +638,14 @@
     )(at, ids, other_ids, got, first, out_w, in_w, latent, scalars)
 
     swapped = lax.ppermute(give, "c", SWAP)
-    total = (keep + swapped.astype(F32)).astype(BF16).reshape(64, 32, 2 * R)
+    total = pl.pallas_call(
+        add_kernel,
+        out_shape=jax.ShapeDtypeStruct((8, NS, 32, 2 * R), BF16),
+        in_specs=[VMEM, VMEM],
+        out_specs=VMEM,
+        compiler_params=PARAMS,
+        name="add",
+    )(keep, swapped).reshape(64, 32, 2 * R)
     block = (xl * NS + z) * 2 + core
     gain = lax.dynamic_slice_in_dim(norm_gain[0], block * half, half, 0)
     total, gain = lax.optimization_barrier((total, gain))

time: 205 us -> 203 us (level)
  waiting for transfers between devices: 7.86 us -> 5.39 us
    ppermute x1, waiting for transfers between devices: 2.56 us -> 0.01 us  [body(): other_ids = lax.ppermute(ids, 'xl', SWAP)]
    pallas_call x0 -> x2, Pallas kernels: none -> 2.2 us  [the longest x1 2.02 us: body(): pl.pallas_call(norm_kernel, out_shape=(jax.ShapeDtypeStruct((16, 2 * TOK,...]
  transfers between devices with their start and end apart: 5 -> 5, of which waited for: 3 -> 2; matrix products, arithmetic and copies ran while one was open for 0% -> 0% of each run, Pallas kernels for 1% -> 3%
where the time goes in v6:
time: 203 us
  blocking collectives  166 us (82%)
  Pallas kernels  26.9 us (13%)
  waiting for transfers between devices  5.39 us (3%)
  starting transfers between devices  2.61 us (1%)
    all_to_all x1, blocking collectives, body(): got = lax.all_to_all(send, PLANE, 0, 0, tiled=True)  46.5 us
    all_to_all x1, blocking collectives, body(): parts = lax.all_to_all(parts, PLANE, 0, 0, tiled=True)  45.3 us
    all_to_all x1, blocking collectives, body(): total = lax.all_to_all(total, ('z',) + SECTION, 0, 0, tiled=True)  41.3 us
    all_to_all x1, blocking collectives, body(): sums = lax.all_to_all(sums, PLANE, 0, 0, tiled=True)  32.9 us
    pallas_call x1, Pallas kernels, body(): pl.pallas_call(functools.partial(chain_kernel, width), out_shape=(jax.Sha...  6.96 us
    pallas_call x1, Pallas kernels, body(): pl.pallas_call(pack_kernel, grid_spec=pltpu.PrefetchScalarGridSpec(num_sc...  6.03 us
    pallas_call x1, Pallas kernels, body(): pl.pallas_call(grads_kernel, out_shape=(jax.ShapeDtypeStruct((8, NS, 32,...  5.2 us
  transfers between devices with their start and end apart: 5, of which 2 were waited for; matrix products, arithmetic and copies ran while one was open for 0% of the time, Pallas kernels for 3%

profile of v6, /device:TPU:32, one launch (start us, length us, event | category | flops | bytes accessed | tf_op | source)
XLA Modules:
  0.0 202.6 jit_solution(5874291626618910643)
XLA Ops:
  0.6 0.7 pad_add_fusion.at_ref
  1.3 6.0 %pack.1 = (bf16[16,32,3072]{2,1,0:T(8,128)(2,1)}, bf16[128,512]{1,0:T(8,128)(2,1)}, bf16[128,512]{1,0:T(8,128)(2,1)}) custom-call(s32[4]{0:T(128)} %pad_add_fusion.at_ref, bf16[64,8192]{1,0:T(8,128)(2,1)} %bitcast.31, bf16[64,8192]{1,0:T(8,128)(2,1)} %bitcast.32, bf16[128,8192]{1,0:T(8,128)(2,1)} %bitcast.19, bf16[2,8,2,8,32,128]{5,4,3,2,1,0:T(8,128)(2,1)} %bitcast.21, ...), custom_call_target="tpu_custom_call" | custom-call | tf_op jit(solution)/shard_map/pack/pallas_call | solution.py:519
  7.3 0.0 copy-start.7
  7.4 0.0 copy-start.1
  7.4 0.0 copy-start.2
  7.4 0.0 copy-start.3
  7.4 46.5 %all_to_all.20.after_ref.got_ref = bf16[16,32,3072]{2,1,0:T(8,128)(2,1)S(1)} all-to-all(bf16[16,32,3072]{2,1,0:T(8,128)(2,1)} %get-tuple-element.18), channel_id=1, replica_groups=mesh['xl'=2,'z'=8,'c'=2,'y'=4,'xh'=2] {'xl','y','xh'}, dimensions={0} | all-to-all | bytes 6291456 | tf_op jit(solution)/shard_map/all_to_all | solution.py:559
  53.9 0.1 slice.8
  54.0 0.1 collective-permute-start.2
  54.1 0.7 collective-permute-start
  54.8 1.5 collective-permute-start.1
  56.2 0.0 copy-done.1
  56.2 1.2 start.1.start_ref
  57.5 0.0 copy-start.4
  57.5 0.0 collective-permute-done.2.other_ref
  57.5 3.9 %project.1 = (bf16[16,16,6528]{2,1,0:T(8,128)(2,1)S(1)}, bf16[8,128,512]{2,1,0:T(8,128)(2,1)S(1)}, bf16[8,512,128]{2,1,0:T(8,128)(2,1)S(1)}) custom-call(s32[4]{0:T(128)S(1)} %copy-done.6, bf16[16,32,3072]{2,1,0:T(8,128)(2,1)S(1)} %all_to_all.20.after_ref.got_ref, bf16[16,32,1024]{2,1,0:T(8,128)(2,1)S(1)} %collective-permute-done.2.other_ref, ...), custom_call_target="tpu_custom_call" | custom-call | flops 2000000000 | bytes 9000000 | tf_op jit(solution)/shard_map/project/pallas_call | solution.py:570
  61.4 0.0 collective-permute-done.other_ids_ref
  61.5 0.0 collective-permute-done.1.other_cols_ref
  61.5 2.0 norms.1
  63.5 45.3 %all_to_all.21.parts_ref = bf16[16,16,6528]{2,1,0:T(8,128)(2,1)S(1)} all-to-all(bf16[16,16,6528]{2,1,0:T(8,128)(2,1)S(1)} %get-tuple-element.25), channel_id=1, replica_groups=mesh['xl'=2,'z'=8,'c'=2,'y'=4,'xh'=2] {'xl','y','xh'}, dimensions={0} | all-to-all | bytes 6684672 | tf_op jit(solution)/shard_map/all_to_all | solution.py:597
  108.8 0.4 sums.1
  109.2 32.9 %all_to_all.22.sums_ref = bf16[16,16,4480]{2,1,0:T(8,128)(2,1)S(1)} all-to-all(bf16[16,16,4480]{2,1,0:T(8,128)(2,1)S(1)} %sums.1), channel_id=1, replica_groups=mesh['xl'=2,'z'=8,'c'=2,'y'=4,'xh'=2] {'xl','y','xh'}, dimensions={0} | all-to-all | bytes 4587520 | tf_op jit(solution)/shard_map/all_to_all | solution.py:606
  142.1 0.1 slice_bitcast_fusion
  142.2 0.3 collective-permute-start.3
  142.5 2.6 %collective-permute-done.3.other_ref = bf16[128,4096]{1,0:T(8,128)(2,1)S(1)} collective-permute-done((bf16[128,4096]{1,0:T(8,128)(2,1)S(1)}, bf16[128,4096]{1,0:T(8,128)(2,1)S(1)}, u32[]{:S(2)}, u32[]{:S(2)}) %collective-permute-start.3) | collective-permute-done | bytes 1048608 | tf_op jit(solution)/shard_map/ppermute | solution.py:608
  145.1 7.0 %chain.1 = (bf16[256,2048]{1,0:T(8,128)(2,1)S(1)}, f32[256,128]{1,0:T(8,128)S(1)}) custom-call(s32[4]{0:T(128)S(1)} %copy-done.6, s32[4,8]{1,0:T(4,128)S(1)} %bitcast.28, s32[4,8]{1,0:T(4,128)S(1)} %collective-permute-done.other_ids_ref, bf16[16,16,6528]{2,1,0:T(8,128)(2,1)S(1)} %all_to_all.21.parts_ref, bf16[16,16,4480]{2,1,0:T(8,128)(2,1)S(1)} %all_to_all.22.sums_ref, ...), custom_call_target="tpu_custom_call" | custom-call | tf_op jit(solution)/shard_map/chain/pallas_call | solution.py:609
  152.1 5.2 %grads.1 = (bf16[8,8,32,256]{3,2,1,0:T(8,128)(2,1)}, f32[8,8,32,256]{3,2,1,0:T(8,128)S(1)}) custom-call(s32[4]{0:T(128)S(1)} %copy-done.6, s32[4,8]{1,0:T(4,128)S(1)} %bitcast.29, s32[4,8]{1,0:T(4,128)S(1)} %collective-permute-done.other_ids_ref, bf16[16,32,3072]{2,1,0:T(8,128)(2,1)S(1)} %all_to_all.20.after_ref.got_ref, ...), custom_call_target="tpu_custom_call" | custom-call | tf_op jit(solution)/shard_map/grads/pallas_call | solution.py:627
  157.3 0.1 collective-permute-start.4
  157.4 2.7 %collective-permute-done.4.swapped_ref = bf16[8,8,32,256]{3,2,1,0:T(8,128)(2,1)S(1)} collective-permute-done((bf16[8,8,32,256]{3,2,1,0:T(8,128)(2,1)}, bf16[8,8,32,256]{3,2,1,0:T(8,128)(2,1)S(1)}, u32[]{:S(2)}, u32[]{:S(2)}) %collective-permute-start.4) | collective-permute-done | bytes 1048608 | tf_op jit(solution)/shard_map/ppermute | solution.py:640
  160.2 0.2 add.27
  160.4 41.3 %all_to_all.23 = bf16[64,32,256]{2,1,0:T(8,128)(2,1)S(1)} all-to-all(bf16[64,32,256]{2,1,0:T(8,128)(2,1)S(1)} %bitcast.24), channel_id=1, replica_groups=mesh['xl'=2,'z'=8,'c'=2,'y'=4,'xh'=2] {'z','y','xh'}, dimensions={0} | all-to-all | bytes 2097152 | tf_op jit(solution)/shard_map/all_to_all | solution.py:652
  201.7 0.9 final.1
  (11 shorter events, 0.0 us)
Async XLA Ops:
  7.3 46.7 %copy-start.5 = (s32[1,4,8]{2,1,0:T(4,128)S(1)}, s32[1,4,8]{2,1,0:T(4,128)}, u32[]{:S(2)}) copy-start(s32[1,4,8]{2,1,0:T(4,128)} %param.8) | copy-start | bytes 388
  7.3 47.4 %copy-start.7 = (bf16[128,512]{1,0:T(8,128)(2,1)S(1)}, bf16[128,512]{1,0:T(8,128)(2,1)}, u32[]{:S(2)}) copy-start(bf16[128,512]{1,0:T(8,128)(2,1)} %get-tuple-element.20) | copy-start | bytes 393220
  7.4 48.9 %copy-start.1 = (bf16[1,8192,128]{2,1,0:T(8,128)(2,1)S(1)}, bf16[1,8192,128]{2,1,0:T(8,128)(2,1)}, u32[]{:S(2)}) copy-start(bf16[1,8192,128]{2,1,0:T(8,128)(2,1)} %param.12) | copy-start | bytes 6291460
  7.4 48.8 %copy-start.2 = (bf16[4,32,8192]{2,1,0:T(8,128)(2,1)S(1)}, bf16[4,32,8192]{2,1,0:T(8,128)(2,1)}, u32[]{:S(2)}) copy-start(bf16[4,32,8192]{2,1,0:T(8,128)(2,1)} %first_ref.3) | copy-start | bytes 6291460
  7.4 48.8 %copy-start.3 = (f32[1,8192]{1,0:T(1,128)S(1)}, f32[1,8192]{1,0:T(1,128)}, u32[]{:S(2)}) copy-start(f32[1,8192]{1,0:T(1,128)} %gain_ref.1) | copy-start | bytes 98308
  53.9 2.3 %copy-start = (bf16[1,128,8192]{2,1,0:T(8,128)(2,1)S(1)}, bf16[1,128,8192]{2,1,0:T(8,128)(2,1)}, u32[]{:S(2)}) copy-start(bf16[1,128,8192]{2,1,0:T(8,128)(2,1)} %param.13) | copy-start | bytes 6291460
  54.0 3.5 %collective-permute-start.2 = (bf16[16,32,1024]{2,1,0:T(8,128)(2,1)S(1)}, bf16[16,32,1024]{2,1,0:T(8,128)(2,1)S(1)}, u32[]{:S(2)}, u32[]{:S(2)}) collective-permute-start(bf16[16,32,1024]{2,1,0:T(8,128)(2,1)S(1)} %slice.8), channel_id=1, source_target_pairs={{0,8},{8,0},{1,9},{9,1},{2,10},{10,2},{3,11},{11,3},{4,12},{12,4},... | collective-permute-start | bytes 3145736 | tf_op jit(solution)/shard_map/ppermute | solution.py:560
  54.1 7.3 %collective-permute-start = (s32[4,8]{1,0:T(4,128)S(1)}, s32[4,8]{1,0:T(4,128)S(1)}, u32[]{:S(2)}, u32[]{:S(2)}) collective-permute-start(s32[4,8]{1,0:T(4,128)S(1)} %bitcast.26), channel_id=1, source_target_pairs={{0,128},{128,0},{1,129},{129,1},{2,130},{130,2},{3,131},{131,3},{4... | collective-permute-start | bytes 392 | tf_op jit(solution)/shard_map/ppermute | solution.py:557
  54.8 6.7 %collective-permute-start.1 = (bf16[128,512]{1,0:T(8,128)(2,1)S(1)}, bf16[128,512]{1,0:T(8,128)(2,1)S(1)}, u32[]{:S(2)}, u32[]{:S(2)}) collective-permute-start(bf16[128,512]{1,0:T(8,128)(2,1)S(1)} %copy-done.7), channel_id=1, source_target_pairs={{0,128},{128,0},{1,129},{129,1},{2,130},{130,2},{3,131},{131,3},{4... | collective-permute-start | bytes 393224 | tf_op jit(solution)/shard_map/ppermute | solution.py:558
  56.2 1.3 copy-start.6
  57.5 4.0 %copy-start.4 = (bf16[128,512]{1,0:T(8,128)(2,1)S(1)}, bf16[128,512]{1,0:T(8,128)(2,1)}, u32[]{:S(2)}) copy-start(bf16[128,512]{1,0:T(8,128)(2,1)} %get-tuple-element.19.cols_ref) | copy-start | bytes 393220
  142.2 2.9 %collective-permute-start.3 = (bf16[128,4096]{1,0:T(8,128)(2,1)S(1)}, bf16[128,4096]{1,0:T(8,128)(2,1)S(1)}, u32[]{:S(2)}, u32[]{:S(2)}) collective-permute-start(bf16[128,4096]{1,0:T(8,128)(2,1)S(1)} %slice_bitcast_fusion), channel_id=1, source_target_pairs={{0,8},{8,0},{1,9},{9,1},{2,10},{10,2},{3,11},{11,3},{4,12},{12,4},... | collective-permute-start | bytes 3145736 | tf_op jit(solution)/shard_map/ppermute | solution.py:608
  157.3 2.9 %collective-permute-start.4 = (bf16[8,8,32,256]{3,2,1,0:T(8,128)(2,1)}, bf16[8,8,32,256]{3,2,1,0:T(8,128)(2,1)S(1)}, u32[]{:S(2)}, u32[]{:S(2)}) collective-permute-start(bf16[8,8,32,256]{3,2,1,0:T(8,128)(2,1)} %get-tuple-element.29), channel_id=1, source_target_pairs={{0,8},{8,0},{1,9},{9,1},{2,10},{10,2},{3,11},{11,3},{4,12},{12,4},... | collective-permute-start | bytes 3145736 | tf_op jit(solution)/shard_map/ppermute | solution.py:640

commit v7 on v6

--- a/solution.py
+++ b/solution.py
@@ -71,7 +71,7 @@
 
 def pack_kernel(
     at_ref, in_ref, out_ref, w_out_ref, w_in_ref, gain_ref, first_ref,
-    send_ref, cols_ref, give_ref, turn_ref,
+    send_ref, turn_ref,
 ):
     section = at_ref[1]
 
@@ -98,18 +98,22 @@
             to = c * 256 + zq * BLK
             for h in range(2):
                 lanes = [((4 * zq + j) * 4 + c * 2 + h) * BLK for j in range(4)]
-                for ref, row, at in (
-                    (in_ref, 0, c * HALF + zq * BLK),
-                    (in_ref, 32, c * HALF + 256 + zq * BLK),
-                    (out_ref, 0, c * HALF + 512 + zq * BLK),
-                    (out_ref, 32, c * HALF + 768 + zq * BLK),
-                    (w_out_ref, 0, W_LANE + to),
+                for ref, row, at, other in (
+                    (in_ref, 0, c * HALF + zq * BLK, 0),
+                    (in_ref, 32, c * HALF + 256 + zq * BLK, 0),
+                    (out_ref, 0, c * HALF + 512 + zq * BLK, NS - 1),
+                    (out_ref, 32, c * HALF + 768 + zq * BLK, NS - 1),
+                    (w_out_ref, 0, W_LANE + to, None),
                 ):
-                    pieces.append(
-                        jnp.concatenate(
-                            [ref[row : row + 32, lane : lane + BLK] for lane in lanes], 1
+                    piece = jnp.concatenate(
+                        [ref[row : row + 32, lane : lane + BLK] for lane in lanes], 1
+                    )
+                    if other is not None:
+                        first = jnp.concatenate(
+                            [first_ref[row // 32, :, lane : lane + BLK] for lane in lanes], 1
                         )
-                    )
+                        piece = jnp.where(section == other, first, piece)
+                    pieces.append(piece)
                     places.append((4 * h, at))
     turned = dot(jnp.concatenate(pieces, 0), turn_ref[...]).astype(BF16)
     for n, (first, at) in enumerate(places):
@@ -117,33 +121,6 @@
             send_ref[first + i, :, at : at + BLK] = turned[
                 32 * n : 32 * n + 32, i * BLK : (i + 1) * BLK
             ]
-
-    pieces = []
-    for c in range(2):
-        for zq in range(2):
-            lanes = [
-                pl.multiple_of(((4 * zq + j) * 4 + c * 2 + section // 4) * BLK, BLK)
-                for j in range(4)
-            ]
-            for m in range(MIC):
-                pieces.append(
-                    jnp.concatenate([first_ref[m, :, pl.ds(lane, BLK)] for lane in lanes], 1)
-                )
-    group = pl.multiple_of(section % 4 * BLK, BLK)
-    turned = dot(jnp.concatenate(pieces, 0), turn_ref[:, pl.ds(group, BLK)]).astype(BF16)
-    mine = pl.program_id(0) == at_ref[2]
-
-    def put(ref):
-        for n in range(4):
-            ref[:, n * BLK : (n + 1) * BLK] = turned[n * R : (n + 1) * R]
-
-    @pl.when(mine)
-    def _():
-        put(cols_ref)
-
-    @pl.when(jnp.logical_not(mine))
-    def _():
-        put(give_ref)
 
 
 def start_kernel(first_ref, w_out_ref, w_in_ref, gain_ref, after_ref, start_ref):
@@ -164,6 +141,16 @@
                 - got_ref[x * NS + s - 1, :, pl.ds(b, cols)].astype(F32)
             )
     return jnp.concatenate(pieces, 0)
+
+
+def first_rows(got_ref, at, cols):
+    pieces = []
+    for x in range(2):
+        for m in range(MIC):
+            q = x * NS + (0 if m < 2 else NS - 1)
+            lane = at + m // 2 * 512 + m % 2 * 256
+            pieces.append(got_ref[q, :, pl.ds(lane, cols)])
+    return jnp.concatenate(pieces, 0).astype(F32)
 
 
 def picks_of(at_ref, ids_ref, other_ids_ref):
@@ -252,17 +239,16 @@
 
 
 def norm_kernel(
-    at_ref, ids_ref, other_ids_ref, got_ref, cols_ref, other_cols_ref, before_ref,
-    send_ref, first_ref, block_ref, sem,
+    cols, at_ref, ids_ref, other_ids_ref, got_ref, before_ref, send_ref, block_ref, sem
 ):
     del before_ref
-    cols = cols_ref.shape[1]
     picks = picks_of(at_ref, ids_ref, other_ids_ref)
     placed = [[] for _ in range(MIC)]
+    first = jnp.concatenate(
+        [first_rows(got_ref, 0, cols // 2), first_rows(got_ref, HALF, cols // 2)], 1
+    )
     for x in range(2):
-        rows = jnp.where(at_ref[2] == x, cols_ref[...], other_cols_ref[...])
-        first_ref[x * R : (x + 1) * R, :] = rows
-        rows = rows.astype(F32)
+        rows = first[x * R : (x + 1) * R]
         for e in range(NS):
             for m in range(MIC):
                 total = jnp.zeros((TOK, cols), F32)
@@ -311,12 +297,7 @@
             send_ref[q, :, at] = total
 
 
-def chain_kernel(
-    width, at_ref, ids_ref, other_ids_ref, parts_ref, sums_ref, other_ref,
-    latent_ref, scalar_ref, proj_ref, oo_ref, oi_ref, oo_rows_ref, oi_rows_ref,
-):
-    rows = 2 * R
-    first_core = at_ref[0] == 0
+def gather_kernel(at_ref, ids_ref, other_ids_ref, sums_ref, base_ref, proj_ref):
     for b in range(GRAM):
         upper = b >= SPLIT
         at = (b - SPLIT * upper) * BLK
@@ -324,6 +305,24 @@
         proj_ref[:, b * BLK : (b + 1) * BLK] = block[:, TOK * upper : TOK * upper + TOK].reshape(
             R, BLK
         )
+    for n, pick in enumerate(picks_of(at_ref, ids_ref, other_ids_ref)):
+        rows = slice(n * TOK, (n + 1) * TOK)
+        here = pl.ds(pl.multiple_of(pick * TOK, TOK), TOK)
+        base_ref[rows, :] = proj_ref[here, :]
+        norm = proj_ref[here, NORM * BLK : (NORM + 1) * BLK]
+        norm = norm + pltpu.roll(norm, 96, 1)
+        m = n % 16 // 4
+        base_ref[rows, NORM * BLK : (NORM + 1) * BLK] = (
+            pltpu.roll(norm, BLK - m * NS, 1) if m else norm
+        )
+
+
+def chain_kernel(
+    width, at_ref, parts_ref, base_ref, sums_ref, other_ref,
+    latent_ref, scalar_ref, oo_ref, oi_ref, oo_rows_ref, oi_rows_ref,
+):
+    rows = 2 * R
+    first_core = at_ref[0] == 0
     for b in range(0, GRAMS, 4):
         at = (GRAM - SPLIT + b) * BLK
         mine = sums_ref[:, :, at : at + 4 * BLK].astype(F32)[:, TOK:]
@@ -336,14 +335,9 @@
             oi_ref[:, at] = second
         else:
             oo_ref[:, (b + 4) * BLK : (b + 8) * BLK] = second
-    places = [
-        pl.multiple_of(pick * TOK, TOK) for pick in picks_of(at_ref, ids_ref, other_ids_ref)
-    ]
 
     def spread(at):
-        return jnp.concatenate(
-            [proj_ref[pl.ds(place, TOK), at * BLK : (at + 1) * BLK] for place in places], 0
-        )
+        return base_ref[:, at * BLK : (at + 1) * BLK]
 
     def square(t, s, count=1):
         at = (gram_at(t) + s - t) * BLK
@@ -363,14 +357,6 @@
         return ref[proj_at(s) * R : (proj_at(s) + s) * R, :]
 
     norms = spread(NORM)
-    norms = norms + pltpu.roll(norms, 96, 1)
-    pieces = []
-    for n in range(32):
-        m = n % 16 // 4
-        piece = norms[n * TOK : (n + 1) * TOK]
-        pieces.append(pltpu.roll(piece, BLK - m * NS, 1) if m else piece)
-    norms = jnp.concatenate(pieces, 0)
-
     starts = []
     for s in range(NS):
         pieces = []
@@ -383,6 +369,7 @@
     run_in = [start[:, :R].astype(F32) for start in starts]
     run_out = list(start_out)
     inners, inverses, actives, crossed = [], [], [], []
+    grown_norm = jnp.zeros((rows, R), F32)
     for s in range(NS):
         norm = norms[:, s : s + 1]
         entry_out = []
@@ -392,23 +379,24 @@
             total = jnp.zeros((rows, R), F32)
             for t in range(s):
                 base = spread(proj_at(s) + t)
-                full = base + run_out[t]
-                entry_out.append(full)
-                total = total + actives[t].astype(F32) * (full + base + start_out[t])
-            norm = norm + jnp.sum(total, -1, keepdims=True)
+                entry_out.append(base + run_out[t])
+                total = total + actives[t] * base
+            norm = norm + jnp.sum(2.0 * total + grown_norm, -1, keepdims=True)
         inverse = lax.rsqrt(jnp.maximum(norm, 0.0) * (1.0 / width) + EPS)
         inner = inner * inverse
         active = (inner * jax.nn.sigmoid(inner)).astype(BF16)
         latent_ref[:, s * R : (s + 1) * R] = active
         inners.append(inner)
         inverses.append(inverse)
-        actives.append(active)
+        actives.append(active.astype(F32))
         crossed.append(entry_out)
         grown = dot(active, square(s, s, NS - s))
         if s > 0:
             grown = jnp.concatenate([dot_t(active, above(oo_rows_ref, s)), grown], 1)
+        before = run_out[s]
         for t in range(NS):
             run_out[t] = run_out[t] + grown[:, t * R : (t + 1) * R]
+        grown_norm = grown_norm + actives[s] * (before + run_out[s])
         if s < NS - 1:
             grown = dot(active, cross(s, s + 1, NS - 1 - s))
             for t in range(s + 1, NS):
@@ -436,8 +424,8 @@
 
 
 def grads_kernel(
-    at_ref, ids_ref, other_ids_ref, got_ref, first_ref, out_w_ref, in_w_ref, latent_ref, scalar_ref,
-    give_ref, keep_ref, entry_ref, step_ref,
+    own, at_ref, ids_ref, other_ids_ref, got_ref, out_w_ref, in_w_ref, latent_ref, scalar_ref,
+    result_ref, entry_ref, step_ref,
 ):
     cols = step_ref.shape[1]
     scalars = scalar_ref[...]
@@ -453,34 +441,29 @@
     def d_inner(s):
         return latent_ref[:, (NS + s) * R : (NS + s + 1) * R]
 
-    for side, result_ref in ((1 - at_ref[0], give_ref), (at_ref[0], keep_ref)):
-        here = pl.ds(pl.multiple_of(side * cols, cols), cols)
-        at = pl.multiple_of(side * HALF, HALF)
-
-        def put(s, kind, value, result_ref=result_ref):
-            result_ref[:, s, :, kind * R : (kind + 1) * R] = value.reshape(8, 32, R).astype(
-                result_ref.dtype
-            )
-
-        entry = first_ref[:, here].astype(F32)
-        for s in range(NS):
-            if s > 0:
-                step_ref[...] = stores(got_ref, s, at, cols)
-                entry = entry + jnp.concatenate(
-                    [step_ref[pl.ds(place, TOK), :] for place in places], 0
-                )
-            entry_ref[s] = entry
-            put(s, 0, dot_rows((entry * inverses[s]).astype(BF16), d_inner(s)))
-            entry = entry + dot(active(s), out_w_ref[s, :, here])
-        grad = entry
-        for s in range(NS - 1, -1, -1):
-            put(s, 1, dot_rows(grad.astype(BF16), active(s)))
-            if s > 0:
-                grad = (
-                    grad
-                    + inverses[s] * dot_t(d_inner(s), in_w_ref[s, here, :])
-                    - scales[s] * entry_ref[s]
-                )
+    side = at_ref[0] if own else 1 - at_ref[0]
+    here = pl.ds(pl.multiple_of(side * cols, cols), cols)
+    at = pl.multiple_of(side * HALF, HALF)
+
+    def put(s, kind, value):
+        result_ref[:, s, :, kind * R : (kind + 1) * R] = value.reshape(8, 32, R).astype(
+            result_ref.dtype
+        )
+
+    entry = first_rows(got_ref, at, cols)
+    for s in range(NS):
+        if s > 0:
+            step_ref[...] = stores(got_ref, s, at, cols)
+            entry = entry + jnp.concatenate([step_ref[pl.ds(place, TOK), :] for place in places], 0)
+        entry_ref[s] = entry
+        put(s, 0, dot_rows((entry * inverses[s]).astype(BF16), d_inner(s)))
+        entry = entry + dot(active(s), out_w_ref[s, :, here])
+    grad = entry
+    for s in range(NS - 1, -1, -1):
+        put(s, 1, dot_rows(grad.astype(BF16), active(s)))
+        if s > 0:
+            back = dot_t(d_inner(s), in_w_ref[s, here, :])
+            grad = grad + inverses[s] * back - scales[s] * entry_ref[s]
 
 
 def add_kernel(keep_ref, swapped_ref, total_ref):
@@ -512,11 +495,12 @@
     section = lax.axis_index(SECTION)
     quarter = xl * 2 + core
     at = jnp.stack([core, section, xl, quarter]).astype(jnp.int32)
-    ids = example_ids[0]
     w_in = adapter_in[0]
     w_out = adapter_out[0]
 
-    send, own_cols, give_cols = pl.pallas_call(
+    ids = example_ids[0]
+    other_ids = lax.ppermute(ids, "xl", SWAP)
+    send = pl.pallas_call(
         pack_kernel,
         grid_spec=pltpu.PrefetchScalarGridSpec(
             num_scalar_prefetch=1,
@@ -529,20 +513,12 @@
                     (1, 4, 1, 8, 32, R), lambda i, at: (i, at[3] % 2, at[3] // 2, 0, 0, 0)
                 ),
                 pl.BlockSpec((1, 4, 1, 2, BLK), lambda i, at: (i, at[3] % 2, at[3] // 2, 0, 0)),
-                pl.BlockSpec((MIC, 32, wide), lambda i, at: (0, 0, i)),
+                pl.BlockSpec((2, 32, wide), lambda i, at: (at[1] // (NS - 1), 0, i)),
             ],
-            out_specs=[
-                pl.BlockSpec((8, 32, SENT), lambda i, at: (i, 0, 0)),
-                pl.BlockSpec((R, cols), lambda i, at: (0, 0)),
-                pl.BlockSpec((R, cols), lambda i, at: (0, 0)),
-            ],
+            out_specs=pl.BlockSpec((8, 32, SENT), lambda i, at: (i, 0, 0)),
             scratch_shapes=[pltpu.VMEM((4 * BLK, 4 * BLK), BF16)],
         ),
-        out_shape=(
-            jax.ShapeDtypeStruct((16, 32, SENT), BF16),
-            jax.ShapeDtypeStruct((R, cols), BF16),
-            jax.ShapeDtypeStruct((R, cols), BF16),
-        ),
+        out_shape=jax.ShapeDtypeStruct((16, 32, SENT), BF16),
         compiler_params=LARGE,
         name="pack",
     )(
@@ -554,8 +530,6 @@
         norm_gain.reshape(2, 8, 2, 2, BLK),
         first_input,
     )
-    other_ids = lax.ppermute(ids, "xl", SWAP)
-    other_cols = lax.ppermute(give_cols, "xl", SWAP)
     got = lax.all_to_all(send, PLANE, 0, 0, tiled=True)
     other = lax.ppermute(got[:, :, W_LANE:], "c", SWAP)
     start = pl.pallas_call(
@@ -581,19 +555,16 @@
         cost_estimate=pl.CostEstimate(flops=2000000000, bytes_accessed=9000000, transcendentals=0),
         name="project",
     )(at, got, other, start)
-    parts, first = pl.pallas_call(
-        norm_kernel,
-        out_shape=(
-            jax.ShapeDtypeStruct((16, 2 * TOK, WIDE), BF16),
-            jax.ShapeDtypeStruct((2 * R, cols), BF16),
-        ),
-        in_specs=[SMEM, SMEM, SMEM, VMEM, VMEM, VMEM, pl.BlockSpec(memory_space=pl.ANY)],
-        out_specs=(pl.BlockSpec(memory_space=pl.ANY), VMEM),
+    parts = pl.pallas_call(
+        functools.partial(norm_kernel, cols),
+        out_shape=jax.ShapeDtypeStruct((16, 2 * TOK, WIDE), BF16),
+        in_specs=[SMEM, SMEM, SMEM, VMEM, pl.BlockSpec(memory_space=pl.ANY)],
+        out_specs=pl.BlockSpec(memory_space=pl.ANY),
         scratch_shapes=[pltpu.VMEM((16, 2 * TOK, BLK), BF16), pltpu.SemaphoreType.DMA],
-        input_output_aliases={6: 0},
+        input_output_aliases={4: 0},
         compiler_params=PARAMS,
         name="norms",
-    )(at, ids, other_ids, got, own_cols, other_cols, parts)
+    )(at, ids, other_ids, got, parts)
     parts = lax.all_to_all(parts, PLANE, 0, 0, tiled=True)
     sums = pl.pallas_call(
         sum_kernel,
@@ -606,16 +577,25 @@
     sums = lax.all_to_all(sums, PLANE, 0, 0, tiled=True)
     gram = sums[:, TOK:, (GRAM - SPLIT) * BLK : (GRAM - SPLIT + GRAMS) * BLK]
     other = lax.ppermute(gram.reshape(R, GRAMS * BLK), "c", SWAP)
+    base = pl.pallas_call(
+        gather_kernel,
+        out_shape=jax.ShapeDtypeStruct((2 * R, GRAM * BLK), F32),
+        in_specs=[SMEM, SMEM, SMEM, VMEM],
+        out_specs=VMEM,
+        scratch_shapes=[pltpu.VMEM((R, GRAM * BLK), F32)],
+        compiler_params=PARAMS,
+        cost_estimate=pl.CostEstimate(flops=0, bytes_accessed=7000000, transcendentals=0),
+        name="gather",
+    )(at, ids, other_ids, sums)
     latent, scalars = pl.pallas_call(
         functools.partial(chain_kernel, width),
         out_shape=(
             jax.ShapeDtypeStruct((2 * R, 16 * BLK), BF16),
             jax.ShapeDtypeStruct((2 * R, BLK), F32),
         ),
-        in_specs=[SMEM, SMEM, SMEM, VMEM, VMEM, VMEM],
+        in_specs=[SMEM, VMEM, VMEM, VMEM, VMEM],
         out_specs=(VMEM, VMEM),
         scratch_shapes=[
-            pltpu.VMEM((R, GRAM * BLK), F32),
             pltpu.VMEM((R, OO * BLK), BF16),
             pltpu.VMEM((R, OI * BLK), BF16),
             pltpu.VMEM((OI * R, R), BF16),
@@ -623,21 +603,24 @@
         ],
         compiler_params=PARAMS,
         name="chain",
-    )(at, ids, other_ids, parts, sums, other)
-    give, keep = pl.pallas_call(
-        grads_kernel,
-        out_shape=(
-            jax.ShapeDtypeStruct((8, NS, 32, 2 * R), BF16),
-            jax.ShapeDtypeStruct((8, NS, 32, 2 * R), F32),
-        ),
-        in_specs=[SMEM, SMEM, SMEM] + [VMEM] * 6,
-        out_specs=(VMEM, VMEM),
-        scratch_shapes=[pltpu.VMEM((NS, 2 * R, half), F32), pltpu.VMEM((R, half), F32)],
-        compiler_params=PARAMS,
-        name="grads",
-    )(at, ids, other_ids, got, first, out_w, in_w, latent, scalars)
-
-    swapped = lax.ppermute(give, "c", SWAP)
+    )(at, parts, base, sums, other)
+
+    def grads(own):
+        return pl.pallas_call(
+            functools.partial(grads_kernel, own),
+            out_shape=jax.ShapeDtypeStruct((8, NS, 32, 2 * R), F32 if own else BF16),
+            in_specs=[SMEM, SMEM, SMEM] + [VMEM] * 5,
+            out_specs=VMEM,
+            scratch_shapes=[pltpu.VMEM((NS, 2 * R, half), F32), pltpu.VMEM((R, half), F32)],
+            compiler_params=PARAMS,
+            cost_estimate=pl.CostEstimate(
+                flops=600000000, bytes_accessed=9000000, transcendentals=0
+            ),
+            name="grads_own" if own else "grads_other",
+        )(at, ids, other_ids, got, out_w, in_w, latent, scalars)
+
+    swapped = lax.ppermute(grads(False), "c", SWAP)
+    keep = grads(True)
     total = pl.pallas_call(
         add_kernel,
         out_shape=jax.ShapeDtypeStruct((8, NS, 32, 2 * R), BF16),

time: 203 us -> 205 us (level)
  local copies, waits for them, and re-layouts: 0.24 us -> 4.62 us
  waiting for transfers between devices: 5.39 us -> 1.48 us
    unnamed x16 -> x24, local copies, waits for them, and re-layouts: 0.04 us -> 4.43 us
    ppermute x2 -> x1, waiting for transfers between devices: 2.74 us -> 0.01 us  [body(): swapped = lax.ppermute(grads(False), 'c', SWAP)]
    pallas_call x2 -> x4, Pallas kernels: 7.22 us -> 9.58 us  [the longest x2 6.43 us: grads(): pl.pallas_call(functools.partial(grads_kernel, own), out_shape=jax.ShapeD...]
  transfers between devices with their start and end apart: 5 -> 4, of which waited for: 2 -> 1; matrix products, arithmetic and copies ran while one was open for 0% -> 0% of each run, Pallas kernels for 3% -> 4%
where the time goes in v7:
time: 205 us; the launch traced here: 204 us
  blocking collectives  167 us (81%)
  Pallas kernels  28.6 us (14%)
  local copies, waits for them, and re-layouts  4.62 us (2%)
    all_to_all x1, blocking collectives, body(): got = lax.all_to_all(send, PLANE, 0, 0, tiled=True)  46.5 us
    all_to_all x1, blocking collectives, body(): parts = lax.all_to_all(parts, PLANE, 0, 0, tiled=True)  45.5 us
    all_to_all x1, blocking collectives, body(): total = lax.all_to_all(total, ('z',) + SECTION, 0, 0, tiled=True)  40.9 us
    all_to_all x1, blocking collectives, body(): sums = lax.all_to_all(sums, PLANE, 0, 0, tiled=True)  34 us
    pallas_call x2, Pallas kernels, grads(): pl.pallas_call(functools.partial(grads_kernel, own), out_shape=jax.ShapeD...  6.43 us
    pallas_call x1, Pallas kernels, body(): pl.pallas_call(functools.partial(chain_kernel, width), out_shape=(jax.Sha...  5.61 us
    pallas_call x1, Pallas kernels, body(): pl.pallas_call(pack_kernel, grid_spec=pltpu.PrefetchScalarGridSpec(num_sc...  5.46 us
    unnamed x24, local copies, waits for them, and re-layouts  4.43 us
  transfers between devices with their start and end apart: 4, of which 1 were waited for; matrix products, arithmetic and copies ran while one was open for 0% of the time, Pallas kernels for 4%

profile of v7, /device:TPU:32, one launch (start us, length us, event | category | flops | bytes accessed | tf_op | source)
XLA Modules:
  0.0 204.2 jit_solution(8211158471137105359)
XLA Ops:
  0.6 0.7 pad_add_fusion.at_ref
  1.3 5.5 %pack.1 = bf16[16,32,3072]{2,1,0:T(8,128)(2,1)} custom-call(s32[4]{0:T(128)} %pad_add_fusion.at_ref, bf16[64,8192]{1,0:T(8,128)(2,1)} %bitcast.32, bf16[64,8192]{1,0:T(8,128)(2,1)} %bitcast.33, bf16[128,8192]{1,0:T(8,128)(2,1)} %bitcast.19, bf16[2,8,2,8,32,128]{5,4,3,2,1,0:T(8,128)(2,1)} %bitcast.21, f32[2,8,2,2,128]{4,3,2,1,0:T(2,128)} %bitcast.25, ...), custom_call_target="tpu_custom_call" | custom-call | tf_op jit(solution)/shard_map/pack/pallas_call | solution.py:503
  6.8 0.0 copy-start.2
  6.8 0.0 copy-start.9
  6.8 46.5 %all_to_all.20.after_ref.got_ref = bf16[16,32,3072]{2,1,0:T(8,128)(2,1)S(1)} all-to-all(bf16[16,32,3072]{2,1,0:T(8,128)(2,1)} %pack.1), channel_id=1, replica_groups=mesh['xl'=2,'z'=8,'c'=2,'y'=4,'xh'=2] {'xl','y','xh'}, dimensions={0} | all-to-all | bytes 6291456 | tf_op jit(solution)/shard_map/all_to_all | solution.py:533
  53.3 0.1 slice.8
  53.4 0.1 collective-permute-start.1
  53.5 0.7 collective-permute-start
  54.1 0.7 copy-done
  54.8 1.2 start.1.start_ref
  56.1 0.0 collective-permute-done.1.other_ref
  56.1 3.9 %project.1 = (bf16[16,16,6528]{2,1,0:T(8,128)(2,1)S(1)}, bf16[8,128,512]{2,1,0:T(8,128)(2,1)S(1)}, bf16[8,512,128]{2,1,0:T(8,128)(2,1)S(1)}) custom-call(s32[4]{0:T(128)S(1)} %copy-done.11, bf16[16,32,3072]{2,1,0:T(8,128)(2,1)S(1)} %all_to_all.20.after_ref.got_ref, bf16[16,32,1024]{2,1,0:T(8,128)(2,1)S(1)} %collective-permute-done.1.other_ref, ...), custom_call_target="tpu_custom_call" | custom-call | flops 2000000000 | bytes 9000000 | tf_op jit(solution)/shard_map/project/pallas_call | solution.py:544
  60.0 0.0 collective-permute-done.other_ids_ref
  60.0 2.0 norms.1
  62.0 45.5 %all_to_all.21.parts_ref = bf16[16,16,6528]{2,1,0:T(8,128)(2,1)S(1)} all-to-all(bf16[16,16,6528]{2,1,0:T(8,128)(2,1)S(1)} %norms.1), channel_id=1, replica_groups=mesh['xl'=2,'z'=8,'c'=2,'y'=4,'xh'=2] {'xl','y','xh'}, dimensions={0} | all-to-all | bytes 6684672 | tf_op jit(solution)/shard_map/all_to_all | solution.py:568
  107.5 0.4 sums.1
  107.9 34.0 %all_to_all.22.sums_ref = bf16[16,16,4480]{2,1,0:T(8,128)(2,1)S(1)} all-to-all(bf16[16,16,4480]{2,1,0:T(8,128)(2,1)S(1)} %sums.1), channel_id=1, replica_groups=mesh['xl'=2,'z'=8,'c'=2,'y'=4,'xh'=2] {'xl','y','xh'}, dimensions={0} | all-to-all | bytes 4587520 | tf_op jit(solution)/shard_map/all_to_all | solution.py:577
  141.9 0.1 slice_bitcast_fusion
  142.0 0.3 collective-permute-start.2
  142.3 1.2 gather.1.base_ref
  143.5 1.5 collective-permute-done.2.other_ref
  144.9 5.6 %chain.1 = (bf16[256,2048]{1,0:T(8,128)(2,1)S(1)}, f32[256,128]{1,0:T(8,128)S(1)}) custom-call(s32[4]{0:T(128)S(1)} %copy-done.11, bf16[16,16,6528]{2,1,0:T(8,128)(2,1)S(1)} %all_to_all.21.parts_ref, f32[256,4736]{1,0:T(8,128)S(1)} %gather.1.base_ref, bf16[16,16,4480]{2,1,0:T(8,128)(2,1)S(1)} %all_to_all.22.sums_ref, ...), custom_call_target="tpu_custom_call" | custom-call | tf_op jit(solution)/shard_map/chain/pallas_call | solution.py:590
  150.6 3.7 %grads_other.1 = bf16[8,8,32,256]{3,2,1,0:T(8,128)(2,1)} custom-call(s32[4]{0:T(128)S(1)} %copy-done.11, s32[4,8]{1,0:T(4,128)S(1)} %bitcast.29, s32[4,8]{1,0:T(4,128)S(1)} %collective-permute-done.other_ids_ref, bf16[16,32,3072]{2,1,0:T(8,128)(2,1)S(1)} %all_to_all.20.after_ref.got_ref, bf16[8,128,512]{2,1,0:T(8,128)(2,1)S(1)} %get-tuple-element.11.out_w_ref, ...), custom_call_target="tpu_custom_call" | custom-call | flops 600000000 | bytes 9000000 | tf_op jit(solution)/shard_map/grads_other/pallas_call | solution.py:609
  154.3 0.1 collective-permute-start.3
  154.4 1.2 copy-done.4
  155.6 1.2 copy-done.6
  156.8 1.2 copy-done.8
  158.0 2.8 %grads_own.1.keep_ref = f32[8,8,32,256]{3,2,1,0:T(8,128)S(1)} custom-call(s32[4]{0:T(128)S(1)} %copy-done.11, s32[4,8]{1,0:T(4,128)S(1)} %bitcast.30, s32[4,8]{1,0:T(4,128)S(1)} %collective-permute-done.other_ids_ref, bf16[16,32,3072]{2,1,0:T(8,128)(2,1)S(1)} %all_to_all.20.after_ref.got_ref, bf16[8,128,512]{2,1,0:T(8,128)(2,1)S(1)} %copy-done.4, ...), custom_call_target="tpu_custom_call" | custom-call | flops 600000000 | bytes 9000000 | tf_op jit(solution)/shard_map/grads_own/pallas_call | solution.py:609
  160.8 0.0 collective-permute-done.3.swapped_ref
  160.8 1.5 add.27
  162.3 40.9 %all_to_all.23 = bf16[64,32,256]{2,1,0:T(8,128)(2,1)S(1)} all-to-all(bf16[64,32,256]{2,1,0:T(8,128)(2,1)S(1)} %bitcast.24), channel_id=1, replica_groups=mesh['xl'=2,'z'=8,'c'=2,'y'=4,'xh'=2] {'z','y','xh'}, dimensions={0} | all-to-all | bytes 2097152 | tf_op jit(solution)/shard_map/all_to_all | solution.py:635
  203.2 0.9 final.1
  (19 shorter events, 0.0 us)
Async XLA Ops:
  6.8 46.7 %copy-start.10 = (s32[1,4,8]{2,1,0:T(4,128)S(1)}, s32[1,4,8]{2,1,0:T(4,128)}, u32[]{:S(2)}) copy-start(s32[1,4,8]{2,1,0:T(4,128)} %param.8) | copy-start | bytes 388
  6.8 47.4 %copy-start.1 = (bf16[1,8192,128]{2,1,0:T(8,128)(2,1)S(1)}, bf16[1,8192,128]{2,1,0:T(8,128)(2,1)}, u32[]{:S(2)}) copy-start(bf16[1,8192,128]{2,1,0:T(8,128)(2,1)} %param.12) | copy-start | bytes 6291460
  6.8 47.4 %copy-start.2 = (bf16[4,32,8192]{2,1,0:T(8,128)(2,1)S(1)}, bf16[4,32,8192]{2,1,0:T(8,128)(2,1)}, u32[]{:S(2)}) copy-start(bf16[4,32,8192]{2,1,0:T(8,128)(2,1)} %first_ref.3) | copy-start | bytes 6291460
  6.8 47.4 %copy-start.9 = (f32[1,8192]{1,0:T(1,128)S(1)}, f32[1,8192]{1,0:T(1,128)}, u32[]{:S(2)}) copy-start(f32[1,8192]{1,0:T(1,128)} %gain_ref.1) | copy-start | bytes 98308
  53.3 1.6 copy-start
  53.4 2.8 %collective-permute-start.1 = (bf16[16,32,1024]{2,1,0:T(8,128)(2,1)S(1)}, bf16[16,32,1024]{2,1,0:T(8,128)(2,1)S(1)}, u32[]{:S(2)}, u32[]{:S(2)}) collective-permute-start(bf16[16,32,1024]{2,1,0:T(8,128)(2,1)S(1)} %slice.8), channel_id=1, source_target_pairs={{0,8},{8,0},{1,9},{9,1},{2,10},{10,2},{3,11},{11,3},{4,12},{12,4},... | collective-permute-start | bytes 3145736 | tf_op jit(solution)/shard_map/ppermute | solution.py:534
  53.5 6.5 %collective-permute-start = (s32[4,8]{1,0:T(4,128)S(1)}, s32[4,8]{1,0:T(4,128)S(1)}, u32[]{:S(2)}, u32[]{:S(2)}) collective-permute-start(s32[4,8]{1,0:T(4,128)S(1)} %bitcast.26), channel_id=1, source_target_pairs={{0,128},{128,0},{1,129},{129,1},{2,130},{130,2},{3,131},{131,3},{4... | collective-permute-start | bytes 392 | tf_op jit(solution)/shard_map/ppermute | solution.py:502
  54.8 1.3 copy-start.11
  60.0 90.6 %copy-start.3 = (bf16[8,128,512]{2,1,0:T(8,128)(2,1)}, bf16[8,128,512]{2,1,0:T(8,128)(2,1)S(1)}, u32[]{:S(2)}) copy-start(bf16[8,128,512]{2,1,0:T(8,128)(2,1)S(1)} %get-tuple-element.11.out_w_ref) | copy-start | bytes 3145732
  60.0 90.6 %copy-start.5 = (bf16[8,512,128]{2,1,0:T(8,128)(2,1)}, bf16[8,512,128]{2,1,0:T(8,128)(2,1)S(1)}, u32[]{:S(2)}) copy-start(bf16[8,512,128]{2,1,0:T(8,128)(2,1)S(1)} %get-tuple-element.12.in_w_ref) | copy-start | bytes 3145732
  142.0 2.9 %collective-permute-start.2 = (bf16[128,4096]{1,0:T(8,128)(2,1)S(1)}, bf16[128,4096]{1,0:T(8,128)(2,1)S(1)}, u32[]{:S(2)}, u32[]{:S(2)}) collective-permute-start(bf16[128,4096]{1,0:T(8,128)(2,1)S(1)} %slice_bitcast_fusion), channel_id=1, source_target_pairs={{0,8},{8,0},{1,9},{9,1},{2,10},{10,2},{3,11},{11,3},{4,12},{12,4},... | collective-permute-start | bytes 3145736 | tf_op jit(solution)/shard_map/ppermute | solution.py:579
  150.6 3.7 %copy-start.7 = (bf16[256,2048]{1,0:T(8,128)(2,1)}, bf16[256,2048]{1,0:T(8,128)(2,1)S(1)}, u32[]{:S(2)}) copy-start(bf16[256,2048]{1,0:T(8,128)(2,1)S(1)} %get-tuple-element.14.latent_ref) | copy-start | bytes 3145732
  154.3 6.6 %collective-permute-start.3 = (bf16[8,8,32,256]{3,2,1,0:T(8,128)(2,1)}, bf16[8,8,32,256]{3,2,1,0:T(8,128)(2,1)}, u32[]{:S(2)}, u32[]{:S(2)}) collective-permute-start(bf16[8,8,32,256]{3,2,1,0:T(8,128)(2,1)} %grads_other.1), channel_id=1, source_target_pairs={{0,8},{8,0},{1,9},{9,1},{2,10},{10,2},{3,11},{11,3},{4,12},{12,4},... | collective-permute-start | bytes 3145736 | tf_op jit(solution)/shard_map/ppermute | solution.py:622
  154.4 1.2 copy-start.4
  155.6 1.2 copy-start.6
  156.8 1.2 copy-start.8

commit v8 on v7

--- a/solution.py
+++ b/solution.py
@@ -30,7 +30,7 @@
 WIDE = START + 16 * BLK
 OO = 36
 OI = 28
-LARGE = pltpu.CompilerParams(vmem_limit_bytes=56 * 1024 * 1024)
+LARGE = pltpu.CompilerParams(vmem_limit_bytes=28 * 1024 * 1024)
 PARAMS = pltpu.CompilerParams(vmem_limit_bytes=16 * 1024 * 1024)
 VMEM = pl.BlockSpec(memory_space=pltpu.VMEM)
 SMEM = pl.BlockSpec(memory_space=pltpu.SMEM)

time: 205 us -> 211 us (1.029)
  local copies, waits for them, and re-layouts: 4.62 us -> 12.5 us
    unnamed x24 -> x26, local copies, waits for them, and re-layouts: 4.43 us -> 11.7 us
    pallas_call x1, Pallas kernels: 5.46 us -> 3.06 us  [body(): pl.pallas_call(pack_kernel, grid_spec=pltpu.PrefetchScalarGridSpec(num_sc...]
  transfers between devices with their start and end apart: 4 -> 4, of which waited for: 1 -> 2; matrix products, arithmetic and copies ran while one was open for 0% -> 0% of each run, Pallas kernels for 4% -> 4%
where the time goes in v8:
time: 211 us; the launch traced here: 210 us
  blocking collectives  166 us (79%)
  Pallas kernels  26.6 us (13%)
  local copies, waits for them, and re-layouts  12.5 us (6%)
  waiting for transfers between devices  2.21 us (1%)
    all_to_all x1, blocking collectives, body(): got = lax.all_to_all(send, PLANE, 0, 0, tiled=True)  46 us
    all_to_all x1, blocking collectives, body(): parts = lax.all_to_all(parts, PLANE, 0, 0, tiled=True)  45.5 us
    all_to_all x1, blocking collectives, body(): total = lax.all_to_all(total, ('z',) + SECTION, 0, 0, tiled=True)  40.9 us
    all_to_all x1, blocking collectives, body(): sums = lax.all_to_all(sums, PLANE, 0, 0, tiled=True)  34 us
    unnamed x26, local copies, waits for them, and re-layouts  11.7 us
    pallas_call x2, Pallas kernels, grads(): pl.pallas_call(functools.partial(grads_kernel, own), out_shape=jax.ShapeD...  6.5 us
    pallas_call x1, Pallas kernels, body(): pl.pallas_call(functools.partial(chain_kernel, width), out_shape=(jax.Sha...  6 us
  transfers between devices with their start and end apart: 4, of which 2 were waited for; matrix products, arithmetic and copies ran while one was open for 0% of the time, Pallas kernels for 4%

profile of v8, /device:TPU:32, one launch (start us, length us, event | category | flops | bytes accessed | tf_op | source)
XLA Modules:
  0.0 209.9 jit_solution(5278521122516214364)
XLA Ops:
  0.7 1.6 copy-done
  2.3 1.6 copy-done.1
  3.9 1.6 copy-done.2
  5.5 1.2 copy-done.9
  6.7 1.2 copy-done.10
  7.9 0.8 copy-done.11
  8.7 3.1 %pack.1 = bf16[16,32,3072]{2,1,0:T(8,128)(2,1)S(1)} custom-call(s32[4]{0:T(128)S(1)} %pad_add_fusion.at_ref, bf16[64,8192]{1,0:T(8,128)(2,1)S(1)} %bitcast.25, bf16[64,8192]{1,0:T(8,128)(2,1)S(1)} %bitcast.26, bf16[128,8192]{1,0:T(8,128)(2,1)S(1)} %bitcast.19, bf16[2,8,2,8,32,128]{5,4,3,2,1,0:T(8,128)(2,1)S(1)} %bitcast.21, ...), custom_call_target="tpu_custom_call" | custom-call | tf_op jit(solution)/shard_map/pack/pallas_call | solution.py:503
  11.8 46.0 %all_to_all.20.after_ref.got_ref = bf16[16,32,3072]{2,1,0:T(8,128)(2,1)S(1)} all-to-all(bf16[16,32,3072]{2,1,0:T(8,128)(2,1)S(1)} %pack.1), channel_id=1, replica_groups=mesh['xl'=2,'z'=8,'c'=2,'y'=4,'xh'=2] {'xl','y','xh'}, dimensions={0} | all-to-all | bytes 6291456 | tf_op jit(solution)/shard_map/all_to_all | solution.py:533
  57.9 0.1 collective-permute-start.1
  58.0 0.7 collective-permute-start
  58.6 1.2 start.1.start_ref
  59.9 0.7 collective-permute-done.1.other_ref
  60.6 3.9 %project.1 = (bf16[16,16,6528]{2,1,0:T(8,128)(2,1)S(1)}, bf16[8,128,512]{2,1,0:T(8,128)(2,1)S(1)}, bf16[8,512,128]{2,1,0:T(8,128)(2,1)S(1)}) custom-call(s32[4]{0:T(128)S(1)} %pad_add_fusion.at_ref, bf16[16,32,3072]{2,1,0:T(8,128)(2,1)S(1)} %all_to_all.20.after_ref.got_ref, bf16[16,32,1024]{2,1,0:T(8,128)(2,1)S(1)} %collective-permute-done.1.other_ref, ...), custom_call_target="tpu_custom_call" | custom-call | flops 2000000000 | bytes 9000000 | tf_op jit(solution)/shard_map/project/pallas_call | solution.py:544
  64.6 2.0 norms.1
  66.6 45.5 %all_to_all.21.parts_ref = bf16[16,16,6528]{2,1,0:T(8,128)(2,1)S(1)} all-to-all(bf16[16,16,6528]{2,1,0:T(8,128)(2,1)S(1)} %norms.1), channel_id=1, replica_groups=mesh['xl'=2,'z'=8,'c'=2,'y'=4,'xh'=2] {'xl','y','xh'}, dimensions={0} | all-to-all | bytes 6684672 | tf_op jit(solution)/shard_map/all_to_all | solution.py:568
  112.1 0.4 sums.1
  112.5 34.0 %all_to_all.22.sums_ref = bf16[16,16,4480]{2,1,0:T(8,128)(2,1)S(1)} all-to-all(bf16[16,16,4480]{2,1,0:T(8,128)(2,1)S(1)} %sums.1), channel_id=1, replica_groups=mesh['xl'=2,'z'=8,'c'=2,'y'=4,'xh'=2] {'xl','y','xh'}, dimensions={0} | all-to-all | bytes 4587520 | tf_op jit(solution)/shard_map/all_to_all | solution.py:577
  146.5 0.1 slice_bitcast_fusion
  146.6 0.3 collective-permute-start.2
  146.9 1.2 gather.1.base_ref
  148.1 1.5 collective-permute-done.2.other_ref
  149.6 6.0 %chain.1 = (bf16[256,2048]{1,0:T(8,128)(2,1)S(1)}, f32[256,128]{1,0:T(8,128)S(1)}) custom-call(s32[4]{0:T(128)S(1)} %pad_add_fusion.at_ref, bf16[16,16,6528]{2,1,0:T(8,128)(2,1)S(1)} %all_to_all.21.parts_ref, f32[256,4736]{1,0:T(8,128)S(1)} %gather.1.base_ref, bf16[16,16,4480]{2,1,0:T(8,128)(2,1)S(1)} %all_to_all.22.sums_ref, ...), custom_call_target="tpu_custom_call" | custom-call | tf_op jit(solution)/shard_map/chain/pallas_call | solution.py:590
  155.6 3.8 %grads_other.1 = bf16[8,8,32,256]{3,2,1,0:T(8,128)(2,1)} custom-call(s32[4]{0:T(128)S(1)} %pad_add_fusion.at_ref, s32[4,8]{1,0:T(4,128)S(1)} %bitcast.31, s32[4,8]{1,0:T(4,128)S(1)} %collective-permute-done.other_ids_ref, bf16[16,32,3072]{2,1,0:T(8,128)(2,1)S(1)} %all_to_all.20.after_ref.got_ref, bf16[8,128,512]{2,1,0:T(8,128)(2,1)S(1)} %get-tuple-element.11.out_w_ref, ...), custom_call_target="tpu_custom_call" | custom-call | flops 600000000 | bytes 9000000 | tf_op jit(solution)/shard_map/grads_other/pallas_call | solution.py:609
  159.4 0.1 collective-permute-start.3
  159.5 0.7 constant_dynamic-slice_fusion
  160.2 1.2 copy-done.4
  161.4 1.2 copy-done.6
  162.6 1.2 copy-done.8
  163.9 2.7 %grads_own.1.keep_ref = f32[8,8,32,256]{3,2,1,0:T(8,128)S(1)} custom-call(s32[4]{0:T(128)S(1)} %pad_add_fusion.at_ref, s32[4,8]{1,0:T(4,128)S(1)} %bitcast.32, s32[4,8]{1,0:T(4,128)S(1)} %collective-permute-done.other_ids_ref, bf16[16,32,3072]{2,1,0:T(8,128)(2,1)S(1)} %all_to_all.20.after_ref.got_ref, bf16[8,128,512]{2,1,0:T(8,128)(2,1)S(1)} %copy-done.4, ...), custom_call_target="tpu_custom_call" | custom-call | flops 600000000 | bytes 9000000 | tf_op jit(solution)/shard_map/grads_own/pallas_call | solution.py:609
  166.6 1.4 add.27
  168.1 40.9 %all_to_all.23 = bf16[64,32,256]{2,1,0:T(8,128)(2,1)S(1)} all-to-all(bf16[64,32,256]{2,1,0:T(8,128)(2,1)S(1)} %bitcast.24), channel_id=1, replica_groups=mesh['xl'=2,'z'=8,'c'=2,'y'=4,'xh'=2] {'z','y','xh'}, dimensions={0} | all-to-all | bytes 2097152 | tf_op jit(solution)/shard_map/all_to_all | solution.py:635
  208.9 0.9 final.1
  (21 shorter events, 0.2 us)
Async XLA Ops:
  0.7 1.6 copy-start
  2.3 1.6 copy-start.1
  3.9 1.6 copy-start.2
  5.5 1.2 copy-start.9
  6.7 1.2 copy-start.10
  7.9 0.8 copy-start.11
  11.8 46.2 %copy-start.12 = (s32[1,4,8]{2,1,0:T(4,128)S(1)}, s32[1,4,8]{2,1,0:T(4,128)}, u32[]{:S(2)}) copy-start(s32[1,4,8]{2,1,0:T(4,128)} %param.8) | copy-start | bytes 388
  57.9 2.7 %collective-permute-start.1 = (bf16[16,32,1024]{2,1,0:T(8,128)(2,1)S(1)}, bf16[16,32,1024]{2,1,0:T(8,128)(2,1)S(1)}, u32[]{:S(2)}, u32[]{:S(2)}) collective-permute-start(bf16[16,32,1024]{2,1,0:T(8,128)(2,1)S(1)} %slice.8), channel_id=1, source_target_pairs={{0,8},{8,0},{1,9},{9,1},{2,10},{10,2},{3,11},{11,3},{4,12},{12,4},... | collective-permute-start | bytes 3145736 | tf_op jit(solution)/shard_map/ppermute | solution.py:534
  58.0 6.6 %collective-permute-start = (s32[4,8]{1,0:T(4,128)S(1)}, s32[4,8]{1,0:T(4,128)S(1)}, u32[]{:S(2)}, u32[]{:S(2)}) collective-permute-start(s32[4,8]{1,0:T(4,128)S(1)} %bitcast.28), channel_id=1, source_target_pairs={{0,128},{128,0},{1,129},{129,1},{2,130},{130,2},{3,131},{131,3},{4... | collective-permute-start | bytes 392 | tf_op jit(solution)/shard_map/ppermute | solution.py:502
  64.5 91.1 %copy-start.3 = (bf16[8,128,512]{2,1,0:T(8,128)(2,1)}, bf16[8,128,512]{2,1,0:T(8,128)(2,1)S(1)}, u32[]{:S(2)}) copy-start(bf16[8,128,512]{2,1,0:T(8,128)(2,1)S(1)} %get-tuple-element.11.out_w_ref) | copy-start | bytes 3145732
  64.5 91.1 %copy-start.5 = (bf16[8,512,128]{2,1,0:T(8,128)(2,1)}, bf16[8,512,128]{2,1,0:T(8,128)(2,1)S(1)}, u32[]{:S(2)}) copy-start(bf16[8,512,128]{2,1,0:T(8,128)(2,1)S(1)} %get-tuple-element.12.in_w_ref) | copy-start | bytes 3145732
  146.6 2.9 %collective-permute-start.2 = (bf16[128,4096]{1,0:T(8,128)(2,1)S(1)}, bf16[128,4096]{1,0:T(8,128)(2,1)S(1)}, u32[]{:S(2)}, u32[]{:S(2)}) collective-permute-start(bf16[128,4096]{1,0:T(8,128)(2,1)S(1)} %slice_bitcast_fusion), channel_id=1, source_target_pairs={{0,8},{8,0},{1,9},{9,1},{2,10},{10,2},{3,11},{11,3},{4,12},{12,4},... | collective-permute-start | bytes 3145736 | tf_op jit(solution)/shard_map/ppermute | solution.py:579
  155.6 3.8 %copy-start.7 = (bf16[256,2048]{1,0:T(8,128)(2,1)}, bf16[256,2048]{1,0:T(8,128)(2,1)S(1)}, u32[]{:S(2)}) copy-start(bf16[256,2048]{1,0:T(8,128)(2,1)S(1)} %get-tuple-element.14.latent_ref) | copy-start | bytes 3145732
  159.4 7.2 %collective-permute-start.3 = (bf16[8,8,32,256]{3,2,1,0:T(8,128)(2,1)}, bf16[8,8,32,256]{3,2,1,0:T(8,128)(2,1)}, u32[]{:S(2)}, u32[]{:S(2)}) collective-permute-start(bf16[8,8,32,256]{3,2,1,0:T(8,128)(2,1)} %grads_other.1), channel_id=1, source_target_pairs={{0,8},{8,0},{1,9},{9,1},{2,10},{10,2},{3,11},{11,3},{4,12},{12,4},... | collective-permute-start | bytes 3145736 | tf_op jit(solution)/shard_map/ppermute | solution.py:622
  160.2 1.2 copy-start.4
  161.4 1.2 copy-start.6
  162.6 1.2 copy-start.8

commit v9 on v7

--- a/solution.py
+++ b/solution.py
@@ -174,9 +174,11 @@
 
 
 def project_kernel(
-    at_ref, got_ref, other_ref, start_ref, send_ref, out_w_ref, in_w_ref, wide_ref
+    at_ref, got_ref, other_ref, start_ref, send_ref, out_give_ref, in_give_ref,
+    out_keep_ref, in_keep_ref, wide_ref, out_w_ref, in_w_ref,
 ):
     cols = in_w_ref.shape[1]
+    half = cols // 2
     first_core = at_ref[0] == 0
     for s in range(NS):
         for x in range(2):
@@ -190,6 +192,13 @@
                     row = k * BLK + g * 32
                     lane = cols + g * BLK
                     in_w_ref[s, row : row + 32, :] = part[:, lane : lane + BLK]
+    for out_half_ref, in_half_ref, side in (
+        (out_give_ref, in_give_ref, 1 - at_ref[0]),
+        (out_keep_ref, in_keep_ref, at_ref[0]),
+    ):
+        here = pl.ds(pl.multiple_of(side * half, half), half)
+        out_half_ref[...] = out_w_ref[:, :, here]
+        in_half_ref[...] = in_w_ref[:, here, :]
     for s, running in running_sums(got_ref, cols):
         rounded = running.astype(BF16)
         count = s if s < NS - 1 else NS
@@ -319,7 +328,7 @@
 
 def chain_kernel(
     width, at_ref, parts_ref, base_ref, sums_ref, other_ref,
-    latent_ref, scalar_ref, oo_ref, oi_ref, oo_rows_ref, oi_rows_ref,
+    latent_ref, scalar_ref, again_ref, scalar_again_ref, oo_ref, oi_ref, oo_rows_ref, oi_rows_ref,
 ):
     rows = 2 * R
     first_core = at_ref[0] == 0
@@ -386,6 +395,7 @@
         inner = inner * inverse
         active = (inner * jax.nn.sigmoid(inner)).astype(BF16)
         latent_ref[:, s * R : (s + 1) * R] = active
+        again_ref[:, s * R : (s + 1) * R] = active
         inners.append(inner)
         inverses.append(inverse)
         actives.append(active.astype(F32))
@@ -409,6 +419,7 @@
         sigm = jax.nn.sigmoid(inner)
         d_inner = (grads[s] * sigm * (1.0 + inner * (1.0 - sigm))).astype(BF16)
         latent_ref[:, (NS + s) * R : (NS + s + 1) * R] = d_inner
+        again_ref[:, (NS + s) * R : (NS + s + 1) * R] = d_inner
         inverse = inverses[s]
         total = jnp.sum(d_inner.astype(F32) * inner, -1, keepdims=True)
         scale = inverse * inverse * total * (1.0 / width)
@@ -421,6 +432,7 @@
         scalars = jnp.where(lane == s, inverse, scalars)
         scalars = jnp.where(lane == NS + s, scale, scalars)
     scalar_ref[...] = scalars
+    scalar_again_ref[...] = scalars
 
 
 def grads_kernel(
@@ -442,7 +454,6 @@
         return latent_ref[:, (NS + s) * R : (NS + s + 1) * R]
 
     side = at_ref[0] if own else 1 - at_ref[0]
-    here = pl.ds(pl.multiple_of(side * cols, cols), cols)
     at = pl.multiple_of(side * HALF, HALF)
 
     def put(s, kind, value):
@@ -457,12 +468,12 @@
             entry = entry + jnp.concatenate([step_ref[pl.ds(place, TOK), :] for place in places], 0)
         entry_ref[s] = entry
         put(s, 0, dot_rows((entry * inverses[s]).astype(BF16), d_inner(s)))
-        entry = entry + dot(active(s), out_w_ref[s, :, here])
+        entry = entry + dot(active(s), out_w_ref[s])
     grad = entry
     for s in range(NS - 1, -1, -1):
         put(s, 1, dot_rows(grad.astype(BF16), active(s)))
         if s > 0:
-            back = dot_t(d_inner(s), in_w_ref[s, here, :])
+            back = dot_t(d_inner(s), in_w_ref[s])
             grad = grad + inverses[s] * back - scales[s] * entry_ref[s]
 
 
@@ -541,16 +552,21 @@
         cost_estimate=pl.CostEstimate(flops=600000000, bytes_accessed=7000000, transcendentals=0),
         name="start",
     )(first_input, w_out, w_in, norm_gain, got)
-    parts, out_w, in_w = pl.pallas_call(
+    parts, *weights = pl.pallas_call(
         project_kernel,
-        out_shape=(
-            jax.ShapeDtypeStruct((16, 2 * TOK, WIDE), BF16),
-            jax.ShapeDtypeStruct((NS, R, cols), BF16),
-            jax.ShapeDtypeStruct((NS, cols, R), BF16),
-        ),
+        out_shape=(jax.ShapeDtypeStruct((16, 2 * TOK, WIDE), BF16),)
+        + (
+            jax.ShapeDtypeStruct((NS, R, half), BF16),
+            jax.ShapeDtypeStruct((NS, half, R), BF16),
+        )
+        * 2,
         in_specs=[SMEM, VMEM, VMEM, VMEM],
-        out_specs=(VMEM, VMEM, VMEM),
-        scratch_shapes=[pltpu.VMEM((R, 2 * SPLIT * BLK), F32)],
+        out_specs=(VMEM,) * 5,
+        scratch_shapes=[
+            pltpu.VMEM((R, 2 * SPLIT * BLK), F32),
+            pltpu.VMEM((NS, R, cols), BF16),
+            pltpu.VMEM((NS, cols, R), BF16),
+        ],
         compiler_params=PARAMS,
         cost_estimate=pl.CostEstimate(flops=2000000000, bytes_accessed=9000000, transcendentals=0),
         name="project",
@@ -587,14 +603,15 @@
         cost_estimate=pl.CostEstimate(flops=0, bytes_accessed=7000000, transcendentals=0),
         name="gather",
     )(at, ids, other_ids, sums)
-    latent, scalars = pl.pallas_call(
+    latents = pl.pallas_call(
         functools.partial(chain_kernel, width),
         out_shape=(
             jax.ShapeDtypeStruct((2 * R, 16 * BLK), BF16),
             jax.ShapeDtypeStruct((2 * R, BLK), F32),
-        ),
+        )
+        * 2,
         in_specs=[SMEM, VMEM, VMEM, VMEM, VMEM],
-        out_specs=(VMEM, VMEM),
+        out_specs=(VMEM,) * 4,
         scratch_shapes=[
             pltpu.VMEM((R, OO * BLK), BF16),
             pltpu.VMEM((R, OI * BLK), BF16),
@@ -617,7 +634,7 @@
                 flops=600000000, bytes_accessed=9000000, transcendentals=0
             ),
             name="grads_own" if own else "grads_other",
-        )(at, ids, other_ids, got, out_w, in_w, latent, scalars)
+        )(at, ids, other_ids, got, *weights[2 * own : 2 * own + 2], *latents[2 * own : 2 * own + 2])
 
     swapped = lax.ppermute(grads(False), "c", SWAP)
     keep = grads(True)

time: 205 us -> 204 us (level)
  no operation moved by 1% of the time
where the time goes in v9:
time: 204 us
  blocking collectives  167 us (82%)
  Pallas kernels  28.7 us (14%)
  local copies, waits for them, and re-layouts  4.25 us (2%)
    all_to_all x1, blocking collectives, body(): got = lax.all_to_all(send, PLANE, 0, 0, tiled=True)  46.5 us
    all_to_all x1, blocking collectives, body(): parts = lax.all_to_all(parts, PLANE, 0, 0, tiled=True)  45.4 us
    all_to_all x1, blocking collectives, body(): total = lax.all_to_all(total, ('z',) + SECTION, 0, 0, tiled=True)  40.9 us
    all_to_all x1, blocking collectives, body(): sums = lax.all_to_all(sums, PLANE, 0, 0, tiled=True)  34 us
    pallas_call x2, Pallas kernels, grads(): pl.pallas_call(functools.partial(grads_kernel, own), out_shape=jax.ShapeD...  6.36 us
    pallas_call x1, Pallas kernels, body(): pl.pallas_call(functools.partial(chain_kernel, width), out_shape=(jax.Sha...  5.66 us
    pallas_call x1, Pallas kernels, body(): pl.pallas_call(pack_kernel, grid_spec=pltpu.PrefetchScalarGridSpec(num_sc...  5.46 us
  transfers between devices with their start and end apart: 4, of which 1 were waited for; matrix products, arithmetic and copies ran while one was open for 0% of the time, Pallas kernels for 4%

profile of v9, /device:TPU:32, one launch (start us, length us, event | category | flops | bytes accessed | tf_op | source)
XLA Modules:
  0.0 203.8 jit_solution(18444955509550070670)
XLA Ops:
  0.6 0.7 pad_add_fusion.at_ref
  1.3 5.5 %pack.1 = bf16[16,32,3072]{2,1,0:T(8,128)(2,1)} custom-call(s32[4]{0:T(128)} %pad_add_fusion.at_ref, bf16[64,8192]{1,0:T(8,128)(2,1)} %bitcast.32, bf16[64,8192]{1,0:T(8,128)(2,1)} %bitcast.33, bf16[128,8192]{1,0:T(8,128)(2,1)} %bitcast.19, bf16[2,8,2,8,32,128]{5,4,3,2,1,0:T(8,128)(2,1)} %bitcast.21, f32[2,8,2,2,128]{4,3,2,1,0:T(2,128)} %bitcast.25, ...), custom_call_target="tpu_custom_call" | custom-call | tf_op jit(solution)/shard_map/pack/pallas_call | solution.py:514
  6.8 0.0 copy-start.2
  6.8 0.0 copy-start.9
  6.8 46.5 %all_to_all.20.after_ref.got_ref = bf16[16,32,3072]{2,1,0:T(8,128)(2,1)S(1)} all-to-all(bf16[16,32,3072]{2,1,0:T(8,128)(2,1)} %pack.1), channel_id=1, replica_groups=mesh['xl'=2,'z'=8,'c'=2,'y'=4,'xh'=2] {'xl','y','xh'}, dimensions={0} | all-to-all | bytes 6291456 | tf_op jit(solution)/shard_map/all_to_all | solution.py:544
  53.3 0.1 slice.8
  53.4 0.1 collective-permute-start.1
  53.5 0.7 collective-permute-start
  54.1 0.7 copy-done
  54.8 1.2 start.1.start_ref
  56.1 0.0 collective-permute-done.1.other_ref
  56.1 3.9 %project.1 = (bf16[16,16,6528]{2,1,0:T(8,128)(2,1)S(1)}, bf16[8,128,256]{2,1,0:T(8,128)(2,1)S(1)}, bf16[8,256,128]{2,1,0:T(8,128)(2,1)S(1)}, bf16[8,128,256]{2,1,0:T(8,128)(2,1)S(1)}, bf16[8,256,128]{2,1,0:T(8,128)(2,1)S(1)}) custom-call(s32[4]{0:T(128)S(1)} %copy-done.11, bf16[16,32,3072]{2,1,0:T(8,128)(2,1)S(1)} %all_to_all.20.after_ref.got_ref, ...), custom_call_target="tpu_custom_call" | custom-call | flops 2000000000 | bytes 9000000 | tf_op jit(solution)/shard_map/project/pallas_call | solution.py:555
  60.1 0.0 collective-permute-done.other_ids_ref
  60.1 2.0 norms.1
  62.1 45.4 %all_to_all.21.parts_ref = bf16[16,16,6528]{2,1,0:T(8,128)(2,1)S(1)} all-to-all(bf16[16,16,6528]{2,1,0:T(8,128)(2,1)S(1)} %norms.1), channel_id=1, replica_groups=mesh['xl'=2,'z'=8,'c'=2,'y'=4,'xh'=2] {'xl','y','xh'}, dimensions={0} | all-to-all | bytes 6684672 | tf_op jit(solution)/shard_map/all_to_all | solution.py:584
  107.6 0.4 sums.1
  108.0 34.0 %all_to_all.22.sums_ref = bf16[16,16,4480]{2,1,0:T(8,128)(2,1)S(1)} all-to-all(bf16[16,16,4480]{2,1,0:T(8,128)(2,1)S(1)} %sums.1), channel_id=1, replica_groups=mesh['xl'=2,'z'=8,'c'=2,'y'=4,'xh'=2] {'xl','y','xh'}, dimensions={0} | all-to-all | bytes 4587520 | tf_op jit(solution)/shard_map/all_to_all | solution.py:593
  142.0 0.1 slice_bitcast_fusion
  142.1 0.3 collective-permute-start.2
  142.4 1.2 gather.1.base_ref
  143.6 1.5 collective-permute-done.2.other_ref
  145.0 5.7 %chain.1 = (bf16[256,2048]{1,0:T(8,128)(2,1)S(1)}, f32[256,128]{1,0:T(8,128)S(1)}, bf16[256,2048]{1,0:T(8,128)(2,1)S(1)}, f32[256,128]{1,0:T(8,128)S(1)}) custom-call(s32[4]{0:T(128)S(1)} %copy-done.11, bf16[16,16,6528]{2,1,0:T(8,128)(2,1)S(1)} %all_to_all.21.parts_ref, f32[256,4736]{1,0:T(8,128)S(1)} %gather.1.base_ref, ...), custom_call_target="tpu_custom_call" | custom-call | tf_op jit(solution)/shard_map/chain/pallas_call | solution.py:606
  150.7 3.6 %grads_other.1 = bf16[8,8,32,256]{3,2,1,0:T(8,128)(2,1)} custom-call(s32[4]{0:T(128)S(1)} %copy-done.11, s32[4,8]{1,0:T(4,128)S(1)} %bitcast.29, s32[4,8]{1,0:T(4,128)S(1)} %collective-permute-done.other_ids_ref, bf16[16,32,3072]{2,1,0:T(8,128)(2,1)S(1)} %all_to_all.20.after_ref.got_ref, bf16[8,128,256]{2,1,0:T(8,128)(2,1)S(1)} %get-tuple-element.20.out_w_ref, ...), custom_call_target="tpu_custom_call" | custom-call | flops 600000000 | bytes 9000000 | tf_op jit(solution)/shard_map/grads_other/pallas_call | solution.py:626
  154.3 0.1 collective-permute-start.3
  154.5 1.2 copy-done.4
  155.7 1.0 copy-done.6
  156.7 1.0 copy-done.8
  157.8 2.8 %grads_own.1.keep_ref = f32[8,8,32,256]{3,2,1,0:T(8,128)S(1)} custom-call(s32[4]{0:T(128)S(1)} %copy-done.11, s32[4,8]{1,0:T(4,128)S(1)} %bitcast.30, s32[4,8]{1,0:T(4,128)S(1)} %collective-permute-done.other_ids_ref, bf16[16,32,3072]{2,1,0:T(8,128)(2,1)S(1)} %all_to_all.20.after_ref.got_ref, bf16[8,128,256]{2,1,0:T(8,128)(2,1)S(1)} %copy-done.6, ...), custom_call_target="tpu_custom_call" | custom-call | flops 600000000 | bytes 9000000 | tf_op jit(solution)/shard_map/grads_own/pallas_call | solution.py:626
  160.5 0.0 collective-permute-done.3.swapped_ref
  160.5 1.5 add.27
  162.0 40.9 %all_to_all.23 = bf16[64,32,256]{2,1,0:T(8,128)(2,1)S(1)} all-to-all(bf16[64,32,256]{2,1,0:T(8,128)(2,1)S(1)} %bitcast.24), channel_id=1, replica_groups=mesh['xl'=2,'z'=8,'c'=2,'y'=4,'xh'=2] {'z','y','xh'}, dimensions={0} | all-to-all | bytes 2097152 | tf_op jit(solution)/shard_map/all_to_all | solution.py:652
  202.9 0.9 final.1
  (19 shorter events, 0.0 us)
Async XLA Ops:
  6.8 46.7 %copy-start.10 = (s32[1,4,8]{2,1,0:T(4,128)S(1)}, s32[1,4,8]{2,1,0:T(4,128)}, u32[]{:S(2)}) copy-start(s32[1,4,8]{2,1,0:T(4,128)} %param.8) | copy-start | bytes 388
  6.8 47.4 %copy-start.1 = (bf16[1,8192,128]{2,1,0:T(8,128)(2,1)S(1)}, bf16[1,8192,128]{2,1,0:T(8,128)(2,1)}, u32[]{:S(2)}) copy-start(bf16[1,8192,128]{2,1,0:T(8,128)(2,1)} %param.12) | copy-start | bytes 6291460
  6.8 47.4 %copy-start.2 = (bf16[4,32,8192]{2,1,0:T(8,128)(2,1)S(1)}, bf16[4,32,8192]{2,1,0:T(8,128)(2,1)}, u32[]{:S(2)}) copy-start(bf16[4,32,8192]{2,1,0:T(8,128)(2,1)} %first_ref.3) | copy-start | bytes 6291460
  6.8 47.4 %copy-start.9 = (f32[1,8192]{1,0:T(1,128)S(1)}, f32[1,8192]{1,0:T(1,128)}, u32[]{:S(2)}) copy-start(f32[1,8192]{1,0:T(1,128)} %gain_ref.1) | copy-start | bytes 98308
  53.3 1.6 copy-start
  53.4 2.7 %collective-permute-start.1 = (bf16[16,32,1024]{2,1,0:T(8,128)(2,1)S(1)}, bf16[16,32,1024]{2,1,0:T(8,128)(2,1)S(1)}, u32[]{:S(2)}, u32[]{:S(2)}) collective-permute-start(bf16[16,32,1024]{2,1,0:T(8,128)(2,1)S(1)} %slice.8), channel_id=1, source_target_pairs={{0,8},{8,0},{1,9},{9,1},{2,10},{10,2},{3,11},{11,3},{4,12},{12,4},... | collective-permute-start | bytes 3145736 | tf_op jit(solution)/shard_map/ppermute | solution.py:545
  53.5 6.6 %collective-permute-start = (s32[4,8]{1,0:T(4,128)S(1)}, s32[4,8]{1,0:T(4,128)S(1)}, u32[]{:S(2)}, u32[]{:S(2)}) collective-permute-start(s32[4,8]{1,0:T(4,128)S(1)} %bitcast.26), channel_id=1, source_target_pairs={{0,128},{128,0},{1,129},{129,1},{2,130},{130,2},{3,131},{131,3},{4... | collective-permute-start | bytes 392 | tf_op jit(solution)/shard_map/ppermute | solution.py:513
  54.8 1.3 copy-start.11
  60.1 2.0 copy-start.5
  60.1 2.0 copy-start.7
  142.1 2.9 %collective-permute-start.2 = (bf16[128,4096]{1,0:T(8,128)(2,1)S(1)}, bf16[128,4096]{1,0:T(8,128)(2,1)S(1)}, u32[]{:S(2)}, u32[]{:S(2)}) collective-permute-start(bf16[128,4096]{1,0:T(8,128)(2,1)S(1)} %slice_bitcast_fusion), channel_id=1, source_target_pairs={{0,8},{8,0},{1,9},{9,1},{2,10},{10,2},{3,11},{11,3},{4,12},{12,4},... | collective-permute-start | bytes 3145736 | tf_op jit(solution)/shard_map/ppermute | solution.py:595
  150.7 3.6 %copy-start.3 = (bf16[256,2048]{1,0:T(8,128)(2,1)}, bf16[256,2048]{1,0:T(8,128)(2,1)S(1)}, u32[]{:S(2)}) copy-start(bf16[256,2048]{1,0:T(8,128)(2,1)S(1)} %get-tuple-element.18.latent_ref) | copy-start | bytes 3145732
  154.3 6.2 %collective-permute-start.3 = (bf16[8,8,32,256]{3,2,1,0:T(8,128)(2,1)}, bf16[8,8,32,256]{3,2,1,0:T(8,128)(2,1)}, u32[]{:S(2)}, u32[]{:S(2)}) collective-permute-start(bf16[8,8,32,256]{3,2,1,0:T(8,128)(2,1)} %grads_other.1), channel_id=1, source_target_pairs={{0,8},{8,0},{1,9},{9,1},{2,10},{10,2},{3,11},{11,3},{4,12},{12,4},... | collective-permute-start | bytes 3145736 | tf_op jit(solution)/shard_map/ppermute | solution.py:639
  154.5 1.2 copy-start.4
  155.7 1.0 copy-start.6
  156.7 1.0 copy-start.8

commit v10 on v7

--- a/solution.py
+++ b/solution.py
@@ -318,17 +318,14 @@
 
 
 def chain_kernel(
-    width, at_ref, parts_ref, base_ref, sums_ref, other_ref,
+    width, at_ref, parts_ref, base_ref, gram_ref, other_ref,
     latent_ref, scalar_ref, oo_ref, oi_ref, oo_rows_ref, oi_rows_ref,
 ):
     rows = 2 * R
     first_core = at_ref[0] == 0
     for b in range(0, GRAMS, 4):
-        at = (GRAM - SPLIT + b) * BLK
-        mine = sums_ref[:, :, at : at + 4 * BLK].astype(F32)[:, TOK:]
-        mine = mine.reshape(R, 4 * BLK).astype(BF16)
         at = slice(b * BLK, (b + 4) * BLK)
-        theirs = other_ref[:, at]
+        mine, theirs = gram_ref[:, at], other_ref[:, at]
         oo_ref[:, at] = jnp.where(first_core, mine, theirs)
         second = jnp.where(first_core, theirs, mine)
         if b < OI:
@@ -424,10 +421,12 @@
 
 
 def grads_kernel(
-    own, at_ref, ids_ref, other_ids_ref, got_ref, out_w_ref, in_w_ref, latent_ref, scalar_ref,
-    result_ref, entry_ref, step_ref,
+    at_ref, ids_ref, other_ids_ref, got_ref, out_w_ref, in_w_ref, latent_ref, scalar_ref,
+    give_ref, keep_ref, entry_ref, step_ref,
 ):
     cols = step_ref.shape[1]
+    half = cols // 2
+    first_core = at_ref[0] == 0
     scalars = scalar_ref[...]
     inverses = [scalars[:, s : s + 1] for s in range(NS)]
     scales = [scalars[:, NS + s : NS + s + 1] for s in range(NS)]
@@ -441,28 +440,30 @@
     def d_inner(s):
         return latent_ref[:, (NS + s) * R : (NS + s + 1) * R]
 
-    side = at_ref[0] if own else 1 - at_ref[0]
-    here = pl.ds(pl.multiple_of(side * cols, cols), cols)
-    at = pl.multiple_of(side * HALF, HALF)
-
     def put(s, kind, value):
-        result_ref[:, s, :, kind * R : (kind + 1) * R] = value.reshape(8, 32, R).astype(
-            result_ref.dtype
+        low, high = value[:half].reshape(8, 32, R), value[half:].reshape(8, 32, R)
+        at = slice(kind * R, (kind + 1) * R)
+        give_ref[:, s, :, at] = jnp.where(first_core, high, low).astype(BF16)
+        keep_ref[:, s, :, at] = jnp.where(first_core, low, high)
+
+    def both(part, *args):
+        return jnp.concatenate(
+            [part(got_ref, *args, 0, half), part(got_ref, *args, HALF, half)], 1
         )
 
-    entry = first_rows(got_ref, at, cols)
+    entry = both(first_rows)
     for s in range(NS):
         if s > 0:
-            step_ref[...] = stores(got_ref, s, at, cols)
+            step_ref[...] = both(stores, s)
             entry = entry + jnp.concatenate([step_ref[pl.ds(place, TOK), :] for place in places], 0)
         entry_ref[s] = entry
         put(s, 0, dot_rows((entry * inverses[s]).astype(BF16), d_inner(s)))
-        entry = entry + dot(active(s), out_w_ref[s, :, here])
+        entry = entry + dot(active(s), out_w_ref[s])
     grad = entry
     for s in range(NS - 1, -1, -1):
         put(s, 1, dot_rows(grad.astype(BF16), active(s)))
         if s > 0:
-            back = dot_t(d_inner(s), in_w_ref[s, here, :])
+            back = dot_t(d_inner(s), in_w_ref[s])
             grad = grad + inverses[s] * back - scales[s] * entry_ref[s]
 
 
@@ -576,7 +577,8 @@
     )(parts)
     sums = lax.all_to_all(sums, PLANE, 0, 0, tiled=True)
     gram = sums[:, TOK:, (GRAM - SPLIT) * BLK : (GRAM - SPLIT + GRAMS) * BLK]
-    other = lax.ppermute(gram.reshape(R, GRAMS * BLK), "c", SWAP)
+    gram = gram.reshape(R, GRAMS * BLK)
+    other = lax.ppermute(gram, "c", SWAP)
     base = pl.pallas_call(
         gather_kernel,
         out_shape=jax.ShapeDtypeStruct((2 * R, GRAM * BLK), F32),
@@ -603,24 +605,21 @@
         ],
         compiler_params=PARAMS,
         name="chain",
-    )(at, parts, base, sums, other)
-
-    def grads(own):
-        return pl.pallas_call(
-            functools.partial(grads_kernel, own),
-            out_shape=jax.ShapeDtypeStruct((8, NS, 32, 2 * R), F32 if own else BF16),
-            in_specs=[SMEM, SMEM, SMEM] + [VMEM] * 5,
-            out_specs=VMEM,
-            scratch_shapes=[pltpu.VMEM((NS, 2 * R, half), F32), pltpu.VMEM((R, half), F32)],
-            compiler_params=PARAMS,
-            cost_estimate=pl.CostEstimate(
-                flops=600000000, bytes_accessed=9000000, transcendentals=0
-            ),
-            name="grads_own" if own else "grads_other",
-        )(at, ids, other_ids, got, out_w, in_w, latent, scalars)
-
-    swapped = lax.ppermute(grads(False), "c", SWAP)
-    keep = grads(True)
+    )(at, parts, base, gram, other)
+
+    give, keep = pl.pallas_call(
+        grads_kernel,
+        out_shape=(
+            jax.ShapeDtypeStruct((8, NS, 32, 2 * R), BF16),
+            jax.ShapeDtypeStruct((8, NS, 32, 2 * R), F32),
+        ),
+        in_specs=[SMEM, SMEM, SMEM] + [VMEM] * 5,
+        out_specs=(VMEM, VMEM),
+        scratch_shapes=[pltpu.VMEM((NS, 2 * R, cols), F32), pltpu.VMEM((R, cols), F32)],
+        compiler_params=PARAMS,
+        name="grads",
+    )(at, ids, other_ids, got, out_w, in_w, latent, scalars)
+    swapped = lax.ppermute(give, "c", SWAP)
     total = pl.pallas_call(
         add_kernel,
         out_shape=jax.ShapeDtypeStruct((8, NS, 32, 2 * R), BF16),

time: 205 us -> 201 us (0.980)
  local copies, waits for them, and re-layouts: 4.62 us -> 0.93 us
  waiting for transfers between devices: 1.48 us -> 4.22 us
  Pallas kernels: 28.6 us -> 26.4 us
    unnamed x24 -> x12, local copies, waits for them, and re-layouts: 4.43 us -> 0.74 us
    ppermute x2, waiting for transfers between devices: 1.48 us -> 4.22 us  [the longest x1 2.74 us: body(): swapped = lax.ppermute(give, 'c', SWAP)]
    pallas_call x2 -> x1, Pallas kernels: 6.43 us -> 5.06 us  [body(): pl.pallas_call(grads_kernel, out_shape=(jax.ShapeDtypeStruct((8, NS, 32,...]
  transfers between devices with their start and end apart: 4 -> 4, of which waited for: 1 -> 2; matrix products, arithmetic and copies ran while one was open for 0% -> 0% of each run, Pallas kernels for 4% -> 3%
where the time goes in v10:
time: 201 us
  blocking collectives  167 us (83%)
  Pallas kernels  26.4 us (13%)
  waiting for transfers between devices  4.22 us (2%)
    all_to_all x1, blocking collectives, body(): got = lax.all_to_all(send, PLANE, 0, 0, tiled=True)  46.5 us
    all_to_all x1, blocking collectives, body(): parts = lax.all_to_all(parts, PLANE, 0, 0, tiled=True)  45.5 us
    all_to_all x1, blocking collectives, body(): total = lax.all_to_all(total, ('z',) + SECTION, 0, 0, tiled=True)  40.8 us
    all_to_all x1, blocking collectives, body(): sums = lax.all_to_all(sums, PLANE, 0, 0, tiled=True)  34 us
    pallas_call x1, Pallas kernels, body(): pl.pallas_call(functools.partial(chain_kernel, width), out_shape=(jax.Sha...  6.01 us
    pallas_call x1, Pallas kernels, body(): pl.pallas_call(pack_kernel, grid_spec=pltpu.PrefetchScalarGridSpec(num_sc...  5.47 us
    pallas_call x1, Pallas kernels, body(): pl.pallas_call(grads_kernel, out_shape=(jax.ShapeDtypeStruct((8, NS, 32,...  5.06 us
  transfers between devices with their start and end apart: 4, of which 2 were waited for; matrix products, arithmetic and copies ran while one was open for 0% of the time, Pallas kernels for 3%

profile of v10, /device:TPU:32, one launch (start us, length us, event | category | flops | bytes accessed | tf_op | source)
XLA Modules:
  0.0 200.8 jit_solution(4209822094578459328)
XLA Ops:
  0.6 0.6 pad_add_fusion.at_ref
  1.2 5.5 %pack.1 = bf16[16,32,3072]{2,1,0:T(8,128)(2,1)} custom-call(s32[4]{0:T(128)} %pad_add_fusion.at_ref, bf16[64,8192]{1,0:T(8,128)(2,1)} %bitcast.31, bf16[64,8192]{1,0:T(8,128)(2,1)} %bitcast.32, bf16[128,8192]{1,0:T(8,128)(2,1)} %bitcast.19, bf16[2,8,2,8,32,128]{5,4,3,2,1,0:T(8,128)(2,1)} %bitcast.21, f32[2,8,2,2,128]{4,3,2,1,0:T(2,128)} %bitcast.25, ...), custom_call_target="tpu_custom_call" | custom-call | tf_op jit(solution)/shard_map/pack/pallas_call | solution.py:504
  6.7 0.0 copy-start.2
  6.7 0.0 copy-start.3
  6.7 46.5 %all_to_all.20.after_ref.got_ref = bf16[16,32,3072]{2,1,0:T(8,128)(2,1)S(1)} all-to-all(bf16[16,32,3072]{2,1,0:T(8,128)(2,1)} %pack.1), channel_id=1, replica_groups=mesh['xl'=2,'z'=8,'c'=2,'y'=4,'xh'=2] {'xl','y','xh'}, dimensions={0} | all-to-all | bytes 6291456 | tf_op jit(solution)/shard_map/all_to_all | solution.py:534
  53.2 0.1 slice.8
  53.3 0.1 collective-permute-start.1
  53.4 0.0 copy-done.4
  53.4 0.7 collective-permute-start
  54.1 0.0 copy-done.1
  54.1 0.0 copy-done.2
  54.1 0.0 copy-done.3
  54.1 0.7 copy-done
  54.8 1.2 start.1.start_ref
  56.1 0.0 collective-permute-done.1.other_ref
  56.1 3.9 %project.1 = (bf16[16,16,6528]{2,1,0:T(8,128)(2,1)S(1)}, bf16[8,128,512]{2,1,0:T(8,128)(2,1)S(1)}, bf16[8,512,128]{2,1,0:T(8,128)(2,1)S(1)}) custom-call(s32[4]{0:T(128)S(1)} %copy-done.5, bf16[16,32,3072]{2,1,0:T(8,128)(2,1)S(1)} %all_to_all.20.after_ref.got_ref, bf16[16,32,1024]{2,1,0:T(8,128)(2,1)S(1)} %collective-permute-done.1.other_ref, ...), custom_call_target="tpu_custom_call" | custom-call | flops 2000000000 | bytes 9000000 | tf_op jit(solution)/shard_map/project/pallas_call | solution.py:545
  60.0 0.0 collective-permute-done.other_ids_ref
  60.0 2.0 norms.1
  62.0 45.5 %all_to_all.21.parts_ref = bf16[16,16,6528]{2,1,0:T(8,128)(2,1)S(1)} all-to-all(bf16[16,16,6528]{2,1,0:T(8,128)(2,1)S(1)} %norms.1), channel_id=1, replica_groups=mesh['xl'=2,'z'=8,'c'=2,'y'=4,'xh'=2] {'xl','y','xh'}, dimensions={0} | all-to-all | bytes 6684672 | tf_op jit(solution)/shard_map/all_to_all | solution.py:569
  107.5 0.4 sums.1
  107.9 34.0 %all_to_all.22.sums_ref = bf16[16,16,4480]{2,1,0:T(8,128)(2,1)S(1)} all-to-all(bf16[16,16,4480]{2,1,0:T(8,128)(2,1)S(1)} %sums.1), channel_id=1, replica_groups=mesh['xl'=2,'z'=8,'c'=2,'y'=4,'xh'=2] {'xl','y','xh'}, dimensions={0} | all-to-all | bytes 4587520 | tf_op jit(solution)/shard_map/all_to_all | solution.py:578
  141.9 0.1 slice_bitcast_fusion.gram_ref
  142.0 0.3 collective-permute-start.2
  142.3 1.2 gather.1.base_ref
  143.5 1.5 collective-permute-done.2.other_ref
  144.9 6.0 %chain.1 = (bf16[256,2048]{1,0:T(8,128)(2,1)S(1)}, f32[256,128]{1,0:T(8,128)S(1)}) custom-call(s32[4]{0:T(128)S(1)} %copy-done.5, bf16[16,16,6528]{2,1,0:T(8,128)(2,1)S(1)} %all_to_all.21.parts_ref, f32[256,4736]{1,0:T(8,128)S(1)} %gather.1.base_ref, bf16[128,4096]{1,0:T(8,128)(2,1)S(1)} %slice_bitcast_fusion.gram_ref, ...), custom_call_target="tpu_custom_call" | custom-call | tf_op jit(solution)/shard_map/chain/pallas_call | solution.py:592
  151.0 5.1 %grads.1 = (bf16[8,8,32,256]{3,2,1,0:T(8,128)(2,1)}, f32[8,8,32,256]{3,2,1,0:T(8,128)S(1)}) custom-call(s32[4]{0:T(128)S(1)} %copy-done.5, s32[4,8]{1,0:T(4,128)S(1)} %bitcast.29, s32[4,8]{1,0:T(4,128)S(1)} %collective-permute-done.other_ids_ref, bf16[16,32,3072]{2,1,0:T(8,128)(2,1)S(1)} %all_to_all.20.after_ref.got_ref, ...), custom_call_target="tpu_custom_call" | custom-call | tf_op jit(solution)/shard_map/grads/pallas_call | solution.py:610
  156.0 0.1 collective-permute-start.3
  156.2 2.7 %collective-permute-done.3.swapped_ref = bf16[8,8,32,256]{3,2,1,0:T(8,128)(2,1)S(1)} collective-permute-done((bf16[8,8,32,256]{3,2,1,0:T(8,128)(2,1)}, bf16[8,8,32,256]{3,2,1,0:T(8,128)(2,1)S(1)}, u32[]{:S(2)}, u32[]{:S(2)}) %collective-permute-start.3) | collective-permute-done | bytes 1048608 | tf_op jit(solution)/shard_map/ppermute | solution.py:622
  158.9 0.2 add.27
  159.1 40.8 %all_to_all.23 = bf16[64,32,256]{2,1,0:T(8,128)(2,1)S(1)} all-to-all(bf16[64,32,256]{2,1,0:T(8,128)(2,1)S(1)} %bitcast.24), channel_id=1, replica_groups=mesh['xl'=2,'z'=8,'c'=2,'y'=4,'xh'=2] {'z','y','xh'}, dimensions={0} | all-to-all | bytes 2097152 | tf_op jit(solution)/shard_map/all_to_all | solution.py:634
  199.9 0.9 final.1
  (6 shorter events, 0.0 us)
Async XLA Ops:
  6.7 46.7 %copy-start.4 = (s32[1,4,8]{2,1,0:T(4,128)S(1)}, s32[1,4,8]{2,1,0:T(4,128)}, u32[]{:S(2)}) copy-start(s32[1,4,8]{2,1,0:T(4,128)} %param.8) | copy-start | bytes 388
  6.7 47.4 %copy-start.1 = (bf16[1,8192,128]{2,1,0:T(8,128)(2,1)S(1)}, bf16[1,8192,128]{2,1,0:T(8,128)(2,1)}, u32[]{:S(2)}) copy-start(bf16[1,8192,128]{2,1,0:T(8,128)(2,1)} %param.12) | copy-start | bytes 6291460
  6.7 47.4 %copy-start.2 = (bf16[4,32,8192]{2,1,0:T(8,128)(2,1)S(1)}, bf16[4,32,8192]{2,1,0:T(8,128)(2,1)}, u32[]{:S(2)}) copy-start(bf16[4,32,8192]{2,1,0:T(8,128)(2,1)} %first_ref.3) | copy-start | bytes 6291460
  6.7 47.4 %copy-start.3 = (f32[1,8192]{1,0:T(1,128)S(1)}, f32[1,8192]{1,0:T(1,128)}, u32[]{:S(2)}) copy-start(f32[1,8192]{1,0:T(1,128)} %gain_ref.1) | copy-start | bytes 98308
  53.2 1.6 copy-start
  53.3 2.8 %collective-permute-start.1 = (bf16[16,32,1024]{2,1,0:T(8,128)(2,1)S(1)}, bf16[16,32,1024]{2,1,0:T(8,128)(2,1)S(1)}, u32[]{:S(2)}, u32[]{:S(2)}) collective-permute-start(bf16[16,32,1024]{2,1,0:T(8,128)(2,1)S(1)} %slice.8), channel_id=1, source_target_pairs={{0,8},{8,0},{1,9},{9,1},{2,10},{10,2},{3,11},{11,3},{4,12},{12,4},... | collective-permute-start | bytes 3145736 | tf_op jit(solution)/shard_map/ppermute | solution.py:535
  53.4 6.6 %collective-permute-start = (s32[4,8]{1,0:T(4,128)S(1)}, s32[4,8]{1,0:T(4,128)S(1)}, u32[]{:S(2)}, u32[]{:S(2)}) collective-permute-start(s32[4,8]{1,0:T(4,128)S(1)} %bitcast.26), channel_id=1, source_target_pairs={{0,128},{128,0},{1,129},{129,1},{2,130},{130,2},{3,131},{131,3},{4... | collective-permute-start | bytes 392 | tf_op jit(solution)/shard_map/ppermute | solution.py:503
  54.8 1.3 copy-start.5
  142.0 2.9 %collective-permute-start.2 = (bf16[128,4096]{1,0:T(8,128)(2,1)S(1)}, bf16[128,4096]{1,0:T(8,128)(2,1)S(1)}, u32[]{:S(2)}, u32[]{:S(2)}) collective-permute-start(bf16[128,4096]{1,0:T(8,128)(2,1)S(1)} %slice_bitcast_fusion.gram_ref), channel_id=1, source_target_pairs={{0,8},{8,0},{1,9},{9,1},{2,10},{10,2},{3,11},{11,3},{4,12},{12,4},... | collective-permute-start | bytes 3145736 | tf_op jit(solution)/shard_map/ppermute | solution.py:581
  156.0 2.9 %collective-permute-start.3 = (bf16[8,8,32,256]{3,2,1,0:T(8,128)(2,1)}, bf16[8,8,32,256]{3,2,1,0:T(8,128)(2,1)S(1)}, u32[]{:S(2)}, u32[]{:S(2)}) collective-permute-start(bf16[8,8,32,256]{3,2,1,0:T(8,128)(2,1)} %get-tuple-element.19), channel_id=1, source_target_pairs={{0,8},{8,0},{1,9},{9,1},{2,10},{10,2},{3,11},{11,3},{4,12},{12,4},... | collective-permute-start | bytes 3145736 | tf_op jit(solution)/shard_map/ppermute | solution.py:622

commit v11 on v10

--- a/solution.py
+++ b/solution.py
@@ -69,13 +69,16 @@
     return high, (x - high.astype(F32)).astype(BF16)
 
 
-def pack_kernel(
-    at_ref, in_ref, out_ref, w_out_ref, w_in_ref, gain_ref, first_ref,
-    send_ref, turn_ref,
-):
-    section = at_ref[1]
-
-    @pl.when(pl.program_id(0) == 0)
+def section_here():
+    return lax.axis_index("y") * 2 + lax.axis_index("xh")
+
+
+def pack_kernel(in_ref, out_ref, w_out_ref, w_in_ref, gain_ref, first_ref, send_ref, turn_ref):
+    section = section_here()
+    quarter = lax.axis_index("xl") * 2 + lax.axis_index("c")
+    zq = pl.program_id(1)
+
+    @pl.when((pl.program_id(0) == 0) & (zq == 0))
     def _():
         shape = (4 * BLK, 4 * BLK)
         row = lax.broadcasted_iota(jnp.int32, shape, 0)
@@ -84,43 +87,45 @@
         same = same & (row % 32 == col % 32)
         turn_ref[...] = jnp.where(same, 1.0, 0.0).astype(BF16)
 
-    gain = gain_ref[...].reshape(8, BLK).T
-    for s in range(NS):
-        for j in range(4):
-            column = 2 * j + s // 4
-            scale = gain[(s % 4) * 32 : (s % 4) * 32 + 32, column : column + 1]
-            to = W_LANE + 512 + j * BLK
-            send_ref[s, :, to : to + BLK] = (w_in_ref[0, j, 0, s].astype(F32) * scale).astype(BF16)
+    @pl.when(zq == 0)
+    def _():
+        near = quarter % 2 * 4
+        gain = gain_ref[0, pl.ds(near, 4), quarter // 2].reshape(8, BLK).T
+        for s in range(NS):
+            for j in range(4):
+                column = 2 * j + s // 4
+                scale = gain[(s % 4) * 32 : (s % 4) * 32 + 32, column : column + 1]
+                to = W_LANE + 512 + j * BLK
+                rows = w_in_ref[0, near + j, quarter // 2, s].astype(F32)
+                send_ref[s, :, to : to + BLK] = (rows * scale).astype(BF16)
 
     pieces, places = [], []
+    micro = section // (NS - 1) * 2
+    rank = pl.multiple_of(quarter * 32, 32)
     for c in range(2):
-        for zq in range(2):
-            to = c * 256 + zq * BLK
-            for h in range(2):
-                lanes = [((4 * zq + j) * 4 + c * 2 + h) * BLK for j in range(4)]
-                for ref, row, at, other in (
-                    (in_ref, 0, c * HALF + zq * BLK, 0),
-                    (in_ref, 32, c * HALF + 256 + zq * BLK, 0),
-                    (out_ref, 0, c * HALF + 512 + zq * BLK, NS - 1),
-                    (out_ref, 32, c * HALF + 768 + zq * BLK, NS - 1),
-                    (w_out_ref, 0, W_LANE + to, None),
-                ):
-                    piece = jnp.concatenate(
-                        [ref[row : row + 32, lane : lane + BLK] for lane in lanes], 1
-                    )
-                    if other is not None:
-                        first = jnp.concatenate(
-                            [first_ref[row // 32, :, lane : lane + BLK] for lane in lanes], 1
-                        )
-                        piece = jnp.where(section == other, first, piece)
-                    pieces.append(piece)
-                    places.append((4 * h, at))
+        for h in range(2):
+            lanes = [(j * 4 + c * 2 + h) * BLK for j in range(4)]
+
+            def piece_of(ref, *at, lanes=lanes):
+                return jnp.concatenate([ref[*at, lane : lane + BLK] for lane in lanes], 1)
+
+            for ref, half, at, other in (
+                (in_ref, 0, c * HALF, 0),
+                (in_ref, 1, c * HALF + 256, 0),
+                (out_ref, 0, c * HALF + 512, NS - 1),
+                (out_ref, 1, c * HALF + 768, NS - 1),
+            ):
+                piece = piece_of(ref, slice(half * 32, half * 32 + 32))
+                first = piece_of(first_ref, micro + half, slice(None))
+                pieces.append(jnp.where(section == other, first, piece))
+                places.append((4 * h, at))
+            pieces.append(piece_of(w_out_ref, pl.ds(rank, 32)))
+            places.append((4 * h, W_LANE + c * 256))
     turned = dot(jnp.concatenate(pieces, 0), turn_ref[...]).astype(BF16)
     for n, (first, at) in enumerate(places):
+        to = pl.ds(pl.multiple_of(at + zq * BLK, BLK), BLK)
         for i in range(4):
-            send_ref[first + i, :, at : at + BLK] = turned[
-                32 * n : 32 * n + 32, i * BLK : (i + 1) * BLK
-            ]
+            send_ref[first + i, :, to] = turned[32 * n : 32 * n + 32, i * BLK : (i + 1) * BLK]
 
 
 def start_kernel(first_ref, w_out_ref, w_in_ref, gain_ref, after_ref, start_ref):
@@ -153,10 +158,10 @@
     return jnp.concatenate(pieces, 0).astype(F32)
 
 
-def picks_of(at_ref, ids_ref, other_ids_ref):
+def picks_of(ids_ref, other_ids_ref):
     picks = []
     for x in range(2):
-        here = at_ref[2] == x
+        here = lax.axis_index("xl") == x
         for m in range(MIC):
             for j in range(4):
                 picks.append(x * NS + jnp.where(here, ids_ref[m, j], other_ids_ref[m, j]))
@@ -174,10 +179,10 @@
 
 
 def project_kernel(
-    at_ref, got_ref, other_ref, start_ref, send_ref, out_w_ref, in_w_ref, wide_ref
+    got_ref, other_ref, start_ref, send_ref, out_w_ref, in_w_ref, wide_ref
 ):
     cols = in_w_ref.shape[1]
-    first_core = at_ref[0] == 0
+    first_core = lax.axis_index("c") == 0
     for s in range(NS):
         for x in range(2):
             mine = got_ref[x * NS + s, :, W_LANE:SENT]
@@ -239,10 +244,10 @@
 
 
 def norm_kernel(
-    cols, at_ref, ids_ref, other_ids_ref, got_ref, before_ref, send_ref, block_ref, sem
+    cols, ids_ref, other_ids_ref, got_ref, before_ref, send_ref, block_ref, sem
 ):
     del before_ref
-    picks = picks_of(at_ref, ids_ref, other_ids_ref)
+    picks = picks_of(ids_ref, other_ids_ref)
     placed = [[] for _ in range(MIC)]
     first = jnp.concatenate(
         [first_rows(got_ref, 0, cols // 2), first_rows(got_ref, HALF, cols // 2)], 1
@@ -297,7 +302,7 @@
             send_ref[q, :, at] = total
 
 
-def gather_kernel(at_ref, ids_ref, other_ids_ref, sums_ref, base_ref, proj_ref):
+def gather_kernel(ids_ref, other_ids_ref, sums_ref, base_ref, proj_ref):
     for b in range(GRAM):
         upper = b >= SPLIT
         at = (b - SPLIT * upper) * BLK
@@ -305,7 +310,7 @@
         proj_ref[:, b * BLK : (b + 1) * BLK] = block[:, TOK * upper : TOK * upper + TOK].reshape(
             R, BLK
         )
-    for n, pick in enumerate(picks_of(at_ref, ids_ref, other_ids_ref)):
+    for n, pick in enumerate(picks_of(ids_ref, other_ids_ref)):
         rows = slice(n * TOK, (n + 1) * TOK)
         here = pl.ds(pl.multiple_of(pick * TOK, TOK), TOK)
         base_ref[rows, :] = proj_ref[here, :]
@@ -318,11 +323,11 @@
 
 
 def chain_kernel(
-    width, at_ref, parts_ref, base_ref, gram_ref, other_ref,
+    width, parts_ref, base_ref, gram_ref, other_ref,
     latent_ref, scalar_ref, oo_ref, oi_ref, oo_rows_ref, oi_rows_ref,
 ):
     rows = 2 * R
-    first_core = at_ref[0] == 0
+    first_core = lax.axis_index("c") == 0
     for b in range(0, GRAMS, 4):
         at = slice(b * BLK, (b + 4) * BLK)
         mine, theirs = gram_ref[:, at], other_ref[:, at]
@@ -421,17 +426,17 @@
 
 
 def grads_kernel(
-    at_ref, ids_ref, other_ids_ref, got_ref, out_w_ref, in_w_ref, latent_ref, scalar_ref,
+    ids_ref, other_ids_ref, got_ref, out_w_ref, in_w_ref, latent_ref, scalar_ref,
     give_ref, keep_ref, entry_ref, step_ref,
 ):
     cols = step_ref.shape[1]
     half = cols // 2
-    first_core = at_ref[0] == 0
+    first_core = lax.axis_index("c") == 0
     scalars = scalar_ref[...]
     inverses = [scalars[:, s : s + 1] for s in range(NS)]
     scales = [scalars[:, NS + s : NS + s + 1] for s in range(NS)]
     places = [
-        pl.multiple_of(pick * TOK, TOK) for pick in picks_of(at_ref, ids_ref, other_ids_ref)
+        pl.multiple_of(pick * TOK, TOK) for pick in picks_of(ids_ref, other_ids_ref)
     ]
 
     def active(s):
@@ -489,41 +494,32 @@
     width = first_input.shape[2]
     cols = width // 16
     half = cols // 2
-    wide = width // 2
     core = lax.axis_index("c")
     xl = lax.axis_index("xl")
     z = lax.axis_index("z")
-    section = lax.axis_index(SECTION)
-    quarter = xl * 2 + core
-    at = jnp.stack([core, section, xl, quarter]).astype(jnp.int32)
     w_in = adapter_in[0]
     w_out = adapter_out[0]
 
     ids = example_ids[0]
     other_ids = lax.ppermute(ids, "xl", SWAP)
+    quarter = width // 4
     send = pl.pallas_call(
         pack_kernel,
-        grid_spec=pltpu.PrefetchScalarGridSpec(
-            num_scalar_prefetch=1,
-            grid=(2,),
-            in_specs=[
-                pl.BlockSpec((64, wide), lambda i, at: (0, i)),
-                pl.BlockSpec((64, wide), lambda i, at: (0, i)),
-                pl.BlockSpec((32, wide), lambda i, at: (at[3], i)),
-                pl.BlockSpec(
-                    (1, 4, 1, 8, 32, R), lambda i, at: (i, at[3] % 2, at[3] // 2, 0, 0, 0)
-                ),
-                pl.BlockSpec((1, 4, 1, 2, BLK), lambda i, at: (i, at[3] % 2, at[3] // 2, 0, 0)),
-                pl.BlockSpec((2, 32, wide), lambda i, at: (at[1] // (NS - 1), 0, i)),
-            ],
-            out_specs=pl.BlockSpec((8, 32, SENT), lambda i, at: (i, 0, 0)),
-            scratch_shapes=[pltpu.VMEM((4 * BLK, 4 * BLK), BF16)],
-        ),
+        grid=(2, 2),
+        in_specs=[
+            pl.BlockSpec((64, quarter), lambda i, j: (0, 2 * i + j)),
+            pl.BlockSpec((64, quarter), lambda i, j: (0, 2 * i + j)),
+            pl.BlockSpec((R, quarter), lambda i, j: (0, 2 * i + j)),
+            pl.BlockSpec((1, 8, 2, 8, 32, R), lambda i, j: (i, 0, 0, 0, 0, 0)),
+            pl.BlockSpec((1, 8, 2, 2, BLK), lambda i, j: (i, 0, 0, 0, 0)),
+            pl.BlockSpec((MIC, 32, quarter), lambda i, j: (0, 0, 2 * i + j)),
+        ],
+        out_specs=pl.BlockSpec((8, 32, SENT), lambda i, j: (i, 0, 0)),
+        scratch_shapes=[pltpu.VMEM((4 * BLK, 4 * BLK), BF16)],
         out_shape=jax.ShapeDtypeStruct((16, 32, SENT), BF16),
         compiler_params=LARGE,
         name="pack",
     )(
-        at,
         in_store.reshape(64, width),
         out_store.reshape(64, width),
         w_out,
@@ -549,23 +545,23 @@
             jax.ShapeDtypeStruct((NS, R, cols), BF16),
             jax.ShapeDtypeStruct((NS, cols, R), BF16),
         ),
-        in_specs=[SMEM, VMEM, VMEM, VMEM],
+        in_specs=[VMEM, VMEM, VMEM],
         out_specs=(VMEM, VMEM, VMEM),
         scratch_shapes=[pltpu.VMEM((R, 2 * SPLIT * BLK), F32)],
         compiler_params=PARAMS,
         cost_estimate=pl.CostEstimate(flops=2000000000, bytes_accessed=9000000, transcendentals=0),
         name="project",
-    )(at, got, other, start)
+    )(got, other, start)
     parts = pl.pallas_call(
         functools.partial(norm_kernel, cols),
         out_shape=jax.ShapeDtypeStruct((16, 2 * TOK, WIDE), BF16),
-        in_specs=[SMEM, SMEM, SMEM, VMEM, pl.BlockSpec(memory_space=pl.ANY)],
+        in_specs=[SMEM, SMEM, VMEM, pl.BlockSpec(memory_space=pl.ANY)],
         out_specs=pl.BlockSpec(memory_space=pl.ANY),
         scratch_shapes=[pltpu.VMEM((16, 2 * TOK, BLK), BF16), pltpu.SemaphoreType.DMA],
-        input_output_aliases={4: 0},
+        input_output_aliases={3: 0},
         compiler_params=PARAMS,
         name="norms",
-    )(at, ids, other_ids, got, parts)
+    )(ids, other_ids, got, parts)
     parts = lax.all_to_all(parts, PLANE, 0, 0, tiled=True)
     sums = pl.pallas_call(
         sum_kernel,
@@ -582,20 +578,20 @@
     base = pl.pallas_call(
         gather_kernel,
         out_shape=jax.ShapeDtypeStruct((2 * R, GRAM * BLK), F32),
-        in_specs=[SMEM, SMEM, SMEM, VMEM],
+        in_specs=[SMEM, SMEM, VMEM],
         out_specs=VMEM,
         scratch_shapes=[pltpu.VMEM((R, GRAM * BLK), F32)],
         compiler_params=PARAMS,
         cost_estimate=pl.CostEstimate(flops=0, bytes_accessed=7000000, transcendentals=0),
         name="gather",
-    )(at, ids, other_ids, sums)
+    )(ids, other_ids, sums)
     latent, scalars = pl.pallas_call(
         functools.partial(chain_kernel, width),
         out_shape=(
             jax.ShapeDtypeStruct((2 * R, 16 * BLK), BF16),
             jax.ShapeDtypeStruct((2 * R, BLK), F32),
         ),
-        in_specs=[SMEM, VMEM, VMEM, VMEM, VMEM],
+        in_specs=[VMEM] * 4,
         out_specs=(VMEM, VMEM),
         scratch_shapes=[
             pltpu.VMEM((R, OO * BLK), BF16),
@@ -605,7 +601,7 @@
         ],
         compiler_params=PARAMS,
         name="chain",
-    )(at, parts, base, gram, other)
+    )(parts, base, gram, other)
 
     give, keep = pl.pallas_call(
         grads_kernel,
@@ -613,12 +609,12 @@
             jax.ShapeDtypeStruct((8, NS, 32, 2 * R), BF16),
             jax.ShapeDtypeStruct((8, NS, 32, 2 * R), F32),
         ),
-        in_specs=[SMEM, SMEM, SMEM] + [VMEM] * 5,
+        in_specs=[SMEM, SMEM] + [VMEM] * 5,
         out_specs=(VMEM, VMEM),
         scratch_shapes=[pltpu.VMEM((NS, 2 * R, cols), F32), pltpu.VMEM((R, cols), F32)],
         compiler_params=PARAMS,
         name="grads",
-    )(at, ids, other_ids, got, out_w, in_w, latent, scalars)
+    )(ids, other_ids, got, out_w, in_w, latent, scalars)
     swapped = lax.ppermute(give, "c", SWAP)
     total = pl.pallas_call(
         add_kernel,

time: 201 us -> 201 us (level)
    pallas_call x1, Pallas kernels: 5.47 us -> 7.63 us  [body(): pl.pallas_call(pack_kernel, grid=(2, 2), in_specs=[pl.BlockSpec((64, quar...]
where the time goes in v11:
time: 201 us
  blocking collectives  167 us (83%)
  Pallas kernels  27.3 us (14%)
  waiting for transfers between devices  4.22 us (2%)
    all_to_all x1, blocking collectives, body(): got = lax.all_to_all(send, PLANE, 0, 0, tiled=True)  46.5 us
    all_to_all x1, blocking collectives, body(): parts = lax.all_to_all(parts, PLANE, 0, 0, tiled=True)  45.5 us
    all_to_all x1, blocking collectives, body(): total = lax.all_to_all(total, ('z',) + SECTION, 0, 0, tiled=True)  40.8 us
    all_to_all x1, blocking collectives, body(): sums = lax.all_to_all(sums, PLANE, 0, 0, tiled=True)  34 us
    pallas_call x1, Pallas kernels, body(): pl.pallas_call(pack_kernel, grid=(2, 2), in_specs=[pl.BlockSpec((64, quar...  7.63 us
    pallas_call x1, Pallas kernels, body(): pl.pallas_call(functools.partial(chain_kernel, width), out_shape=(jax.Sha...  5.46 us
    pallas_call x1, Pallas kernels, body(): pl.pallas_call(grads_kernel, out_shape=(jax.ShapeDtypeStruct((8, NS, 32,...  4.99 us
  transfers between devices with their start and end apart: 4, of which 2 were waited for; matrix products, arithmetic and copies ran while one was open for 0% of the time, Pallas kernels for 3%

profile of v11, /device:TPU:32, one launch (start us, length us, event | category | flops | bytes accessed | tf_op | source)
XLA Modules:
  0.0 201.1 jit_solution(16207509104486650918)
XLA Ops:
  0.6 7.6 %pack.1 = bf16[16,32,3072]{2,1,0:T(8,128)(2,1)} custom-call(bf16[64,8192]{1,0:T(8,128)(2,1)} %bitcast.27, bf16[64,8192]{1,0:T(8,128)(2,1)} %bitcast.28, bf16[128,8192]{1,0:T(8,128)(2,1)} %bitcast.15, bf16[2,8,2,8,32,128]{5,4,3,2,1,0:T(8,128)(2,1)} %bitcast.17, f32[2,8,2,2,128]{4,3,2,1,0:T(2,128)} %bitcast.21, bf16[4,32,8192]{2,1,0:T(8,128)(2,1)} %first_ref.3), custom_call_target="tpu_custom_call" | custom-call | tf_op jit(solution)/shard_map/pack/pallas_call | solution.py:506
  8.3 0.0 copy-start.4
  8.3 0.0 copy-start.2
  8.3 0.0 copy-start.3
  8.3 46.5 %all_to_all.20.after_ref.got_ref = bf16[16,32,3072]{2,1,0:T(8,128)(2,1)S(1)} all-to-all(bf16[16,32,3072]{2,1,0:T(8,128)(2,1)} %pack.1), channel_id=1, replica_groups=mesh['xl'=2,'z'=8,'c'=2,'y'=4,'xh'=2] {'xl','y','xh'}, dimensions={0} | all-to-all | bytes 6291456 | tf_op jit(solution)/shard_map/all_to_all | solution.py:530
  54.8 0.1 slice.8
  54.8 0.1 collective-permute-start.1
  54.9 0.0 copy-done.4
  55.0 0.7 collective-permute-start
  55.6 0.0 copy-done.1
  55.6 0.0 copy-done.2
  55.6 0.0 copy-done.3
  55.6 0.7 copy-done
  56.4 1.2 start.1.start_ref
  57.6 0.0 collective-permute-done.1.other_ref
  57.6 3.3 %project.1 = (bf16[16,16,6528]{2,1,0:T(8,128)(2,1)S(1)}, bf16[8,128,512]{2,1,0:T(8,128)(2,1)S(1)}, bf16[8,512,128]{2,1,0:T(8,128)(2,1)S(1)}) custom-call(bf16[16,32,3072]{2,1,0:T(8,128)(2,1)S(1)} %all_to_all.20.after_ref.got_ref, bf16[16,32,1024]{2,1,0:T(8,128)(2,1)S(1)} %collective-permute-done.1.other_ref, bf16[128,256]{1,0:T(8,128)(2,1)S(1)} %start.1.start_ref), custom_call_target="tpu_custom_call" | custom-call | flops 2000000000 | bytes 9000000 | tf_op jit(solution)/shard_map/project/pallas_call | solution.py:541
  61.0 0.0 collective-permute-done.other_ids_ref
  61.0 2.0 norms.1
  63.0 45.5 %all_to_all.21.parts_ref = bf16[16,16,6528]{2,1,0:T(8,128)(2,1)S(1)} all-to-all(bf16[16,16,6528]{2,1,0:T(8,128)(2,1)S(1)} %norms.1), channel_id=1, replica_groups=mesh['xl'=2,'z'=8,'c'=2,'y'=4,'xh'=2] {'xl','y','xh'}, dimensions={0} | all-to-all | bytes 6684672 | tf_op jit(solution)/shard_map/all_to_all | solution.py:565
  108.5 0.4 sums.1
  108.9 34.0 %all_to_all.22.sums_ref = bf16[16,16,4480]{2,1,0:T(8,128)(2,1)S(1)} all-to-all(bf16[16,16,4480]{2,1,0:T(8,128)(2,1)S(1)} %sums.1), channel_id=1, replica_groups=mesh['xl'=2,'z'=8,'c'=2,'y'=4,'xh'=2] {'xl','y','xh'}, dimensions={0} | all-to-all | bytes 4587520 | tf_op jit(solution)/shard_map/all_to_all | solution.py:574
  142.9 0.1 slice_bitcast_fusion.gram_ref
  143.0 0.3 collective-permute-start.2
  143.3 1.2 gather.1.base_ref
  144.4 1.5 collective-permute-done.2.other_ref
  145.9 5.5 %chain.1 = (bf16[256,2048]{1,0:T(8,128)(2,1)S(1)}, f32[256,128]{1,0:T(8,128)S(1)}) custom-call(bf16[16,16,6528]{2,1,0:T(8,128)(2,1)S(1)} %all_to_all.21.parts_ref, f32[256,4736]{1,0:T(8,128)S(1)} %gather.1.base_ref, bf16[128,4096]{1,0:T(8,128)(2,1)S(1)} %slice_bitcast_fusion.gram_ref, bf16[128,4096]{1,0:T(8,128)(2,1)S(1)} %collective-permute-done.2.other_ref), custom_call_target="tpu_custom_call" | custom-call | tf_op jit(solution)/shard_map/chain/pallas_call | solution.py:588
  151.4 5.0 %grads.1 = (bf16[8,8,32,256]{3,2,1,0:T(8,128)(2,1)}, f32[8,8,32,256]{3,2,1,0:T(8,128)S(1)}) custom-call(s32[4,8]{1,0:T(4,128)S(1)} %bitcast.25, s32[4,8]{1,0:T(4,128)S(1)} %collective-permute-done.other_ids_ref, bf16[16,32,3072]{2,1,0:T(8,128)(2,1)S(1)} %all_to_all.20.after_ref.got_ref, bf16[8,128,512]{2,1,0:T(8,128)(2,1)S(1)} %get-tuple-element.13.out_w_ref, ...), custom_call_target="tpu_custom_call" | custom-call | tf_op jit(solution)/shard_map/grads/pallas_call | solution.py:606
  156.4 0.1 collective-permute-start.3
  156.5 2.7 %collective-permute-done.3.swapped_ref = bf16[8,8,32,256]{3,2,1,0:T(8,128)(2,1)S(1)} collective-permute-done((bf16[8,8,32,256]{3,2,1,0:T(8,128)(2,1)}, bf16[8,8,32,256]{3,2,1,0:T(8,128)(2,1)S(1)}, u32[]{:S(2)}, u32[]{:S(2)}) %collective-permute-start.3) | collective-permute-done | bytes 1048608 | tf_op jit(solution)/shard_map/ppermute | solution.py:618
  159.2 0.2 add.13
  159.4 40.8 %all_to_all.23 = bf16[64,32,256]{2,1,0:T(8,128)(2,1)S(1)} all-to-all(bf16[64,32,256]{2,1,0:T(8,128)(2,1)S(1)} %bitcast.20), channel_id=1, replica_groups=mesh['xl'=2,'z'=8,'c'=2,'y'=4,'xh'=2] {'z','y','xh'}, dimensions={0} | all-to-all | bytes 2097152 | tf_op jit(solution)/shard_map/all_to_all | solution.py:630
  200.2 0.9 final.1
  (3 shorter events, 0.0 us)
Async XLA Ops:
  8.3 46.7 %copy-start.4 = (s32[1,4,8]{2,1,0:T(4,128)S(1)}, s32[1,4,8]{2,1,0:T(4,128)}, u32[]{:S(2)}) copy-start(s32[1,4,8]{2,1,0:T(4,128)} %param.8) | copy-start | bytes 388
  8.3 47.3 %copy-start.1 = (bf16[1,8192,128]{2,1,0:T(8,128)(2,1)S(1)}, bf16[1,8192,128]{2,1,0:T(8,128)(2,1)}, u32[]{:S(2)}) copy-start(bf16[1,8192,128]{2,1,0:T(8,128)(2,1)} %param.12) | copy-start | bytes 6291460
  8.3 47.3 %copy-start.2 = (bf16[4,32,8192]{2,1,0:T(8,128)(2,1)S(1)}, bf16[4,32,8192]{2,1,0:T(8,128)(2,1)}, u32[]{:S(2)}) copy-start(bf16[4,32,8192]{2,1,0:T(8,128)(2,1)} %first_ref.3) | copy-start | bytes 6291460
  8.3 47.3 %copy-start.3 = (f32[1,8192]{1,0:T(1,128)S(1)}, f32[1,8192]{1,0:T(1,128)}, u32[]{:S(2)}) copy-start(f32[1,8192]{1,0:T(1,128)} %gain_ref.1) | copy-start | bytes 98308
  54.8 1.6 copy-start
  54.8 2.8 %collective-permute-start.1 = (bf16[16,32,1024]{2,1,0:T(8,128)(2,1)S(1)}, bf16[16,32,1024]{2,1,0:T(8,128)(2,1)S(1)}, u32[]{:S(2)}, u32[]{:S(2)}) collective-permute-start(bf16[16,32,1024]{2,1,0:T(8,128)(2,1)S(1)} %slice.8), channel_id=1, source_target_pairs={{0,8},{8,0},{1,9},{9,1},{2,10},{10,2},{3,11},{11,3},{4,12},{12,4},... | collective-permute-start | bytes 3145736 | tf_op jit(solution)/shard_map/ppermute | solution.py:531
  55.0 6.0 %collective-permute-start = (s32[4,8]{1,0:T(4,128)S(1)}, s32[4,8]{1,0:T(4,128)S(1)}, u32[]{:S(2)}, u32[]{:S(2)}) collective-permute-start(s32[4,8]{1,0:T(4,128)S(1)} %bitcast.22), channel_id=1, source_target_pairs={{0,128},{128,0},{1,129},{129,1},{2,130},{130,2},{3,131},{131,3},{4... | collective-permute-start | bytes 392 | tf_op jit(solution)/shard_map/ppermute | solution.py:504
  143.0 2.9 %collective-permute-start.2 = (bf16[128,4096]{1,0:T(8,128)(2,1)S(1)}, bf16[128,4096]{1,0:T(8,128)(2,1)S(1)}, u32[]{:S(2)}, u32[]{:S(2)}) collective-permute-start(bf16[128,4096]{1,0:T(8,128)(2,1)S(1)} %slice_bitcast_fusion.gram_ref), channel_id=1, source_target_pairs={{0,8},{8,0},{1,9},{9,1},{2,10},{10,2},{3,11},{11,3},{4,12},{12,4},... | collective-permute-start | bytes 3145736 | tf_op jit(solution)/shard_map/ppermute | solution.py:577
  156.4 2.9 %collective-permute-start.3 = (bf16[8,8,32,256]{3,2,1,0:T(8,128)(2,1)}, bf16[8,8,32,256]{3,2,1,0:T(8,128)(2,1)S(1)}, u32[]{:S(2)}, u32[]{:S(2)}) collective-permute-start(bf16[8,8,32,256]{3,2,1,0:T(8,128)(2,1)} %get-tuple-element.19), channel_id=1, source_target_pairs={{0,8},{8,0},{1,9},{9,1},{2,10},{10,2},{3,11},{11,3},{4,12},{12,4},... | collective-permute-start | bytes 3145736 | tf_op jit(solution)/shard_map/ppermute | solution.py:618

commit v12 on v11

--- a/solution.py
+++ b/solution.py
@@ -73,12 +73,12 @@
     return lax.axis_index("y") * 2 + lax.axis_index("xh")
 
 
-def pack_kernel(in_ref, out_ref, w_out_ref, w_in_ref, gain_ref, first_ref, send_ref, turn_ref):
+def pack_kernel(
+    in_ref, out_ref, w_out_ref, w_in_ref, gain_ref, first_ref, send_ref, turn_ref
+):
     section = section_here()
-    quarter = lax.axis_index("xl") * 2 + lax.axis_index("c")
-    zq = pl.program_id(1)
-
-    @pl.when((pl.program_id(0) == 0) & (zq == 0))
+
+    @pl.when(pl.program_id(0) == 0)
     def _():
         shape = (4 * BLK, 4 * BLK)
         row = lax.broadcasted_iota(jnp.int32, shape, 0)
@@ -87,45 +87,43 @@
         same = same & (row % 32 == col % 32)
         turn_ref[...] = jnp.where(same, 1.0, 0.0).astype(BF16)
 
-    @pl.when(zq == 0)
-    def _():
-        near = quarter % 2 * 4
-        gain = gain_ref[0, pl.ds(near, 4), quarter // 2].reshape(8, BLK).T
-        for s in range(NS):
-            for j in range(4):
-                column = 2 * j + s // 4
-                scale = gain[(s % 4) * 32 : (s % 4) * 32 + 32, column : column + 1]
-                to = W_LANE + 512 + j * BLK
-                rows = w_in_ref[0, near + j, quarter // 2, s].astype(F32)
-                send_ref[s, :, to : to + BLK] = (rows * scale).astype(BF16)
+    gain = gain_ref[...].reshape(8, BLK).T
+    for s in range(NS):
+        for j in range(4):
+            column = 2 * j + s // 4
+            scale = gain[(s % 4) * 32 : (s % 4) * 32 + 32, column : column + 1]
+            to = W_LANE + 512 + j * BLK
+            send_ref[s, :, to : to + BLK] = (w_in_ref[0, j, 0, s].astype(F32) * scale).astype(BF16)
 
     pieces, places = [], []
-    micro = section // (NS - 1) * 2
-    rank = pl.multiple_of(quarter * 32, 32)
     for c in range(2):
-        for h in range(2):
-            lanes = [(j * 4 + c * 2 + h) * BLK for j in range(4)]
-
-            def piece_of(ref, *at, lanes=lanes):
-                return jnp.concatenate([ref[*at, lane : lane + BLK] for lane in lanes], 1)
-
-            for ref, half, at, other in (
-                (in_ref, 0, c * HALF, 0),
-                (in_ref, 1, c * HALF + 256, 0),
-                (out_ref, 0, c * HALF + 512, NS - 1),
-                (out_ref, 1, c * HALF + 768, NS - 1),
-            ):
-                piece = piece_of(ref, slice(half * 32, half * 32 + 32))
-                first = piece_of(first_ref, micro + half, slice(None))
-                pieces.append(jnp.where(section == other, first, piece))
-                places.append((4 * h, at))
-            pieces.append(piece_of(w_out_ref, pl.ds(rank, 32)))
-            places.append((4 * h, W_LANE + c * 256))
+        for zq in range(2):
+            to = c * 256 + zq * BLK
+            for h in range(2):
+                lanes = [((4 * zq + j) * 4 + c * 2 + h) * BLK for j in range(4)]
+                for ref, row, at, other in (
+                    (in_ref, 0, c * HALF + zq * BLK, 0),
+                    (in_ref, 32, c * HALF + 256 + zq * BLK, 0),
+                    (out_ref, 0, c * HALF + 512 + zq * BLK, NS - 1),
+                    (out_ref, 32, c * HALF + 768 + zq * BLK, NS - 1),
+                    (w_out_ref, 0, W_LANE + to, None),
+                ):
+                    piece = jnp.concatenate(
+                        [ref[row : row + 32, lane : lane + BLK] for lane in lanes], 1
+                    )
+                    if other is not None:
+                        first = jnp.concatenate(
+                            [first_ref[row // 32, :, lane : lane + BLK] for lane in lanes], 1
+                        )
+                        piece = jnp.where(section == other, first, piece)
+                    pieces.append(piece)
+                    places.append((4 * h, at))
     turned = dot(jnp.concatenate(pieces, 0), turn_ref[...]).astype(BF16)
     for n, (first, at) in enumerate(places):
-        to = pl.ds(pl.multiple_of(at + zq * BLK, BLK), BLK)
         for i in range(4):
-            send_ref[first + i, :, to] = turned[32 * n : 32 * n + 32, i * BLK : (i + 1) * BLK]
+            send_ref[first + i, :, at : at + BLK] = turned[
+                32 * n : 32 * n + 32, i * BLK : (i + 1) * BLK
+            ]
 
 
 def start_kernel(first_ref, w_out_ref, w_in_ref, gain_ref, after_ref, start_ref):
@@ -502,19 +500,25 @@
 
     ids = example_ids[0]
     other_ids = lax.ppermute(ids, "xl", SWAP)
-    quarter = width // 4
+    wide = width // 2
+
+    def quarter():
+        return lax.axis_index("xl") * 2 + lax.axis_index("c")
+
     send = pl.pallas_call(
         pack_kernel,
-        grid=(2, 2),
+        grid=(2,),
         in_specs=[
-            pl.BlockSpec((64, quarter), lambda i, j: (0, 2 * i + j)),
-            pl.BlockSpec((64, quarter), lambda i, j: (0, 2 * i + j)),
-            pl.BlockSpec((R, quarter), lambda i, j: (0, 2 * i + j)),
-            pl.BlockSpec((1, 8, 2, 8, 32, R), lambda i, j: (i, 0, 0, 0, 0, 0)),
-            pl.BlockSpec((1, 8, 2, 2, BLK), lambda i, j: (i, 0, 0, 0, 0)),
-            pl.BlockSpec((MIC, 32, quarter), lambda i, j: (0, 0, 2 * i + j)),
+            pl.BlockSpec((64, wide), lambda i: (0, i)),
+            pl.BlockSpec((64, wide), lambda i: (0, i)),
+            pl.BlockSpec((32, wide), lambda i: (quarter(), i)),
+            pl.BlockSpec(
+                (1, 4, 1, 8, 32, R), lambda i: (i, quarter() % 2, quarter() // 2, 0, 0, 0)
+            ),
+            pl.BlockSpec((1, 4, 1, 2, BLK), lambda i: (i, quarter() % 2, quarter() // 2, 0, 0)),
+            pl.BlockSpec((2, 32, wide), lambda i: (section_here() // (NS - 1), 0, i)),
         ],
-        out_specs=pl.BlockSpec((8, 32, SENT), lambda i, j: (i, 0, 0)),
+        out_specs=pl.BlockSpec((8, 32, SENT), lambda i: (i, 0, 0)),
         scratch_shapes=[pltpu.VMEM((4 * BLK, 4 * BLK), BF16)],
         out_shape=jax.ShapeDtypeStruct((16, 32, SENT), BF16),
         compiler_params=LARGE,

time: 201 us -> 199 us (0.990)
  Pallas kernels: 27.3 us -> 24.6 us
    pallas_call x1, Pallas kernels: 7.63 us -> 4.89 us  [body(): pl.pallas_call(pack_kernel, grid=(2,), in_specs=[pl.BlockSpec((64, wide),...]
where the time goes in v12:
time: 199 us; the launch traced here: 198 us
  blocking collectives  167 us (84%)
  Pallas kernels  24.6 us (12%)
  waiting for transfers between devices  4.23 us (2%)
    all_to_all x1, blocking collectives, body(): got = lax.all_to_all(send, PLANE, 0, 0, tiled=True)  46.5 us
    all_to_all x1, blocking collectives, body(): parts = lax.all_to_all(parts, PLANE, 0, 0, tiled=True)  45.5 us
    all_to_all x1, blocking collectives, body(): total = lax.all_to_all(total, ('z',) + SECTION, 0, 0, tiled=True)  40.8 us
    all_to_all x1, blocking collectives, body(): sums = lax.all_to_all(sums, PLANE, 0, 0, tiled=True)  34 us
    pallas_call x1, Pallas kernels, body(): pl.pallas_call(functools.partial(chain_kernel, width), out_shape=(jax.Sha...  5.47 us
    pallas_call x1, Pallas kernels, body(): pl.pallas_call(grads_kernel, out_shape=(jax.ShapeDtypeStruct((8, NS, 32,...  4.99 us
    pallas_call x1, Pallas kernels, body(): pl.pallas_call(pack_kernel, grid=(2,), in_specs=[pl.BlockSpec((64, wide),...  4.89 us
  transfers between devices with their start and end apart: 4, of which 2 were waited for; matrix products, arithmetic and copies ran while one was open for 0% of the time, Pallas kernels for 3%

profile of v12, /device:TPU:32, one launch (start us, length us, event | category | flops | bytes accessed | tf_op | source)
XLA Modules:
  0.0 198.4 jit_solution(12412544638964547066)
XLA Ops:
  0.6 4.9 %pack.1 = bf16[16,32,3072]{2,1,0:T(8,128)(2,1)} custom-call(bf16[64,8192]{1,0:T(8,128)(2,1)} %bitcast.27, bf16[64,8192]{1,0:T(8,128)(2,1)} %bitcast.28, bf16[128,8192]{1,0:T(8,128)(2,1)} %bitcast.15, bf16[2,8,2,8,32,128]{5,4,3,2,1,0:T(8,128)(2,1)} %bitcast.17, f32[2,8,2,2,128]{4,3,2,1,0:T(2,128)} %bitcast.21, bf16[4,32,8192]{2,1,0:T(8,128)(2,1)} %first_ref.3), custom_call_target="tpu_custom_call" | custom-call | tf_op jit(solution)/shard_map/pack/pallas_call | solution.py:508
  5.5 0.0 copy-start.4
  5.5 0.0 copy-start.2
  5.5 0.0 copy-start.3
  5.6 46.5 %all_to_all.20.after_ref.got_ref = bf16[16,32,3072]{2,1,0:T(8,128)(2,1)S(1)} all-to-all(bf16[16,32,3072]{2,1,0:T(8,128)(2,1)} %pack.1), channel_id=1, replica_groups=mesh['xl'=2,'z'=8,'c'=2,'y'=4,'xh'=2] {'xl','y','xh'}, dimensions={0} | all-to-all | bytes 6291456 | tf_op jit(solution)/shard_map/all_to_all | solution.py:534
  52.0 0.1 slice.8
  52.1 0.1 collective-permute-start.1
  52.2 0.0 copy-done.4
  52.2 0.7 collective-permute-start
  52.9 0.0 copy-done.1
  52.9 0.0 copy-done.2
  52.9 0.0 copy-done.3
  52.9 0.7 copy-done
  53.6 1.2 start.1.start_ref
  54.9 0.0 collective-permute-done.1.other_ref
  54.9 3.3 %project.1 = (bf16[16,16,6528]{2,1,0:T(8,128)(2,1)S(1)}, bf16[8,128,512]{2,1,0:T(8,128)(2,1)S(1)}, bf16[8,512,128]{2,1,0:T(8,128)(2,1)S(1)}) custom-call(bf16[16,32,3072]{2,1,0:T(8,128)(2,1)S(1)} %all_to_all.20.after_ref.got_ref, bf16[16,32,1024]{2,1,0:T(8,128)(2,1)S(1)} %collective-permute-done.1.other_ref, bf16[128,256]{1,0:T(8,128)(2,1)S(1)} %start.1.start_ref), custom_call_target="tpu_custom_call" | custom-call | flops 2000000000 | bytes 9000000 | tf_op jit(solution)/shard_map/project/pallas_call | solution.py:545
  58.2 0.0 collective-permute-done.other_ids_ref
  58.3 2.0 norms.1
  60.2 45.5 %all_to_all.21.parts_ref = bf16[16,16,6528]{2,1,0:T(8,128)(2,1)S(1)} all-to-all(bf16[16,16,6528]{2,1,0:T(8,128)(2,1)S(1)} %norms.1), channel_id=1, replica_groups=mesh['xl'=2,'z'=8,'c'=2,'y'=4,'xh'=2] {'xl','y','xh'}, dimensions={0} | all-to-all | bytes 6684672 | tf_op jit(solution)/shard_map/all_to_all | solution.py:569
  105.7 0.4 sums.1
  106.2 34.0 %all_to_all.22.sums_ref = bf16[16,16,4480]{2,1,0:T(8,128)(2,1)S(1)} all-to-all(bf16[16,16,4480]{2,1,0:T(8,128)(2,1)S(1)} %sums.1), channel_id=1, replica_groups=mesh['xl'=2,'z'=8,'c'=2,'y'=4,'xh'=2] {'xl','y','xh'}, dimensions={0} | all-to-all | bytes 4587520 | tf_op jit(solution)/shard_map/all_to_all | solution.py:578
  140.1 0.1 slice_bitcast_fusion.gram_ref
  140.2 0.3 collective-permute-start.2
  140.5 1.2 gather.1.base_ref
  141.7 1.5 collective-permute-done.2.other_ref
  143.2 5.5 %chain.1 = (bf16[256,2048]{1,0:T(8,128)(2,1)S(1)}, f32[256,128]{1,0:T(8,128)S(1)}) custom-call(bf16[16,16,6528]{2,1,0:T(8,128)(2,1)S(1)} %all_to_all.21.parts_ref, f32[256,4736]{1,0:T(8,128)S(1)} %gather.1.base_ref, bf16[128,4096]{1,0:T(8,128)(2,1)S(1)} %slice_bitcast_fusion.gram_ref, bf16[128,4096]{1,0:T(8,128)(2,1)S(1)} %collective-permute-done.2.other_ref), custom_call_target="tpu_custom_call" | custom-call | tf_op jit(solution)/shard_map/chain/pallas_call | solution.py:592
  148.6 5.0 %grads.1 = (bf16[8,8,32,256]{3,2,1,0:T(8,128)(2,1)}, f32[8,8,32,256]{3,2,1,0:T(8,128)S(1)}) custom-call(s32[4,8]{1,0:T(4,128)S(1)} %bitcast.25, s32[4,8]{1,0:T(4,128)S(1)} %collective-permute-done.other_ids_ref, bf16[16,32,3072]{2,1,0:T(8,128)(2,1)S(1)} %all_to_all.20.after_ref.got_ref, bf16[8,128,512]{2,1,0:T(8,128)(2,1)S(1)} %get-tuple-element.13.out_w_ref, ...), custom_call_target="tpu_custom_call" | custom-call | tf_op jit(solution)/shard_map/grads/pallas_call | solution.py:610
  153.6 0.1 collective-permute-start.3
  153.8 2.7 %collective-permute-done.3.swapped_ref = bf16[8,8,32,256]{3,2,1,0:T(8,128)(2,1)S(1)} collective-permute-done((bf16[8,8,32,256]{3,2,1,0:T(8,128)(2,1)}, bf16[8,8,32,256]{3,2,1,0:T(8,128)(2,1)S(1)}, u32[]{:S(2)}, u32[]{:S(2)}) %collective-permute-start.3) | collective-permute-done | bytes 1048608 | tf_op jit(solution)/shard_map/ppermute | solution.py:622
  156.5 0.2 add.13
  156.7 40.8 %all_to_all.23 = bf16[64,32,256]{2,1,0:T(8,128)(2,1)S(1)} all-to-all(bf16[64,32,256]{2,1,0:T(8,128)(2,1)S(1)} %bitcast.20), channel_id=1, replica_groups=mesh['xl'=2,'z'=8,'c'=2,'y'=4,'xh'=2] {'z','y','xh'}, dimensions={0} | all-to-all | bytes 2097152 | tf_op jit(solution)/shard_map/all_to_all | solution.py:634
  197.5 0.9 final.1
  (3 shorter events, 0.0 us)
Async XLA Ops:
  5.5 46.7 %copy-start.4 = (s32[1,4,8]{2,1,0:T(4,128)S(1)}, s32[1,4,8]{2,1,0:T(4,128)}, u32[]{:S(2)}) copy-start(s32[1,4,8]{2,1,0:T(4,128)} %param.8) | copy-start | bytes 388
  5.5 47.4 %copy-start.1 = (bf16[1,8192,128]{2,1,0:T(8,128)(2,1)S(1)}, bf16[1,8192,128]{2,1,0:T(8,128)(2,1)}, u32[]{:S(2)}) copy-start(bf16[1,8192,128]{2,1,0:T(8,128)(2,1)} %param.12) | copy-start | bytes 6291460
  5.5 47.4 %copy-start.2 = (bf16[4,32,8192]{2,1,0:T(8,128)(2,1)S(1)}, bf16[4,32,8192]{2,1,0:T(8,128)(2,1)}, u32[]{:S(2)}) copy-start(bf16[4,32,8192]{2,1,0:T(8,128)(2,1)} %first_ref.3) | copy-start | bytes 6291460
  5.5 47.3 %copy-start.3 = (f32[1,8192]{1,0:T(1,128)S(1)}, f32[1,8192]{1,0:T(1,128)}, u32[]{:S(2)}) copy-start(f32[1,8192]{1,0:T(1,128)} %gain_ref.1) | copy-start | bytes 98308
  52.0 1.6 copy-start
  52.1 2.8 %collective-permute-start.1 = (bf16[16,32,1024]{2,1,0:T(8,128)(2,1)S(1)}, bf16[16,32,1024]{2,1,0:T(8,128)(2,1)S(1)}, u32[]{:S(2)}, u32[]{:S(2)}) collective-permute-start(bf16[16,32,1024]{2,1,0:T(8,128)(2,1)S(1)} %slice.8), channel_id=1, source_target_pairs={{0,8},{8,0},{1,9},{9,1},{2,10},{10,2},{3,11},{11,3},{4,12},{12,4},... | collective-permute-start | bytes 3145736 | tf_op jit(solution)/shard_map/ppermute | solution.py:535
  52.2 6.0 %collective-permute-start = (s32[4,8]{1,0:T(4,128)S(1)}, s32[4,8]{1,0:T(4,128)S(1)}, u32[]{:S(2)}, u32[]{:S(2)}) collective-permute-start(s32[4,8]{1,0:T(4,128)S(1)} %bitcast.22), channel_id=1, source_target_pairs={{0,128},{128,0},{1,129},{129,1},{2,130},{130,2},{3,131},{131,3},{4... | collective-permute-start | bytes 392 | tf_op jit(solution)/shard_map/ppermute | solution.py:502
  140.2 2.9 %collective-permute-start.2 = (bf16[128,4096]{1,0:T(8,128)(2,1)S(1)}, bf16[128,4096]{1,0:T(8,128)(2,1)S(1)}, u32[]{:S(2)}, u32[]{:S(2)}) collective-permute-start(bf16[128,4096]{1,0:T(8,128)(2,1)S(1)} %slice_bitcast_fusion.gram_ref), channel_id=1, source_target_pairs={{0,8},{8,0},{1,9},{9,1},{2,10},{10,2},{3,11},{11,3},{4,12},{12,4},... | collective-permute-start | bytes 3145736 | tf_op jit(solution)/shard_map/ppermute | solution.py:581
  153.6 2.9 %collective-permute-start.3 = (bf16[8,8,32,256]{3,2,1,0:T(8,128)(2,1)}, bf16[8,8,32,256]{3,2,1,0:T(8,128)(2,1)S(1)}, u32[]{:S(2)}, u32[]{:S(2)}) collective-permute-start(bf16[8,8,32,256]{3,2,1,0:T(8,128)(2,1)} %get-tuple-element.19), channel_id=1, source_target_pairs={{0,8},{8,0},{1,9},{9,1},{2,10},{10,2},{3,11},{11,3},{4,12},{12,4},... | collective-permute-start | bytes 3145736 | tf_op jit(solution)/shard_map/ppermute | solution.py:622

commit v13 on v12

--- a/solution.py
+++ b/solution.py
@@ -176,75 +176,7 @@
         yield s, running
 
 
-def project_kernel(
-    got_ref, other_ref, start_ref, send_ref, out_w_ref, in_w_ref, wide_ref
-):
-    cols = in_w_ref.shape[1]
-    first_core = lax.axis_index("c") == 0
-    for s in range(NS):
-        for x in range(2):
-            mine = got_ref[x * NS + s, :, W_LANE:SENT]
-            theirs = other_ref[x * NS + s]
-            for c in range(2):
-                part = jnp.where(first_core == (c == 0), mine, theirs)
-                k = 2 * x + c
-                out_w_ref[s, 32 * k : 32 * k + 32, :] = part[:, :cols]
-                for g in range(4):
-                    row = k * BLK + g * 32
-                    lane = cols + g * BLK
-                    in_w_ref[s, row : row + 32, :] = part[:, lane : lane + BLK]
-    for s, running in running_sums(got_ref, cols):
-        rounded = running.astype(BF16)
-        count = s if s < NS - 1 else NS
-        at = proj_at(s) * BLK
-        wide_ref[:, at : at + count * BLK] = dot_t(
-            rounded, out_w_ref[0:count].reshape(count * R, cols)
-        )
-        at = inner_at(s) * BLK
-        wide_ref[:, at : at + BLK] = dot(rounded, in_w_ref[s])
-    for b in (NORM, GRAM + GRAMS):
-        wide_ref[:, b * BLK : (b + 1) * BLK] = jnp.zeros((R, BLK), F32)
-
-    square = [(t, s) for t in range(NS) for s in range(t, NS)]
-
-    @pl.when(first_core)
-    def _():
-        for t in range(5):
-            at = (GRAM + gram_at(t)) * BLK
-            wide_ref[:, at : at + (NS - t) * BLK] = dot_t(
-                out_w_ref[t], out_w_ref[t:NS].reshape((NS - t) * R, cols)
-            )
-        for i in range(gram_at(5), GRAMS):
-            t, s = square[i]
-            at = (GRAM + i) * BLK
-            wide_ref[:, at : at + BLK] = dot_t(out_w_ref[t], out_w_ref[s])
-
-    @pl.when(jnp.logical_not(first_core))
-    def _():
-        for t in range(NS - 1):
-            for s in range(t + 1, NS):
-                at = (GRAM + cross_at(t) + s - t - 1) * BLK
-                wide_ref[:, at : at + BLK] = dot(out_w_ref[t], in_w_ref[s])
-        for i in range(GRAMS, OO):
-            t, s = square[i]
-            at = (GRAM + OI + i - GRAMS) * BLK
-            wide_ref[:, at : at + BLK] = dot_t(out_w_ref[t], out_w_ref[s])
-
-    for b in range(SPLIT):
-        pair = [
-            wide_ref[:, at * BLK : (at + 1) * BLK].reshape(16, TOK, BLK) for at in (b, SPLIT + b)
-        ]
-        send_ref[:, :, b * BLK : (b + 1) * BLK] = jnp.concatenate(pair, 1).astype(BF16)
-    for g in range(8):
-        at = START + g * 2 * R
-        for q in range(16):
-            send_ref[q, :, at : at + 2 * R] = start_ref[g * 16 : (g + 1) * 16, :]
-
-
-def norm_kernel(
-    cols, ids_ref, other_ids_ref, got_ref, before_ref, send_ref, block_ref, sem
-):
-    del before_ref
+def placed_rows(ids_ref, other_ids_ref, got_ref, cols):
     picks = picks_of(ids_ref, other_ids_ref)
     placed = [[] for _ in range(MIC)]
     first = jnp.concatenate(
@@ -261,7 +193,27 @@
                         picks[16 * x + n] == x * NS + e, rows[n * TOK : (n + 1) * TOK], total
                     )
                 placed[m].append(total)
-    placed = [jnp.concatenate(blocks, 0) for blocks in placed]
+    return [jnp.concatenate(blocks, 0) for blocks in placed]
+
+
+def project_kernel(
+    ids_ref, other_ids_ref, got_ref, other_ref, start_ref, send_ref, out_w_ref, in_w_ref, wide_ref
+):
+    cols = in_w_ref.shape[1]
+    first_core = lax.axis_index("c") == 0
+    for s in range(NS):
+        for x in range(2):
+            mine = got_ref[x * NS + s, :, W_LANE:SENT]
+            theirs = other_ref[x * NS + s]
+            for c in range(2):
+                part = jnp.where(first_core == (c == 0), mine, theirs)
+                k = 2 * x + c
+                out_w_ref[s, 32 * k : 32 * k + 32, :] = part[:, :cols]
+                for g in range(4):
+                    row = k * BLK + g * 32
+                    lane = cols + g * BLK
+                    in_w_ref[s, row : row + 32, :] = part[:, lane : lane + BLK]
+    placed = placed_rows(ids_ref, other_ids_ref, got_ref, cols)
     lane = lax.broadcasted_iota(jnp.int32, (R, BLK), 1)
     norms = jnp.zeros((R, BLK), F32)
     for m in range(MIC):
@@ -272,14 +224,54 @@
             entry = running + placed[m]
             part = jnp.sum(entry * entry, -1, keepdims=True)
             norms = jnp.where(lane == m * NS + s, part, norms)
+        rounded = running.astype(BF16)
+        count = s if s < NS - 1 else NS
+        at = proj_at(s) * BLK
+        wide_ref[:, at : at + count * BLK] = dot_t(
+            rounded, out_w_ref[0:count].reshape(count * R, cols)
+        )
+        at = inner_at(s) * BLK
+        wide_ref[:, at : at + BLK] = dot(rounded, in_w_ref[s])
     high = norms.astype(BF16).astype(F32)
-    norms = jnp.where(lane < 32, high, pltpu.roll(norms - high, 32, 1)).reshape(16, TOK, BLK)
-    block_ref[...] = jnp.concatenate([norms, jnp.zeros_like(norms)], 1).astype(BF16)
-    copy = pltpu.make_async_copy(
-        block_ref, send_ref.at[:, :, NORM * BLK : (NORM + 1) * BLK], sem
+    wide_ref[:, NORM * BLK : (NORM + 1) * BLK] = jnp.where(
+        lane < 32, high, pltpu.roll(norms - high, 32, 1)
     )
-    copy.start()
-    copy.wait()
+    wide_ref[:, (GRAM + GRAMS) * BLK :] = jnp.zeros((R, BLK), F32)
+
+    square = [(t, s) for t in range(NS) for s in range(t, NS)]
+
+    @pl.when(first_core)
+    def _():
+        for t in range(5):
+            at = (GRAM + gram_at(t)) * BLK
+            wide_ref[:, at : at + (NS - t) * BLK] = dot_t(
+                out_w_ref[t], out_w_ref[t:NS].reshape((NS - t) * R, cols)
+            )
+        for i in range(gram_at(5), GRAMS):
+            t, s = square[i]
+            at = (GRAM + i) * BLK
+            wide_ref[:, at : at + BLK] = dot_t(out_w_ref[t], out_w_ref[s])
+
+    @pl.when(jnp.logical_not(first_core))
+    def _():
+        for t in range(NS - 1):
+            for s in range(t + 1, NS):
+                at = (GRAM + cross_at(t) + s - t - 1) * BLK
+                wide_ref[:, at : at + BLK] = dot(out_w_ref[t], in_w_ref[s])
+        for i in range(GRAMS, OO):
+            t, s = square[i]
+            at = (GRAM + OI + i - GRAMS) * BLK
+            wide_ref[:, at : at + BLK] = dot_t(out_w_ref[t], out_w_ref[s])
+
+    for b in range(SPLIT):
+        pair = [
+            wide_ref[:, at * BLK : (at + 1) * BLK].reshape(16, TOK, BLK) for at in (b, SPLIT + b)
+        ]
+        send_ref[:, :, b * BLK : (b + 1) * BLK] = jnp.concatenate(pair, 1).astype(BF16)
+    for g in range(8):
+        at = START + g * 2 * R
+        for q in range(16):
+            send_ref[q, :, at : at + 2 * R] = start_ref[g * 16 : (g + 1) * 16, :]
 
 
 def sum_kernel(parts_ref, send_ref):
@@ -531,6 +523,7 @@
         norm_gain.reshape(2, 8, 2, 2, BLK),
         first_input,
     )
+    send, other_ids = lax.optimization_barrier((send, other_ids))
     got = lax.all_to_all(send, PLANE, 0, 0, tiled=True)
     other = lax.ppermute(got[:, :, W_LANE:], "c", SWAP)
     start = pl.pallas_call(
@@ -549,23 +542,13 @@
             jax.ShapeDtypeStruct((NS, R, cols), BF16),
             jax.ShapeDtypeStruct((NS, cols, R), BF16),
         ),
-        in_specs=[VMEM, VMEM, VMEM],
+        in_specs=[SMEM, SMEM, VMEM, VMEM, VMEM],
         out_specs=(VMEM, VMEM, VMEM),
         scratch_shapes=[pltpu.VMEM((R, 2 * SPLIT * BLK), F32)],
         compiler_params=PARAMS,
         cost_estimate=pl.CostEstimate(flops=2000000000, bytes_accessed=9000000, transcendentals=0),
         name="project",
-    )(got, other, start)
-    parts = pl.pallas_call(
-        functools.partial(norm_kernel, cols),
-        out_shape=jax.ShapeDtypeStruct((16, 2 * TOK, WIDE), BF16),
-        in_specs=[SMEM, SMEM, VMEM, pl.BlockSpec(memory_space=pl.ANY)],
-        out_specs=pl.BlockSpec(memory_space=pl.ANY),
-        scratch_shapes=[pltpu.VMEM((16, 2 * TOK, BLK), BF16), pltpu.SemaphoreType.DMA],
-        input_output_aliases={3: 0},
-        compiler_params=PARAMS,
-        name="norms",
-    )(ids, other_ids, got, parts)
+    )(ids, other_ids, got, other, start)
     parts = lax.all_to_all(parts, PLANE, 0, 0, tiled=True)
     sums = pl.pallas_call(
         sum_kernel,

time: 199 us -> 199 us (level)
  transfers between devices with their start and end apart: 4 -> 4, of which waited for: 2 -> 2; matrix products, arithmetic and copies ran while one was open for 0% -> 0% of each run, Pallas kernels for 3% -> 4%
where the time goes in v13:
time: 199 us; the launch traced here: 198 us
  blocking collectives  166 us (83%)
  Pallas kernels  23.9 us (12%)
  waiting for transfers between devices  4.22 us (2%)
  starting transfers between devices  2.08 us (1%)
    all_to_all x1, blocking collectives, body(): got = lax.all_to_all(send, PLANE, 0, 0, tiled=True)  45.9 us
    all_to_all x1, blocking collectives, body(): parts = lax.all_to_all(parts, PLANE, 0, 0, tiled=True)  45.2 us
    all_to_all x1, blocking collectives, body(): total = lax.all_to_all(total, ('z',) + SECTION, 0, 0, tiled=True)  40.8 us
    all_to_all x1, blocking collectives, body(): sums = lax.all_to_all(sums, PLANE, 0, 0, tiled=True)  34 us
    pallas_call x1, Pallas kernels, body(): pl.pallas_call(functools.partial(chain_kernel, width), out_shape=(jax.Sha...  5.47 us
    pallas_call x1, Pallas kernels, body(): pl.pallas_call(grads_kernel, out_shape=(jax.ShapeDtypeStruct((8, NS, 32,...  4.96 us
    pallas_call x1, Pallas kernels, body(): pl.pallas_call(pack_kernel, grid=(2,), in_specs=[pl.BlockSpec((64, wide),...  4.81 us
    pallas_call x1, Pallas kernels, body(): pl.pallas_call(project_kernel, out_shape=(jax.ShapeDtypeStruct((16, 2 * T...  4.72 us
  transfers between devices with their start and end apart: 4, of which 2 were waited for; matrix products, arithmetic and copies ran while one was open for 0% of the time, Pallas kernels for 4%

profile of v13, /device:TPU:32, one launch (start us, length us, event | category | flops | bytes accessed | tf_op | source)
XLA Modules:
  0.0 198.4 jit_solution(17478229089043204336)
XLA Ops:
  0.6 1.6 collective-permute-start
  2.2 4.8 %pack.1 = bf16[16,32,3072]{2,1,0:T(8,128)(2,1)} custom-call(bf16[64,8192]{1,0:T(8,128)(2,1)} %bitcast.27, bf16[64,8192]{1,0:T(8,128)(2,1)} %bitcast.28, bf16[128,8192]{1,0:T(8,128)(2,1)} %bitcast.15, bf16[2,8,2,8,32,128]{5,4,3,2,1,0:T(8,128)(2,1)} %bitcast.17, f32[2,8,2,2,128]{4,3,2,1,0:T(2,128)} %bitcast.21, bf16[4,32,8192]{2,1,0:T(8,128)(2,1)} %first_ref.3), custom_call_target="tpu_custom_call" | custom-call | tf_op jit(solution)/shard_map/pack/pallas_call | solution.py:500
  7.0 0.0 copy-start.3
  7.0 0.0 collective-permute-done.other_ids_ref
  7.0 0.0 copy-start.1
  7.0 0.0 copy-start.2
  7.0 45.9 %all_to_all.20.after_ref.got_ref = bf16[16,32,3072]{2,1,0:T(8,128)(2,1)S(1)} all-to-all(bf16[16,32,3072]{2,1,0:T(8,128)(2,1)} %pack.1), channel_id=1, replica_groups=mesh['xl'=2,'z'=8,'c'=2,'y'=4,'xh'=2] {'xl','y','xh'}, dimensions={0} | all-to-all | bytes 6291456 | tf_op jit(solution)/shard_map/all_to_all | solution.py:527
  52.9 0.0 copy-start
  52.9 0.1 slice.8
  53.0 0.1 collective-permute-start.1
  53.1 0.0 copy-done.3
  53.2 0.0 copy-done.1
  53.2 0.0 copy-done.2
  53.2 1.4 copy-done
  54.5 1.2 start.1.start_ref
  55.8 0.0 collective-permute-done.1.other_ref
  55.8 0.0 copy-done.4
  55.8 4.7 %project.1 = (bf16[16,16,6528]{2,1,0:T(8,128)(2,1)S(1)}, bf16[8,128,512]{2,1,0:T(8,128)(2,1)S(1)}, bf16[8,512,128]{2,1,0:T(8,128)(2,1)S(1)}) custom-call(s32[4,8]{1,0:T(4,128)S(1)} %bitcast.23, s32[4,8]{1,0:T(4,128)S(1)} %collective-permute-done.other_ids_ref, bf16[16,32,3072]{2,1,0:T(8,128)(2,1)S(1)} %all_to_all.20.after_ref.got_ref, ...), custom_call_target="tpu_custom_call" | custom-call | flops 2000000000 | bytes 9000000 | tf_op jit(solution)/shard_map/project/pallas_call | solution.py:538
  60.5 45.2 %all_to_all.21.parts_ref = bf16[16,16,6528]{2,1,0:T(8,128)(2,1)S(1)} all-to-all(bf16[16,16,6528]{2,1,0:T(8,128)(2,1)S(1)} %get-tuple-element.19), channel_id=1, replica_groups=mesh['xl'=2,'z'=8,'c'=2,'y'=4,'xh'=2] {'xl','y','xh'}, dimensions={0} | all-to-all | bytes 6684672 | tf_op jit(solution)/shard_map/all_to_all | solution.py:552
  105.8 0.4 sums.1
  106.2 34.0 %all_to_all.22.sums_ref = bf16[16,16,4480]{2,1,0:T(8,128)(2,1)S(1)} all-to-all(bf16[16,16,4480]{2,1,0:T(8,128)(2,1)S(1)} %sums.1), channel_id=1, replica_groups=mesh['xl'=2,'z'=8,'c'=2,'y'=4,'xh'=2] {'xl','y','xh'}, dimensions={0} | all-to-all | bytes 4587520 | tf_op jit(solution)/shard_map/all_to_all | solution.py:561
  140.2 0.1 slice_bitcast_fusion.gram_ref
  140.3 0.3 collective-permute-start.2
  140.6 1.2 gather.1.base_ref
  141.7 1.5 collective-permute-done.2.other_ref
  143.2 5.5 %chain.1 = (bf16[256,2048]{1,0:T(8,128)(2,1)S(1)}, f32[256,128]{1,0:T(8,128)S(1)}) custom-call(bf16[16,16,6528]{2,1,0:T(8,128)(2,1)S(1)} %all_to_all.21.parts_ref, f32[256,4736]{1,0:T(8,128)S(1)} %gather.1.base_ref, bf16[128,4096]{1,0:T(8,128)(2,1)S(1)} %slice_bitcast_fusion.gram_ref, bf16[128,4096]{1,0:T(8,128)(2,1)S(1)} %collective-permute-done.2.other_ref), custom_call_target="tpu_custom_call" | custom-call | tf_op jit(solution)/shard_map/chain/pallas_call | solution.py:575
  148.7 5.0 %grads.1 = (bf16[8,8,32,256]{3,2,1,0:T(8,128)(2,1)}, f32[8,8,32,256]{3,2,1,0:T(8,128)S(1)}) custom-call(s32[4,8]{1,0:T(4,128)S(1)} %bitcast.25, s32[4,8]{1,0:T(4,128)S(1)} %collective-permute-done.other_ids_ref, bf16[16,32,3072]{2,1,0:T(8,128)(2,1)S(1)} %all_to_all.20.after_ref.got_ref, bf16[8,128,512]{2,1,0:T(8,128)(2,1)S(1)} %get-tuple-element.17.out_w_ref, ...), custom_call_target="tpu_custom_call" | custom-call | tf_op jit(solution)/shard_map/grads/pallas_call | solution.py:593
  153.7 0.1 collective-permute-start.3
  153.8 2.7 %collective-permute-done.3.swapped_ref = bf16[8,8,32,256]{3,2,1,0:T(8,128)(2,1)S(1)} collective-permute-done((bf16[8,8,32,256]{3,2,1,0:T(8,128)(2,1)}, bf16[8,8,32,256]{3,2,1,0:T(8,128)(2,1)S(1)}, u32[]{:S(2)}, u32[]{:S(2)}) %collective-permute-start.3) | collective-permute-done | bytes 1048608 | tf_op jit(solution)/shard_map/ppermute | solution.py:605
  156.5 0.2 add.13
  156.7 40.8 %all_to_all.23 = bf16[64,32,256]{2,1,0:T(8,128)(2,1)S(1)} all-to-all(bf16[64,32,256]{2,1,0:T(8,128)(2,1)S(1)} %bitcast.20), channel_id=1, replica_groups=mesh['xl'=2,'z'=8,'c'=2,'y'=4,'xh'=2] {'z','y','xh'}, dimensions={0} | all-to-all | bytes 2097152 | tf_op jit(solution)/shard_map/all_to_all | solution.py:617
  197.5 0.9 final.1
  (2 shorter events, 0.0 us)
Async XLA Ops:
  0.6 6.4 %collective-permute-start = (s32[4,8]{1,0:T(4,128)}, s32[4,8]{1,0:T(4,128)S(1)}, u32[]{:S(2)}, u32[]{:S(2)}) collective-permute-start(s32[4,8]{1,0:T(4,128)} %bitcast.22), channel_id=1, source_target_pairs={{0,128},{128,0},{1,129},{129,1},{2,130},{130,2},{3,131},{131,3},{4... | collective-permute-start | bytes 392 | tf_op jit(solution)/shard_map/ppermute | solution.py:494
  7.0 46.1 %copy-start.3 = (f32[1,8192]{1,0:T(1,128)S(1)}, f32[1,8192]{1,0:T(1,128)}, u32[]{:S(2)}) copy-start(f32[1,8192]{1,0:T(1,128)} %gain_ref.1) | copy-start | bytes 98308
  7.0 46.1 %copy-start.1 = (bf16[1,8192,128]{2,1,0:T(8,128)(2,1)S(1)}, bf16[1,8192,128]{2,1,0:T(8,128)(2,1)}, u32[]{:S(2)}) copy-start(bf16[1,8192,128]{2,1,0:T(8,128)(2,1)} %param.12) | copy-start | bytes 6291460
  7.0 46.1 %copy-start.2 = (bf16[4,32,8192]{2,1,0:T(8,128)(2,1)S(1)}, bf16[4,32,8192]{2,1,0:T(8,128)(2,1)}, u32[]{:S(2)}) copy-start(bf16[4,32,8192]{2,1,0:T(8,128)(2,1)} %first_ref.3) | copy-start | bytes 6291460
  52.9 1.6 copy-start
  53.0 2.8 %collective-permute-start.1 = (bf16[16,32,1024]{2,1,0:T(8,128)(2,1)S(1)}, bf16[16,32,1024]{2,1,0:T(8,128)(2,1)S(1)}, u32[]{:S(2)}, u32[]{:S(2)}) collective-permute-start(bf16[16,32,1024]{2,1,0:T(8,128)(2,1)S(1)} %slice.8), channel_id=1, source_target_pairs={{0,8},{8,0},{1,9},{9,1},{2,10},{10,2},{3,11},{11,3},{4,12},{12,4},... | collective-permute-start | bytes 3145736 | tf_op jit(solution)/shard_map/ppermute | solution.py:528
  54.5 1.3 copy-start.4
  140.3 2.9 %collective-permute-start.2 = (bf16[128,4096]{1,0:T(8,128)(2,1)S(1)}, bf16[128,4096]{1,0:T(8,128)(2,1)S(1)}, u32[]{:S(2)}, u32[]{:S(2)}) collective-permute-start(bf16[128,4096]{1,0:T(8,128)(2,1)S(1)} %slice_bitcast_fusion.gram_ref), channel_id=1, source_target_pairs={{0,8},{8,0},{1,9},{9,1},{2,10},{10,2},{3,11},{11,3},{4,12},{12,4},... | collective-permute-start | bytes 3145736 | tf_op jit(solution)/shard_map/ppermute | solution.py:564
  153.7 2.9 %collective-permute-start.3 = (bf16[8,8,32,256]{3,2,1,0:T(8,128)(2,1)}, bf16[8,8,32,256]{3,2,1,0:T(8,128)(2,1)S(1)}, u32[]{:S(2)}, u32[]{:S(2)}) collective-permute-start(bf16[8,8,32,256]{3,2,1,0:T(8,128)(2,1)} %get-tuple-element.23), channel_id=1, source_target_pairs={{0,8},{8,0},{1,9},{9,1},{2,10},{10,2},{3,11},{11,3},{4,12},{12,4},... | collective-permute-start | bytes 3145736 | tf_op jit(solution)/shard_map/ppermute | solution.py:605

commit v14 on v13

--- a/solution.py
+++ b/solution.py
@@ -126,12 +126,13 @@
             ]
 
 
-def start_kernel(first_ref, w_out_ref, w_in_ref, gain_ref, after_ref, start_ref):
+def start_kernel(first_ref, w_out_ref, w_in_ref, gain_ref, after_ref, start_ref, sum_ref):
     del after_ref
     flat = first_ref[...].reshape(R, first_ref.shape[2])
     scaled = (flat.astype(F32) * gain_ref[...]).astype(BF16)
-    start_ref[:, :R] = dot(scaled, w_in_ref[...]).astype(BF16)
-    start_ref[:, R:] = dot_t(flat, w_out_ref[...]).astype(BF16)
+    both = jnp.concatenate([dot(scaled, w_in_ref[...]), dot_t(flat, w_out_ref[...])], 1)
+    sum_ref[...] = jnp.where(pl.program_id(0) == 0, 0.0, sum_ref[...]) + both
+    start_ref[...] = sum_ref[...].astype(BF16)
 
 
 def stores(got_ref, s, at, cols):
@@ -526,12 +527,21 @@
     send, other_ids = lax.optimization_barrier((send, other_ids))
     got = lax.all_to_all(send, PLANE, 0, 0, tiled=True)
     other = lax.ppermute(got[:, :, W_LANE:], "c", SWAP)
+    run = width // 4
     start = pl.pallas_call(
         start_kernel,
+        grid=(4,),
         out_shape=jax.ShapeDtypeStruct((R, 2 * R), BF16),
-        in_specs=[VMEM, VMEM, VMEM, VMEM, pl.BlockSpec(memory_space=pl.ANY)],
-        out_specs=VMEM,
-        compiler_params=PARAMS,
+        in_specs=[
+            pl.BlockSpec((MIC, 32, run), lambda i: (0, 0, i)),
+            pl.BlockSpec((R, run), lambda i: (0, i)),
+            pl.BlockSpec((run, R), lambda i: (i, 0)),
+            pl.BlockSpec((1, run), lambda i: (0, i)),
+            pl.BlockSpec(memory_space=pl.ANY),
+        ],
+        out_specs=pl.BlockSpec((R, 2 * R), lambda i: (0, 0)),
+        scratch_shapes=[pltpu.VMEM((R, 2 * R), F32)],
+        compiler_params=LARGE,
         cost_estimate=pl.CostEstimate(flops=600000000, bytes_accessed=7000000, transcendentals=0),
         name="start",
     )(first_input, w_out, w_in, norm_gain, got)

time: 199 us -> 205 us (1.030)
  Pallas kernels: 23.9 us -> 27.5 us
  local copies, waits for them, and re-layouts: 1.57 us -> 5.03 us
    pallas_call x1, Pallas kernels: 1.25 us -> 4.84 us  [body(): pl.pallas_call(start_kernel, grid=(4,), out_shape=jax.ShapeDtypeStruct((R...]
    unnamed x10, local copies, waits for them, and re-layouts: 1.39 us -> 4.18 us
  transfers between devices with their start and end apart: 4 -> 4, of which waited for: 2 -> 2; matrix products, arithmetic and copies ran while one was open for 0% -> 0% of each run, Pallas kernels for 4% -> 5%
where the time goes in v14:
time: 205 us
  blocking collectives  166 us (81%)
  Pallas kernels  27.5 us (13%)
  local copies, waits for them, and re-layouts  5.03 us (2%)
  waiting for transfers between devices  3.53 us (2%)
  starting transfers between devices  2.08 us (1%)
    all_to_all x1, blocking collectives, body(): got = lax.all_to_all(send, PLANE, 0, 0, tiled=True)  45.6 us
    all_to_all x1, blocking collectives, body(): parts = lax.all_to_all(parts, PLANE, 0, 0, tiled=True)  44.8 us
    all_to_all x1, blocking collectives, body(): total = lax.all_to_all(total, ('z',) + SECTION, 0, 0, tiled=True)  42.6 us
    all_to_all x1, blocking collectives, body(): sums = lax.all_to_all(sums, PLANE, 0, 0, tiled=True)  32.7 us
    pallas_call x1, Pallas kernels, body(): pl.pallas_call(functools.partial(chain_kernel, width), out_shape=(jax.Sha...  5.47 us
    pallas_call x1, Pallas kernels, body(): pl.pallas_call(grads_kernel, out_shape=(jax.ShapeDtypeStruct((8, NS, 32,...  4.97 us
    pallas_call x1, Pallas kernels, body(): pl.pallas_call(start_kernel, grid=(4,), out_shape=jax.ShapeDtypeStruct((R...  4.84 us
    pallas_call x1, Pallas kernels, body(): pl.pallas_call(pack_kernel, grid=(2,), in_specs=[pl.BlockSpec((64, wide),...  4.81 us
  transfers between devices with their start and end apart: 4, of which 2 were waited for; matrix products, arithmetic and copies ran while one was open for 0% of the time, Pallas kernels for 5%

profile of v14, /device:TPU:32, one launch (start us, length us, event | category | flops | bytes accessed | tf_op | source)
XLA Modules:
  0.0 204.6 jit_solution(16151387612118476392)
XLA Ops:
  0.6 1.6 collective-permute-start
  2.2 4.8 %pack.1 = bf16[16,32,3072]{2,1,0:T(8,128)(2,1)} custom-call(bf16[64,8192]{1,0:T(8,128)(2,1)} %bitcast.26, bf16[64,8192]{1,0:T(8,128)(2,1)} %bitcast.27, bf16[128,8192]{1,0:T(8,128)(2,1)} %bitcast.22, bf16[2,8,2,8,32,128]{5,4,3,2,1,0:T(8,128)(2,1)} %bitcast.24, f32[2,8,2,2,128]{4,3,2,1,0:T(2,128)} %bitcast.28, bf16[4,32,8192]{2,1,0:T(8,128)(2,1)} %first_ref.3), custom_call_target="tpu_custom_call" | custom-call | tf_op jit(solution)/shard_map/pack/pallas_call | solution.py:501
  7.0 0.0 collective-permute-done.other_ids_ref
  7.0 45.6 %all_to_all.20.after_ref.got_ref = bf16[16,32,3072]{2,1,0:T(8,128)(2,1)S(1)} all-to-all(bf16[16,32,3072]{2,1,0:T(8,128)(2,1)} %pack.1), channel_id=1, replica_groups=mesh['xl'=2,'z'=8,'c'=2,'y'=4,'xh'=2] {'xl','y','xh'}, dimensions={0} | all-to-all | bytes 6291456 | tf_op jit(solution)/shard_map/all_to_all | solution.py:528
  52.7 0.1 slice.8
  52.7 0.1 collective-permute-start.1
  52.8 1.4 copy-done
  54.3 0.0 copy-start.4
  54.3 4.8 %start.1.start_ref = bf16[128,256]{1,0:T(8,128)(2,1)} custom-call(bf16[4,32,8192]{2,1,0:T(8,128)(2,1)} %first_ref.3, bf16[128,8192]{1,0:T(8,128)(2,1)} %bitcast.23, bf16[8192,128]{1,0:T(8,128)(2,1)} %bitcast.25, f32[1,8192]{1,0:T(1,128)} %gain_ref.1, bf16[16,32,3072]{2,1,0:T(8,128)(2,1)} %copy-done), custom_call_target="tpu_custom_call" | custom-call | flops 600000000 | bytes 7000000 | tf_op jit(solution)/shard_map/start/pallas_call | solution.py:531
  59.1 0.0 collective-permute-done.1.other_ref
  59.1 0.0 copy-done.4
  59.1 0.0 copy-start.1
  59.1 1.9 copy-done.1
  61.0 0.8 copy-done.3
  61.9 4.7 %project.1 = (bf16[16,16,6528]{2,1,0:T(8,128)(2,1)S(1)}, bf16[8,128,512]{2,1,0:T(8,128)(2,1)S(1)}, bf16[8,512,128]{2,1,0:T(8,128)(2,1)S(1)}) custom-call(s32[4,8]{1,0:T(4,128)S(1)} %bitcast.18, s32[4,8]{1,0:T(4,128)S(1)} %collective-permute-done.other_ids_ref, bf16[16,32,3072]{2,1,0:T(8,128)(2,1)S(1)} %copy-done.1, ...), custom_call_target="tpu_custom_call" | custom-call | flops 2000000000 | bytes 9000000 | tf_op jit(solution)/shard_map/project/pallas_call | solution.py:548
  66.6 44.8 %all_to_all.21.parts_ref = bf16[16,16,6528]{2,1,0:T(8,128)(2,1)S(1)} all-to-all(bf16[16,16,6528]{2,1,0:T(8,128)(2,1)S(1)} %get-tuple-element.19), channel_id=1, replica_groups=mesh['xl'=2,'z'=8,'c'=2,'y'=4,'xh'=2] {'xl','y','xh'}, dimensions={0} | all-to-all | bytes 6684672 | tf_op jit(solution)/shard_map/all_to_all | solution.py:562
  111.4 0.4 sums.1
  111.9 32.7 %all_to_all.22.sums_ref = bf16[16,16,4480]{2,1,0:T(8,128)(2,1)S(1)} all-to-all(bf16[16,16,4480]{2,1,0:T(8,128)(2,1)S(1)} %sums.1), channel_id=1, replica_groups=mesh['xl'=2,'z'=8,'c'=2,'y'=4,'xh'=2] {'xl','y','xh'}, dimensions={0} | all-to-all | bytes 4587520 | tf_op jit(solution)/shard_map/all_to_all | solution.py:571
  144.6 0.1 slice_bitcast_fusion.gram_ref
  144.7 0.3 collective-permute-start.2
  144.9 1.2 gather.1.base_ref
  146.1 0.0 copy-start.2
  146.1 1.5 collective-permute-done.2.other_ref
  147.6 5.5 %chain.1 = (bf16[256,2048]{1,0:T(8,128)(2,1)S(1)}, f32[256,128]{1,0:T(8,128)S(1)}) custom-call(bf16[16,16,6528]{2,1,0:T(8,128)(2,1)S(1)} %all_to_all.21.parts_ref, f32[256,4736]{1,0:T(8,128)S(1)} %gather.1.base_ref, bf16[128,4096]{1,0:T(8,128)(2,1)S(1)} %slice_bitcast_fusion.gram_ref, bf16[128,4096]{1,0:T(8,128)(2,1)S(1)} %collective-permute-done.2.other_ref), custom_call_target="tpu_custom_call" | custom-call | tf_op jit(solution)/shard_map/chain/pallas_call | solution.py:585
  153.1 0.0 copy-done.2
  153.1 5.0 %grads.1 = (bf16[8,8,32,256]{3,2,1,0:T(8,128)(2,1)}, f32[8,8,32,256]{3,2,1,0:T(8,128)S(1)}) custom-call(s32[4,8]{1,0:T(4,128)S(1)} %bitcast.20, s32[4,8]{1,0:T(4,128)S(1)} %collective-permute-done.other_ids_ref, bf16[16,32,3072]{2,1,0:T(8,128)(2,1)S(1)} %copy-done.2, bf16[8,128,512]{2,1,0:T(8,128)(2,1)S(1)} %get-tuple-element.17.out_w_ref, ...), custom_call_target="tpu_custom_call" | custom-call | tf_op jit(solution)/shard_map/grads/pallas_call | solution.py:603
  158.0 0.1 collective-permute-start.3
  158.2 0.7 constant_dynamic-slice_fusion
  158.9 2.1 %collective-permute-done.3.swapped_ref = bf16[8,8,32,256]{3,2,1,0:T(8,128)(2,1)S(1)} collective-permute-done((bf16[8,8,32,256]{3,2,1,0:T(8,128)(2,1)}, bf16[8,8,32,256]{3,2,1,0:T(8,128)(2,1)S(1)}, u32[]{:S(2)}, u32[]{:S(2)}) %collective-permute-start.3) | collective-permute-done | bytes 1048608 | tf_op jit(solution)/shard_map/ppermute | solution.py:615
  160.9 0.2 add.13
  161.1 42.6 %all_to_all.23 = bf16[64,32,256]{2,1,0:T(8,128)(2,1)S(1)} all-to-all(bf16[64,32,256]{2,1,0:T(8,128)(2,1)S(1)} %bitcast.16), channel_id=1, replica_groups=mesh['xl'=2,'z'=8,'c'=2,'y'=4,'xh'=2] {'z','y','xh'}, dimensions={0} | all-to-all | bytes 2097152 | tf_op jit(solution)/shard_map/all_to_all | solution.py:627
  203.7 0.9 final.1
  (2 shorter events, 0.0 us)
Async XLA Ops:
  0.6 6.4 %collective-permute-start = (s32[4,8]{1,0:T(4,128)}, s32[4,8]{1,0:T(4,128)S(1)}, u32[]{:S(2)}, u32[]{:S(2)}) collective-permute-start(s32[4,8]{1,0:T(4,128)} %bitcast.17), channel_id=1, source_target_pairs={{0,128},{128,0},{1,129},{129,1},{2,130},{130,2},{3,131},{131,3},{4... | collective-permute-start | bytes 392 | tf_op jit(solution)/shard_map/ppermute | solution.py:495
  52.6 1.6 copy-start
  52.7 6.4 %collective-permute-start.1 = (bf16[16,32,1024]{2,1,0:T(8,128)(2,1)S(1)}, bf16[16,32,1024]{2,1,0:T(8,128)(2,1)S(1)}, u32[]{:S(2)}, u32[]{:S(2)}) collective-permute-start(bf16[16,32,1024]{2,1,0:T(8,128)(2,1)S(1)} %slice.8), channel_id=1, source_target_pairs={{0,8},{8,0},{1,9},{9,1},{2,10},{10,2},{3,11},{11,3},{4,12},{12,4},... | collective-permute-start | bytes 3145736 | tf_op jit(solution)/shard_map/ppermute | solution.py:529
  54.3 4.8 %copy-start.4 = (s32[1,4,8]{2,1,0:T(4,128)S(1)}, s32[1,4,8]{2,1,0:T(4,128)}, u32[]{:S(2)}) copy-start(s32[1,4,8]{2,1,0:T(4,128)} %param.8) | copy-start | bytes 388
  59.1 1.9 copy-start.1
  61.0 0.8 copy-start.3
  144.7 2.9 %collective-permute-start.2 = (bf16[128,4096]{1,0:T(8,128)(2,1)S(1)}, bf16[128,4096]{1,0:T(8,128)(2,1)S(1)}, u32[]{:S(2)}, u32[]{:S(2)}) collective-permute-start(bf16[128,4096]{1,0:T(8,128)(2,1)S(1)} %slice_bitcast_fusion.gram_ref), channel_id=1, source_target_pairs={{0,8},{8,0},{1,9},{9,1},{2,10},{10,2},{3,11},{11,3},{4,12},{12,4},... | collective-permute-start | bytes 3145736 | tf_op jit(solution)/shard_map/ppermute | solution.py:574
  146.1 7.0 %copy-start.2 = (bf16[16,32,3072]{2,1,0:T(8,128)(2,1)S(1)}, bf16[16,32,3072]{2,1,0:T(8,128)(2,1)}, u32[]{:S(2)}) copy-start(bf16[16,32,3072]{2,1,0:T(8,128)(2,1)} %copy-done) | copy-start | bytes 9437188
  158.0 2.9 %collective-permute-start.3 = (bf16[8,8,32,256]{3,2,1,0:T(8,128)(2,1)}, bf16[8,8,32,256]{3,2,1,0:T(8,128)(2,1)S(1)}, u32[]{:S(2)}, u32[]{:S(2)}) collective-permute-start(bf16[8,8,32,256]{3,2,1,0:T(8,128)(2,1)} %get-tuple-element.23), channel_id=1, source_target_pairs={{0,8},{8,0},{1,9},{9,1},{2,10},{10,2},{3,11},{11,3},{4,12},{12,4},... | collective-permute-start | bytes 3145736 | tf_op jit(solution)/shard_map/ppermute | solution.py:615

commit v15 on v13

--- a/solution.py
+++ b/solution.py
@@ -438,8 +438,8 @@
     def put(s, kind, value):
         low, high = value[:half].reshape(8, 32, R), value[half:].reshape(8, 32, R)
         at = slice(kind * R, (kind + 1) * R)
-        give_ref[:, s, :, at] = jnp.where(first_core, high, low).astype(BF16)
-        keep_ref[:, s, :, at] = jnp.where(first_core, low, high)
+        give_ref[s, :, :, at] = jnp.where(first_core, high, low).astype(BF16)
+        keep_ref[s, :, :, at] = jnp.where(first_core, low, high)
 
     def both(part, *args):
         return jnp.concatenate(
@@ -468,9 +468,9 @@
 
 
 def final_kernel(parts_ref, gain_ref, in_ref, out_ref):
-    total = parts_ref[0].astype(F32)
+    total = parts_ref[:, 0].astype(F32)
     for i in range(1, 8):
-        total = total + parts_ref[i].astype(F32)
+        total = total + parts_ref[:, i].astype(F32)
     gain = gain_ref[...].T
     for j in range(8):
         scale = gain[(j % 4) * 32 : (j % 4) * 32 + 32, j // 4 : j // 4 + 1]
@@ -593,8 +593,8 @@
     give, keep = pl.pallas_call(
         grads_kernel,
         out_shape=(
-            jax.ShapeDtypeStruct((8, NS, 32, 2 * R), BF16),
-            jax.ShapeDtypeStruct((8, NS, 32, 2 * R), F32),
+            jax.ShapeDtypeStruct((NS, 8, 32, 2 * R), BF16),
+            jax.ShapeDtypeStruct((NS, 8, 32, 2 * R), F32),
         ),
         in_specs=[SMEM, SMEM] + [VMEM] * 5,
         out_specs=(VMEM, VMEM),
@@ -605,7 +605,7 @@
     swapped = lax.ppermute(give, "c", SWAP)
     total = pl.pallas_call(
         add_kernel,
-        out_shape=jax.ShapeDtypeStruct((8, NS, 32, 2 * R), BF16),
+        out_shape=jax.ShapeDtypeStruct((NS, 8, 32, 2 * R), BF16),
         in_specs=[VMEM, VMEM],
         out_specs=VMEM,
         compiler_params=PARAMS,
@@ -614,7 +614,7 @@
     block = (xl * NS + z) * 2 + core
     gain = lax.dynamic_slice_in_dim(norm_gain[0], block * half, half, 0)
     total, gain = lax.optimization_barrier((total, gain))
-    total = lax.all_to_all(total, ("z",) + SECTION, 0, 0, tiled=True)
+    total = lax.all_to_all(total, SECTION + ("z",), 0, 0, tiled=True)
     grad_in, grad_out = pl.pallas_call(
         final_kernel,
         out_shape=(

time: 199 us -> 199 us (level)
  no operation moved by 1% of the time
where the time goes in v15:
time: 199 us
  blocking collectives  166 us (83%)
  Pallas kernels  23.9 us (12%)
  waiting for transfers between devices  4.22 us (2%)
  starting transfers between devices  2.08 us (1%)
    all_to_all x1, blocking collectives, body(): got = lax.all_to_all(send, PLANE, 0, 0, tiled=True)  45.9 us
    all_to_all x1, blocking collectives, body(): parts = lax.all_to_all(parts, PLANE, 0, 0, tiled=True)  45.2 us
    all_to_all x1, blocking collectives, body(): total = lax.all_to_all(total, SECTION + ('z',), 0, 0, tiled=True)  41.2 us
    all_to_all x1, blocking collectives, body(): sums = lax.all_to_all(sums, PLANE, 0, 0, tiled=True)  34 us
    pallas_call x1, Pallas kernels, body(): pl.pallas_call(functools.partial(chain_kernel, width), out_shape=(jax.Sha...  5.47 us
    pallas_call x1, Pallas kernels, body(): pl.pallas_call(grads_kernel, out_shape=(jax.ShapeDtypeStruct((NS, 8, 32,...  4.96 us
    pallas_call x1, Pallas kernels, body(): pl.pallas_call(pack_kernel, grid=(2,), in_specs=[pl.BlockSpec((64, wide),...  4.81 us
    pallas_call x1, Pallas kernels, body(): pl.pallas_call(project_kernel, out_shape=(jax.ShapeDtypeStruct((16, 2 * T...  4.72 us
  transfers between devices with their start and end apart: 4, of which 2 were waited for; matrix products, arithmetic and copies ran while one was open for 0% of the time, Pallas kernels for 4%

profile of v15, /device:TPU:32, one launch (start us, length us, event | category | flops | bytes accessed | tf_op | source)
XLA Modules:
  0.0 198.8 jit_solution(3813724529274606819)
XLA Ops:
  0.6 1.6 collective-permute-start
  2.2 4.8 %pack.1 = bf16[16,32,3072]{2,1,0:T(8,128)(2,1)} custom-call(bf16[64,8192]{1,0:T(8,128)(2,1)} %bitcast.27, bf16[64,8192]{1,0:T(8,128)(2,1)} %bitcast.28, bf16[128,8192]{1,0:T(8,128)(2,1)} %bitcast.15, bf16[2,8,2,8,32,128]{5,4,3,2,1,0:T(8,128)(2,1)} %bitcast.17, f32[2,8,2,2,128]{4,3,2,1,0:T(2,128)} %bitcast.21, bf16[4,32,8192]{2,1,0:T(8,128)(2,1)} %first_ref.3), custom_call_target="tpu_custom_call" | custom-call | tf_op jit(solution)/shard_map/pack/pallas_call | solution.py:500
  7.0 0.0 copy-start.3
  7.0 0.0 collective-permute-done.other_ids_ref
  7.0 0.0 copy-start.1
  7.0 0.0 copy-start.2
  7.0 45.9 %all_to_all.20.after_ref.got_ref = bf16[16,32,3072]{2,1,0:T(8,128)(2,1)S(1)} all-to-all(bf16[16,32,3072]{2,1,0:T(8,128)(2,1)} %pack.1), channel_id=1, replica_groups=mesh['xl'=2,'z'=8,'c'=2,'y'=4,'xh'=2] {'xl','y','xh'}, dimensions={0} | all-to-all | bytes 6291456 | tf_op jit(solution)/shard_map/all_to_all | solution.py:527
  52.9 0.0 copy-start
  52.9 0.1 slice.8
  53.0 0.1 collective-permute-start.1
  53.1 0.0 copy-done.3
  53.2 0.0 copy-done.1
  53.2 0.0 copy-done.2
  53.2 1.4 copy-done
  54.5 1.2 start.1.start_ref
  55.8 0.0 collective-permute-done.1.other_ref
  55.8 0.0 copy-done.4
  55.8 4.7 %project.1 = (bf16[16,16,6528]{2,1,0:T(8,128)(2,1)S(1)}, bf16[8,128,512]{2,1,0:T(8,128)(2,1)S(1)}, bf16[8,512,128]{2,1,0:T(8,128)(2,1)S(1)}) custom-call(s32[4,8]{1,0:T(4,128)S(1)} %bitcast.23, s32[4,8]{1,0:T(4,128)S(1)} %collective-permute-done.other_ids_ref, bf16[16,32,3072]{2,1,0:T(8,128)(2,1)S(1)} %all_to_all.20.after_ref.got_ref, ...), custom_call_target="tpu_custom_call" | custom-call | flops 2000000000 | bytes 9000000 | tf_op jit(solution)/shard_map/project/pallas_call | solution.py:538
  60.5 45.2 %all_to_all.21.parts_ref = bf16[16,16,6528]{2,1,0:T(8,128)(2,1)S(1)} all-to-all(bf16[16,16,6528]{2,1,0:T(8,128)(2,1)S(1)} %get-tuple-element.19), channel_id=1, replica_groups=mesh['xl'=2,'z'=8,'c'=2,'y'=4,'xh'=2] {'xl','y','xh'}, dimensions={0} | all-to-all | bytes 6684672 | tf_op jit(solution)/shard_map/all_to_all | solution.py:552
  105.8 0.4 sums.1
  106.2 34.0 %all_to_all.22.sums_ref = bf16[16,16,4480]{2,1,0:T(8,128)(2,1)S(1)} all-to-all(bf16[16,16,4480]{2,1,0:T(8,128)(2,1)S(1)} %sums.1), channel_id=1, replica_groups=mesh['xl'=2,'z'=8,'c'=2,'y'=4,'xh'=2] {'xl','y','xh'}, dimensions={0} | all-to-all | bytes 4587520 | tf_op jit(solution)/shard_map/all_to_all | solution.py:561
  140.2 0.1 slice_bitcast_fusion.gram_ref
  140.3 0.3 collective-permute-start.2
  140.6 1.2 gather.1.base_ref
  141.7 1.5 collective-permute-done.2.other_ref
  143.2 5.5 %chain.1 = (bf16[256,2048]{1,0:T(8,128)(2,1)S(1)}, f32[256,128]{1,0:T(8,128)S(1)}) custom-call(bf16[16,16,6528]{2,1,0:T(8,128)(2,1)S(1)} %all_to_all.21.parts_ref, f32[256,4736]{1,0:T(8,128)S(1)} %gather.1.base_ref, bf16[128,4096]{1,0:T(8,128)(2,1)S(1)} %slice_bitcast_fusion.gram_ref, bf16[128,4096]{1,0:T(8,128)(2,1)S(1)} %collective-permute-done.2.other_ref), custom_call_target="tpu_custom_call" | custom-call | tf_op jit(solution)/shard_map/chain/pallas_call | solution.py:575
  148.7 5.0 %grads.1 = (bf16[8,8,32,256]{3,2,1,0:T(8,128)(2,1)}, f32[8,8,32,256]{3,2,1,0:T(8,128)S(1)}) custom-call(s32[4,8]{1,0:T(4,128)S(1)} %bitcast.25, s32[4,8]{1,0:T(4,128)S(1)} %collective-permute-done.other_ids_ref, bf16[16,32,3072]{2,1,0:T(8,128)(2,1)S(1)} %all_to_all.20.after_ref.got_ref, bf16[8,128,512]{2,1,0:T(8,128)(2,1)S(1)} %get-tuple-element.17.out_w_ref, ...), custom_call_target="tpu_custom_call" | custom-call | tf_op jit(solution)/shard_map/grads/pallas_call | solution.py:593
  153.7 0.1 collective-permute-start.3
  153.8 2.7 %collective-permute-done.3.swapped_ref = bf16[8,8,32,256]{3,2,1,0:T(8,128)(2,1)S(1)} collective-permute-done((bf16[8,8,32,256]{3,2,1,0:T(8,128)(2,1)}, bf16[8,8,32,256]{3,2,1,0:T(8,128)(2,1)S(1)}, u32[]{:S(2)}, u32[]{:S(2)}) %collective-permute-start.3) | collective-permute-done | bytes 1048608 | tf_op jit(solution)/shard_map/ppermute | solution.py:605
  156.5 0.2 add.13
  156.7 41.2 %all_to_all.23 = bf16[64,32,256]{2,1,0:T(8,128)(2,1)S(1)} all-to-all(bf16[64,32,256]{2,1,0:T(8,128)(2,1)S(1)} %bitcast.20), channel_id=1, replica_groups=mesh['xl'=2,'z'=8,'c'=2,'y'=4,'xh'=2] {'y','xh','z'}, dimensions={0} | all-to-all | bytes 2097152 | tf_op jit(solution)/shard_map/all_to_all | solution.py:617
  197.9 0.9 final.1
  (2 shorter events, 0.0 us)
Async XLA Ops:
  0.6 6.4 %collective-permute-start = (s32[4,8]{1,0:T(4,128)}, s32[4,8]{1,0:T(4,128)S(1)}, u32[]{:S(2)}, u32[]{:S(2)}) collective-permute-start(s32[4,8]{1,0:T(4,128)} %bitcast.22), channel_id=1, source_target_pairs={{0,128},{128,0},{1,129},{129,1},{2,130},{130,2},{3,131},{131,3},{4... | collective-permute-start | bytes 392 | tf_op jit(solution)/shard_map/ppermute | solution.py:494
  7.0 46.1 %copy-start.3 = (f32[1,8192]{1,0:T(1,128)S(1)}, f32[1,8192]{1,0:T(1,128)}, u32[]{:S(2)}) copy-start(f32[1,8192]{1,0:T(1,128)} %gain_ref.1) | copy-start | bytes 98308
  7.0 46.1 %copy-start.1 = (bf16[1,8192,128]{2,1,0:T(8,128)(2,1)S(1)}, bf16[1,8192,128]{2,1,0:T(8,128)(2,1)}, u32[]{:S(2)}) copy-start(bf16[1,8192,128]{2,1,0:T(8,128)(2,1)} %param.12) | copy-start | bytes 6291460
  7.0 46.1 %copy-start.2 = (bf16[4,32,8192]{2,1,0:T(8,128)(2,1)S(1)}, bf16[4,32,8192]{2,1,0:T(8,128)(2,1)}, u32[]{:S(2)}) copy-start(bf16[4,32,8192]{2,1,0:T(8,128)(2,1)} %first_ref.3) | copy-start | bytes 6291460
  52.9 1.6 copy-start
  53.0 2.8 %collective-permute-start.1 = (bf16[16,32,1024]{2,1,0:T(8,128)(2,1)S(1)}, bf16[16,32,1024]{2,1,0:T(8,128)(2,1)S(1)}, u32[]{:S(2)}, u32[]{:S(2)}) collective-permute-start(bf16[16,32,1024]{2,1,0:T(8,128)(2,1)S(1)} %slice.8), channel_id=1, source_target_pairs={{0,8},{8,0},{1,9},{9,1},{2,10},{10,2},{3,11},{11,3},{4,12},{12,4},... | collective-permute-start | bytes 3145736 | tf_op jit(solution)/shard_map/ppermute | solution.py:528
  54.5 1.3 copy-start.4
  140.3 2.9 %collective-permute-start.2 = (bf16[128,4096]{1,0:T(8,128)(2,1)S(1)}, bf16[128,4096]{1,0:T(8,128)(2,1)S(1)}, u32[]{:S(2)}, u32[]{:S(2)}) collective-permute-start(bf16[128,4096]{1,0:T(8,128)(2,1)S(1)} %slice_bitcast_fusion.gram_ref), channel_id=1, source_target_pairs={{0,8},{8,0},{1,9},{9,1},{2,10},{10,2},{3,11},{11,3},{4,12},{12,4},... | collective-permute-start | bytes 3145736 | tf_op jit(solution)/shard_map/ppermute | solution.py:564
  153.7 2.9 %collective-permute-start.3 = (bf16[8,8,32,256]{3,2,1,0:T(8,128)(2,1)}, bf16[8,8,32,256]{3,2,1,0:T(8,128)(2,1)S(1)}, u32[]{:S(2)}, u32[]{:S(2)}) collective-permute-start(bf16[8,8,32,256]{3,2,1,0:T(8,128)(2,1)} %get-tuple-element.23), channel_id=1, source_target_pairs={{0,8},{8,0},{1,9},{9,1},{2,10},{10,2},{3,11},{11,3},{4,12},{12,4},... | collective-permute-start | bytes 3145736 | tf_op jit(solution)/shard_map/ppermute | solution.py:605

commit v16 on v13

--- a/solution.py
+++ b/solution.py
@@ -126,12 +126,17 @@
             ]
 
 
-def start_kernel(first_ref, w_out_ref, w_in_ref, gain_ref, after_ref, start_ref):
+def start_in_kernel(first_ref, w_in_ref, gain_ref, after_ref, start_ref):
     del after_ref
     flat = first_ref[...].reshape(R, first_ref.shape[2])
     scaled = (flat.astype(F32) * gain_ref[...]).astype(BF16)
-    start_ref[:, :R] = dot(scaled, w_in_ref[...]).astype(BF16)
-    start_ref[:, R:] = dot_t(flat, w_out_ref[...]).astype(BF16)
+    start_ref[...] = dot(scaled, w_in_ref[...]).astype(BF16)
+
+
+def start_out_kernel(first_ref, w_out_ref, after_ref, start_ref):
+    del after_ref
+    flat = first_ref[...].reshape(R, first_ref.shape[2])
+    start_ref[...] = dot_t(flat, w_out_ref[...]).astype(BF16)
 
 
 def stores(got_ref, s, at, cols):
@@ -197,7 +202,8 @@
 
 
 def project_kernel(
-    ids_ref, other_ids_ref, got_ref, other_ref, start_ref, send_ref, out_w_ref, in_w_ref, wide_ref
+    ids_ref, other_ids_ref, got_ref, other_ref, start_in_ref, start_out_ref,
+    send_ref, out_w_ref, in_w_ref, wide_ref,
 ):
     cols = in_w_ref.shape[1]
     first_core = lax.axis_index("c") == 0
@@ -271,7 +277,8 @@
     for g in range(8):
         at = START + g * 2 * R
         for q in range(16):
-            send_ref[q, :, at : at + 2 * R] = start_ref[g * 16 : (g + 1) * 16, :]
+            send_ref[q, :, at : at + R] = start_in_ref[g * 16 : (g + 1) * 16, :]
+            send_ref[q, :, at + R : at + 2 * R] = start_out_ref[g * 16 : (g + 1) * 16, :]
 
 
 def sum_kernel(parts_ref, send_ref):
@@ -526,15 +533,22 @@
     send, other_ids = lax.optimization_barrier((send, other_ids))
     got = lax.all_to_all(send, PLANE, 0, 0, tiled=True)
     other = lax.ppermute(got[:, :, W_LANE:], "c", SWAP)
-    start = pl.pallas_call(
-        start_kernel,
-        out_shape=jax.ShapeDtypeStruct((R, 2 * R), BF16),
-        in_specs=[VMEM, VMEM, VMEM, VMEM, pl.BlockSpec(memory_space=pl.ANY)],
-        out_specs=VMEM,
-        compiler_params=PARAMS,
-        cost_estimate=pl.CostEstimate(flops=600000000, bytes_accessed=7000000, transcendentals=0),
-        name="start",
-    )(first_input, w_out, w_in, norm_gain, got)
+
+    def start(kernel, name, *arrays):
+        return pl.pallas_call(
+            kernel,
+            out_shape=jax.ShapeDtypeStruct((R, R), BF16),
+            in_specs=[VMEM] * len(arrays) + [pl.BlockSpec(memory_space=pl.ANY)],
+            out_specs=VMEM,
+            compiler_params=PARAMS,
+            cost_estimate=pl.CostEstimate(
+                flops=300000000, bytes_accessed=4000000, transcendentals=0
+            ),
+            name=name,
+        )(*arrays, got)
+
+    start_in = start(start_in_kernel, "start_in", first_input, w_in, norm_gain)
+    start_out = start(start_out_kernel, "start_out", first_input, w_out)
     parts, out_w, in_w = pl.pallas_call(
         project_kernel,
         out_shape=(
@@ -542,13 +556,13 @@
             jax.ShapeDtypeStruct((NS, R, cols), BF16),
             jax.ShapeDtypeStruct((NS, cols, R), BF16),
         ),
-        in_specs=[SMEM, SMEM, VMEM, VMEM, VMEM],
+        in_specs=[SMEM, SMEM, VMEM, VMEM, VMEM, VMEM],
         out_specs=(VMEM, VMEM, VMEM),
         scratch_shapes=[pltpu.VMEM((R, 2 * SPLIT * BLK), F32)],
         compiler_params=PARAMS,
         cost_estimate=pl.CostEstimate(flops=2000000000, bytes_accessed=9000000, transcendentals=0),
         name="project",
-    )(ids, other_ids, got, other, start)
+    )(ids, other_ids, got, other, start_in, start_out)
     parts = lax.all_to_all(parts, PLANE, 0, 0, tiled=True)
     sums = pl.pallas_call(
         sum_kernel,

time: 199 us -> 198 us (level)
  no operation moved by 1% of the time
where the time goes in v16:
time: 198 us
  blocking collectives  165 us (83%)
  Pallas kernels  24.1 us (12%)
  waiting for transfers between devices  4.23 us (2%)
  starting transfers between devices  2.07 us (1%)
    all_to_all x1, blocking collectives, body(): got = lax.all_to_all(send, PLANE, 0, 0, tiled=True)  45.8 us
    all_to_all x1, blocking collectives, body(): parts = lax.all_to_all(parts, PLANE, 0, 0, tiled=True)  45.1 us
    all_to_all x1, blocking collectives, body(): total = lax.all_to_all(total, ('z',) + SECTION, 0, 0, tiled=True)  41.5 us
    all_to_all x1, blocking collectives, body(): sums = lax.all_to_all(sums, PLANE, 0, 0, tiled=True)  32.8 us
    pallas_call x1, Pallas kernels, body(): pl.pallas_call(functools.partial(chain_kernel, width), out_shape=(jax.Sha...  5.47 us
    pallas_call x1, Pallas kernels, body(): pl.pallas_call(grads_kernel, out_shape=(jax.ShapeDtypeStruct((8, NS, 32,...  4.96 us
    pallas_call x1, Pallas kernels, body(): pl.pallas_call(pack_kernel, grid=(2,), in_specs=[pl.BlockSpec((64, wide),...  4.81 us
    pallas_call x1, Pallas kernels, body(): pl.pallas_call(project_kernel, out_shape=(jax.ShapeDtypeStruct((16, 2 * T...  4.79 us
  transfers between devices with their start and end apart: 4, of which 2 were waited for; matrix products, arithmetic and copies ran while one was open for 0% of the time, Pallas kernels for 4%

profile of v16, /device:TPU:32, one launch (start us, length us, event | category | flops | bytes accessed | tf_op | source)
XLA Modules:
  0.0 197.8 jit_solution(18405734726150325771)
XLA Ops:
  0.6 1.6 collective-permute-start
  2.2 4.8 %pack.1 = bf16[16,32,3072]{2,1,0:T(8,128)(2,1)} custom-call(bf16[64,8192]{1,0:T(8,128)(2,1)} %bitcast.27, bf16[64,8192]{1,0:T(8,128)(2,1)} %bitcast.28, bf16[128,8192]{1,0:T(8,128)(2,1)} %bitcast.15, bf16[2,8,2,8,32,128]{5,4,3,2,1,0:T(8,128)(2,1)} %bitcast.17, f32[2,8,2,2,128]{4,3,2,1,0:T(2,128)} %bitcast.21, bf16[4,32,8192]{2,1,0:T(8,128)(2,1)} %first_ref.5), custom_call_target="tpu_custom_call" | custom-call | tf_op jit(solution)/shard_map/pack/pallas_call | solution.py:507
  7.0 0.0 collective-permute-done.other_ids_ref
  7.0 45.8 %all_to_all.20.after_ref.got_ref = bf16[16,32,3072]{2,1,0:T(8,128)(2,1)S(1)} all-to-all(bf16[16,32,3072]{2,1,0:T(8,128)(2,1)} %pack.1), channel_id=1, replica_groups=mesh['xl'=2,'z'=8,'c'=2,'y'=4,'xh'=2] {'xl','y','xh'}, dimensions={0} | all-to-all | bytes 6291456 | tf_op jit(solution)/shard_map/all_to_all | solution.py:534
  52.8 0.1 slice.8
  52.9 0.0 copy-start.2
  52.9 0.0 copy-start.3
  52.9 0.1 collective-permute-start.1
  53.0 0.0 copy-done.1
  53.0 1.4 copy-done
  54.4 0.7 start_out.1.start_out_ref
  55.1 0.0 copy-done.2
  55.1 0.0 copy-done.3
  55.1 0.0 copy-start.4
  55.1 0.7 start_in.1.start_in_ref
  55.8 0.0 collective-permute-done.1.other_ref
  55.8 0.0 copy-done.4
  55.9 4.8 %project.1 = (bf16[16,16,6528]{2,1,0:T(8,128)(2,1)S(1)}, bf16[8,128,512]{2,1,0:T(8,128)(2,1)S(1)}, bf16[8,512,128]{2,1,0:T(8,128)(2,1)S(1)}) custom-call(s32[4,8]{1,0:T(4,128)S(1)} %bitcast.23, s32[4,8]{1,0:T(4,128)S(1)} %collective-permute-done.other_ids_ref, bf16[16,32,3072]{2,1,0:T(8,128)(2,1)S(1)} %all_to_all.20.after_ref.got_ref, ...), custom_call_target="tpu_custom_call" | custom-call | flops 2000000000 | bytes 9000000 | tf_op jit(solution)/shard_map/project/pallas_call | solution.py:552
  60.7 45.1 %all_to_all.21.parts_ref = bf16[16,16,6528]{2,1,0:T(8,128)(2,1)S(1)} all-to-all(bf16[16,16,6528]{2,1,0:T(8,128)(2,1)S(1)} %get-tuple-element.19), channel_id=1, replica_groups=mesh['xl'=2,'z'=8,'c'=2,'y'=4,'xh'=2] {'xl','y','xh'}, dimensions={0} | all-to-all | bytes 6684672 | tf_op jit(solution)/shard_map/all_to_all | solution.py:566
  105.7 0.4 sums.1
  106.1 32.8 %all_to_all.22.sums_ref = bf16[16,16,4480]{2,1,0:T(8,128)(2,1)S(1)} all-to-all(bf16[16,16,4480]{2,1,0:T(8,128)(2,1)S(1)} %sums.1), channel_id=1, replica_groups=mesh['xl'=2,'z'=8,'c'=2,'y'=4,'xh'=2] {'xl','y','xh'}, dimensions={0} | all-to-all | bytes 4587520 | tf_op jit(solution)/shard_map/all_to_all | solution.py:575
  138.9 0.1 slice_bitcast_fusion.gram_ref
  139.0 0.3 collective-permute-start.2
  139.3 1.2 gather.1.base_ref
  140.4 1.5 collective-permute-done.2.other_ref
  141.9 5.5 %chain.1 = (bf16[256,2048]{1,0:T(8,128)(2,1)S(1)}, f32[256,128]{1,0:T(8,128)S(1)}) custom-call(bf16[16,16,6528]{2,1,0:T(8,128)(2,1)S(1)} %all_to_all.21.parts_ref, f32[256,4736]{1,0:T(8,128)S(1)} %gather.1.base_ref, bf16[128,4096]{1,0:T(8,128)(2,1)S(1)} %slice_bitcast_fusion.gram_ref, bf16[128,4096]{1,0:T(8,128)(2,1)S(1)} %collective-permute-done.2.other_ref), custom_call_target="tpu_custom_call" | custom-call | tf_op jit(solution)/shard_map/chain/pallas_call | solution.py:589
  147.4 5.0 %grads.1 = (bf16[8,8,32,256]{3,2,1,0:T(8,128)(2,1)}, f32[8,8,32,256]{3,2,1,0:T(8,128)S(1)}) custom-call(s32[4,8]{1,0:T(4,128)S(1)} %bitcast.25, s32[4,8]{1,0:T(4,128)S(1)} %collective-permute-done.other_ids_ref, bf16[16,32,3072]{2,1,0:T(8,128)(2,1)S(1)} %all_to_all.20.after_ref.got_ref, bf16[8,128,512]{2,1,0:T(8,128)(2,1)S(1)} %get-tuple-element.17.out_w_ref, ...), custom_call_target="tpu_custom_call" | custom-call | tf_op jit(solution)/shard_map/grads/pallas_call | solution.py:607
  152.4 0.1 collective-permute-start.3
  152.5 2.7 %collective-permute-done.3.swapped_ref = bf16[8,8,32,256]{3,2,1,0:T(8,128)(2,1)S(1)} collective-permute-done((bf16[8,8,32,256]{3,2,1,0:T(8,128)(2,1)}, bf16[8,8,32,256]{3,2,1,0:T(8,128)(2,1)S(1)}, u32[]{:S(2)}, u32[]{:S(2)}) %collective-permute-start.3) | collective-permute-done | bytes 1048608 | tf_op jit(solution)/shard_map/ppermute | solution.py:619
  155.2 0.2 add.13
  155.4 41.5 %all_to_all.23 = bf16[64,32,256]{2,1,0:T(8,128)(2,1)S(1)} all-to-all(bf16[64,32,256]{2,1,0:T(8,128)(2,1)S(1)} %bitcast.20), channel_id=1, replica_groups=mesh['xl'=2,'z'=8,'c'=2,'y'=4,'xh'=2] {'z','y','xh'}, dimensions={0} | all-to-all | bytes 2097152 | tf_op jit(solution)/shard_map/all_to_all | solution.py:631
  196.9 0.9 final.1
  (3 shorter events, 0.0 us)
Async XLA Ops:
  0.6 6.4 %collective-permute-start = (s32[4,8]{1,0:T(4,128)}, s32[4,8]{1,0:T(4,128)S(1)}, u32[]{:S(2)}, u32[]{:S(2)}) collective-permute-start(s32[4,8]{1,0:T(4,128)} %bitcast.22), channel_id=1, source_target_pairs={{0,128},{128,0},{1,129},{129,1},{2,130},{130,2},{3,131},{131,3},{4... | collective-permute-start | bytes 392 | tf_op jit(solution)/shard_map/ppermute | solution.py:501
  7.0 46.0 %copy-start.1 = (bf16[1,128,8192]{2,1,0:T(8,128)(2,1)S(1)}, bf16[1,128,8192]{2,1,0:T(8,128)(2,1)}, u32[]{:S(2)}) copy-start(bf16[1,128,8192]{2,1,0:T(8,128)(2,1)} %param.13) | copy-start | bytes 6291460
  52.8 1.6 copy-start
  52.9 2.2 %copy-start.2 = (bf16[1,8192,128]{2,1,0:T(8,128)(2,1)S(1)}, bf16[1,8192,128]{2,1,0:T(8,128)(2,1)}, u32[]{:S(2)}) copy-start(bf16[1,8192,128]{2,1,0:T(8,128)(2,1)} %param.12) | copy-start | bytes 6291460
  52.9 2.2 %copy-start.3 = (f32[1,8192]{1,0:T(1,128)S(1)}, f32[1,8192]{1,0:T(1,128)}, u32[]{:S(2)}) copy-start(f32[1,8192]{1,0:T(1,128)} %gain_ref.1) | copy-start | bytes 98308
  52.9 2.9 %collective-permute-start.1 = (bf16[16,32,1024]{2,1,0:T(8,128)(2,1)S(1)}, bf16[16,32,1024]{2,1,0:T(8,128)(2,1)S(1)}, u32[]{:S(2)}, u32[]{:S(2)}) collective-permute-start(bf16[16,32,1024]{2,1,0:T(8,128)(2,1)S(1)} %slice.8), channel_id=1, source_target_pairs={{0,8},{8,0},{1,9},{9,1},{2,10},{10,2},{3,11},{11,3},{4,12},{12,4},... | collective-permute-start | bytes 3145736 | tf_op jit(solution)/shard_map/ppermute | solution.py:535
  55.1 0.7 copy-start.4
  139.0 2.9 %collective-permute-start.2 = (bf16[128,4096]{1,0:T(8,128)(2,1)S(1)}, bf16[128,4096]{1,0:T(8,128)(2,1)S(1)}, u32[]{:S(2)}, u32[]{:S(2)}) collective-permute-start(bf16[128,4096]{1,0:T(8,128)(2,1)S(1)} %slice_bitcast_fusion.gram_ref), channel_id=1, source_target_pairs={{0,8},{8,0},{1,9},{9,1},{2,10},{10,2},{3,11},{11,3},{4,12},{12,4},... | collective-permute-start | bytes 3145736 | tf_op jit(solution)/shard_map/ppermute | solution.py:578
  152.4 2.9 %collective-permute-start.3 = (bf16[8,8,32,256]{3,2,1,0:T(8,128)(2,1)}, bf16[8,8,32,256]{3,2,1,0:T(8,128)(2,1)S(1)}, u32[]{:S(2)}, u32[]{:S(2)}) collective-permute-start(bf16[8,8,32,256]{3,2,1,0:T(8,128)(2,1)} %get-tuple-element.23), channel_id=1, source_target_pairs={{0,8},{8,0},{1,9},{9,1},{2,10},{10,2},{3,11},{11,3},{4,12},{12,4},... | collective-permute-start | bytes 3145736 | tf_op jit(solution)/shard_map/ppermute | solution.py:619
